TPU v7x, 32 devices: a whole 2x2x4 slice. The times are simulated.
32 devices in a mesh: tp: 4 (over y, x), dp: 8 (over z, core).
Axes of the slice: x: 2, y: 2, z: 4, core: 2. Of those that a mesh axis runs over, the one named last changes fastest.
Arguments:
- tokens: bfloat16 [2, 8, 256, 2048], P(None, 'dp', 'tp'), may hold values from -6 to 6
- cotangent: bfloat16 [2, 8, 256, 2048], P(None, 'dp', 'tp'), may hold values from -6 to 6
- routes: int32 [2, 8, 256, 8], P(None, 'dp'), may hold values from 0 to 15, all different within a row; in each aligned block of 256 rows (0 to 255, 256 to 511, ..., all dimensions but the last counted through in order) at most 160 rows name the same one
- lengths: int32 [2, 8, 2], P(None, 'dp'), may hold values from 0 to 256, as said below
- attn_gain: float32 [2048], replicated, may hold values from 0.5 to 1.5
- qkv_weight: bfloat16 [2048, 3, 2048], P(None, None, 'tp'), may hold values from -0.125 to 0.125
- qk_gain: float32 [2, 2048], P(None, 'tp'), may hold values from 0.5 to 1.5
- out_weight: bfloat16 [2048, 2048], P('tp'), may hold values from -0.5 to 0.5
- moe_gain: float32 [2048], replicated, may hold values from 0.5 to 1.5
- router: bfloat16 [2048, 16], replicated, may hold values from -0.0625 to 0.0625
- w_gateup: bfloat16 [16, 2048, 2, 1024], P('dp', None, None, 'tp'), may hold values from -0.125 to 0.125
- w_down: bfloat16 [16, 1024, 2048], P('dp', 'tp'), may hold values from -6 to 6
Outputs:
- out: bfloat16 [2, 8, 256, 2048], P(None, 'dp', 'tp')
- token_grad: bfloat16 [2, 8, 256, 2048], P(None, 'dp', 'tp')
- attn_gain_grad: float32 [2048], replicated
- qkv_weight_grad: float32 [2048, 3, 2048], P(None, None, 'tp')
- qk_gain_grad: float32 [2, 2048], P(None, 'tp')
- out_weight_grad: float32 [2048, 2048], P('tp')
- moe_gain_grad: float32 [2048], replicated
- router_grad: float32 [2048, 16], replicated
- gateup_grad: float32 [16, 2048, 2, 1024], P('dp', None, None, 'tp')
- down_grad: float32 [16, 1024, 2048], P('dp', 'tp')
Inputs may be any that keep to these rules, and one draw needn't show every extreme that they name: `lengths`: row (m, g) gives block (m, g): up to two sequences laid from the block's first row, a zero length standing for none; the shorter one and the padding after both cover fewer than 64 rows together. In every draw some block holds one sequence of all 256 rows. `routes`: each row names 8 different experts; the 256 rows of one block name one expert at most 160 times.
All inputs are finite; a program needn't handle non-finite values.
Results may differ from a plain program's by a relative error of at most 0.025.
Values may be sent and summed in bfloat16 or wider, within the bound.
No kernel may reach another device: no remote copies, remote signals or barrier semaphores. Data moves between devices by JAX's collectives and lax.ppermute only.
A program may use at most 384 MiB of HBM per device.

v0:
```python
import jax
import jax.numpy as jnp
from jax import lax
from jax.sharding import PartitionSpec as P

HD = 128
TOP = 8


EPSILON = 1e-05


def rms_scale(values):
    return lax.rsqrt(jnp.mean(values * values, axis=-1, keepdims=True) + EPSILON)


def layout(lengths_row, group_rows):
    places = jnp.arange(group_rows, dtype=jnp.int32)
    first_len = lengths_row[0]
    live_end = lengths_row[0] + lengths_row[1]
    segment = (places >= first_len).astype(jnp.int32) + (places >= live_end).astype(jnp.int32)
    starts = jnp.where(segment == 0, 0, jnp.where(segment == 1, first_len, live_end))
    return (places, segment, places - starts)


def rotary(position, half_dim):
    frequency = jnp.exp(
        jnp.arange(half_dim, dtype=jnp.float32) * (-2.0 * jnp.log(10000.0) / (2 * half_dim))
    )
    angles = position.astype(jnp.float32)[:, None] * frequency[None, :]
    return (jnp.cos(angles)[:, None, :], jnp.sin(angles)[:, None, :])


def rotate(values, cosine, sine_table):
    half_dim = values.shape[-1] // 2
    upper_half = values[..., :half_dim]
    lower_half = values[..., half_dim:]
    return jnp.concatenate(
        [
            upper_half * cosine - lower_half * sine_table,
            lower_half * cosine + upper_half * sine_table,
        ],
        axis=-1,
    )


def rotate_back(grads, cosine, sine_table):
    half_dim = grads.shape[-1] // 2
    upper_half = grads[..., :half_dim]
    lower_half = grads[..., half_dim:]
    return jnp.concatenate(
        [
            upper_half * cosine + lower_half * sine_table,
            lower_half * cosine - upper_half * sine_table,
        ],
        axis=-1,
    )


def contract(left, right, left_dim, right_dim):
    return lax.dot_general(
        left, right, (((left_dim,), (right_dim,)), ((), ())), preferred_element_type=jnp.float32
    )


def inner_of(rows_in, gate_up):
    quarter = gate_up.shape[2]
    return jnp.dot(
        rows_in, gate_up.reshape(gate_up.shape[0], 2 * quarter), preferred_element_type=jnp.float32
    )


def expert_forward(rows_in, gate_up, down_proj):
    quarter = down_proj.shape[0]
    inner_pre = inner_of(rows_in, gate_up)
    active = (jax.nn.silu(inner_pre[:, :quarter]) * inner_pre[:, quarter:]).astype(jnp.bfloat16)
    return (
        inner_pre,
        jnp.dot(active, down_proj, preferred_element_type=jnp.float32).astype(jnp.bfloat16),
    )


def expert_backward(rows_in, inner_pre, grads_out, gate_up, down_proj):
    quarter = down_proj.shape[0]
    gate_pre = inner_pre[:, :quarter]
    up_pre = inner_pre[:, quarter:]
    sigmoid_gate = jax.nn.sigmoid(gate_pre)
    silu_gate = gate_pre * sigmoid_gate
    active = (silu_gate * up_pre).astype(jnp.bfloat16)
    d_active = contract(grads_out, down_proj, 1, 1)
    d_gate = d_active * up_pre * sigmoid_gate * (1.0 + gate_pre * (1.0 - sigmoid_gate))
    d_up = d_active * silu_gate
    d_inner = jnp.concatenate([d_gate, d_up], axis=1).astype(jnp.bfloat16)
    part_down = contract(active, grads_out, 0, 0)
    part_gate_up = contract(rows_in, d_inner, 0, 0).reshape(gate_up.shape)
    d_rows = contract(d_inner, gate_up.reshape(gate_up.shape[0], 2 * quarter), 1, 1).astype(
        jnp.bfloat16
    )
    return (part_gate_up, part_down, d_rows)


def shards(
    tokens,
    cotangent,
    routes,
    lengths,
    attn_gain,
    qkv_weight,
    qk_gain,
    out_weight,
    moe_gain,
    router,
    w_gateup,
    w_down,
):
    tp_size = lax.axis_size("tp")
    dp_size = lax.axis_size("dp")
    tp_rank = lax.axis_index("tp")
    micro_count = tokens.shape[0]
    shard_rows = tokens.shape[2]
    model_width = tokens.shape[3]
    group_rows = shard_rows * tp_size
    experts = router.shape[1]
    per_group = w_gateup.shape[0]
    columns = qkv_weight.shape[2]
    head_count = columns // HD
    quarter = w_down.shape[1]
    capacity = tp_size * ((5 * group_rows * TOP // (4 * experts) + tp_size - 1) // tp_size)
    score_scale = HD ** (-0.5)
    expert_ids = jnp.arange(experts, dtype=jnp.int32)
    route_total = group_rows * TOP
    qkv_matrix = qkv_weight.reshape(model_width, 3 * columns)
    grad_attn_gain = jnp.zeros((model_width,), jnp.float32)
    grad_qkv = jnp.zeros((model_width, 3 * columns), jnp.float32)
    grad_qk = jnp.zeros((2, columns), jnp.float32)
    grad_out = jnp.zeros(out_weight.shape, jnp.float32)
    grad_moe_gain = jnp.zeros((model_width,), jnp.float32)
    grad_router = jnp.zeros(router.shape, jnp.float32)
    gate_up_sums = [jnp.zeros(w_gateup.shape[1:], jnp.float32) for local_expert in range(per_group)]
    down_sums = [jnp.zeros(w_down.shape[1:], jnp.float32) for local_expert in range(per_group)]
    outputs = []
    input_grads = []
    for micro_step in range(micro_count):
        gathered = lax.all_gather(tokens[micro_step, 0], "tp", axis=0, tiled=True)
        x_full = gathered.astype(jnp.float32)
        x_scale = rms_scale(x_full)
        x_hat = x_full * x_scale
        normed_low = (x_hat * attn_gain).astype(jnp.bfloat16)
        packed = jnp.dot(normed_low, qkv_matrix, preferred_element_type=jnp.float32).reshape(
            group_rows, 3, columns
        )
        query_raw = packed[:, 0]
        key_raw = packed[:, 1]
        value_raw = packed[:, 2]
        query_sq, key_sq = lax.psum(
            (jnp.sum(query_raw * query_raw, axis=1), jnp.sum(key_raw * key_raw, axis=1)), "tp"
        )
        query_scale = lax.rsqrt(query_sq / model_width + EPSILON)[:, None]
        key_scale = lax.rsqrt(key_sq / model_width + EPSILON)[:, None]
        query_hat = query_raw * query_scale
        key_hat = key_raw * key_scale
        places, segment, position = layout(lengths[micro_step, 0], group_rows)
        cosine, sine_table = rotary(position, HD // 2)
        query_used = rotate(
            (query_hat * qk_gain[0]).reshape(group_rows, head_count, HD), cosine, sine_table
        ).astype(jnp.bfloat16)
        key_used = rotate(
            (key_hat * qk_gain[1]).reshape(group_rows, head_count, HD), cosine, sine_table
        ).astype(jnp.bfloat16)
        value_used = value_raw.reshape(group_rows, head_count, HD).astype(jnp.bfloat16)
        allowed = (segment[:, None] == segment[None, :]) & (places[None, :] <= places[:, None])
        scores = (
            jnp.einsum("qhd,khd->hqk", query_used, key_used, preferred_element_type=jnp.float32)
            * score_scale
        )
        masked = jnp.where(allowed[None], scores, -1e30)
        top_score = jnp.max(masked, axis=-1, keepdims=True)
        exponent = jnp.where(allowed[None], jnp.exp(masked - top_score), 0.0)
        row_total = jnp.sum(exponent, axis=-1, keepdims=True)
        log_total = top_score + jnp.log(row_total)
        softmax_weights = exponent / row_total
        attended = (
            jnp.einsum(
                "hqk,khd->qhd",
                softmax_weights.astype(jnp.bfloat16),
                value_used,
                preferred_element_type=jnp.float32,
            )
            .reshape(group_rows, columns)
            .astype(jnp.bfloat16)
        )
        branch = lax.psum_scatter(
            jnp.dot(attended, out_weight, preferred_element_type=jnp.float32),
            "tp",
            scatter_dimension=0,
            tiled=True,
        )
        hidden_own = tokens[micro_step, 0].astype(jnp.float32) + branch
        hidden_full, cot_full = (
            lax.all_gather(hidden_own, "tp", axis=0, tiled=True),
            lax.all_gather(cotangent[micro_step, 0].astype(jnp.float32), "tp", axis=0, tiled=True),
        )
        h_scale = rms_scale(hidden_full)
        h_hat = hidden_full * h_scale
        moe_low = (h_hat * moe_gain).astype(jnp.bfloat16)
        logits = jnp.dot(moe_low, router, preferred_element_type=jnp.float32)
        gate_all = jax.nn.softmax(logits, axis=-1)
        route_rows = routes[micro_step, 0]
        choose = route_rows[:, :, None] == expert_ids[None, None, :]
        route_gates = jnp.sum(jnp.where(choose, gate_all[:, None, :], 0.0), axis=-1)
        flat_choose = choose.reshape(route_total, experts).astype(jnp.int32)
        slot_ranks = jnp.sum((jnp.cumsum(flat_choose, axis=0) - 1) * flat_choose, axis=1)
        slot_of = route_rows.reshape(route_total) * capacity + slot_ranks
        owners = (
            jnp.zeros((experts * capacity,), jnp.int32)
            .at[slot_of]
            .set(jnp.arange(route_total, dtype=jnp.int32))
        )
        filled = jnp.zeros((experts * capacity,), jnp.bool_).at[slot_of].set(True)
        owner_rows = owners // TOP
        send_rows = jnp.where(
            filled[:, None], moe_low[owner_rows], jnp.zeros((), jnp.bfloat16)
        ).reshape(experts, capacity, model_width)
        live = (segment < 2).astype(jnp.float32)
        d_mixed = cot_full * live[:, None]
        slot_gate = jnp.where(filled, route_gates.reshape(route_total)[owners], 0.0)
        grad_rows = (
            (d_mixed[owner_rows] * slot_gate[:, None])
            .astype(jnp.bfloat16)
            .reshape(experts, capacity, model_width)
        )
        serve_rows_in = lax.all_to_all(send_rows, "dp", split_axis=0, concat_axis=0, tiled=True)
        grads_in = lax.all_to_all(grad_rows, "dp", split_axis=0, concat_axis=0, tiled=True)
        slot_count = serve_rows_in.shape[1]
        split_rows = serve_rows_in.reshape(dp_size, per_group, slot_count, model_width)
        results = []
        inners = []
        for run_local_expert in range(per_group):
            run_inner_pre, result = expert_forward(
                split_rows[:, run_local_expert].reshape(dp_size * slot_count, model_width),
                w_gateup[run_local_expert],
                w_down[run_local_expert],
            )
            results.append(result.reshape(dp_size, slot_count, model_width))
            inners.append(run_inner_pre.reshape(dp_size, slot_count, 2 * quarter))
        serve_result = jnp.stack(results, axis=1).reshape(experts, slot_count, model_width)
        serve_inner_pre = jnp.stack(inners, axis=1).reshape(experts, slot_count, 2 * quarter)
        returned = lax.all_to_all(serve_result, "dp", split_axis=0, concat_axis=0, tiled=True)
        outcome = (returned, serve_rows_in, grads_in, serve_inner_pre)
        returned = outcome[0]
        kept_rows = outcome[1]
        grad_arrived = outcome[2]
        inner_kept = outcome[3]
        kept_split = kept_rows.reshape(dp_size, per_group, capacity, model_width)
        grad_split = grad_arrived.reshape(dp_size, per_group, capacity, model_width)
        inner_split = inner_kept.reshape(dp_size, per_group, capacity, 2 * quarter)
        back_rows = []
        new_gate_up = []
        new_down = []
        for local_expert in range(per_group):
            rows_in = kept_split[:, local_expert].reshape(dp_size * capacity, model_width)
            inner_pre = inner_split[:, local_expert].reshape(dp_size * capacity, 2 * quarter)
            part_gate_up, part_down, d_rows = expert_backward(
                rows_in,
                inner_pre,
                grad_split[:, local_expert].reshape(dp_size * capacity, model_width),
                w_gateup[local_expert],
                w_down[local_expert],
            )
            new_gate_up.append(gate_up_sums[local_expert] + part_gate_up)
            new_down.append(down_sums[local_expert] + part_down)
            back_rows.append(d_rows.reshape(dp_size, capacity, model_width))
        gate_up_sums = new_gate_up
        down_sums = new_down
        stacked_back = jnp.stack(back_rows, axis=1).reshape(experts, capacity, model_width)
        grad_back = lax.all_to_all(stacked_back, "dp", split_axis=0, concat_axis=0, tiled=True)
        flat_back = returned.reshape(experts * capacity, model_width)
        flat_grad = grad_back.reshape(experts * capacity, model_width)
        positions = slot_of.reshape(group_rows, TOP)
        mixed_part = jnp.zeros((group_rows, model_width), jnp.float32)
        routed_grad = jnp.zeros((group_rows, model_width), jnp.float32)
        gate_columns = []
        for route_slot in range(TOP):
            chosen = flat_back[positions[:, route_slot]].astype(jnp.float32)
            mixed_part = mixed_part + route_gates[:, route_slot : route_slot + 1] * chosen
            gate_columns.append(jnp.sum(chosen * d_mixed, axis=1))
            routed_grad = routed_grad + flat_grad[positions[:, route_slot]].astype(jnp.float32)
        mixed_full, expert_grad, gate_grad = (
            lax.psum(mixed_part.astype(jnp.bfloat16), "tp").astype(jnp.float32),
            lax.psum(routed_grad.astype(jnp.bfloat16), "tp").astype(jnp.float32),
            lax.psum(jnp.stack(gate_columns, axis=1).astype(jnp.bfloat16), "tp").astype(
                jnp.float32
            ),
        )
        own_mixed = lax.dynamic_slice_in_dim(mixed_full, tp_rank * shard_rows, shard_rows, 0)
        outputs.append((hidden_own + own_mixed).astype(jnp.bfloat16))
        d_choice = jnp.sum(jnp.where(choose, gate_grad[:, :, None], 0.0), axis=1)
        d_logits = (
            gate_all * (d_choice - jnp.sum(gate_all * d_choice, axis=1, keepdims=True))
        ).astype(jnp.bfloat16)
        grad_router = grad_router + contract(moe_low, d_logits, 0, 0)
        d_moe_in = expert_grad + contract(d_logits, router, 1, 1)
        grad_moe_gain = grad_moe_gain + jnp.sum(d_moe_in * h_hat, axis=0)
        d_h_hat = d_moe_in * moe_gain
        d_hidden = d_mixed + h_scale * (
            d_h_hat - h_hat * jnp.mean(d_h_hat * h_hat, axis=1, keepdims=True)
        )
        d_branch = d_hidden.astype(jnp.bfloat16)
        grad_out = grad_out + contract(attended, d_branch, 0, 0)
        d_attended = (
            contract(d_branch, out_weight, 1, 1)
            .astype(jnp.bfloat16)
            .reshape(group_rows, head_count, HD)
        )
        scores_again = (
            jnp.einsum("qhd,khd->hqk", query_used, key_used, preferred_element_type=jnp.float32)
            * score_scale
        )
        weights_again = jnp.where(allowed[None], jnp.exp(scores_again - log_total), 0.0)
        d_weights = jnp.einsum(
            "qhd,khd->hqk", d_attended, value_used, preferred_element_type=jnp.float32
        )
        row_delta = jnp.sum(weights_again * d_weights, axis=-1, keepdims=True)
        d_scores = (weights_again * (d_weights - row_delta) * score_scale).astype(jnp.bfloat16)
        d_query = jnp.einsum("hqk,khd->qhd", d_scores, key_used, preferred_element_type=jnp.float32)
        d_key = jnp.einsum("hqk,qhd->khd", d_scores, query_used, preferred_element_type=jnp.float32)
        d_value = jnp.einsum(
            "hqk,qhd->khd",
            weights_again.astype(jnp.bfloat16),
            d_attended,
            preferred_element_type=jnp.float32,
        )
        d_query_norm = rotate_back(d_query, cosine, sine_table).reshape(group_rows, columns)
        d_key_norm = rotate_back(d_key, cosine, sine_table).reshape(group_rows, columns)
        grad_qk = grad_qk + jnp.stack(
            [jnp.sum(d_query_norm * query_hat, axis=0), jnp.sum(d_key_norm * key_hat, axis=0)]
        )
        d_query_hat = d_query_norm * qk_gain[0]
        d_key_hat = d_key_norm * qk_gain[1]
        query_dot, key_dot = lax.psum(
            (jnp.sum(d_query_hat * query_hat, axis=1), jnp.sum(d_key_hat * key_hat, axis=1)), "tp"
        )
        d_query_raw = query_scale * (d_query_hat - query_hat * (query_dot / model_width)[:, None])
        d_key_raw = key_scale * (d_key_hat - key_hat * (key_dot / model_width)[:, None])
        d_packed = (
            jnp.stack([d_query_raw, d_key_raw, d_value.reshape(group_rows, columns)], axis=1)
            .reshape(group_rows, 3 * columns)
            .astype(jnp.bfloat16)
        )
        grad_qkv = grad_qkv + contract(normed_low, d_packed, 0, 0)
        d_normed = lax.psum(contract(d_packed, qkv_matrix, 1, 1).astype(jnp.bfloat16), "tp").astype(
            jnp.float32
        )
        grad_attn_gain = grad_attn_gain + jnp.sum(d_normed * x_hat, axis=0)
        d_x_hat = d_normed * attn_gain
        d_tokens = d_hidden + x_scale * (
            d_x_hat - x_hat * jnp.mean(d_x_hat * x_hat, axis=1, keepdims=True)
        )
        input_grads.append(
            lax.dynamic_slice_in_dim(d_tokens, tp_rank * shard_rows, shard_rows, 0).astype(
                jnp.bfloat16
            )
        )
    summed = (
        lax.psum(grad_attn_gain.astype(jnp.bfloat16), "dp").astype(jnp.float32),
        lax.psum(grad_qkv.astype(jnp.bfloat16), "dp").astype(jnp.float32),
        lax.psum(grad_qk.astype(jnp.bfloat16), "dp").astype(jnp.float32),
        lax.psum(grad_out.astype(jnp.bfloat16), "dp").astype(jnp.float32),
        lax.psum(grad_moe_gain.astype(jnp.bfloat16), "dp").astype(jnp.float32),
        lax.psum(grad_router.astype(jnp.bfloat16), "dp").astype(jnp.float32),
    )
    return (
        jnp.stack(outputs)[:, None],
        jnp.stack(input_grads)[:, None],
        summed[0],
        summed[1].reshape(qkv_weight.shape),
        summed[2],
        summed[3],
        summed[4],
        summed[5],
        jnp.stack(gate_up_sums),
        jnp.stack(down_sums),
    )


def solution(mesh):
    return jax.shard_map(
        shards,
        mesh=mesh,
        in_specs=(
            P(None, "dp", "tp", None),
            P(None, "dp", "tp", None),
            P(None, "dp", None, None),
            P(None, "dp", None),
            P(),
            P(None, None, "tp"),
            P(None, "tp"),
            P("tp", None),
            P(),
            P(),
            P("dp", None, None, "tp"),
            P("dp", "tp", None),
        ),
        out_specs=(
            P(None, "dp", "tp", None),
            P(None, "dp", "tp", None),
            P(),
            P(None, None, "tp"),
            P(None, "tp"),
            P("tp", None),
            P(),
            P(),
            P("dp", None, None, "tp"),
            P("dp", "tp", None),
        ),
        check_vma=False,
    )
```

profile of v0, /device:TPU:0, one launch (start us, length us, event | category | flops | bytes accessed | tf_op | source)
XLA Modules:
  0.0 2836.2 jit_solution(8854223125618917086)
XLA Ops:
  27.7 12.1 all-gather.15.cloned.1.call-done
  49.2 19.7 all-gather.17.cloned.1.call-done
  85.3 9.0 all-reduce.1
  110.5 26.0 reduce-scatter.3.cloned.1.call-done
  136.5 38.9 %reduce-scatter.5.cloned.1.call-done = f32[64,2048]{1,0:T(8,128)} async-done(((f32[256,2048]{1,0:T(8,128)}), f32[64,2048]{1,0:T(8,128)}) %reduce-scatter.5.cloned.1.call-update) | async-done | bytes 524304 | tf_op jit(solution)/shard_map/reduce_scatter | solution.py:192
  193.4 9.1 scatter_custom_fusion
  203.8 9.3 all-gather.13.cloned.1.call-done
  215.0 35.8 %all-gather.11.cloned.1.call-done = f32[256,2048]{1,0:T(8,128)} async-done(((f32[64,2048]{1,0:T(8,128)}), f32[256,2048]{1,0:T(8,128)}) %all-gather.11.cloned.1.call-update) | async-done | bytes 2097168 | tf_op jit(solution)/shard_map/all_gather | solution.py:200
  255.9 21.9 gather_fusion
  277.8 10.1 broadcast_select_fusion.1
  300.5 9.3 scatter_custom_fusion.2
  318.0 10.7 gather_fusion.9
  328.6 10.0 broadcast_select_fusion
  338.6 183.6 %all-to-all-done = bf16[16,160,2048]{2,1,0:T(8,128)(2,1)} async-done(((bf16[16,160,2048]{2,1,0:T(8,128)(2,1)}), bf16[16,160,2048]{2,1,0:T(8,128)(2,1)}, u32[]{:S(2)}, u32[]{:S(2)}) %all-to-all-start) | async-done | bytes 10485792 | tf_op jit(solution)/shard_map/all_to_all | solution.py:232
  536.1 10.1 fusion.200
  567.0 8.9 pad_maximum_fusion
  576.0 180.2 %all-to-all-done.2 = bf16[16,160,2048]{2,1,0:T(8,128)(2,1)} async-done(((bf16[16,160,2048]{2,1,0:T(8,128)(2,1)}), bf16[16,160,2048]{2,1,0:T(8,128)(2,1)}, u32[]{:S(2)}, u32[]{:S(2)}) %all-to-all-start.2) | async-done | bytes 10485792 | tf_op jit(solution)/shard_map/all_to_all | solution.py:232
  761.5 10.4 fusion.201
  792.8 9.1 pad_maximum_fusion.1
  801.9 188.5 %all-to-all-done.1 = bf16[16,160,2048]{2,1,0:T(8,128)(2,1)} async-done(((bf16[16,160,2048]{2,1,0:T(8,128)(2,1)}), bf16[16,160,2048]{2,1,0:T(8,128)(2,1)}, u32[]{:S(2)}, u32[]{:S(2)}) %all-to-all-start.1) | async-done | bytes 10485792 | tf_op jit(solution)/shard_map/all_to_all | solution.py:248
  1013.3 9.0 gather_fusion.7
  1031.1 8.8 gather_fusion.5
  1039.9 9.0 gather_fusion.4
  1057.6 9.1 gather_fusion.2
  1081.2 143.2 %all-to-all-done.3 = bf16[16,160,2048]{2,1,0:T(8,128)(2,1)} async-done(((bf16[16,160,2048]{2,1,0:T(8,128)(2,1)}), bf16[16,160,2048]{2,1,0:T(8,128)(2,1)}, u32[]{:S(2)}, u32[]{:S(2)}) %all-to-all-start.3) | async-done | bytes 10485792 | tf_op jit(solution)/shard_map/all_to_all | solution.py:248
  1232.1 9.1 gather_fusion.16
  1249.8 8.9 gather_fusion.14
  1284.8 8.9 gather_fusion.10
  1299.5 9.1 all-reduce.4
  1310.1 13.6 gather_fusion.29
  1323.8 21.3 gather_fusion.28
  1345.1 12.2 multiply_convert_fusion
  1365.2 13.6 gather_fusion.19
  1379.0 21.3 gather_fusion.18
  1400.3 12.2 multiply_convert_fusion.1
  1412.5 179.0 %all-to-all-done.6 = bf16[16,160,2048]{2,1,0:T(8,128)(2,1)} async-done(((bf16[16,160,2048]{2,1,0:T(8,128)(2,1)}), bf16[16,160,2048]{2,1,0:T(8,128)(2,1)}, u32[]{:S(2)}, u32[]{:S(2)}) %all-to-all-start.6) | async-done | bytes 10485792 | tf_op jit(solution)/shard_map/all_to_all | solution.py:233
  1597.1 10.2 fusion.199
  1625.9 9.1 pad_maximum_fusion.3
  1635.0 190.9 %all-to-all-done.4 = bf16[16,160,2048]{2,1,0:T(8,128)(2,1)} async-done(((bf16[16,160,2048]{2,1,0:T(8,128)(2,1)}), bf16[16,160,2048]{2,1,0:T(8,128)(2,1)}, u32[]{:S(2)}, u32[]{:S(2)}) %all-to-all-start.4) | async-done | bytes 10485792 | tf_op jit(solution)/shard_map/all_to_all | solution.py:233
  1831.3 10.3 fusion.198
  1860.0 8.9 pad_maximum_fusion.2
  1869.0 191.1 %all-to-all-done.7 = bf16[16,160,2048]{2,1,0:T(8,128)(2,1)} async-done(((bf16[16,160,2048]{2,1,0:T(8,128)(2,1)}), bf16[16,160,2048]{2,1,0:T(8,128)(2,1)}, u32[]{:S(2)}, u32[]{:S(2)}) %all-to-all-start.7) | async-done | bytes 10485792 | tf_op jit(solution)/shard_map/all_to_all | solution.py:276
  2097.9 8.8 gather_fusion.36
  2106.7 9.2 gather_fusion.35
  2115.9 8.8 gather_fusion.34
  2124.7 8.9 gather_fusion.33
  2133.6 8.8 gather_fusion.32
  2142.4 8.9 gather_fusion.31
  2151.4 8.8 gather_fusion.30
  2160.2 134.2 %all-to-all-done.5 = bf16[16,160,2048]{2,1,0:T(8,128)(2,1)} async-done(((bf16[16,160,2048]{2,1,0:T(8,128)(2,1)}), bf16[16,160,2048]{2,1,0:T(8,128)(2,1)}, u32[]{:S(2)}, u32[]{:S(2)}) %all-to-all-start.5) | async-done | bytes 10485792 | tf_op jit(solution)/shard_map/all_to_all | solution.py:276
  2294.4 8.8 gather_fusion.27
  2303.2 9.0 gather_fusion.26
  2312.3 8.8 gather_fusion.25
  2321.1 8.8 gather_fusion.24
  2338.7 9.3 gather_fusion.22
  2347.9 8.8 gather_fusion.21
  2356.8 8.8 gather_fusion.20
  2392.4 50.1 %all-reduce.15.cloned.1.call-done = (bf16[256,2048]{1,0:T(8,128)(2,1)}, bf16[256,2048]{1,0:T(8,128)(2,1)}) async-done(((bf16[256,2048]{1,0:T(8,128)(2,1)}, bf16[256,2048]{1,0:T(8,128)(2,1)}), (bf16[256,2048]{1,0:T(8,128)(2,1)}, bf16[256,2048]{1,0:T(8,128)(2,1)})) %all-reduce.15.cloned.1.call-update) | async-done | bytes 2097168 | tf_op jit(solution)/shard_map/psum | solution.py:290
  2507.7 8.9 all-reduce
  2530.8 9.2 add_bitcast_fusion
  2577.9 24.6 copy.240
  2604.9 30.9 %all-reduce.13.cloned.1.call-done = (bf16[256,2048]{1,0:T(8,128)(2,1)}, bf16[256,2048]{1,0:T(8,128)(2,1)}, bf16[256,2048]{1,0:T(8,128)(2,1)}, bf16[256,2048]{1,0:T(8,128)(2,1)}) async-done(((bf16[256,2048]{1,0:T(8,128)(2,1)}, bf16[256,2048]{1,0:T(8,128)(2,1)}, bf16[256,2048]{1,0:T(8,128)(2,1)}, bf16[256,2048]{1,0:T(8,128)(2,1)}), (bf16[256,2048]{1,0:T(8,128)(2,1)}, bf16[256,2048]{1,0:T(8,128)(2,1)}, ...) | async-done | bytes 4194320 | tf_op jit(solution)/shard_map/psum | solution.py:289
  2642.0 30.0 %all-reduce.2 = (bf16[2048]{0:T(1024)(128)(2,1)S(1)}, bf16[2,512]{1,0:T(2,128)(2,1)S(1)}, bf16[2048]{0:T(1024)(128)(2,1)S(1)}) all-reduce(bf16[2048]{0:T(1024)(128)(2,1)S(1)} %add_convert_fusion.11, bf16[2,512]{1,0:T(2,128)(2,1)S(1)} %fusion.167, bf16[2048]{0:T(1024)(128)(2,1)S(1)} %add_convert_fusion.10), channel_id=1, replica_groups=mesh['tp'=4,'dp'=8] {'dp'}, use_global_device_ids=true, to_apply=%region_78.79 | all-reduce | flops 5120 | bytes 20480 | tf_op jit(solution)/shard_map/psum | solution.py:365
  2680.9 136.2 %all-reduce.11.cloned.1.call-done = (bf16[2048,3,512]{2,0,1:T(8,128)(2,1)}, bf16[512,2048]{1,0:T(8,128)(2,1)}, bf16[2048,16]{0,1:T(8,128)(2,1)}) async-done(((bf16[2048,3,512]{2,0,1:T(8,128)(2,1)}, bf16[512,2048]{1,0:T(8,128)(2,1)}, bf16[2048,16]{0,1:T(8,128)(2,1)}), (bf16[2048,3,512]{2,0,1:T(8,128)(2,1)}, bf16[512,2048]{1,0:T(8,128)(2,1)}, bf16[2048,16]{0,1:T(8,128)(2,1)})) %all-reduce.11.cloned.1.call-update) | async-done | bytes 8454160 | tf_op jit(solution)/shard_map/psum | solution.py:366
  (767 shorter events, 546.3 us)
Async XLA Ops:
  7.2 91.9 %copy-start = (bf16[512,2048]{1,0:T(8,128)(2,1)S(1)}, bf16[512,2048]{1,0:T(8,128)(2,1)}, u32[]{:S(2)}) copy-start(bf16[512,2048]{1,0:T(8,128)(2,1)} %param.19) | copy-start | bytes 6291460
  7.2 32.6 %all-gather.15.cloned.1.call-start = ((), (), s32[]{:S(2)}) async-start(), calls=%async_computation.14 | async-start | bytes 1310720 | tf_op jit(solution)/shard_map/all_gather | solution.py:144
  9.3 59.6 %all-gather.17.cloned.1.call-start = ((), (), s32[]{:S(2)}) async-start(), calls=%async_computation.15 | async-start | bytes 1310720 | tf_op jit(solution)/shard_map/all_gather | solution.py:144
  10.0 126.5 %reduce-scatter.3.cloned.1.call-start = ((), (), s32[]{:S(2)}) async-start(), calls=%async_computation.10 | async-start | bytes 2621440 | tf_op jit(solution)/shard_map/reduce_scatter | solution.py:192
  16.6 77.8 %copy-start.151 = (f32[1,512]{1,0:T(1,128)}, f32[1,512]{1,0:T(1,128)S(1)}, u32[]{:S(2)}) copy-start(f32[1,512]{1,0:T(1,128)S(1)} %get-tuple-element.231) | copy-start | bytes 6148
  16.6 79.2 %copy-start.153 = (f32[1,512]{1,0:T(1,128)}, f32[1,512]{1,0:T(1,128)S(1)}, u32[]{:S(2)}) copy-start(f32[1,512]{1,0:T(1,128)S(1)} %get-tuple-element.232) | copy-start | bytes 6148
  17.4 24.0 copy-start.138
  27.7 68.4 %copy-start.76 = (f32[256,64]{1,0:T(8,128)}, f32[256,64]{1,0:T(8,128)S(1)}, u32[]{:S(2)}) copy-start(f32[256,64]{1,0:T(8,128)S(1)} %get-tuple-element.237) | copy-start | bytes 196612
  27.7 68.4 %copy-start.78 = (f32[256,64]{1,0:T(8,128)}, f32[256,64]{1,0:T(8,128)S(1)}, u32[]{:S(2)}) copy-start(f32[256,64]{1,0:T(8,128)S(1)} %get-tuple-element.238) | copy-start | bytes 196612
  27.7 77.7 %copy-start.80 = (f32[256,64]{1,0:T(8,128)}, f32[256,64]{1,0:T(8,128)S(1)}, u32[]{:S(2)}) copy-start(f32[256,64]{1,0:T(8,128)S(1)} %get-tuple-element.245) | copy-start | bytes 196612
  101.1 74.2 %reduce-scatter.5.cloned.1.call-start = ((), (), s32[]{:S(2)}) async-start(), calls=%async_computation.12 | async-start | bytes 2621440 | tf_op jit(solution)/shard_map/reduce_scatter | solution.py:192
  110.4 64.9 %copy-start.63 = (bf16[2,1,64,2048]{3,2,1,0:T(8,128)(2,1)S(1)}, bf16[2,1,64,2048]{3,2,1,0:T(8,128)(2,1)}, u32[]{:S(2)}) copy-start(bf16[2,1,64,2048]{3,2,1,0:T(8,128)(2,1)} %param.12) | copy-start | bytes 1572868
  110.4 67.8 %copy-start.179 = (s32[2,1,256,8]{2,3,1,0:T(8,128)S(1)}, s32[2,1,256,8]{2,3,1,0:T(8,128)}, u32[]{:S(2)}) copy-start(s32[2,1,256,8]{2,3,1,0:T(8,128)} %param.14) | copy-start | bytes 49156
  110.5 102.7 %all-gather.13.cloned.1.call-start = ((), (), s32[]{:S(2)}) async-start(), calls=%async_computation.13 | async-start | bytes 2621440 | tf_op jit(solution)/shard_map/all_gather | solution.py:200
  177.7 73.1 %all-gather.11.cloned.1.call-start = ((), (), s32[]{:S(2)}) async-start(), calls=%async_computation.11 | async-start | bytes 2621440 | tf_op jit(solution)/shard_map/all_gather | solution.py:200
  179.0 73.8 %copy-start.54 = (s32[1,1,256,8]{3,2,1,0:T(8,128)}, s32[1,1,256,8]{3,2,1,0:T(8,128)S(1)}, u32[]{:S(2)}) copy-start(s32[1,1,256,8]{3,2,1,0:T(8,128)S(1)} %copy.267) | copy-start | bytes 24580
  193.4 59.4 %copy-start.207 = (pred[2048]{0:T(1024)(128)(4,1)}, pred[2048]{0:T(1024)(128)(4,1)S(1)}, u32[]{:S(2)}) copy-start(pred[2048]{0:T(1024)(128)(4,1)S(1)} %broadcast.727) | copy-start | bytes 6148
  203.8 52.1 %copy-start.136 = (s32[3072]{0:T(1024)}, s32[3072]{0:T(1024)S(1)}, u32[]{:S(2)}) copy-start(s32[3072]{0:T(1024)S(1)} %pad_clamp_fusion.3) | copy-start | bytes 36868
  203.8 49.0 %copy-start.134 = (f32[2048]{0:T(1024)S(1)}, f32[2048]{0:T(1024)}, u32[]{:S(2)}) copy-start(f32[2048]{0:T(1024)} %param.20) | copy-start | bytes 24580
  215.0 40.9 %copy-start.184 = (f32[256]{0:T(256)}, f32[256]{0:T(256)S(1)}, u32[]{:S(2)}) copy-start(f32[256]{0:T(256)S(1)} %add_rsqrt_fusion) | copy-start | bytes 3076
  255.9 748.8 %copy-start.2 = (bf16[256,2048]{1,0:T(8,128)(2,1)}, bf16[256,2048]{1,0:T(8,128)(2,1)S(1)}, u32[]{:S(2)}) copy-start(bf16[256,2048]{1,0:T(8,128)(2,1)S(1)} %get-tuple-element.224) | copy-start | bytes 3145732
  287.9 234.2 %all-to-all-start = ((bf16[16,160,2048]{2,1,0:T(8,128)(2,1)}), bf16[16,160,2048]{2,1,0:T(8,128)(2,1)}, u32[]{:S(2)}, u32[]{:S(2)}) async-start(bf16[16,160,2048]{2,1,0:T(8,128)(2,1)} %broadcast_select_fusion.1), calls=%async_computation.1 | async-start | bytes 20971520 | tf_op jit(solution)/shard_map/all_to_all | solution.py:232
  522.1 234.0 %all-to-all-start.2 = ((bf16[16,160,2048]{2,1,0:T(8,128)(2,1)}), bf16[16,160,2048]{2,1,0:T(8,128)(2,1)}, u32[]{:S(2)}, u32[]{:S(2)}) async-start(bf16[16,160,2048]{2,1,0:T(8,128)(2,1)} %broadcast_select_fusion), calls=%async_computation.4 | async-start | bytes 20971520 | tf_op jit(solution)/shard_map/all_to_all | solution.py:232
  756.1 234.2 %all-to-all-start.1 = ((bf16[16,160,2048]{2,1,0:T(8,128)(2,1)}), bf16[16,160,2048]{2,1,0:T(8,128)(2,1)}, u32[]{:S(2)}, u32[]{:S(2)}) async-start(bf16[16,160,2048]{2,1,0:T(8,128)(2,1)} %bitcast.375), calls=%async_computation.2 | async-start | bytes 20971520 | tf_op jit(solution)/shard_map/all_to_all | solution.py:248
  990.3 234.0 %all-to-all-start.3 = ((bf16[16,160,2048]{2,1,0:T(8,128)(2,1)}), bf16[16,160,2048]{2,1,0:T(8,128)(2,1)}, u32[]{:S(2)}, u32[]{:S(2)}) async-start(bf16[16,160,2048]{2,1,0:T(8,128)(2,1)} %bitcast.372), calls=%async_computation.5 | async-start | bytes 20971520 | tf_op jit(solution)/shard_map/all_to_all | solution.py:248
  995.5 79.9 %all-gather.19.cloned.1.call-start = ((), (), s32[]{:S(2)}) async-start(), calls=%async_computation.16 | async-start | bytes 2621440 | tf_op jit(solution)/shard_map/all_gather | solution.py:201
  997.8 295.9 %all-gather.21.cloned.1.call-start = ((), (), s32[]{:S(2)}) async-start(), calls=%async_computation.17 | async-start | bytes 2621440 | tf_op jit(solution)/shard_map/all_gather | solution.py:201
  1002.9 221.5 %copy-start.190 = (s32[1024]{0:T(1024)}, s32[1024]{0:T(1024)S(1)}, u32[]{:S(2)}) copy-start(s32[1024]{0:T(1024)S(1)} %get-tuple-element.263) | copy-start | bytes 12292
  1002.9 229.2 %copy-start.189 = (s32[1024]{0:T(1024)}, s32[1024]{0:T(1024)S(1)}, u32[]{:S(2)}) copy-start(s32[1024]{0:T(1024)S(1)} %get-tuple-element.264) | copy-start | bytes 12292
  1002.9 238.2 %copy-start.192 = (s32[1024]{0:T(1024)}, s32[1024]{0:T(1024)S(1)}, u32[]{:S(2)}) copy-start(s32[1024]{0:T(1024)S(1)} %get-tuple-element.265) | copy-start | bytes 12292
  1002.9 246.9 %copy-start.191 = (s32[1024]{0:T(1024)}, s32[1024]{0:T(1024)S(1)}, u32[]{:S(2)}) copy-start(s32[1024]{0:T(1024)S(1)} %get-tuple-element.266) | copy-start | bytes 12292
  1002.9 255.8 %copy-start.194 = (s32[1024]{0:T(1024)}, s32[1024]{0:T(1024)S(1)}, u32[]{:S(2)}) copy-start(s32[1024]{0:T(1024)S(1)} %get-tuple-element.267) | copy-start | bytes 12292
  1002.9 264.4 %copy-start.193 = (s32[1024]{0:T(1024)}, s32[1024]{0:T(1024)S(1)}, u32[]{:S(2)}) copy-start(s32[1024]{0:T(1024)S(1)} %get-tuple-element.268) | copy-start | bytes 12292
  1003.0 273.1 %copy-start.196 = (s32[1024]{0:T(1024)}, s32[1024]{0:T(1024)S(1)}, u32[]{:S(2)}) copy-start(s32[1024]{0:T(1024)S(1)} %get-tuple-element.269) | copy-start | bytes 12292
  1003.0 281.8 %copy-start.195 = (s32[1024]{0:T(1024)}, s32[1024]{0:T(1024)S(1)}, u32[]{:S(2)}) copy-start(s32[1024]{0:T(1024)S(1)} %get-tuple-element.270) | copy-start | bytes 12292
  1004.6 17.7 copy-start.200
  1004.6 26.4 copy-start.199
  1004.6 35.2 %copy-start.202 = (s32[1024]{0:T(1024)}, s32[1024]{0:T(1024)S(1)}, u32[]{:S(2)}) copy-start(s32[1024]{0:T(1024)S(1)} %get-tuple-element.275) | copy-start | bytes 12292
  1004.6 44.3 %copy-start.201 = (s32[1024]{0:T(1024)}, s32[1024]{0:T(1024)S(1)}, u32[]{:S(2)}) copy-start(s32[1024]{0:T(1024)S(1)} %get-tuple-element.276) | copy-start | bytes 12292
  1004.7 52.9 %copy-start.204 = (s32[1024]{0:T(1024)}, s32[1024]{0:T(1024)S(1)}, u32[]{:S(2)}) copy-start(s32[1024]{0:T(1024)S(1)} %get-tuple-element.277) | copy-start | bytes 12292
  1004.7 62.0 %copy-start.203 = (s32[1024]{0:T(1024)}, s32[1024]{0:T(1024)S(1)}, u32[]{:S(2)}) copy-start(s32[1024]{0:T(1024)S(1)} %get-tuple-element.278) | copy-start | bytes 12292
  1013.3 62.1 %copy-start.17 = (bf16[256,2048]{1,0:T(8,128)(2,1)}, bf16[256,2048]{1,0:T(8,128)(2,1)S(1)}, u32[]{:S(2)}) copy-start(bf16[256,2048]{1,0:T(8,128)(2,1)S(1)} %gather_fusion.8) | copy-start | bytes 3145732
  1232.0 61.6 %copy-start.20 = (bf16[256,2048]{1,0:T(8,128)(2,1)}, bf16[256,2048]{1,0:T(8,128)(2,1)S(1)}, u32[]{:S(2)}) copy-start(bf16[256,2048]{1,0:T(8,128)(2,1)S(1)} %gather_fusion.17) | copy-start | bytes 3145732
  1293.6 15.0 copy-start.156
  1310.1 13.6 copy-start.160
  1357.3 234.2 %all-to-all-start.6 = ((bf16[16,160,2048]{2,1,0:T(8,128)(2,1)}), bf16[16,160,2048]{2,1,0:T(8,128)(2,1)}, u32[]{:S(2)}, u32[]{:S(2)}) async-start(bf16[16,160,2048]{2,1,0:T(8,128)(2,1)} %multiply_convert_fusion), calls=%async_computation.8 | async-start | bytes 20971520 | tf_op jit(solution)/shard_map/all_to_all | solution.py:233
  1363.1 15.8 copy-start.130
  1363.1 15.8 copy-start.163
  1365.2 13.7 copy-start.158
  1365.2 13.8 copy-start.137
  1591.5 234.4 %all-to-all-start.4 = ((bf16[16,160,2048]{2,1,0:T(8,128)(2,1)}), bf16[16,160,2048]{2,1,0:T(8,128)(2,1)}, u32[]{:S(2)}, u32[]{:S(2)}) async-start(bf16[16,160,2048]{2,1,0:T(8,128)(2,1)} %multiply_convert_fusion.1), calls=%async_computation.6 | async-start | bytes 20971520 | tf_op jit(solution)/shard_map/all_to_all | solution.py:233
  1825.9 234.2 %all-to-all-start.7 = ((bf16[16,160,2048]{2,1,0:T(8,128)(2,1)}), bf16[16,160,2048]{2,1,0:T(8,128)(2,1)}, u32[]{:S(2)}, u32[]{:S(2)}) async-start(bf16[16,160,2048]{2,1,0:T(8,128)(2,1)} %bitcast.374), calls=%async_computation.9 | async-start | bytes 20971520 | tf_op jit(solution)/shard_map/all_to_all | solution.py:276
  2060.2 234.1 %all-to-all-start.5 = ((bf16[16,160,2048]{2,1,0:T(8,128)(2,1)}), bf16[16,160,2048]{2,1,0:T(8,128)(2,1)}, u32[]{:S(2)}, u32[]{:S(2)}) async-start(bf16[16,160,2048]{2,1,0:T(8,128)(2,1)} %bitcast.373), calls=%async_computation.7 | async-start | bytes 20971520 | tf_op jit(solution)/shard_map/all_to_all | solution.py:276
  2065.5 377.0 %all-reduce.15.cloned.1.call-start = ((), (), s32[]{:S(2)}) async-start(), calls=%async_computation.20 | async-start | bytes 4194304 | tf_op jit(solution)/shard_map/psum | solution.py:290
  2069.6 12.6 slice-start.14
  2374.6 261.2 %all-reduce.13.cloned.1.call-start = ((), (), s32[]{:S(2)}) async-start(), calls=%async_computation.19 | async-start | bytes 8388608 | tf_op jit(solution)/shard_map/psum | solution.py:289
  2387.7 54.8 %copy-start.85 = (bf16[2048,16]{0,1:T(8,128)(2,1)S(1)}, bf16[2048,16]{0,1:T(8,128)(2,1)}, u32[]{:S(2)}) copy-start(bf16[2048,16]{0,1:T(8,128)(2,1)} %param.21) | copy-start | bytes 196612
  2387.7 54.8 %copy-start.135 = (f32[2048]{0:T(1024)S(1)}, f32[2048]{0:T(1024)}, u32[]{:S(2)}) copy-start(f32[2048]{0:T(1024)} %param.20) | copy-start | bytes 24580
  2387.7 54.8 %copy-start.166 = (f32[256]{0:T(256)S(1)}, f32[256]{0:T(256)}, u32[]{:S(2)}) copy-start(f32[256]{0:T(256)} %copy-done.165) | copy-start | bytes 3076
  2525.0 15.0 slice-start
  2530.7 286.3 %all-reduce.11.cloned.1.call-start = ((), (), s32[]{:S(2)}) async-start(), calls=%async_computation.18 | async-start | bytes 16908288 | tf_op jit(solution)/shard_map/psum | solution.py:366
  2577.9 24.7 copy-start.72
  2577.9 24.7 copy-start.73
  2641.8 35.1 %copy-start.209 = (f32[64]{0:T(128)S(1)}, f32[64]{0:T(128)}, u32[]{:S(2)}) copy-start(f32[64]{0:T(128)} %dynamic-slice.1) | copy-start | bytes 772
  (182 other events, 788.6 us)
Sparse Core Ops, SparseCore 0:
  10.4 29.3 all-gather.14
  42.2 26.6 all-gather.16
  101.2 35.1 reduce-scatter.2
  140.2 35.1 reduce-scatter.4
  177.8 35.3 all-gather.12
  215.4 35.2 all-gather.10
  998.2 35.6 all-gather.18
  1035.8 35.2 all-gather.20
  2374.7 67.7 all-reduce.14
  2530.9 104.8 all-reduce.12
  2638.9 178.0 all-reduce.10
where the time goes:
time: 2850 us; the launch traced here: 2840 us
  waiting for transfers between devices  1750 us (61%)
  local copies, waits for them, and re-layouts  575 us (20%)
  other arithmetic  211 us (7%)
  matrix products  178 us (6%)
  blocking collectives  57 us (2%)
  starting transfers between devices  43.7 us (2%)
    all_to_all x2, waiting for transfers between devices, shards(): lax.all_to_all(grad_rows, 'dp', split_axis=0, concat_axis=0, tiled=True)  370 us
    all_to_all x2, waiting for transfers between devices, shards(): lax.all_to_all(send_rows, 'dp', split_axis=0, concat_axis=0, tiled=True)  364 us
    all_to_all x2, waiting for transfers between devices, shards(): lax.all_to_all(serve_result, 'dp', split_axis=0, concat_axis=0, tiled=True)  332 us
    all_to_all x2, waiting for transfers between devices, shards(): lax.all_to_all(stacked_back, 'dp', split_axis=0, concat_axis=0, tiled=True)  325 us
    gather x16, local copies, waits for them, and re-layouts, shards(): flat_grad[positions[:, route_slot]].astype(jnp.float32)  141 us
    gather x16, local copies, waits for them, and re-layouts, shards(): chosen = flat_back[positions[:, route_slot]].astype(jnp.float32)  139 us
    psum x1, waiting for transfers between devices, shards(): lax.psum(grad_qkv.astype(jnp.bfloat16), 'dp').astype(jnp.float32)  136 us
    dot_general x28, matrix products, contract(): lax.dot_general(left, right, (((left_dim,), (right_dim,)), ((), ())), pre...  108 us
  transfers between devices with their start and end apart: 19, of which 17 were waited for; matrix products, arithmetic and copies ran while one was open for 23% of the time, Pallas kernels for 0%

commit v1 on v0

v1 whole, which is shorter than its diff:
```python
import jax
import jax.numpy as jnp
from jax import lax
from jax.sharding import PartitionSpec as P

HD = 128
EPSILON = 1e-05
LANES = 128
BF = jnp.bfloat16
F32 = jnp.float32


def rms_scale(values):
    return lax.rsqrt(jnp.mean(values * values, axis=-1, keepdims=True) + EPSILON)


def contract(left, right, left_dim, right_dim):
    return lax.dot_general(
        left, right, (((left_dim,), (right_dim,)), ((), ())), preferred_element_type=F32
    )


def rotate(values, cosine, sine, sign):
    half = values.shape[-1] // 2
    first, second = values[..., :half], values[..., half:]
    return jnp.concatenate(
        [first * cosine - sign * (second * sine), second * cosine + sign * (first * sine)], axis=-1
    )


def swap_tp(value, bits):
    size = lax.axis_size("tp")
    return lax.ppermute(value, "tp", [(i, i ^ bits) for i in range(size)])


def swap_dp(value, bits):
    size = lax.axis_size("dp")
    return lax.ppermute(value, "dp", [(i, i ^ bits) for i in range(size)])


def add_low(*terms):
    total = terms[0].astype(F32)
    for term in terms[1:]:
        total = total + term.astype(F32)
    return total


def gather_tp(rows):
    size = lax.axis_size("tp")
    return jnp.concatenate([rows] + [swap_tp(rows, k) for k in range(1, size)], axis=0)


def scatter_tp(rows):
    size = lax.axis_size("tp")
    n = rows.shape[0] // size
    return add_low(rows[:n], *[swap_tp(rows[k * n : (k + 1) * n], k) for k in range(1, size)])


def sum_tp(rows):
    size = lax.axis_size("tp")
    n = rows.shape[0] // size
    total = rows
    for k in range(1, size):
        other = swap_tp(rows, k)
        total = total + jnp.concatenate(
            [other[(j ^ k) * n : (j ^ k) * n + n] for j in range(size)], axis=0
        )
    return total


def gather_plane(rows):
    near, far = swap_tp(rows, 1), swap_tp(rows, 2)
    half = rows.shape[0] // 2
    return jnp.concatenate(
        [rows, near, far, swap_tp(near[:half], 2), swap_tp(far[half:], 1)], axis=0
    )


def gather_all(rows, partners):
    rows = jnp.concatenate([swap_dp(rows, 2 * k) if k else rows for k in partners], axis=0)
    rows = gather_plane(rows)
    return jnp.concatenate([rows, swap_dp(rows, 1)], axis=0)


def scatter_plane(rows):
    n, w = rows.shape[0] // 4, rows.shape[1] // LANES // 2 * LANES
    a, b = rows[:, :w], rows[:, w:]
    got_a = swap_tp(jnp.concatenate([a[n : 2 * n], a[3 * n :]], axis=0), 1)
    got_b = swap_tp(b[2 * n :], 2)
    sum_a = add_low(jnp.concatenate([a[:n], a[2 * n : 3 * n]], axis=0), got_a).astype(BF)
    sum_b = add_low(b[: 2 * n], got_b).astype(BF)
    end_a = add_low(sum_a[:n], swap_tp(sum_a[n:], 2))
    end_b = add_low(sum_b[:n], swap_tp(sum_b[n:], 1))
    return jnp.concatenate([end_a, end_b], axis=1).astype(BF)


def scatter_all(rows, partners):
    n = rows.shape[0] // 2
    rows = add_low(rows[:n], swap_dp(rows[n:], 1)).astype(BF)
    rows = scatter_plane(rows)
    n = rows.shape[0] // len(partners)
    pieces = [rows[i * n : (i + 1) * n] for i in range(len(partners))]
    return add_low(*[swap_dp(p, 2 * k) if k else p for p, k in zip(pieces, partners)])


def sum_dp(value):
    return lax.psum(value.astype(BF), "dp").astype(F32)


def experts_of(moe_all, cot_all, router, gate_up, down_all, local_ids):
    width, experts = router.shape
    local = len(gate_up)
    quarter = down_all.shape[0] // local
    expert_ids = jnp.arange(experts, dtype=jnp.int32)
    d_all = cot_all[:, :width]
    mask_all = cot_all[:, width : width + experts].astype(F32)
    probs_all = jax.nn.softmax(jnp.dot(moe_all, router, preferred_element_type=F32), axis=-1)
    gates_all = probs_all * mask_all
    scaled, inner_grads, gate_terms, grads = [], [], [], []
    d_active_all = contract(d_all, down_all, 1, 1)
    for e in range(local):
        here = expert_ids[None, :] == local_ids[e]
        gate = jnp.sum(jnp.where(here, gates_all, 0.0), axis=1, keepdims=True)
        picked = jnp.sum(jnp.where(here, mask_all, 0.0), axis=1, keepdims=True)
        inner = jnp.dot(moe_all, gate_up[e], preferred_element_type=F32)
        gate_pre, up_pre = inner[:, :quarter], inner[:, quarter:]
        sigmoid = jax.nn.sigmoid(gate_pre)
        silu = gate_pre * sigmoid
        active = silu * up_pre
        d_raw = d_active_all[:, e * quarter : (e + 1) * quarter]
        gate_terms.append(jnp.sum(active * d_raw, axis=1, keepdims=True) * picked)
        scaled.append((active * gate).astype(BF))
        d_active = d_raw * gate
        d_gate = d_active * up_pre * sigmoid * (1.0 + gate_pre * (1.0 - sigmoid))
        d_up = d_active * silu
        inner_grads.append(jnp.concatenate([d_gate, d_up], axis=1).astype(BF))
        grads.append(contract(moe_all, inner_grads[e], 0, 0))
    scaled = jnp.concatenate(scaled, axis=1)
    mixed_part = jnp.dot(scaled, down_all, preferred_element_type=F32).astype(BF)
    d_rows = sum(contract(inner_grads[e], gate_up[e], 1, 1) for e in range(local)).astype(BF)
    return mixed_part, d_rows, gate_terms, grads, contract(scaled, d_all, 0, 0)


def shards(
    tokens, cotangent, routes, lengths, attn_gain, qkv_weight, qk_gain, out_weight, moe_gain,
    router, w_gateup, w_down,
):
    tp_size = lax.axis_size("tp")
    dp_size = lax.axis_size("dp")
    tp_rank = lax.axis_index("tp")
    dp_rank = lax.axis_index("dp")
    micro_count, _, own_rows, width = tokens.shape
    group = own_rows * tp_size
    experts = router.shape[1]
    local = w_gateup.shape[0]
    columns = qkv_weight.shape[2]
    heads = columns // HD
    quarter = w_down.shape[1]
    score_scale = HD ** (-0.5)

    qkv_matrix = qkv_weight.reshape(width, 3 * columns)
    gate_up = [w_gateup[e].reshape(width, 2 * quarter) for e in range(local)]
    down_all = w_down.reshape(local * quarter, width)
    expert_ids = jnp.arange(experts, dtype=jnp.int32)
    local_ids = dp_rank * local + jnp.arange(local, dtype=jnp.int32)

    places = jnp.concatenate(
        [(tp_rank ^ k) * own_rows + jnp.arange(own_rows, dtype=jnp.int32) for k in range(tp_size)]
    )
    own_places = tp_rank * own_rows + jnp.arange(own_rows, dtype=jnp.int32)
    frequency = jnp.exp(
        jnp.arange(HD // 2, dtype=F32) * (-2.0 * jnp.log(10000.0) / HD)
    )

    state = []
    for m in range(micro_count):
        first_len = lengths[m, 0, 0]
        live_end = first_len + lengths[m, 0, 1]
        live_own = (own_places < live_end).astype(F32)[:, None]
        d_mixed = cotangent[m, 0].astype(F32) * live_own
        own_routes = lax.dynamic_slice_in_dim(routes[m, 0], tp_rank * own_rows, own_rows, 0)
        chosen = jnp.any(own_routes[:, :, None] == expert_ids[None, None, :], axis=1)
        mask = jnp.pad(chosen.astype(BF), ((0, 0), (0, -experts % LANES)))
        sent = jnp.concatenate([d_mixed.astype(BF), mask], axis=1)
        state.append(dict(first_len=first_len, live_end=live_end, d_mixed=d_mixed, chosen=chosen,
                          cot_sent=sent))

    grad_gate_up = [0.0] * local
    grad_down = 0.0
    grad_out = 0.0
    grad_qkv = 0.0
    grad_qk = 0.0
    grad_router = 0.0
    grad_moe_gain = 0.0
    grad_attn_gain = 0.0
    outputs, input_grads = [], []

    for m in range(micro_count):
        s = state[m]
        x_own = tokens[m, 0].astype(F32)
        x_scale = rms_scale(x_own)
        x_hat = x_own * x_scale
        normed = gather_tp((x_hat * attn_gain).astype(BF))
        packed = jnp.dot(normed, qkv_matrix, preferred_element_type=F32)
        query_raw = packed[:, :columns]
        key_raw = packed[:, columns : 2 * columns]
        value_raw = packed[:, 2 * columns :]
        squares = sum_tp(
            jnp.stack([jnp.sum(query_raw * query_raw, axis=1), jnp.sum(key_raw * key_raw, axis=1)], axis=1)
        )
        scales = lax.rsqrt(squares / width + EPSILON)
        query_scale, key_scale = scales[:, :1], scales[:, 1:]
        query_hat = query_raw * query_scale
        key_hat = key_raw * key_scale
        segment = (places >= s["first_len"]).astype(jnp.int32) + (places >= s["live_end"]).astype(jnp.int32)
        starts = jnp.where(segment == 0, 0, jnp.where(segment == 1, s["first_len"], s["live_end"]))
        angles = (places - starts).astype(F32)[:, None] * frequency[None, :]
        cosine, sine = jnp.cos(angles)[:, None, :], jnp.sin(angles)[:, None, :]
        shape = (group, heads, HD)
        query = rotate((query_hat * qk_gain[0]).reshape(shape), cosine, sine, 1.0).astype(BF)
        key = rotate((key_hat * qk_gain[1]).reshape(shape), cosine, sine, 1.0).astype(BF)
        value = value_raw.reshape(shape).astype(BF)
        allowed = (segment[:, None] == segment[None, :]) & (places[None, :] <= places[:, None])
        scores = jnp.einsum("qhd,khd->hqk", query, key, preferred_element_type=F32) * score_scale
        masked = jnp.where(allowed[None], scores, -1e30)
        top_score = jnp.max(masked, axis=-1, keepdims=True)
        exponent = jnp.where(allowed[None], jnp.exp(masked - top_score), 0.0)
        weights = exponent / jnp.sum(exponent, axis=-1, keepdims=True)
        weights_low = weights.astype(BF)
        attended = (
            jnp.einsum("hqk,khd->qhd", weights_low, value, preferred_element_type=F32)
            .reshape(group, columns)
            .astype(BF)
        )
        branch = scatter_tp(jnp.dot(attended, out_weight, preferred_element_type=F32).astype(BF))
        hidden = x_own + branch
        h_scale = rms_scale(hidden)
        h_hat = hidden * h_scale
        moe_own = (h_hat * moe_gain).astype(BF)
        s.update(x_scale=x_scale, x_hat=x_hat, normed=normed, query_hat=query_hat, key_hat=key_hat,
                 query_scale=query_scale, key_scale=key_scale, cosine=cosine, sine=sine, query=query,
                 key=key, value=value, weights=weights, weights_low=weights_low, attended=attended,
                 hidden=hidden, h_scale=h_scale, h_hat=h_hat, moe_own=moe_own)

    lanes = jnp.arange(experts + (-experts % LANES), dtype=jnp.int32)
    outer = dp_size // 2
    span = min(outer, 4)
    for m in range(micro_count):
        s = state[m]
        back = mixed = 0.0
        for first in range(0, outer, span):
            partners = range(first, first + span)
            cot_sent, moe_sent = s["cot_sent"], s["moe_own"]
            if first:
                cot_sent, moe_sent, back, mixed = lax.optimization_barrier(
                    (cot_sent, moe_sent, back, mixed)
                )
            cot_all = gather_all(cot_sent, partners)
            moe_all = gather_all(moe_sent, partners)
            mixed_part, d_rows, gate_terms, more_gate_up, more_down = experts_of(
                moe_all, cot_all, router, gate_up, down_all, local_ids
            )
            grad_gate_up = [old + new for old, new in zip(grad_gate_up, more_gate_up)]
            grad_down = grad_down + more_down
            gate_part = sum(
                jnp.where(lanes[None, :] == local_ids[e], gate_terms[e], 0.0) for e in range(local)
            ).astype(BF)
            back = back + scatter_all(jnp.concatenate([d_rows, gate_part], axis=1), partners)
            mixed = mixed + scatter_all(mixed_part, partners)
        outputs.append((s["hidden"] + mixed).astype(BF))
        s["back"] = back

    for m in range(micro_count):
        s = state[m]
        back = s["back"]
        expert_grad = back[:, :width]
        probs = jax.nn.softmax(jnp.dot(s["moe_own"], router, preferred_element_type=F32), axis=-1)
        d_choice = back[:, width : width + experts]
        d_logits = (probs * (d_choice - jnp.sum(probs * d_choice, axis=1, keepdims=True))).astype(BF)
        grad_router = grad_router + contract(s["moe_own"], d_logits, 0, 0)
        d_moe_in = expert_grad + contract(d_logits, router, 1, 1)
        h_hat = s["h_hat"]
        grad_moe_gain = grad_moe_gain + jnp.sum(d_moe_in * h_hat, axis=0)
        d_h_hat = d_moe_in * moe_gain
        d_hidden = s["d_mixed"] + s["h_scale"] * (
            d_h_hat - h_hat * jnp.mean(d_h_hat * h_hat, axis=1, keepdims=True)
        )
        d_branch = gather_tp(d_hidden.astype(BF))
        grad_out = grad_out + contract(s["attended"], d_branch, 0, 0)
        query, key, value = s["query"], s["key"], s["value"]
        shape = (group, heads, HD)
        d_attended = contract(d_branch, out_weight, 1, 1).astype(BF).reshape(shape)
        weights = s["weights"]
        d_weights = jnp.einsum("qhd,khd->hqk", d_attended, value, preferred_element_type=F32)
        row_delta = jnp.sum(weights * d_weights, axis=-1, keepdims=True)
        d_scores = (weights * (d_weights - row_delta) * score_scale).astype(BF)
        d_query = jnp.einsum("hqk,khd->qhd", d_scores, key, preferred_element_type=F32)
        d_key = jnp.einsum("hqk,qhd->khd", d_scores, query, preferred_element_type=F32)
        d_value = jnp.einsum("hqk,qhd->khd", s["weights_low"], d_attended, preferred_element_type=F32)
        d_query_norm = rotate(d_query, s["cosine"], s["sine"], -1.0).reshape(group, columns)
        d_key_norm = rotate(d_key, s["cosine"], s["sine"], -1.0).reshape(group, columns)
        grad_qk = grad_qk + jnp.stack(
            [jnp.sum(d_query_norm * s["query_hat"], axis=0), jnp.sum(d_key_norm * s["key_hat"], axis=0)]
        )
        d_query_hat = d_query_norm * qk_gain[0]
        d_key_hat = d_key_norm * qk_gain[1]
        dots = sum_tp(
            jnp.stack(
                [jnp.sum(d_query_hat * s["query_hat"], axis=1), jnp.sum(d_key_hat * s["key_hat"], axis=1)],
                axis=1,
            )
        ) / width
        d_query_raw = s["query_scale"] * (d_query_hat - s["query_hat"] * dots[:, :1])
        d_key_raw = s["key_scale"] * (d_key_hat - s["key_hat"] * dots[:, 1:])
        d_packed = jnp.concatenate(
            [d_query_raw, d_key_raw, d_value.reshape(group, columns)], axis=1
        ).astype(BF)
        grad_qkv = grad_qkv + contract(s["normed"], d_packed, 0, 0)
        d_normed = scatter_tp(contract(d_packed, qkv_matrix, 1, 1).astype(BF))
        x_hat = s["x_hat"]
        grad_attn_gain = grad_attn_gain + jnp.sum(d_normed * x_hat, axis=0)
        d_x_hat = d_normed * attn_gain
        d_tokens = d_hidden + s["x_scale"] * (
            d_x_hat - x_hat * jnp.mean(d_x_hat * x_hat, axis=1, keepdims=True)
        )
        input_grads.append(d_tokens.astype(BF))

    small = jnp.concatenate([grad_attn_gain[None], grad_moe_gain[None], grad_router.T], axis=0)
    small = lax.psum(small, ("dp", "tp"))
    return (
        jnp.stack(outputs)[:, None],
        jnp.stack(input_grads)[:, None],
        small[0],
        sum_dp(grad_qkv).reshape(qkv_weight.shape),
        lax.psum(grad_qk, "dp"),
        sum_dp(grad_out),
        small[1],
        small[2:].T,
        jnp.stack(grad_gate_up).reshape(w_gateup.shape),
        grad_down.reshape(w_down.shape),
    )


def solution(mesh):
    return jax.shard_map(
        shards,
        mesh=mesh,
        in_specs=(
            P(None, "dp", "tp", None),
            P(None, "dp", "tp", None),
            P(None, "dp", None, None),
            P(None, "dp", None),
            P(),
            P(None, None, "tp"),
            P(None, "tp"),
            P("tp", None),
            P(),
            P(),
            P("dp", None, None, "tp"),
            P("dp", "tp", None),
        ),
        out_specs=(
            P(None, "dp", "tp", None),
            P(None, "dp", "tp", None),
            P(),
            P(None, None, "tp"),
            P(None, "tp"),
            P("tp", None),
            P(),
            P(),
            P("dp", None, None, "tp"),
            P("dp", "tp", None),
        ),
        check_vma=False,
    )
```

time: 2850 us -> 1200 us (0.42)
  waiting for transfers between devices: 1750 us -> 506 us
  local copies, waits for them, and re-layouts: 575 us -> 140 us
  starting transfers between devices: 43.7 us -> 146 us
  other arithmetic: 211 us -> 128 us
  matrix products: 178 us -> 234 us
  blocking collectives: 57 us -> 19.6 us
    all_to_all x8 -> x0, waiting for transfers between devices: 1390 us -> none  [the longest x2 370 us: shards(): lax.all_to_all(grad_rows, 'dp', split_axis=0, concat_axis=0, tiled=True)]
    gather x38 -> x0, local copies, waits for them, and re-layouts: 383 us -> none  [the longest x16 141 us: shards(): flat_grad[positions[:, route_slot]].astype(jnp.float32)]
    ppermute x0 -> x100, waiting for transfers between devices: none -> 260 us  [the longest x68 198 us: swap_tp(): return lax.ppermute(value, 'tp', [(i, i ^ bits) for i in range(size)])]
    ppermute x0 -> x100, starting transfers between devices: none -> 146 us  [the longest x68 84.2 us: swap_tp(): return lax.ppermute(value, 'tp', [(i, i ^ bits) for i in range(size)])]
    all_gather x6 -> x0, waiting for transfers between devices: 76.9 us -> none  [the longest x2 45.1 us: shards(): lax.all_gather(hidden_own, 'tp', axis=0, tiled=True)]
    reduce_scatter x2 -> x0, waiting for transfers between devices: 64.8 us -> none  [shards(): lax.psum_scatter(jnp.dot(attended, out_weight, preferred_element_type=jnp...]
    all_to_all x8 -> x0, starting transfers between devices: 42.6 us -> none  [the longest x2 10.9 us: shards(): lax.all_to_all(grad_rows, 'dp', split_axis=0, concat_axis=0, tiled=True)]
    psum x4 -> x1, blocking collectives: 57 us -> 19.6 us  [shards(): lax.psum(grad_qk, 'dp')]
  transfers between devices with their start and end apart: 19 -> 102, of which waited for: 17 -> 38; matrix products, arithmetic and copies ran while one was open for 23% -> 30% of each run, Pallas kernels for 0% -> 0%
where the time goes in v1:
time: 1200 us; the launch traced here: 1190 us
  waiting for transfers between devices  506 us (42%)
  matrix products  234 us (20%)
  starting transfers between devices  146 us (12%)
  local copies, waits for them, and re-layouts  140 us (12%)
  other arithmetic  128 us (11%)
  between operations  19.9 us (2%)
  blocking collectives  19.6 us (2%)
    ppermute x68, waiting for transfers between devices, swap_tp(): return lax.ppermute(value, 'tp', [(i, i ^ bits) for i in range(size)])  198 us
    psum x1, waiting for transfers between devices, sum_dp(): return lax.psum(value.astype(BF), 'dp').astype(F32)  177 us
    dot_general x24, matrix products, contract(): lax.dot_general(left, right, (((left_dim,), (right_dim,)), ((), ())), pre...  145 us
    ppermute x68, starting transfers between devices, swap_tp(): return lax.ppermute(value, 'tp', [(i, i ^ bits) for i in range(size)])  84.2 us
    psum x1, waiting for transfers between devices, shards(): small = lax.psum(small, ('dp', 'tp'))  69.3 us
    ppermute x32, waiting for transfers between devices, swap_dp(): return lax.ppermute(value, 'dp', [(i, i ^ bits) for i in range(size)])  62.5 us
    ppermute x32, starting transfers between devices, swap_dp(): return lax.ppermute(value, 'dp', [(i, i ^ bits) for i in range(size)])  62.1 us
    unnamed x393, local copies, waits for them, and re-layouts  60.2 us
  transfers between devices with their start and end apart: 102, of which 38 were waited for; matrix products, arithmetic and copies ran while one was open for 30% of the time, Pallas kernels for 0%

profile of v1, /device:TPU:0, one launch (start us, length us, event | category | flops | bytes accessed | tf_op | source)
XLA Modules:
  0.0 1193.4 jit_solution(461861610553552195)
XLA Ops:
  32.0 6.1 fusion.202
  41.4 8.8 copy.127
  162.7 17.2 %collective-permute-done.53 = bf16[256,2176]{1,0:T(8,128)(2,1)} collective-permute-done((bf16[256,2176]{1,0:T(8,128)(2,1)}, bf16[256,2176]{1,0:T(8,128)(2,1)}, u32[]{:S(2)}, u32[]{:S(2)}) %collective-permute-start.53) | collective-permute-done | bytes 1114144 | tf_op jit(solution)/shard_map/ppermute | solution.py:33
  190.2 7.2 collective-permute-done.20
  215.9 6.2 collective-permute-done.22
  227.8 16.4 %collective-permute-done.10 = bf16[64,2048]{1,0:T(8,128)(2,1)S(1)} collective-permute-done((bf16[64,2048]{1,0:T(8,128)(2,1)S(1)}, bf16[64,2048]{1,0:T(8,128)(2,1)S(1)}, u32[]{:S(2)}, u32[]{:S(2)}) %collective-permute-start.10) | collective-permute-done | bytes 262176 | tf_op jit(solution)/shard_map/ppermute | solution.py:38
  250.9 19.3 %collective-permute-done.45 = bf16[256,2048]{1,0:T(8,128)(2,1)S(1)} collective-permute-done((bf16[256,2048]{1,0:T(8,128)(2,1)S(1)}, bf16[256,2048]{1,0:T(8,128)(2,1)S(1)}, u32[]{:S(2)}, u32[]{:S(2)}) %collective-permute-start.45) | collective-permute-done | bytes 1048608 | tf_op jit(solution)/shard_map/ppermute | solution.py:33
  273.2 18.4 %collective-permute-done.12 = bf16[256,2048]{1,0:T(8,128)(2,1)S(1)} collective-permute-done((bf16[256,2048]{1,0:T(8,128)(2,1)S(1)}, bf16[256,2048]{1,0:T(8,128)(2,1)S(1)}, u32[]{:S(2)}, u32[]{:S(2)}) %collective-permute-start.12) | collective-permute-done | bytes 1048608 | tf_op jit(solution)/shard_map/ppermute | solution.py:33
  298.6 9.0 collective-permute-done.47
  310.9 4.7 collective-permute-done.14
  322.4 9.6 fusion.6
  331.9 6.3 fusion.10
  344.2 7.9 fusion.240
  357.9 7.9 fusion.238
  365.8 6.3 fusion.241
  372.0 6.3 fusion.239
  384.8 4.9 select_reduce_fusion.1
  392.6 4.1 multiply_convert_fusion.1
  396.7 6.1 fusion.36
  402.7 8.7 fusion.37
  415.7 4.1 multiply_convert_fusion.5
  419.8 8.2 fusion.38
  428.0 6.1 convolution_add_fusion.1
  434.2 6.1 convolution_convert_fusion
  445.6 6.4 fusion.35
  452.0 14.5 %add_convert_fusion = bf16[2048,2048]{1,0:T(8,128)(2,1)} fusion(f32[2048,2048]{1,0:T(8,128)} %fusion.37, bf16[2048,512]{1,0:T(8,128)(2,1)} %bitcast.263, bf16[2048,256]{0,1:T(8,128)(2,1)} %get-tuple-element.107, bf16[2048,256]{0,1:T(8,128)(2,1)S(1)} %copy-done.66), kind=kOutput, calls=%fused_computation.4 | convolution fusion | flops 4307550208 | bytes 29360128 | tf_op jit(solution)/shard_map/dot_general | solution.py:18
  468.1 4.7 pad_maximum_fusion.1
  472.8 15.0 %add_convert_fusion.1 = bf16[2048,2048]{1,0:T(8,128)(2,1)} fusion(f32[2048,2048]{1,0:T(8,128)} %fusion.38, bf16[2048,512]{1,0:T(8,128)(2,1)} %bitcast.264, bf16[2048,256]{0,1:T(8,128)(2,1)} %get-tuple-element.103, bf16[2048,256]{0,1:T(8,128)(2,1)} %get-tuple-element.102), kind=kOutput, calls=%fused_computation.5 | convolution fusion | flops 4307550208 | bytes 29360128 | tf_op jit(solution)/shard_map/dot_general | solution.py:18
  487.8 6.7 convolution_convert_fusion.1
  501.8 10.0 convolution_add_fusion
  511.9 7.2 copy.177
  519.1 7.3 copy.178
  526.4 4.8 pad_maximum_fusion.2
  531.7 10.2 fusion.4
  541.9 4.1 add_convert_fusion.5
  551.2 5.4 add_convert_fusion.6
  569.4 4.2 collective-permute-done.61
  579.9 16.0 %collective-permute-done.28 = bf16[512,1024]{1,0:T(8,128)(2,1)} collective-permute-done((bf16[512,1024]{1,0:T(8,128)(2,1)}, bf16[512,1024]{1,0:T(8,128)(2,1)}, u32[]{:S(2)}, u32[]{:S(2)}) %collective-permute-start.28) | collective-permute-done | bytes 1048608 | tf_op jit(solution)/shard_map/ppermute | solution.py:33
  602.2 18.4 %collective-permute-done.84 = bf16[512,1024]{1,0:T(8,128)(2,1)S(1)} collective-permute-done((bf16[512,1024]{1,0:T(8,128)(2,1)S(1)}, bf16[512,1024]{1,0:T(8,128)(2,1)S(1)}, u32[]{:S(2)}, u32[]{:S(2)}) %collective-permute-start.84) | collective-permute-done | bytes 1048608 | tf_op jit(solution)/shard_map/ppermute | solution.py:33
  622.2 20.8 %collective-permute-done.67 = bf16[512,1024]{1,0:T(8,128)(2,1)S(1)} collective-permute-done((bf16[512,1024]{1,0:T(8,128)(2,1)S(1)}, bf16[512,1024]{1,0:T(8,128)(2,1)S(1)}, u32[]{:S(2)}, u32[]{:S(2)}) %collective-permute-start.67) | collective-permute-done | bytes 1048608 | tf_op jit(solution)/shard_map/ppermute | solution.py:33
  648.3 6.0 collective-permute-done.62
  659.5 6.0 collective-permute-done.29
  668.9 5.2 collective-permute-start.63
  674.4 5.8 collective-permute-done.85
  680.2 6.2 collective-permute-start.64
  686.6 3.8 collective-permute-done.68
  690.9 5.3 collective-permute-start.88
  699.0 8.5 collective-permute-done.88
  707.5 11.2 collective-permute-done.89
  722.3 17.1 %collective-permute-start.30 = (bf16[64,2048]{1,0:T(8,128)(2,1)S(1)}, bf16[64,2048]{1,0:T(8,128)(2,1)S(1)}, u32[]{:S(2)}, u32[]{:S(2)}) collective-permute-start(bf16[64,2048]{1,0:T(8,128)(2,1)S(1)} %get-tuple-element.172), channel_id=1, source_target_pairs={{0,2},{1,3},{2,0},{3,1},{4,6},{5,7},{6,4},{7,5},{8,10},{9,11},{10,... | collective-permute-start | bytes 786440 | tf_op jit(solution)/shard_map/ppermute | solution.py:38
  739.5 4.4 collective-permute-done.72
  743.9 4.9 collective-permute-start.32
  749.5 21.5 %collective-permute-done.31 = bf16[64,2048]{1,0:T(8,128)(2,1)S(1)} collective-permute-done((bf16[64,2048]{1,0:T(8,128)(2,1)S(1)}, bf16[64,2048]{1,0:T(8,128)(2,1)S(1)}, u32[]{:S(2)}, u32[]{:S(2)}) %collective-permute-start.31) | collective-permute-done | bytes 262176 | tf_op jit(solution)/shard_map/ppermute | solution.py:38
  784.8 5.1 collective-permute-done.92
  839.7 4.8 convolution_convert_fusion.4
  854.1 7.7 fusion.95
  863.7 9.5 add_convert_fusion.2
  873.1 8.6 copy.176
  881.8 9.6 pad_maximum_fusion
  891.5 10.2 fusion.14
  902.5 19.6 %psum.30 = f32[2,512]{1,0:T(2,128)} all-reduce(f32[2,512]{1,0:T(2,128)S(1)} %maximum_add_fusion), channel_id=1, replica_groups=mesh['tp'=4,'dp'=8] {'dp'}, use_global_device_ids=true, to_apply=%region_56.57 | all-reduce | flops 1024 | bytes 8192 | tf_op jit(solution)/shard_map/psum | solution.py:335
  924.9 69.3 %all-reduce.6.cloned.1.call-done = f32[18,2048]{1,0:T(8,128)} async-done(((f32[18,2048]{1,0:T(8,128)}), f32[18,2048]{1,0:T(8,128)}) %all-reduce.6.cloned.1.call-update) | async-done | bytes 147472 | tf_op jit(solution)/shard_map/psum | solution.py:329
  997.3 176.8 %all-reduce.8.cloned.1.call-done = (bf16[2048,3,512]{2,0,1:T(8,128)(2,1)}, bf16[512,2048]{1,0:T(8,128)(2,1)}) async-done(((bf16[2048,3,512]{2,0,1:T(8,128)(2,1)}, bf16[512,2048]{1,0:T(8,128)(2,1)}), (bf16[2048,3,512]{2,0,1:T(8,128)(2,1)}, bf16[512,2048]{1,0:T(8,128)(2,1)})) %all-reduce.8.cloned.1.call-update) | async-done | bytes 8388624 | tf_op jit(solution)/shard_map/psum | solution.py:107
  1174.1 9.5 reshape.739
  (788 shorter events, 375.2 us)
Async XLA Ops:
  7.2 987.0 %all-reduce.6.cloned.1.call-start = ((), (), s32[]{:S(2)}) async-start(), calls=%async_computation | async-start | bytes 393216 | tf_op jit(solution)/shard_map/psum | solution.py:329
  11.2 46.2 %collective-permute-start = (bf16[64,2048]{1,0:T(8,128)(2,1)}, bf16[64,2048]{1,0:T(8,128)(2,1)}, u32[]{:S(2)}, u32[]{:S(2)}) collective-permute-start(bf16[64,2048]{1,0:T(8,128)(2,1)} %get-tuple-element.212), channel_id=1, source_target_pairs={{0,8},{8,0},{16,24},{24,16},{1,9},{9,1},{17,25},{25,17},{2,10},{10... | collective-permute-start | bytes 786440 | tf_op jit(solution)/shard_map/ppermute | solution.py:33
  14.2 43.3 %collective-permute-start.1 = (bf16[64,2048]{1,0:T(8,128)(2,1)}, bf16[64,2048]{1,0:T(8,128)(2,1)}, u32[]{:S(2)}, u32[]{:S(2)}) collective-permute-start(bf16[64,2048]{1,0:T(8,128)(2,1)} %get-tuple-element.212), channel_id=1, source_target_pairs={{0,16},{8,24},{16,0},{24,8},{1,17},{9,25},{17,1},{25,9},{2,18},{10... | collective-permute-start | bytes 786440 | tf_op jit(solution)/shard_map/ppermute | solution.py:33
  15.7 43.9 %collective-permute-start.2 = (bf16[64,2048]{1,0:T(8,128)(2,1)}, bf16[64,2048]{1,0:T(8,128)(2,1)}, u32[]{:S(2)}, u32[]{:S(2)}) collective-permute-start(bf16[64,2048]{1,0:T(8,128)(2,1)} %get-tuple-element.212), channel_id=1, source_target_pairs={{0,24},{8,16},{16,8},{24,0},{1,25},{9,17},{17,9},{25,1},{2,26},{10... | collective-permute-start | bytes 786440 | tf_op jit(solution)/shard_map/ppermute | solution.py:33
  15.7 49.6 %collective-permute-start.33 = (bf16[64,2048]{1,0:T(8,128)(2,1)}, bf16[64,2048]{1,0:T(8,128)(2,1)}, u32[]{:S(2)}, u32[]{:S(2)}) collective-permute-start(bf16[64,2048]{1,0:T(8,128)(2,1)} %get-tuple-element.213), channel_id=1, source_target_pairs={{0,8},{8,0},{16,24},{24,16},{1,9},{9,1},{17,25},{25,17},{2,10},{10... | collective-permute-start | bytes 786440 | tf_op jit(solution)/shard_map/ppermute | solution.py:33
  17.7 47.8 %collective-permute-start.34 = (bf16[64,2048]{1,0:T(8,128)(2,1)}, bf16[64,2048]{1,0:T(8,128)(2,1)}, u32[]{:S(2)}, u32[]{:S(2)}) collective-permute-start(bf16[64,2048]{1,0:T(8,128)(2,1)} %get-tuple-element.213), channel_id=1, source_target_pairs={{0,16},{8,24},{16,0},{24,8},{1,17},{9,25},{17,1},{25,9},{2,18},{10... | collective-permute-start | bytes 786440 | tf_op jit(solution)/shard_map/ppermute | solution.py:33
  57.5 68.0 %collective-permute-start.50 = (bf16[64,2176]{1,0:T(8,128)(2,1)}, bf16[64,2176]{1,0:T(8,128)(2,1)}, u32[]{:S(2)}, u32[]{:S(2)}) collective-permute-start(bf16[64,2176]{1,0:T(8,128)(2,1)} %get-tuple-element.253), channel_id=1, source_target_pairs={{0,2},{1,3},{2,0},{3,1},{4,6},{5,7},{6,4},{7,5},{8,10},{9,11},{10,... | collective-permute-start | bytes 835592 | tf_op jit(solution)/shard_map/ppermute | solution.py:38
  59.5 68.1 %collective-permute-start.51 = (bf16[64,2176]{1,0:T(8,128)(2,1)}, bf16[64,2176]{1,0:T(8,128)(2,1)}, u32[]{:S(2)}, u32[]{:S(2)}) collective-permute-start(bf16[64,2176]{1,0:T(8,128)(2,1)} %get-tuple-element.253), channel_id=1, source_target_pairs={{0,4},{1,5},{2,6},{3,7},{4,0},{5,1},{6,2},{7,3},{8,12},{9,13},{10,... | collective-permute-start | bytes 835592 | tf_op jit(solution)/shard_map/ppermute | solution.py:38
  65.3 62.7 %collective-permute-start.52 = (bf16[64,2176]{1,0:T(8,128)(2,1)}, bf16[64,2176]{1,0:T(8,128)(2,1)}, u32[]{:S(2)}, u32[]{:S(2)}) collective-permute-start(bf16[64,2176]{1,0:T(8,128)(2,1)} %get-tuple-element.253), channel_id=1, source_target_pairs={{0,6},{1,7},{2,4},{3,5},{4,2},{5,3},{6,0},{7,1},{8,14},{9,15},{10,... | collective-permute-start | bytes 835592 | tf_op jit(solution)/shard_map/ppermute | solution.py:38
  65.5 70.1 %collective-permute-start.17 = (bf16[64,2176]{1,0:T(8,128)(2,1)}, bf16[64,2176]{1,0:T(8,128)(2,1)}, u32[]{:S(2)}, u32[]{:S(2)}) collective-permute-start(bf16[64,2176]{1,0:T(8,128)(2,1)} %get-tuple-element.244), channel_id=1, source_target_pairs={{0,2},{1,3},{2,0},{3,1},{4,6},{5,7},{6,4},{7,5},{8,10},{9,11},{10,... | collective-permute-start | bytes 835592 | tf_op jit(solution)/shard_map/ppermute | solution.py:38
  90.8 48.1 %collective-permute-start.18 = (bf16[64,2176]{1,0:T(8,128)(2,1)}, bf16[64,2176]{1,0:T(8,128)(2,1)}, u32[]{:S(2)}, u32[]{:S(2)}) collective-permute-start(bf16[64,2176]{1,0:T(8,128)(2,1)} %get-tuple-element.244), channel_id=1, source_target_pairs={{0,4},{1,5},{2,6},{3,7},{4,0},{5,1},{6,2},{7,3},{8,12},{9,13},{10,... | collective-permute-start | bytes 835592 | tf_op jit(solution)/shard_map/ppermute | solution.py:38
  147.1 32.8 %collective-permute-start.53 = (bf16[256,2176]{1,0:T(8,128)(2,1)}, bf16[256,2176]{1,0:T(8,128)(2,1)}, u32[]{:S(2)}, u32[]{:S(2)}) collective-permute-start(bf16[256,2176]{1,0:T(8,128)(2,1)} %pad_maximum_fusion.22), channel_id=1, source_target_pairs={{0,8},{8,0},{16,24},{24,16},{1,9},{9,1},{17,25},{25,17},{2,10},{10... | collective-permute-start | bytes 3342344 | tf_op jit(solution)/shard_map/ppermute | solution.py:33
  147.5 37.7 %collective-permute-start.54 = (bf16[256,2176]{1,0:T(8,128)(2,1)}, bf16[256,2176]{1,0:T(8,128)(2,1)}, u32[]{:S(2)}, u32[]{:S(2)}) collective-permute-start(bf16[256,2176]{1,0:T(8,128)(2,1)} %pad_maximum_fusion.22), channel_id=1, source_target_pairs={{0,16},{8,24},{16,0},{24,8},{1,17},{9,25},{17,1},{25,9},{2,18},{10... | collective-permute-start | bytes 3342344 | tf_op jit(solution)/shard_map/ppermute | solution.py:33
  150.3 47.1 %collective-permute-start.20 = (bf16[256,2176]{1,0:T(8,128)(2,1)}, bf16[256,2176]{1,0:T(8,128)(2,1)}, u32[]{:S(2)}, u32[]{:S(2)}) collective-permute-start(bf16[256,2176]{1,0:T(8,128)(2,1)} %pad_maximum_fusion.21), channel_id=1, source_target_pairs={{0,8},{8,0},{16,24},{24,16},{1,9},{9,1},{17,25},{25,17},{2,10},{10... | collective-permute-start | bytes 3342344 | tf_op jit(solution)/shard_map/ppermute | solution.py:33
  151.9 51.1 %collective-permute-start.21 = (bf16[256,2176]{1,0:T(8,128)(2,1)}, bf16[256,2176]{1,0:T(8,128)(2,1)}, u32[]{:S(2)}, u32[]{:S(2)}) collective-permute-start(bf16[256,2176]{1,0:T(8,128)(2,1)} %pad_maximum_fusion.21), channel_id=1, source_target_pairs={{0,16},{8,24},{16,0},{24,8},{1,17},{9,25},{17,1},{25,9},{2,18},{10... | collective-permute-start | bytes 3342344 | tf_op jit(solution)/shard_map/ppermute | solution.py:33
  160.3 62.9 %collective-permute-start.42 = (bf16[64,2048]{1,0:T(8,128)(2,1)S(1)}, bf16[64,2048]{1,0:T(8,128)(2,1)S(1)}, u32[]{:S(2)}, u32[]{:S(2)}) collective-permute-start(bf16[64,2048]{1,0:T(8,128)(2,1)S(1)} %get-tuple-element.281), channel_id=1, source_target_pairs={{0,2},{1,3},{2,0},{3,1},{4,6},{5,7},{6,4},{7,5},{8,10},{9,11},{10,... | collective-permute-start | bytes 786440 | tf_op jit(solution)/shard_map/ppermute | solution.py:38
  179.9 45.0 %collective-permute-start.43 = (bf16[64,2048]{1,0:T(8,128)(2,1)S(1)}, bf16[64,2048]{1,0:T(8,128)(2,1)S(1)}, u32[]{:S(2)}, u32[]{:S(2)}) collective-permute-start(bf16[64,2048]{1,0:T(8,128)(2,1)S(1)} %get-tuple-element.281), channel_id=1, source_target_pairs={{0,4},{1,5},{2,6},{3,7},{4,0},{5,1},{6,2},{7,3},{8,12},{9,13},{10,... | collective-permute-start | bytes 786440 | tf_op jit(solution)/shard_map/ppermute | solution.py:38
  185.2 42.5 %collective-permute-start.44 = (bf16[64,2048]{1,0:T(8,128)(2,1)S(1)}, bf16[64,2048]{1,0:T(8,128)(2,1)S(1)}, u32[]{:S(2)}, u32[]{:S(2)}) collective-permute-start(bf16[64,2048]{1,0:T(8,128)(2,1)S(1)} %get-tuple-element.281), channel_id=1, source_target_pairs={{0,6},{1,7},{2,4},{3,5},{4,2},{5,3},{6,0},{7,1},{8,14},{9,15},{10,... | collective-permute-start | bytes 786440 | tf_op jit(solution)/shard_map/ppermute | solution.py:38
  222.1 95.5 %collective-permute-start.57 = (bf16[1024,2176]{1,0:T(8,128)(2,1)S(1)}, bf16[1024,2176]{1,0:T(8,128)(2,1)S(1)}, u32[]{:S(2)}, u32[]{:S(2)}) collective-permute-start(bf16[1024,2176]{1,0:T(8,128)(2,1)S(1)} %get-tuple-element.204), channel_id=1, source_target_pairs={{0,1},{1,0},{2,3},{3,2},{4,5},{5,4},{6,7},{7,6},{8,9},{9,8},{10,11... | collective-permute-start | bytes 13369352 | tf_op jit(solution)/shard_map/ppermute | solution.py:38
  223.2 21.0 %collective-permute-start.10 = (bf16[64,2048]{1,0:T(8,128)(2,1)S(1)}, bf16[64,2048]{1,0:T(8,128)(2,1)S(1)}, u32[]{:S(2)}, u32[]{:S(2)}) collective-permute-start(bf16[64,2048]{1,0:T(8,128)(2,1)S(1)} %get-tuple-element.93), channel_id=1, source_target_pairs={{0,4},{1,5},{2,6},{3,7},{4,0},{5,1},{6,2},{7,3},{8,12},{9,13},{10,... | collective-permute-start | bytes 786440 | tf_op jit(solution)/shard_map/ppermute | solution.py:38
  224.9 20.8 %collective-permute-start.11 = (bf16[64,2048]{1,0:T(8,128)(2,1)S(1)}, bf16[64,2048]{1,0:T(8,128)(2,1)S(1)}, u32[]{:S(2)}, u32[]{:S(2)}) collective-permute-start(bf16[64,2048]{1,0:T(8,128)(2,1)S(1)} %get-tuple-element.93), channel_id=1, source_target_pairs={{0,6},{1,7},{2,4},{3,5},{4,2},{5,3},{6,0},{7,1},{8,14},{9,15},{10,... | collective-permute-start | bytes 786440 | tf_op jit(solution)/shard_map/ppermute | solution.py:38
  226.1 20.7 %collective-permute-start.9 = (bf16[64,2048]{1,0:T(8,128)(2,1)S(1)}, bf16[64,2048]{1,0:T(8,128)(2,1)S(1)}, u32[]{:S(2)}, u32[]{:S(2)}) collective-permute-start(bf16[64,2048]{1,0:T(8,128)(2,1)S(1)} %get-tuple-element.93), channel_id=1, source_target_pairs={{0,2},{1,3},{2,0},{3,1},{4,6},{5,7},{6,4},{7,5},{8,10},{9,11},{10,... | collective-permute-start | bytes 786440 | tf_op jit(solution)/shard_map/ppermute | solution.py:38
  227.7 92.3 %collective-permute-start.24 = (bf16[1024,2176]{1,0:T(8,128)(2,1)}, bf16[1024,2176]{1,0:T(8,128)(2,1)S(1)}, u32[]{:S(2)}, u32[]{:S(2)}) collective-permute-start(bf16[1024,2176]{1,0:T(8,128)(2,1)} %get-tuple-element.200), channel_id=1, source_target_pairs={{0,1},{1,0},{2,3},{3,2},{4,5},{5,4},{6,7},{7,6},{8,9},{9,8},{10,11... | collective-permute-start | bytes 13369352 | tf_op jit(solution)/shard_map/ppermute | solution.py:38
  244.2 26.0 %collective-permute-start.45 = (bf16[256,2048]{1,0:T(8,128)(2,1)S(1)}, bf16[256,2048]{1,0:T(8,128)(2,1)S(1)}, u32[]{:S(2)}, u32[]{:S(2)}) collective-permute-start(bf16[256,2048]{1,0:T(8,128)(2,1)S(1)} %pad_maximum_fusion.27), channel_id=1, source_target_pairs={{0,8},{8,0},{16,24},{24,16},{1,9},{9,1},{17,25},{25,17},{2,10},{10... | collective-permute-start | bytes 3145736 | tf_op jit(solution)/shard_map/ppermute | solution.py:33
  245.7 26.1 %collective-permute-start.46 = (bf16[256,2048]{1,0:T(8,128)(2,1)S(1)}, bf16[256,2048]{1,0:T(8,128)(2,1)S(1)}, u32[]{:S(2)}, u32[]{:S(2)}) collective-permute-start(bf16[256,2048]{1,0:T(8,128)(2,1)S(1)} %pad_maximum_fusion.27), channel_id=1, source_target_pairs={{0,16},{8,24},{16,0},{24,8},{1,17},{9,25},{17,1},{25,9},{2,18},{10... | collective-permute-start | bytes 3145736 | tf_op jit(solution)/shard_map/ppermute | solution.py:33
  247.0 44.6 %collective-permute-start.12 = (bf16[256,2048]{1,0:T(8,128)(2,1)S(1)}, bf16[256,2048]{1,0:T(8,128)(2,1)S(1)}, u32[]{:S(2)}, u32[]{:S(2)}) collective-permute-start(bf16[256,2048]{1,0:T(8,128)(2,1)S(1)} %pad_maximum_fusion.24), channel_id=1, source_target_pairs={{0,8},{8,0},{16,24},{24,16},{1,9},{9,1},{17,25},{25,17},{2,10},{10... | collective-permute-start | bytes 3145736 | tf_op jit(solution)/shard_map/ppermute | solution.py:33
  270.2 26.1 %collective-permute-start.13 = (bf16[256,2048]{1,0:T(8,128)(2,1)S(1)}, bf16[256,2048]{1,0:T(8,128)(2,1)S(1)}, u32[]{:S(2)}, u32[]{:S(2)}) collective-permute-start(bf16[256,2048]{1,0:T(8,128)(2,1)S(1)} %pad_maximum_fusion.24), channel_id=1, source_target_pairs={{0,16},{8,24},{16,0},{24,8},{1,17},{9,25},{17,1},{25,9},{2,18},{10... | collective-permute-start | bytes 3145736 | tf_op jit(solution)/shard_map/ppermute | solution.py:33
  271.9 35.7 %collective-permute-start.47 = (bf16[128,2048]{1,0:T(8,128)(2,1)S(1)}, bf16[128,2048]{1,0:T(8,128)(2,1)S(1)}, u32[]{:S(2)}, u32[]{:S(2)}) collective-permute-start(bf16[128,2048]{1,0:T(8,128)(2,1)S(1)} %slice.923), channel_id=1, source_target_pairs={{0,16},{8,24},{16,0},{24,8},{1,17},{9,25},{17,1},{25,9},{2,18},{10... | collective-permute-start | bytes 1572872 | tf_op jit(solution)/shard_map/ppermute | solution.py:33
  296.3 19.3 %collective-permute-start.14 = (bf16[128,2048]{1,0:T(8,128)(2,1)S(1)}, bf16[128,2048]{1,0:T(8,128)(2,1)S(1)}, u32[]{:S(2)}, u32[]{:S(2)}) collective-permute-start(bf16[128,2048]{1,0:T(8,128)(2,1)S(1)} %slice.873), channel_id=1, source_target_pairs={{0,16},{8,24},{16,0},{24,8},{1,17},{9,25},{17,1},{25,9},{2,18},{10... | collective-permute-start | bytes 1572872 | tf_op jit(solution)/shard_map/ppermute | solution.py:33
  310.9 27.3 %collective-permute-start.49 = (bf16[1024,2048]{1,0:T(8,128)(2,1)}, bf16[1024,2048]{1,0:T(8,128)(2,1)}, u32[]{:S(2)}, u32[]{:S(2)}) collective-permute-start(bf16[1024,2048]{1,0:T(8,128)(2,1)} %get-tuple-element.228), channel_id=1, source_target_pairs={{0,1},{1,0},{2,3},{3,2},{4,5},{5,4},{6,7},{7,6},{8,9},{9,8},{10,11... | collective-permute-start | bytes 12582920 | tf_op jit(solution)/shard_map/ppermute | solution.py:38
  317.6 34.4 %collective-permute-start.16 = (bf16[1024,2048]{1,0:T(8,128)(2,1)}, bf16[1024,2048]{1,0:T(8,128)(2,1)}, u32[]{:S(2)}, u32[]{:S(2)}) collective-permute-start(bf16[1024,2048]{1,0:T(8,128)(2,1)} %get-tuple-element.216), channel_id=1, source_target_pairs={{0,1},{1,0},{2,3},{3,2},{4,5},{5,4},{6,7},{7,6},{8,9},{9,8},{10,11... | collective-permute-start | bytes 12582920 | tf_op jit(solution)/shard_map/ppermute | solution.py:38
  445.1 96.8 %collective-permute-start.58 = (bf16[1024,2048]{1,0:T(8,128)(2,1)}, bf16[1024,2048]{1,0:T(8,128)(2,1)}, u32[]{:S(2)}, u32[]{:S(2)}) collective-permute-start(bf16[1024,2048]{1,0:T(8,128)(2,1)} %slice.933), channel_id=1, source_target_pairs={{0,1},{1,0},{2,3},{3,2},{4,5},{5,4},{6,7},{7,6},{8,9},{9,8},{10,11... | collective-permute-start | bytes 12582920 | tf_op jit(solution)/shard_map/ppermute | solution.py:38
  472.8 87.3 %collective-permute-start.83 = (bf16[1024,2176]{1,0:T(8,128)(2,1)}, bf16[1024,2176]{1,0:T(8,128)(2,1)}, u32[]{:S(2)}, u32[]{:S(2)}) collective-permute-start(bf16[1024,2176]{1,0:T(8,128)(2,1)} %pad_maximum_fusion.1), channel_id=1, source_target_pairs={{0,1},{1,0},{2,3},{3,2},{4,5},{5,4},{6,7},{7,6},{8,9},{9,8},{10,11... | collective-permute-start | bytes 13369352 | tf_op jit(solution)/shard_map/ppermute | solution.py:38
  500.8 50.4 %collective-permute-start.25 = (bf16[1024,2048]{1,0:T(8,128)(2,1)}, bf16[1024,2048]{1,0:T(8,128)(2,1)}, u32[]{:S(2)}, u32[]{:S(2)}) collective-permute-start(bf16[1024,2048]{1,0:T(8,128)(2,1)} %slice.883), channel_id=1, source_target_pairs={{0,1},{1,0},{2,3},{3,2},{4,5},{5,4},{6,7},{7,6},{8,9},{9,8},{10,11... | collective-permute-start | bytes 12582920 | tf_op jit(solution)/shard_map/ppermute | solution.py:38
  531.2 33.3 %collective-permute-start.66 = (bf16[1024,2176]{1,0:T(8,128)(2,1)}, bf16[1024,2176]{1,0:T(8,128)(2,1)}, u32[]{:S(2)}, u32[]{:S(2)}) collective-permute-start(bf16[1024,2176]{1,0:T(8,128)(2,1)} %pad_maximum_fusion.2), channel_id=1, source_target_pairs={{0,1},{1,0},{2,3},{3,2},{4,5},{5,4},{6,7},{7,6},{8,9},{9,8},{10,11... | collective-permute-start | bytes 13369352 | tf_op jit(solution)/shard_map/ppermute | solution.py:38
  547.2 26.3 %collective-permute-start.61 = (bf16[512,1024]{1,0:T(8,128)(2,1)}, bf16[512,1024]{1,0:T(8,128)(2,1)}, u32[]{:S(2)}, u32[]{:S(2)}) collective-permute-start(bf16[512,1024]{1,0:T(8,128)(2,1)} %slice.941), channel_id=1, source_target_pairs={{0,16},{8,24},{16,0},{24,8},{1,17},{9,25},{17,1},{25,9},{2,18},{10... | collective-permute-start | bytes 3145736 | tf_op jit(solution)/shard_map/ppermute | solution.py:33
  549.4 26.9 %collective-permute-start.59 = (bf16[512,1024]{1,0:T(8,128)(2,1)}, bf16[512,1024]{1,0:T(8,128)(2,1)S(1)}, u32[]{:S(2)}, u32[]{:S(2)}) collective-permute-start(bf16[512,1024]{1,0:T(8,128)(2,1)} %pad_maximum_fusion.28), channel_id=1, source_target_pairs={{0,8},{8,0},{16,24},{24,16},{1,9},{9,1},{17,25},{25,17},{2,10},{10... | collective-permute-start | bytes 3145736 | tf_op jit(solution)/shard_map/ppermute | solution.py:33
  557.7 38.3 %collective-permute-start.28 = (bf16[512,1024]{1,0:T(8,128)(2,1)}, bf16[512,1024]{1,0:T(8,128)(2,1)}, u32[]{:S(2)}, u32[]{:S(2)}) collective-permute-start(bf16[512,1024]{1,0:T(8,128)(2,1)} %slice.891), channel_id=1, source_target_pairs={{0,16},{8,24},{16,0},{24,8},{1,17},{9,25},{17,1},{25,9},{2,18},{10... | collective-permute-start | bytes 3145736 | tf_op jit(solution)/shard_map/ppermute | solution.py:33
  560.0 38.4 %collective-permute-start.26 = (bf16[512,1024]{1,0:T(8,128)(2,1)}, bf16[512,1024]{1,0:T(8,128)(2,1)}, u32[]{:S(2)}, u32[]{:S(2)}) collective-permute-start(bf16[512,1024]{1,0:T(8,128)(2,1)} %pad_maximum_fusion.25), channel_id=1, source_target_pairs={{0,8},{8,0},{16,24},{24,16},{1,9},{9,1},{17,25},{25,17},{2,10},{10... | collective-permute-start | bytes 3145736 | tf_op jit(solution)/shard_map/ppermute | solution.py:33
  568.2 52.4 %collective-permute-start.84 = (bf16[512,1024]{1,0:T(8,128)(2,1)S(1)}, bf16[512,1024]{1,0:T(8,128)(2,1)S(1)}, u32[]{:S(2)}, u32[]{:S(2)}) collective-permute-start(bf16[512,1024]{1,0:T(8,128)(2,1)S(1)} %pad_maximum_fusion.31), channel_id=1, source_target_pairs={{0,8},{8,0},{16,24},{24,16},{1,9},{9,1},{17,25},{25,17},{2,10},{10... | collective-permute-start | bytes 3145736 | tf_op jit(solution)/shard_map/ppermute | solution.py:33
  573.5 71.8 %collective-permute-start.86 = (bf16[512,1152]{1,0:T(8,128)(2,1)S(1)}, bf16[512,1152]{1,0:T(8,128)(2,1)S(1)}, u32[]{:S(2)}, u32[]{:S(2)}) collective-permute-start(bf16[512,1152]{1,0:T(8,128)(2,1)S(1)} %slice.1005), channel_id=1, source_target_pairs={{0,16},{8,24},{16,0},{24,8},{1,17},{9,25},{17,1},{25,9},{2,18},{10... | collective-permute-start | bytes 3538952 | tf_op jit(solution)/shard_map/ppermute | solution.py:33
  576.3 66.7 %collective-permute-start.67 = (bf16[512,1024]{1,0:T(8,128)(2,1)S(1)}, bf16[512,1024]{1,0:T(8,128)(2,1)S(1)}, u32[]{:S(2)}, u32[]{:S(2)}) collective-permute-start(bf16[512,1024]{1,0:T(8,128)(2,1)S(1)} %pad_maximum_fusion.29), channel_id=1, source_target_pairs={{0,8},{8,0},{16,24},{24,16},{1,9},{9,1},{17,25},{25,17},{2,10},{10... | collective-permute-start | bytes 3145736 | tf_op jit(solution)/shard_map/ppermute | solution.py:33
  596.0 50.7 %collective-permute-start.69 = (bf16[512,1152]{1,0:T(8,128)(2,1)S(1)}, bf16[512,1152]{1,0:T(8,128)(2,1)S(1)}, u32[]{:S(2)}, u32[]{:S(2)}) collective-permute-start(bf16[512,1152]{1,0:T(8,128)(2,1)S(1)} %slice.962), channel_id=1, source_target_pairs={{0,16},{8,24},{16,0},{24,8},{1,17},{9,25},{17,1},{25,9},{2,18},{10... | collective-permute-start | bytes 3538952 | tf_op jit(solution)/shard_map/ppermute | solution.py:33
  598.5 55.8 %collective-permute-start.62 = (bf16[256,1024]{1,0:T(8,128)(2,1)S(1)}, bf16[256,1024]{1,0:T(8,128)(2,1)S(1)}, u32[]{:S(2)}, u32[]{:S(2)}) collective-permute-start(bf16[256,1024]{1,0:T(8,128)(2,1)S(1)} %slice.943), channel_id=1, source_target_pairs={{0,8},{8,0},{16,24},{24,16},{1,9},{9,1},{17,25},{25,17},{2,10},{10... | collective-permute-start | bytes 1572872 | tf_op jit(solution)/shard_map/ppermute | solution.py:33
  620.6 37.1 %collective-permute-start.60 = (bf16[256,1024]{1,0:T(8,128)(2,1)S(1)}, bf16[256,1024]{1,0:T(8,128)(2,1)S(1)}, u32[]{:S(2)}, u32[]{:S(2)}) collective-permute-start(bf16[256,1024]{1,0:T(8,128)(2,1)S(1)} %slice.939), channel_id=1, source_target_pairs={{0,16},{8,24},{16,0},{24,8},{1,17},{9,25},{17,1},{25,9},{2,18},{10... | collective-permute-start | bytes 1572872 | tf_op jit(solution)/shard_map/ppermute | solution.py:33
  643.0 22.5 %collective-permute-start.29 = (bf16[256,1024]{1,0:T(8,128)(2,1)S(1)}, bf16[256,1024]{1,0:T(8,128)(2,1)S(1)}, u32[]{:S(2)}, u32[]{:S(2)}) collective-permute-start(bf16[256,1024]{1,0:T(8,128)(2,1)S(1)} %slice.893), channel_id=1, source_target_pairs={{0,8},{8,0},{16,24},{24,16},{1,9},{9,1},{17,25},{25,17},{2,10},{10... | collective-permute-start | bytes 1572872 | tf_op jit(solution)/shard_map/ppermute | solution.py:33
  645.4 23.5 %collective-permute-start.27 = (bf16[256,1024]{1,0:T(8,128)(2,1)S(1)}, bf16[256,1024]{1,0:T(8,128)(2,1)S(1)}, u32[]{:S(2)}, u32[]{:S(2)}) collective-permute-start(bf16[256,1024]{1,0:T(8,128)(2,1)S(1)} %slice.889), channel_id=1, source_target_pairs={{0,16},{8,24},{16,0},{24,8},{1,17},{9,25},{17,1},{25,9},{2,18},{10... | collective-permute-start | bytes 1572872 | tf_op jit(solution)/shard_map/ppermute | solution.py:33
  646.7 33.5 %collective-permute-start.85 = (bf16[256,1024]{1,0:T(8,128)(2,1)S(1)}, bf16[256,1024]{1,0:T(8,128)(2,1)S(1)}, u32[]{:S(2)}, u32[]{:S(2)}) collective-permute-start(bf16[256,1024]{1,0:T(8,128)(2,1)S(1)} %slice.1003), channel_id=1, source_target_pairs={{0,16},{8,24},{16,0},{24,8},{1,17},{9,25},{17,1},{25,9},{2,18},{10... | collective-permute-start | bytes 1572872 | tf_op jit(solution)/shard_map/ppermute | solution.py:33
  654.3 36.2 %collective-permute-start.68 = (bf16[256,1024]{1,0:T(8,128)(2,1)S(1)}, bf16[256,1024]{1,0:T(8,128)(2,1)S(1)}, u32[]{:S(2)}, u32[]{:S(2)}) collective-permute-start(bf16[256,1024]{1,0:T(8,128)(2,1)S(1)} %slice.960), channel_id=1, source_target_pairs={{0,16},{8,24},{16,0},{24,8},{1,17},{9,25},{17,1},{25,9},{2,18},{10... | collective-permute-start | bytes 1572872 | tf_op jit(solution)/shard_map/ppermute | solution.py:33
  657.7 32.9 %collective-permute-start.87 = (bf16[256,1152]{1,0:T(8,128)(2,1)S(1)}, bf16[256,1152]{1,0:T(8,128)(2,1)S(1)}, u32[]{:S(2)}, u32[]{:S(2)}) collective-permute-start(bf16[256,1152]{1,0:T(8,128)(2,1)S(1)} %slice.1007), channel_id=1, source_target_pairs={{0,8},{8,0},{16,24},{24,16},{1,9},{9,1},{17,25},{25,17},{2,10},{10... | collective-permute-start | bytes 1769480 | tf_op jit(solution)/shard_map/ppermute | solution.py:33
  665.5 31.8 %collective-permute-start.70 = (bf16[256,1152]{1,0:T(8,128)(2,1)S(1)}, bf16[256,1152]{1,0:T(8,128)(2,1)S(1)}, u32[]{:S(2)}, u32[]{:S(2)}) collective-permute-start(bf16[256,1152]{1,0:T(8,128)(2,1)S(1)} %slice.964), channel_id=1, source_target_pairs={{0,8},{8,0},{16,24},{24,16},{1,9},{9,1},{17,25},{25,17},{2,10},{10... | collective-permute-start | bytes 1769480 | tf_op jit(solution)/shard_map/ppermute | solution.py:33
  668.9 103.4 %collective-permute-start.63 = (bf16[64,2048]{1,0:T(8,128)(2,1)S(1)}, bf16[64,2048]{1,0:T(8,128)(2,1)S(1)}, u32[]{:S(2)}, u32[]{:S(2)}) collective-permute-start(bf16[64,2048]{1,0:T(8,128)(2,1)S(1)} %get-tuple-element.175), channel_id=1, source_target_pairs={{0,2},{1,3},{2,0},{3,1},{4,6},{5,7},{6,4},{7,5},{8,10},{9,11},{10,... | collective-permute-start | bytes 786440 | tf_op jit(solution)/shard_map/ppermute | solution.py:38
  680.2 92.2 %collective-permute-start.64 = (bf16[64,2048]{1,0:T(8,128)(2,1)S(1)}, bf16[64,2048]{1,0:T(8,128)(2,1)S(1)}, u32[]{:S(2)}, u32[]{:S(2)}) collective-permute-start(bf16[64,2048]{1,0:T(8,128)(2,1)S(1)} %get-tuple-element.177), channel_id=1, source_target_pairs={{0,4},{1,5},{2,6},{3,7},{4,0},{5,1},{6,2},{7,3},{8,12},{9,13},{10,... | collective-permute-start | bytes 786440 | tf_op jit(solution)/shard_map/ppermute | solution.py:38
  696.2 22.5 %collective-permute-start.89 = (bf16[64,2176]{1,0:T(8,128)(2,1)S(1)}, bf16[64,2176]{1,0:T(8,128)(2,1)S(1)}, u32[]{:S(2)}, u32[]{:S(2)}) collective-permute-start(bf16[64,2176]{1,0:T(8,128)(2,1)S(1)} %get-tuple-element.157), channel_id=1, source_target_pairs={{0,4},{1,5},{2,6},{3,7},{4,0},{5,1},{6,2},{7,3},{8,12},{9,13},{10,... | collective-permute-start | bytes 835592 | tf_op jit(solution)/shard_map/ppermute | solution.py:38
  697.3 21.4 %collective-permute-start.90 = (bf16[64,2176]{1,0:T(8,128)(2,1)S(1)}, bf16[64,2176]{1,0:T(8,128)(2,1)S(1)}, u32[]{:S(2)}, u32[]{:S(2)}) collective-permute-start(bf16[64,2176]{1,0:T(8,128)(2,1)S(1)} %get-tuple-element.156), channel_id=1, source_target_pairs={{0,6},{1,7},{2,4},{3,5},{4,2},{5,3},{6,0},{7,1},{8,14},{9,15},{10,... | collective-permute-start | bytes 835592 | tf_op jit(solution)/shard_map/ppermute | solution.py:38
  718.7 25.2 %collective-permute-start.72 = (bf16[64,2176]{1,0:T(8,128)(2,1)S(1)}, bf16[64,2176]{1,0:T(8,128)(2,1)S(1)}, u32[]{:S(2)}, u32[]{:S(2)}) collective-permute-start(bf16[64,2176]{1,0:T(8,128)(2,1)S(1)} %get-tuple-element.154), channel_id=1, source_target_pairs={{0,4},{1,5},{2,6},{3,7},{4,0},{5,1},{6,2},{7,3},{8,12},{9,13},{10,... | collective-permute-start | bytes 835592 | tf_op jit(solution)/shard_map/ppermute | solution.py:38
  718.7 25.2 %collective-permute-start.73 = (bf16[64,2176]{1,0:T(8,128)(2,1)S(1)}, bf16[64,2176]{1,0:T(8,128)(2,1)S(1)}, u32[]{:S(2)}, u32[]{:S(2)}) collective-permute-start(bf16[64,2176]{1,0:T(8,128)(2,1)S(1)} %get-tuple-element.153), channel_id=1, source_target_pairs={{0,6},{1,7},{2,4},{3,5},{4,2},{5,3},{6,0},{7,1},{8,14},{9,15},{10,... | collective-permute-start | bytes 835592 | tf_op jit(solution)/shard_map/ppermute | solution.py:38
  722.3 27.1 %collective-permute-start.30 = (bf16[64,2048]{1,0:T(8,128)(2,1)S(1)}, bf16[64,2048]{1,0:T(8,128)(2,1)S(1)}, u32[]{:S(2)}, u32[]{:S(2)}) collective-permute-start(bf16[64,2048]{1,0:T(8,128)(2,1)S(1)} %get-tuple-element.172), channel_id=1, source_target_pairs={{0,2},{1,3},{2,0},{3,1},{4,6},{5,7},{6,4},{7,5},{8,10},{9,11},{10,... | collective-permute-start | bytes 786440 | tf_op jit(solution)/shard_map/ppermute | solution.py:38
  743.9 27.1 %collective-permute-start.31 = (bf16[64,2048]{1,0:T(8,128)(2,1)S(1)}, bf16[64,2048]{1,0:T(8,128)(2,1)S(1)}, u32[]{:S(2)}, u32[]{:S(2)}) collective-permute-start(bf16[64,2048]{1,0:T(8,128)(2,1)S(1)} %get-tuple-element.174), channel_id=1, source_target_pairs={{0,4},{1,5},{2,6},{3,7},{4,0},{5,1},{6,2},{7,3},{8,12},{9,13},{10,... | collective-permute-start | bytes 786440 | tf_op jit(solution)/shard_map/ppermute | solution.py:38
  743.9 27.1 %collective-permute-start.32 = (bf16[64,2048]{1,0:T(8,128)(2,1)S(1)}, bf16[64,2048]{1,0:T(8,128)(2,1)S(1)}, u32[]{:S(2)}, u32[]{:S(2)}) collective-permute-start(bf16[64,2048]{1,0:T(8,128)(2,1)S(1)} %get-tuple-element.173), channel_id=1, source_target_pairs={{0,6},{1,7},{2,4},{3,5},{4,2},{5,3},{6,0},{7,1},{8,14},{9,15},{10,... | collective-permute-start | bytes 786440 | tf_op jit(solution)/shard_map/ppermute | solution.py:38
  749.4 23.0 %collective-permute-start.65 = (bf16[64,2048]{1,0:T(8,128)(2,1)S(1)}, bf16[64,2048]{1,0:T(8,128)(2,1)S(1)}, u32[]{:S(2)}, u32[]{:S(2)}) collective-permute-start(bf16[64,2048]{1,0:T(8,128)(2,1)S(1)} %get-tuple-element.176), channel_id=1, source_target_pairs={{0,6},{1,7},{2,4},{3,5},{4,2},{5,3},{6,0},{7,1},{8,14},{9,15},{10,... | collective-permute-start | bytes 786440 | tf_op jit(solution)/shard_map/ppermute | solution.py:38
  777.5 22.3 %collective-permute-start.74 = (bf16[64,2048]{1,0:T(8,128)(2,1)S(1)}, bf16[64,2048]{1,0:T(8,128)(2,1)}, u32[]{:S(2)}, u32[]{:S(2)}) collective-permute-start(bf16[64,2048]{1,0:T(8,128)(2,1)S(1)} %get-tuple-element.90), channel_id=1, source_target_pairs={{0,8},{8,0},{16,24},{24,16},{1,9},{9,1},{17,25},{25,17},{2,10},{10... | collective-permute-start | bytes 786440 | tf_op jit(solution)/shard_map/ppermute | solution.py:33
  778.6 21.2 %collective-permute-start.75 = (bf16[64,2048]{1,0:T(8,128)(2,1)S(1)}, bf16[64,2048]{1,0:T(8,128)(2,1)}, u32[]{:S(2)}, u32[]{:S(2)}) collective-permute-start(bf16[64,2048]{1,0:T(8,128)(2,1)S(1)} %get-tuple-element.90), channel_id=1, source_target_pairs={{0,16},{8,24},{16,0},{24,8},{1,17},{9,25},{17,1},{25,9},{2,18},{10... | collective-permute-start | bytes 786440 | tf_op jit(solution)/shard_map/ppermute | solution.py:33
  863.6 310.5 %all-reduce.8.cloned.1.call-start = ((), (), s32[]{:S(2)}) async-start(), calls=%async_computation.1 | async-start | bytes 16777216 | tf_op jit(solution)/shard_map/psum | solution.py:107
  (220 other events, 3337.6 us)
Sparse Core Ops, SparseCore 0:
  863.7 130.4 all-reduce.5
  997.2 176.8 all-reduce.7

commit v2 on v1

v2 whole, which is shorter than its diff:
```python
import functools

import jax
import jax.numpy as jnp
from jax import lax
from jax.experimental import pallas as pl
from jax.experimental.pallas import tpu as pltpu
from jax.sharding import PartitionSpec as P

HD = 128
EPSILON = 1e-05
LANES = 128
BF = jnp.bfloat16
F32 = jnp.float32
VMEM_BYTES = 56 * 1024 * 1024
EXPERT_TILE = 512
COST_SCALE = 8


def rms_scale(values):
    return lax.rsqrt(jnp.mean(values * values, axis=-1, keepdims=True) + EPSILON)


def contract(left, right, left_dim, right_dim):
    return lax.dot_general(
        left, right, (((left_dim,), (right_dim,)), ((), ())), preferred_element_type=F32
    )


def swap_tp(value, bits):
    size = lax.axis_size("tp")
    return lax.ppermute(value, "tp", [(i, i ^ bits) for i in range(size)])


def swap_dp(value, bits):
    size = lax.axis_size("dp")
    return lax.ppermute(value, "dp", [(i, i ^ bits) for i in range(size)])


def sync(*values):
    return lax.optimization_barrier(values)


def after(value, *deps):
    return lax.optimization_barrier((value, *deps))[0]


def add_low(*terms):
    total = terms[0].astype(F32)
    for term in terms[1:]:
        total = total + term.astype(F32)
    return total


def gather_tp(rows):
    size = lax.axis_size("tp")
    return jnp.concatenate([rows] + [swap_tp(rows, k) for k in range(1, size)], axis=-2)


def scatter_tp(rows):
    size = lax.axis_size("tp")
    n = rows.shape[-2] // size
    pieces = [rows[..., k * n : (k + 1) * n, :] for k in range(size)]
    return add_low(*[swap_tp(p, k) if k else p for k, p in enumerate(pieces)])


def scatter_tp_first(rows, later):
    size = lax.axis_size("tp")
    n = rows.shape[-2] // size
    pieces = [rows[..., k * n : (k + 1) * n, :] for k in range(size)]
    *pieces, later = lax.optimization_barrier((*pieces, later))
    return add_low(*[swap_tp(p, k) if k else p for k, p in enumerate(pieces)]), later


def sum_tp(rows):
    size = lax.axis_size("tp")
    n = rows.shape[-2] // size
    total = rows
    for k in range(1, size):
        other = swap_tp(rows, k)
        total = total + jnp.concatenate(
            [other[..., (j ^ k) * n : (j ^ k) * n + n, :] for j in range(size)], axis=-2
        )
    return total


def gather_outer(rows, partners):
    return jnp.concatenate([swap_dp(rows, 2 * k) if k else rows for k in partners], axis=-2)


def gather_plane_near(rows):
    return swap_tp(rows, 1), swap_tp(rows, 2)


def gather_plane_far(rows, near, far):
    n = rows.shape[-2] // 2

    def top(value):
        return value[..., :n, :]

    def low(value):
        return value[..., n:, :]

    sent_a, sent_b = lax.optimization_barrier((top(near), low(far)))
    far_a, far_b = swap_tp(sent_a, 2), swap_tp(sent_b, 1)
    return jnp.concatenate(
        [top(rows), top(far), top(near), far_a, low(rows), low(near), low(far), far_b], axis=-2
    )


def scatter_core(own, other):
    return add_low(own, swap_dp(other, 1)).astype(BF)


def cut(rows, count):
    n = rows.shape[-2] // count
    return [rows[..., i * n : (i + 1) * n, :] for i in range(count)]


def scatter_plane_near(rows):
    keep_a, send_a, keep_b, send_b = cut(rows, 4)
    send_a, send_b = lax.optimization_barrier((send_a, send_b))
    got_a, got_b = swap_tp(send_a, 1), swap_tp(send_b, 2)
    return add_low(keep_a, got_a).astype(BF), add_low(keep_b, got_b).astype(BF)


def scatter_plane_far(part_a, part_b):
    (keep_a, send_a), (keep_b, send_b) = cut(part_a, 2), cut(part_b, 2)
    send_a, send_b = lax.optimization_barrier((send_a, send_b))
    got_a, got_b = swap_tp(send_a, 2), swap_tp(send_b, 1)
    return add_low(keep_a, got_a).astype(BF), add_low(keep_b, got_b).astype(BF)


def scatter_outer(part_a, part_b, partners):
    half = len(partners) // 2
    pieces = cut(part_a, half) + cut(part_b, half)
    return add_low(*[swap_dp(p, 2 * k) if k else p for p, k in zip(pieces, partners)])


def sum_dp(value):
    return lax.psum(value.astype(BF), "dp").astype(F32)


def call_kernel(body, ins, outs, grid=(), in_specs=None, out_specs=None, flops=0, moved=0, **extra):
    whole = pl.BlockSpec(memory_space=pltpu.VMEM)
    return pl.pallas_call(
        body,
        out_shape=outs,
        grid=grid,
        in_specs=in_specs or [whole] * len(ins),
        out_specs=out_specs or [whole] * len(outs),
        compiler_params=pltpu.CompilerParams(vmem_limit_bytes=VMEM_BYTES),
        cost_estimate=pl.CostEstimate(
            flops=flops // COST_SCALE, bytes_accessed=moved // COST_SCALE, transcendentals=0
        ),
        **extra,
    )(*ins)


def project_kernel(rows_ref, weight_ref, packed_ref, squares_ref):
    part = pl.program_id(0)
    packed = jnp.dot(rows_ref[...], weight_ref[...], preferred_element_type=F32)
    packed_ref[...] = packed
    lane = lax.broadcasted_iota(jnp.int32, squares_ref.shape, 1)

    @pl.when(part == 0)
    def _():
        squares_ref[...] = jnp.zeros_like(squares_ref)

    @pl.when(part < 2)
    def _():
        total = jnp.sum(packed * packed, axis=1, keepdims=True)
        squares_ref[...] += jnp.where(lane == part, total, 0.0)


def project(normed, qkv_parts):
    micro, group, width = normed.shape
    columns = qkv_parts.shape[2]
    rows = micro * group
    packed, squares = call_kernel(
        project_kernel,
        (normed.reshape(rows, width), qkv_parts),
        [
            jax.ShapeDtypeStruct((rows, 3 * columns), F32),
            jax.ShapeDtypeStruct((rows, LANES), F32),
        ],
        grid=(3,),
        in_specs=[
            pl.BlockSpec((rows, width), lambda i: (0, 0)),
            pl.BlockSpec((None, width, columns), lambda i: (i, 0, 0)),
        ],
        out_specs=[
            pl.BlockSpec((rows, columns), lambda i: (0, i)),
            pl.BlockSpec((rows, LANES), lambda i: (0, 0)),
        ],
        flops=2 * rows * width * 3 * columns,
        moved=2 * width * 3 * columns,
    )
    return packed.reshape(micro, group, 3 * columns), squares.reshape(micro, group, LANES)


def attend_kernel(
    packed_ref, squares_ref, gain_ref, cos_ref, sin_ref, allowed_ref, out_weight_ref,
    used_ref, weights_ref, attended_ref, branch_ref, *, width,
):
    columns = packed_ref.shape[1] // 3
    heads = columns // HD
    cosine, sine = cos_ref[...], sin_ref[...]
    allowed = allowed_ref[...] > 0.0
    scales = lax.rsqrt(squares_ref[:, :2] / width + EPSILON)
    for h in range(heads):
        used = []
        for part in range(2):
            at = slice(part * columns + h * HD, part * columns + (h + 1) * HD)
            values = packed_ref[:, at] * scales[:, part : part + 1]
            values = values * gain_ref[part : part + 1, h * HD : (h + 1) * HD]
            values = (values * cosine + pltpu.roll(values, HD // 2, 1) * sine).astype(BF)
            used_ref[:, at] = values
            used.append(values)
        at = slice(2 * columns + h * HD, 2 * columns + (h + 1) * HD)
        value = packed_ref[:, at].astype(BF)
        used_ref[:, at] = value
        scores = contract(used[0], used[1], 1, 1) * HD ** (-0.5)
        masked = jnp.where(allowed, scores, -1e30)
        top_score = jnp.max(masked, axis=-1, keepdims=True)
        exponent = jnp.where(allowed, jnp.exp(masked - top_score), 0.0)
        weights = exponent / jnp.sum(exponent, axis=-1, keepdims=True)
        weights_ref[h] = weights
        attended_ref[:, h * HD : (h + 1) * HD] = jnp.dot(
            weights.astype(BF), value, preferred_element_type=F32
        ).astype(BF)
    branch_ref[...] = jnp.dot(
        attended_ref[...], out_weight_ref[...], preferred_element_type=F32
    ).astype(BF)


def attend(packed, squares, gain, cosine, sine, allowed, out_weight):
    micro, group = packed.shape[:2]
    columns, width = out_weight.shape
    heads = columns // HD

    def each(*shape):
        return pl.BlockSpec((None,) + shape, lambda m: (m,) + (0,) * len(shape))

    return call_kernel(
        functools.partial(attend_kernel, width=width),
        (packed, squares, gain, cosine, sine, allowed, out_weight),
        [
            jax.ShapeDtypeStruct((micro, group, 3 * columns), BF),
            jax.ShapeDtypeStruct((micro, heads, group, group), F32),
            jax.ShapeDtypeStruct((micro, group, columns), BF),
            jax.ShapeDtypeStruct((micro, group, width), BF),
        ],
        grid=(micro,),
        in_specs=[
            each(group, 3 * columns),
            each(group, LANES),
            pl.BlockSpec((2, columns), lambda m: (0, 0)),
            each(group, HD),
            each(group, HD),
            each(group, group),
            pl.BlockSpec((columns, width), lambda m: (0, 0)),
        ],
        out_specs=[
            each(group, 3 * columns),
            each(heads, group, group),
            each(group, columns),
            each(group, width),
        ],
        flops=2 * micro * group * columns * (width + 2 * group),
        moved=16 * micro * group * width,
    )


def attend_back_kernel(
    d_branch_ref, out_weight_ref, used_ref, weights_ref, packed_ref, squares_ref, gain_ref, cos_ref,
    sin_ref, d_hat_ref, d_value_ref, dots_ref, gain_grad_ref, *, width,
):
    columns = packed_ref.shape[1] // 3
    heads = columns // HD
    cosine, sine = cos_ref[...], sin_ref[...]
    scales = lax.rsqrt(squares_ref[:, :2] / width + EPSILON)
    d_attended = contract(d_branch_ref[...], out_weight_ref[...], 1, 1).astype(BF)
    dots = [0.0, 0.0]
    gain_grad_ref[...] = jnp.zeros_like(gain_grad_ref)
    for h in range(heads):
        own = slice(h * HD, (h + 1) * HD)
        query, key, value = (
            used_ref[:, part * columns + h * HD : part * columns + (h + 1) * HD] for part in range(3)
        )
        d_out = d_attended[:, own]
        weights = weights_ref[h]
        d_weights = contract(d_out, value, 1, 1)
        row_delta = jnp.sum(weights * d_weights, axis=-1, keepdims=True)
        d_scores = (weights * (d_weights - row_delta) * HD ** (-0.5)).astype(BF)
        d_value_ref[:, own] = contract(weights.astype(BF), d_out, 0, 0).astype(BF)
        grads = (
            jnp.dot(d_scores, key, preferred_element_type=F32),
            contract(d_scores, query, 0, 0),
        )
        for part in range(2):
            at = slice(part * columns + h * HD, part * columns + (h + 1) * HD)
            hat = packed_ref[:, at] * scales[:, part : part + 1]
            grad = grads[part] * cosine - pltpu.roll(grads[part], HD // 2, 1) * sine
            gain_grad_ref[part : part + 1, own] = jnp.sum(grad * hat, axis=0, keepdims=True)
            grad = grad * gain_ref[part : part + 1, own]
            d_hat_ref[:, at] = grad
            dots[part] = dots[part] + jnp.sum(grad * hat, axis=1, keepdims=True)
    lane = lax.broadcasted_iota(jnp.int32, dots_ref.shape, 1)
    dots_ref[...] = jnp.where(lane == 0, dots[0], jnp.where(lane == 1, dots[1], 0.0))


def attend_back(m, d_branch, out_weight, used, weights, packed, squares, gain, cosine, sine):
    group = packed.shape[1]
    columns, width = out_weight.shape
    heads = columns // HD

    def pick(*shape):
        return pl.BlockSpec((None,) + shape, lambda i: (m,) + (0,) * len(shape))

    def full(*shape):
        return pl.BlockSpec(shape, lambda i: (0,) * len(shape))

    return call_kernel(
        functools.partial(attend_back_kernel, width=width),
        (d_branch, out_weight, used, weights, packed, squares, gain, cosine, sine),
        [
            jax.ShapeDtypeStruct((group, 2 * columns), F32),
            jax.ShapeDtypeStruct((group, columns), BF),
            jax.ShapeDtypeStruct((group, LANES), F32),
            jax.ShapeDtypeStruct((8, columns), F32),
        ],
        grid=(1,),
        in_specs=[
            pick(group, width),
            full(columns, width),
            pick(group, 3 * columns),
            pick(heads, group, group),
            pick(group, 3 * columns),
            pick(group, LANES),
            full(2, columns),
            pick(group, HD),
            pick(group, HD),
        ],
        out_specs=[
            full(group, 2 * columns),
            full(group, columns),
            full(group, LANES),
            full(8, columns),
        ],
        flops=2 * group * columns * (width + 5 * group),
        moved=20 * group * width,
    )


def unproject_kernel(
    d_hat_ref, d_value_ref, dots_ref, packed_ref, squares_ref, weight_ref, normed_ref, d_packed_ref,
    d_normed_ref, gain_grad_ref, *, width,
):
    columns = d_value_ref.shape[1]
    scales = lax.rsqrt(squares_ref[:, :2] / width + EPSILON)
    for part in range(2):
        at = slice(part * columns, (part + 1) * columns)
        scale = scales[:, part : part + 1]
        hat = packed_ref[:, at] * scale
        mean = dots_ref[:, part : part + 1] / width
        d_packed_ref[:, at] = (scale * (d_hat_ref[:, at] - hat * mean)).astype(BF)
    d_packed_ref[:, 2 * columns :] = d_value_ref[...]
    total = 0.0
    for part in range(3):
        at = slice(part * columns, (part + 1) * columns)
        total = total + contract(d_packed_ref[:, at], weight_ref[part], 1, 1)
    d_normed_ref[...] = total.astype(BF)
    column = jnp.sum(total * normed_ref[...].astype(F32), axis=0, keepdims=True)
    gain_grad_ref[...] = jnp.broadcast_to(column, gain_grad_ref.shape)


def unproject(m, d_hat, d_value, dots, packed, squares, qkv_parts, normed):
    group, columns = d_value.shape
    width = qkv_parts.shape[1]

    def pick(*shape):
        return pl.BlockSpec((None,) + shape, lambda i: (m,) + (0,) * len(shape))

    def full(*shape):
        return pl.BlockSpec(shape, lambda i: (0,) * len(shape))

    return call_kernel(
        functools.partial(unproject_kernel, width=width),
        (d_hat, d_value, dots, packed, squares, qkv_parts, normed),
        [
            jax.ShapeDtypeStruct((group, 3 * columns), BF),
            jax.ShapeDtypeStruct((group, width), BF),
            jax.ShapeDtypeStruct((8, width), F32),
        ],
        grid=(1,),
        in_specs=[
            full(group, 2 * columns),
            full(group, columns),
            pick(group, LANES),
            pick(group, 3 * columns),
            pick(group, LANES),
            full(3, width, columns),
            pick(group, width),
        ],
        out_specs=[full(group, 3 * columns), full(group, width), full(8, width)],
        flops=2 * group * width * 3 * columns,
        moved=2 * width * 3 * columns + 8 * group * width,
    )


def rows_product_kernel(*refs, count):
    lefts, rights, starts, out_ref = refs[:count], refs[count : 2 * count], refs[2 * count : -1], refs[-1]
    total = starts[0][...] if starts else 0.0
    for left, right in zip(lefts, rights):
        total = total + contract(left[...], right[...], 0, 0)
    out_ref[...] = total


def rows_product(lefts, rights, start, tile, width, columns):
    count = len(lefts)
    rows = sum(left.shape[0] for left in lefts)
    once = pl.Buffered(1)
    starts = [] if start is None else [start]
    return call_kernel(
        functools.partial(rows_product_kernel, count=count),
        (*lefts, *rights, *starts),
        [jax.ShapeDtypeStruct((width, columns), F32)],
        grid=(width // tile,),
        in_specs=[pl.BlockSpec((left.shape[0], tile), lambda i: (0, i)) for left in lefts]
        + [
            pl.BlockSpec((right.shape[0], columns), lambda i: (0, 0), pipeline_mode=once)
            for right in rights
        ]
        + [pl.BlockSpec((tile, columns), lambda i: (i, 0)) for _ in starts],
        out_specs=[pl.BlockSpec((tile, columns), lambda i: (i, 0))],
        flops=2 * rows * width * columns,
        moved=2 * rows * (width + columns) + 4 * width * columns,
    )[0]


def qkv_product_kernel(left_ref, right_ref, out_ref):
    out_ref[...] = contract(left_ref[...], right_ref[...], 0, 0).astype(BF)


def qkv_product(normed, d_packed):
    rows, width = normed.shape
    columns = d_packed.shape[1] // 3
    tile = min(width, 1024)
    return call_kernel(
        qkv_product_kernel,
        (normed, d_packed),
        [jax.ShapeDtypeStruct((3, width, columns), BF)],
        grid=(3, width // tile),
        in_specs=[
            pl.BlockSpec((rows, tile), lambda p, i: (0, i)),
            pl.BlockSpec((rows, columns), lambda p, i: (0, p)),
        ],
        out_specs=[pl.BlockSpec((None, tile, columns), lambda p, i: (p, i, 0))],
        flops=2 * rows * width * 3 * columns,
        moved=2 * width * 3 * columns,
    )[0]


def experts_kernel(
    ids_ref, moe_ref, cot_ref, router_ref, gate_up_ref, down_ref, d_rows_ref, scaled_ref, d_inner_ref,
    *, experts, local,
):
    width = moe_ref.shape[1]
    quarter = down_ref.shape[0] // local
    rows = moe_ref[...]
    lane = lax.broadcasted_iota(jnp.int32, (rows.shape[0], LANES), 1)
    logits = jnp.dot(rows, router_ref[...], preferred_element_type=F32)
    logits = jnp.where(lane < experts, logits, -1e30)
    exponent = jnp.exp(logits - jnp.max(logits, axis=1, keepdims=True))
    probs = exponent / jnp.sum(exponent, axis=1, keepdims=True)
    mask = cot_ref[:, width:].astype(F32)
    gates = probs * mask
    back = jnp.zeros_like(probs)
    for e in range(local):
        here = lane == ids_ref[0] + e
        gate = jnp.sum(jnp.where(here, gates, 0.0), axis=1, keepdims=True)
        at = slice(e * quarter, (e + 1) * quarter)
        gate_at = slice(2 * e * quarter, (2 * e + 1) * quarter)
        up_at = slice((2 * e + 1) * quarter, (2 * e + 2) * quarter)
        d_raw = contract(cot_ref[:, :width], down_ref[at, :], 1, 1)
        gate_pre = jnp.dot(rows, gate_up_ref[:, gate_at], preferred_element_type=F32)
        up_pre = jnp.dot(rows, gate_up_ref[:, up_at], preferred_element_type=F32)
        sigmoid = 1.0 / (1.0 + jnp.exp(-gate_pre))
        silu = gate_pre * sigmoid
        active = silu * up_pre
        term = jnp.sum(active * d_raw, axis=1, keepdims=True)
        back = jnp.where(here, term, back)
        scaled_ref[:, at] = (active * gate).astype(BF)
        d_active = d_raw * gate
        d_inner_ref[:, gate_at] = (
            d_active * up_pre * sigmoid * (1.0 + gate_pre * (1.0 - sigmoid))
        ).astype(BF)
        d_inner_ref[:, up_at] = (d_active * silu).astype(BF)
    d_rows_ref[:, width:] = jnp.where(mask > 0.0, back, 0.0).astype(BF)
    d_rows_ref[:, :width] = contract(d_inner_ref[...], gate_up_ref[...], 1, 1).astype(BF)


def run_experts(first_id, moe_all, cot_all, router_wide, gate_up, down, experts, local):
    total, width = moe_all.shape
    tile = min(total, EXPERT_TILE)
    inner = gate_up.shape[1]
    once = pl.Buffered(1)
    return call_kernel(
        functools.partial(experts_kernel, experts=experts, local=local),
        (first_id, moe_all, cot_all, router_wide, gate_up, down),
        [
            jax.ShapeDtypeStruct((total, width + LANES), BF),
            jax.ShapeDtypeStruct((total, inner // 2), BF),
            jax.ShapeDtypeStruct((total, inner), BF),
        ],
        grid=(total // tile,),
        in_specs=[
            pl.BlockSpec(memory_space=pltpu.SMEM),
            pl.BlockSpec((tile, width), lambda i: (i, 0)),
            pl.BlockSpec((tile, width + LANES), lambda i: (i, 0)),
            pl.BlockSpec((width, LANES), lambda i: (0, 0), pipeline_mode=once),
            pl.BlockSpec((width, inner), lambda i: (0, 0), pipeline_mode=once),
            pl.BlockSpec((inner // 2, width), lambda i: (0, 0), pipeline_mode=once),
        ],
        out_specs=[
            pl.BlockSpec((tile, width + LANES), lambda i: (i, 0)),
            pl.BlockSpec((tile, inner // 2), lambda i: (i, 0)),
            pl.BlockSpec((tile, inner), lambda i: (i, 0)),
        ],
        flops=2 * total * width * inner * 5 // 2,
        moved=total * width * 6,
    )


def shards(
    tokens, cotangent, routes, lengths, attn_gain, qkv_weight, qk_gain, out_weight, moe_gain,
    router, w_gateup, w_down,
):
    tp_size = lax.axis_size("tp")
    dp_size = lax.axis_size("dp")
    tp_rank = lax.axis_index("tp")
    dp_rank = lax.axis_index("dp")
    micro_count, _, own_rows, width = tokens.shape
    group = own_rows * tp_size
    experts = router.shape[1]
    local = w_gateup.shape[0]
    columns = qkv_weight.shape[2]
    quarter = w_down.shape[1]

    qkv_parts = jnp.transpose(qkv_weight, (1, 0, 2))
    gate_up = jnp.concatenate([w_gateup[e].reshape(width, 2 * quarter) for e in range(local)], axis=1)
    down = w_down.reshape(local * quarter, width)
    router_wide = jnp.pad(router, ((0, 0), (0, -experts % LANES)))
    expert_ids = jnp.arange(experts, dtype=jnp.int32)
    first_id = (dp_rank * local).astype(jnp.int32).reshape(1)

    places = jnp.concatenate(
        [(tp_rank ^ k) * own_rows + jnp.arange(own_rows, dtype=jnp.int32) for k in range(tp_size)]
    )
    own_places = tp_rank * own_rows + jnp.arange(own_rows, dtype=jnp.int32)
    frequency = jnp.exp(
        jnp.arange(HD // 2, dtype=F32) * (-2.0 * jnp.log(10000.0) / HD)
    )

    first_len = lengths[:, 0, 0][:, None]
    live_end = first_len + lengths[:, 0, 1][:, None]
    live_own = (own_places[None, :] < live_end).astype(F32)[:, :, None]
    d_mixed = cotangent[:, 0].astype(F32) * live_own
    own_routes = lax.dynamic_slice_in_dim(routes[:, 0], tp_rank * own_rows, own_rows, 1)
    chosen = jnp.any(own_routes[..., None] == expert_ids, axis=2)
    mask = jnp.pad(chosen.astype(BF), ((0, 0), (0, 0), (0, -experts % LANES)))
    cot_sent = jnp.concatenate([d_mixed.astype(BF), mask], axis=2)

    grad_router = 0.0
    grad_moe_gain = 0.0

    outer = dp_size // 2
    span = min(outer, 4)
    parts = [range(first, first + span) for first in range(0, outer, span)]
    zone = parts[0]

    x_own = tokens[:, 0].astype(F32)
    x_scale = rms_scale(x_own)
    x_hat = x_own * x_scale

    def experts_of(moe_half, cot_half):
        return run_experts(first_id, moe_half, cot_half, router_wide, gate_up, down, experts, local)

    def gate_up_grads(start, moe, ran):
        inner = 2 * local * quarter
        return rows_product(moe, [r[2] for r in ran], start, 256, width, inner)

    def down_grads(start, cot, ran):
        return rows_product([r[1] for r in ran], cot, start, 256, local * quarter, width)

    def mix(ran):
        return jnp.dot(ran[1], down, preferred_element_type=F32).astype(BF)

    normed = gather_tp((x_hat * attn_gain).astype(BF))
    cot_z = [swap_dp(cot_sent, 2 * k) for k in zone[1:-1]]
    normed, cot_late = sync(normed, cot_sent)
    cot_z.append(swap_dp(cot_late, 2 * zone[-1]))

    segment = (places >= first_len).astype(jnp.int32) + (places >= live_end).astype(jnp.int32)
    starts = jnp.where(segment == 0, 0, jnp.where(segment == 1, first_len, live_end))
    angles = (places - starts).astype(F32)[:, :, None] * frequency
    cosine, sine = jnp.cos(angles), jnp.sin(angles)
    cosine = jnp.concatenate([cosine, cosine], axis=2)
    sine = jnp.concatenate([-sine, sine], axis=2)
    allowed = (segment[:, :, None] == segment[:, None, :]) & (places[None, :] <= places[:, None])

    packed, squares = project(normed, qkv_parts)
    squares = sum_tp(squares)
    used, weights, attended, branch = attend(
        packed, squares, qk_gain, cosine, sine, allowed.astype(F32), out_weight
    )
    branch, *cot_z = sync(branch, cot_sent, *cot_z)
    branch_own, cot_z = scatter_tp_first(branch, jnp.concatenate(cot_z, axis=1))
    cot_z0, cot_z1 = cot_z[0], cot_z[1]
    cot_near0 = gather_plane_near(cot_z0)
    hidden = x_own + branch_own
    h_scale = rms_scale(hidden)
    h_hat = hidden * h_scale
    moe_own = (h_hat * moe_gain).astype(BF)
    moe_z0 = gather_outer(moe_own[0], zone)

    moe_z0, moe_own1, cot_z0, cot_z1, *cot_near0 = sync(moe_z0, moe_own[1], cot_z0, cot_z1, *cot_near0)
    moe_near0 = gather_plane_near(moe_z0)
    moe_z1 = gather_outer(moe_own1, zone)

    moe_z0, moe_z1, cot_z0, cot_z1, *near = sync(moe_z0, moe_z1, cot_z0, cot_z1, *cot_near0, *moe_near0)
    cot_half0 = gather_plane_far(cot_z0, *near[:2])
    moe_half0 = gather_plane_far(moe_z0, *near[2:])

    moe_half0, cot_half0, moe_z1, cot_z1 = sync(moe_half0, cot_half0, moe_z1, cot_z1)
    moe_other0, cot_other0 = swap_dp(moe_half0, 1), swap_dp(cot_half0, 1)
    cot_near1 = gather_plane_near(cot_z1)
    own0 = experts_of(moe_half0, cot_half0)

    moe_other0, cot_other0, moe_z1, cot_z1, *rest = sync(
        moe_other0, cot_other0, moe_z1, cot_z1, *cot_near1, *own0
    )
    cot_near1, own0 = rest[:2], rest[2:]
    moe_near1 = gather_plane_near(moe_z1)
    other0 = experts_of(moe_other0, cot_other0)

    moe_z1, cot_z1, *rest = sync(moe_z1, cot_z1, *cot_near1, *moe_near1, *own0, *other0)
    own0, other0 = rest[4:7], rest[7:]
    core0 = scatter_core(own0[0], other0[0])
    cot_half1 = gather_plane_far(cot_z1, *rest[:2])
    moe_half1 = gather_plane_far(moe_z1, *rest[2:4])
    mix0 = [mix(own0), mix(other0)]
    ran0, moe0, cot0 = (own0, other0), (moe_half0, moe_other0), (cot_half0, cot_other0)
    d_gate_up = gate_up_grads(None, moe0, ran0)

    core0, cot_half1, moe_half1, d_gate_up, *mix0 = sync(core0, cot_half1, moe_half1, d_gate_up, *mix0)
    near0 = scatter_plane_near(core0)
    moe_other1, cot_other1 = swap_dp(moe_half1, 1), swap_dp(cot_half1, 1)
    mix_core0 = scatter_core(*mix0)
    own1 = experts_of(moe_half1, cot_half1)

    moe_other1, cot_other1, mix_core0, *rest = sync(moe_other1, cot_other1, mix_core0, *near0, *own1)
    near0, own1 = rest[:2], rest[2:]
    far0 = scatter_plane_far(*near0)
    other1 = experts_of(moe_other1, cot_other1)

    mix_core0, *rest = sync(mix_core0, *far0, *own1, *other1)
    far0, own1, other1 = rest[:2], rest[2:5], rest[5:]
    core1 = scatter_core(own1[0], other1[0])
    back0 = scatter_outer(*far0, zone)
    mix1 = [mix(own1), mix(other1)]
    ran1, moe1, cot1 = (own1, other1), (moe_half1, moe_other1), (cot_half1, cot_other1)
    d_down = down_grads(None, cot0, ran0)

    core1, back0, mix_core0, d_down, *mix1 = sync(core1, back0, mix_core0, d_down, *mix1)
    near1 = scatter_plane_near(core1)
    mix_core1 = scatter_core(*mix1)
    d_gate_up = gate_up_grads(d_gate_up, moe1, ran1)

    back0, mix_core0, mix_core1, d_gate_up, *near1 = sync(back0, mix_core0, mix_core1, d_gate_up, *near1)
    far1 = scatter_plane_far(*near1)
    d_down = down_grads(d_down, cot1, ran1)

    back0, mix_core0, mix_core1, d_gate_up, d_down, *far1 = sync(
        back0, mix_core0, mix_core1, d_gate_up, d_down, *far1
    )
    back1 = scatter_outer(*far1, zone)
    mix_near0 = scatter_plane_near(mix_core0)
    d_gate_up_out = d_gate_up.reshape(width, local, 2, quarter)
    d_gate_up_out = jnp.stack([d_gate_up_out[:, e] for e in range(local)])
    if len(parts) == 1:
        back1, back0, d_gate_up_out, mix_core1, *mix_near0 = sync(
            back1, back0, d_gate_up_out, mix_core1, *mix_near0
        )
    back = [back0, back1]
    more = [0.0, 0.0]
    if len(parts) > 1:
        for later in parts[1:]:
            for m in range(micro_count):
                sent, moe_sent, d_gate_up, d_down, back[m], more[m] = sync(
                    cot_sent[m], moe_own[m], d_gate_up, d_down, back[m], more[m]
                )
                halves = []
                for rows in (sent, moe_sent):
                    rows = gather_outer(rows, later)
                    rows = gather_plane_far(rows, *gather_plane_near(rows))
                    halves.append((rows, swap_dp(rows, 1)))
                cot, moe = halves
                ran = [experts_of(moe[j], cot[j]) for j in range(2)]
                d_gate_up = gate_up_grads(d_gate_up, moe, ran)
                d_down = down_grads(d_down, cot, ran)
                terms = []
                for pair in ([r[0] for r in ran], [mix(r) for r in ran]):
                    near = scatter_plane_near(scatter_core(*pair))
                    terms.append(scatter_outer(*scatter_plane_far(*near), later))
                back[m], more[m] = back[m] + terms[0], more[m] + terms[1]
        d_gate_up_out = d_gate_up.reshape(width, local, 2, quarter)
        d_gate_up_out = jnp.stack([d_gate_up_out[:, e] for e in range(local)])

    d_branches, d_hiddens = [], []
    for m in range(micro_count):
        expert_grad = back[m][:, :width]
        probs = jax.nn.softmax(jnp.dot(moe_own[m], router, preferred_element_type=F32), axis=-1)
        d_choice = back[m][:, width : width + experts]
        d_logits = (probs * (d_choice - jnp.sum(probs * d_choice, axis=1, keepdims=True))).astype(BF)
        grad_router = grad_router + contract(moe_own[m], d_logits, 0, 0)
        d_moe_in = expert_grad + contract(d_logits, router, 1, 1)
        grad_moe_gain = grad_moe_gain + jnp.sum(d_moe_in * h_hat[m], axis=0)
        d_h_hat = d_moe_in * moe_gain
        d_hiddens.append(
            d_mixed[m]
            + h_scale[m] * (d_h_hat - h_hat[m] * jnp.mean(d_h_hat * h_hat[m], axis=1, keepdims=True))
        )
    d_branch = gather_tp(jnp.stack(d_hiddens).astype(BF))
    d_branch, mix_core1, *mix_near0 = sync(d_branch, mix_core1, *mix_near0)
    backs = [
        attend_back(
            m, d_branch, out_weight, used, weights, packed, squares, qk_gain, cosine, sine
        )
        for m in range(micro_count)
    ]
    grad_qk = sum(gain_grad for _, _, _, gain_grad in backs)[:2]
    dots = sum_tp(jnp.stack([b[2] for b in backs]))
    grad_out = contract(attended.reshape(-1, columns), d_branch.reshape(-1, width), 0, 0).astype(BF)
    dots, grad_out, mix_core1, *mix_near0 = sync(dots, grad_out, mix_core1, *mix_near0)
    mix_far0 = scatter_plane_far(*mix_near0)
    mix_near1 = scatter_plane_near(mix_core1)
    ends = [
        unproject(m, *backs[m][:2], dots, packed, squares, qkv_parts, normed) for m in range(micro_count)
    ]
    d_packed = jnp.concatenate([end[0] for end in ends])
    grad_qkv = qkv_product(normed.reshape(-1, width), d_packed)
    shared = [grad_qkv[p] for p in range(3)]
    shared += [grad_out[:, i : i + columns] for i in range(0, width, columns)]
    shared, *rest = sync(jnp.concatenate(shared), *mix_far0, *mix_near1, ends[0][1], ends[1][1])
    mix_far0, mix_near1, d_normed = rest[:2], rest[2:4], rest[4:]

    shared = lax.psum_scatter(shared, "dp", scatter_dimension=0, tiled=True)
    mix_far1 = scatter_plane_far(*mix_near1)
    d_normed0 = scatter_tp(d_normed[0])
    d_normed0, d_normed1, *rest = sync(d_normed0, d_normed[1], *mix_far0, *mix_far1)
    mix_far0, mix_far1 = rest[:2], rest[2:]
    d_normed1 = scatter_tp(d_normed1)
    grad_attn_gain = sum(end[2] for end in ends)[0] / attn_gain
    wide_qk = jnp.pad(grad_qk, ((0, 0), (0, width - columns)))
    small = jnp.concatenate([grad_attn_gain[None], grad_moe_gain[None], grad_router.T], axis=0)
    d_normed0, d_normed1, small, *rest = sync(d_normed0, d_normed1, small, *mix_far0, *mix_far1)
    mix_far0, mix_far1 = rest[:2], rest[2:]
    total = small
    for k in range(1, tp_size):
        total = total + swap_tp(small, k)
    small = jnp.concatenate([total, wide_qk], axis=0)
    small = small + swap_dp(small, 1)
    input_grads = []
    for m, d_normed in enumerate((d_normed0, d_normed1)):
        d_x_hat = d_normed * attn_gain
        d_tokens = d_hiddens[m] + x_scale[m] * (
            d_x_hat - x_hat[m] * jnp.mean(d_x_hat * x_hat[m], axis=1, keepdims=True)
        )
        input_grads.append(d_tokens.astype(BF))
    shared, small, d_tokens, *rest = sync(shared, small, jnp.stack(input_grads), *mix_far0, *mix_far1)
    mix_far0, mix_far1 = rest[:2], rest[2:]
    shared = lax.all_gather(shared, "dp", axis=0, tiled=True)
    terms = [swap_dp(small, 2 * k) for k in range(1, outer)]
    small = sum(terms, small)
    mixed0 = scatter_outer(*mix_far0, zone)
    small, mixed0, *mix_far1 = sync(small, mixed0, *mix_far1)
    mixed = jnp.stack([mixed0 + more[0], scatter_outer(*mix_far1, zone) + more[1]])
    out = (hidden + mixed).astype(BF)
    shared, out = sync(shared, out)
    total_qkv = shared[: 3 * width].reshape(3, width, columns)
    total_out = shared[3 * width :].reshape(width // columns, columns, columns)
    total_out = jnp.concatenate([piece for piece in total_out], axis=1).astype(F32)
    return (
        out[:, None],
        d_tokens[:, None],
        small[0],
        jnp.transpose(total_qkv.astype(F32), (1, 0, 2)),
        small[-2:, :columns],
        total_out,
        small[1],
        small[2 : 2 + experts].T,
        d_gate_up_out.reshape(w_gateup.shape),
        d_down.reshape(w_down.shape),
    )


def solution(mesh):
    return jax.shard_map(
        shards,
        mesh=mesh,
        in_specs=(
            P(None, "dp", "tp", None),
            P(None, "dp", "tp", None),
            P(None, "dp", None, None),
            P(None, "dp", None),
            P(),
            P(None, None, "tp"),
            P(None, "tp"),
            P("tp", None),
            P(),
            P(),
            P("dp", None, None, "tp"),
            P("dp", "tp", None),
        ),
        out_specs=(
            P(None, "dp", "tp", None),
            P(None, "dp", "tp", None),
            P(),
            P(None, None, "tp"),
            P(None, "tp"),
            P("tp", None),
            P(),
            P(),
            P("dp", None, None, "tp"),
            P("dp", "tp", None),
        ),
        check_vma=False,
    )
```

time: 1200 us -> 880 us (0.73)
  matrix products: 234 us -> 26.7 us
  Pallas kernels: 0 us -> 198 us
  waiting for transfers between devices: 506 us -> 320 us
  other arithmetic: 128 us -> 85 us
  local copies, waits for them, and re-layouts: 140 us -> 99.8 us
  blocking collectives: 19.6 us -> 0 us
    psum x2 -> x0, waiting for transfers between devices: 246 us -> none  [the longest x1 177 us: sum_dp(): return lax.psum(value.astype(BF), 'dp').astype(F32)]
    pallas_call x0 -> x15, Pallas kernels: none -> 198 us  [call_kernel(): pl.pallas_call(body, out_shape=outs, grid=grid, in_specs=in_specs or [who...]
    dot_general x24 -> x5, matrix products: 145 us -> 6.39 us  [contract(): lax.dot_general(left, right, (((left_dim,), (right_dim,)), ((), ())), pre...]
    dot_general x24 -> x6, matrix products: 83.4 us -> 20.3 us  [the longest x4 19.9 us: mix(): return jnp.dot(ran[1], down, preferred_element_type=F32).astype(BF)]
    ppermute x32 -> x33, waiting for transfers between devices: 62.5 us -> 119 us  [swap_dp(): return lax.ppermute(value, 'dp', [(i, i ^ bits) for i in range(size)])]
    ppermute x68 -> x56, waiting for transfers between devices: 198 us -> 154 us  [swap_tp(): return lax.ppermute(value, 'tp', [(i, i ^ bits) for i in range(size)])]
    reduce_scatter x0 -> x1, waiting for transfers between devices: none -> 32.3 us  [shards(): shared = lax.psum_scatter(shared, 'dp', scatter_dimension=0, tiled=True)]
    ppermute x68 -> x56, starting transfers between devices: 84.2 us -> 61.1 us  [swap_tp(): return lax.ppermute(value, 'tp', [(i, i ^ bits) for i in range(size)])]
  transfers between devices with their start and end apart: 102 -> 91, of which waited for: 38 -> 44; matrix products, arithmetic and copies ran while one was open for 30% -> 16% of each run, Pallas kernels for 0% -> 21%
where the time goes in v2:
time: 880 us
  waiting for transfers between devices  320 us (36%)
  Pallas kernels  198 us (22%)
  starting transfers between devices  136 us (15%)
  local copies, waits for them, and re-layouts  99.8 us (11%)
  other arithmetic  85 us (10%)
  matrix products  26.7 us (3%)
  between operations  15.5 us (2%)
    pallas_call x15, Pallas kernels, call_kernel(): pl.pallas_call(body, out_shape=outs, grid=grid, in_specs=in_specs or [who...  198 us
    ppermute x56, waiting for transfers between devices, swap_tp(): return lax.ppermute(value, 'tp', [(i, i ^ bits) for i in range(size)])  154 us
    ppermute x33, waiting for transfers between devices, swap_dp(): return lax.ppermute(value, 'dp', [(i, i ^ bits) for i in range(size)])  119 us
    ppermute x33, starting transfers between devices, swap_dp(): return lax.ppermute(value, 'dp', [(i, i ^ bits) for i in range(size)])  74.8 us
    ppermute x56, starting transfers between devices, swap_tp(): return lax.ppermute(value, 'tp', [(i, i ^ bits) for i in range(size)])  61.1 us
    unnamed x132, local copies, waits for them, and re-layouts  38.9 us
    reduce_scatter x1, waiting for transfers between devices, shards(): shared = lax.psum_scatter(shared, 'dp', scatter_dimension=0, tiled=True)  32.3 us
    convert_element_type x4, other arithmetic, scatter_core(): return add_low(own, swap_dp(other, 1)).astype(BF)  21.9 us
  transfers between devices with their start and end apart: 91, of which 44 were waited for; matrix products, arithmetic and copies ran while one was open for 16% of the time, Pallas kernels for 21%

profile of v2, /device:TPU:0, one launch (start us, length us, event | category | flops | bytes accessed | tf_op | source)
XLA Modules:
  0.0 880.3 jit_solution(14903499123197777887)
XLA Ops:
  10.9 4.1 collective-permute-start.7
  24.5 11.0 %collective-permute-done.2 = bf16[2,64,2048]{2,1,0:T(8,128)(2,1)S(1)} collective-permute-done((bf16[2,64,2048]{2,1,0:T(8,128)(2,1)S(1)}, bf16[2,64,2048]{2,1,0:T(8,128)(2,1)S(1)}, u32[]{:S(2)}, u32[]{:S(2)}) %collective-permute-start.2) | collective-permute-done | bytes 524320 | tf_op jit(solution)/shard_map/ppermute | solution.py:32
  35.5 9.5 %collective-permute-done.1 = bf16[2,64,2048]{2,1,0:T(8,128)(2,1)} collective-permute-done((bf16[2,64,2048]{2,1,0:T(8,128)(2,1)S(1)}, bf16[2,64,2048]{2,1,0:T(8,128)(2,1)}, u32[]{:S(2)}, u32[]{:S(2)}) %collective-permute-start.1) | collective-permute-done | bytes 524320 | tf_op jit(solution)/shard_map/ppermute | solution.py:32
  47.9 8.1 shard_map.195
  62.1 4.2 collective-permute-done.5
  66.6 4.4 collective-permute-done.3
  72.7 7.7 shard_map.196
  88.1 9.4 %collective-permute-done.9 = bf16[2,64,2048]{2,1,0:T(8,128)(2,1)S(1)} collective-permute-done((bf16[2,64,2048]{2,1,0:T(8,128)(2,1)S(1)}, bf16[2,64,2048]{2,1,0:T(8,128)(2,1)S(1)}, u32[]{:S(2)}, u32[]{:S(2)}) %collective-permute-start.9) | collective-permute-done | bytes 524320 | tf_op jit(solution)/shard_map/ppermute | solution.py:32
  97.5 12.7 %collective-permute-done.10 = bf16[2,64,2048]{2,1,0:T(8,128)(2,1)S(1)} collective-permute-done((bf16[2,64,2048]{2,1,0:T(8,128)(2,1)S(1)}, bf16[2,64,2048]{2,1,0:T(8,128)(2,1)S(1)}, u32[]{:S(2)}, u32[]{:S(2)}) %collective-permute-start.10) | collective-permute-done | bytes 524320 | tf_op jit(solution)/shard_map/ppermute | solution.py:32
  113.3 11.7 %collective-permute-start.13 = (bf16[64,2048]{1,0:T(8,128)(2,1)S(1)}, bf16[64,2048]{1,0:T(8,128)(2,1)S(1)}, u32[]{:S(2)}, u32[]{:S(2)}) collective-permute-start(bf16[64,2048]{1,0:T(8,128)(2,1)S(1)} %get-tuple-element.521), channel_id=1, source_target_pairs={{0,4},{1,5},{2,6},{3,7},{4,0},{5,1},{6,2},{7,3},{8,12},{9,13},{10,... | collective-permute-start | bytes 786440 | tf_op jit(solution)/shard_map/ppermute | solution.py:37
  125.0 13.1 %collective-permute-done.13 = bf16[64,2048]{1,0:T(8,128)(2,1)S(1)} collective-permute-done((bf16[64,2048]{1,0:T(8,128)(2,1)S(1)}, bf16[64,2048]{1,0:T(8,128)(2,1)S(1)}, u32[]{:S(2)}, u32[]{:S(2)}) %collective-permute-start.13) | collective-permute-done | bytes 262176 | tf_op jit(solution)/shard_map/ppermute | solution.py:37
  141.8 3.7 collective-permute-start.18
  145.5 5.8 collective-permute-done.19
  151.3 12.9 %collective-permute-done.18 = bf16[64,2048]{1,0:T(8,128)(2,1)S(1)} collective-permute-done((bf16[64,2048]{1,0:T(8,128)(2,1)S(1)}, bf16[64,2048]{1,0:T(8,128)(2,1)S(1)}, u32[]{:S(2)}, u32[]{:S(2)}) %collective-permute-start.18) | collective-permute-done | bytes 262176 | tf_op jit(solution)/shard_map/ppermute | solution.py:37
  174.8 9.0 %collective-permute-done.22 = bf16[128,2048]{1,0:T(8,128)(2,1)S(1)} collective-permute-done((bf16[128,2048]{1,0:T(8,128)(2,1)S(1)}, bf16[128,2048]{1,0:T(8,128)(2,1)S(1)}, u32[]{:S(2)}, u32[]{:S(2)}) %collective-permute-start.22) | collective-permute-done | bytes 524320 | tf_op jit(solution)/shard_map/ppermute | solution.py:32
  188.0 6.2 collective-permute-done.24
  201.9 4.7 fusion.33
  211.3 20.2 %shard_map.197 = (bf16[1024,2176]{1,0:T(8,128)(2,1)}, bf16[1024,512]{1,0:T(8,128)(2,1)}, bf16[1024,1024]{1,0:T(8,128)(2,1)}) custom-call(s32[1]{0:T(128)} %bitcast.17.ids_ref, bf16[1024,2048]{1,0:T(8,128)(2,1)} %constant_dynamic-update-slice_fusion.moe_ref.refs_0_, bf16[1024,2176]{1,0:T(8,128)(2,1)} %constant_dynamic-update-slice_fusion.4.cot_ref.refs_2_, ...), custom_call_target="tpu_custom_call" | custom-call | flops 1342177280 | bytes 1572864 | tf_op jit(solution)/shard_map/pallas_call | solution.py:146
  233.8 20.4 %shard_map.198 = (bf16[1024,2176]{1,0:T(8,128)(2,1)}, bf16[1024,512]{1,0:T(8,128)(2,1)}, bf16[1024,1024]{1,0:T(8,128)(2,1)}) custom-call(s32[1]{0:T(128)} %bitcast.17.ids_ref, bf16[1024,2048]{1,0:T(8,128)(2,1)} %collective-permute-done.26.moe_ref.refs_1_, bf16[1024,2176]{1,0:T(8,128)(2,1)} %collective-permute-done.27.cot_ref.refs_3_, ...), custom_call_target="tpu_custom_call" | custom-call | flops 1342177280 | bytes 1572864 | tf_op jit(solution)/shard_map/pallas_call | solution.py:146
  257.6 5.5 convolution_convert_fusion.3
  274.7 15.0 %shard_map.199.refs_4_ = f32[2048,1024]{1,0:T(8,128)} custom-call(bf16[1024,2048]{1,0:T(8,128)(2,1)} %constant_dynamic-update-slice_fusion.moe_ref.refs_0_, bf16[1024,2048]{1,0:T(8,128)(2,1)} %collective-permute-done.26.moe_ref.refs_1_, bf16[1024,1024]{1,0:T(8,128)(2,1)} %get-tuple-element.271.refs_2_, bf16[1024,1024]{1,0:T(8,128)(2,1)} %get-tuple-element.272.refs_3_), custom_call_target="tpu_custom_call" | custom-call | flops 1073741824 | bytes 2621440 | tf_op jit(solution)/shard_map/pallas_call | solution.py:146
  289.6 5.7 convolution_convert_fusion.2
  305.2 6.3 add_convert_fusion.1
  316.9 20.1 %shard_map.200 = (bf16[1024,2176]{1,0:T(8,128)(2,1)}, bf16[1024,512]{1,0:T(8,128)(2,1)}, bf16[1024,1024]{1,0:T(8,128)(2,1)}) custom-call(s32[1]{0:T(128)} %bitcast.17.ids_ref, bf16[1024,2048]{1,0:T(8,128)(2,1)} %constant_dynamic-update-slice_fusion.14.moe_ref.refs_0_, bf16[1024,2176]{1,0:T(8,128)(2,1)} %copy-done.5, bf16[2048,128]{1,0:T(8,128)(2,1)} %pad.17.router_ref, ...), custom_call_target="tpu_custom_call" | custom-call | flops 1342177280 | bytes 1572864 | tf_op jit(solution)/shard_map/pallas_call | solution.py:146
  337.0 3.7 collective-permute-done.40
  344.7 6.0 add_convert_fusion.3
  352.9 20.2 %shard_map.201 = (bf16[1024,2176]{1,0:T(8,128)(2,1)}, bf16[1024,512]{1,0:T(8,128)(2,1)}, bf16[1024,1024]{1,0:T(8,128)(2,1)}) custom-call(s32[1]{0:T(128)} %bitcast.17.ids_ref, bf16[1024,2048]{1,0:T(8,128)(2,1)} %collective-permute-done.37.moe_ref.refs_1_, bf16[1024,2176]{1,0:T(8,128)(2,1)} %collective-permute-done.38.cot_ref.refs_3_, ...), custom_call_target="tpu_custom_call" | custom-call | flops 1342177280 | bytes 1572864 | tf_op jit(solution)/shard_map/pallas_call | solution.py:146
  373.5 10.3 %shard_map.202.refs_4_ = f32[512,2048]{1,0:T(8,128)} custom-call(bf16[1024,512]{1,0:T(8,128)(2,1)} %get-tuple-element.273.refs_0_, bf16[1024,512]{1,0:T(8,128)(2,1)} %get-tuple-element.274.refs_1_, bf16[1024,2176]{1,0:T(8,128)(2,1)} %constant_dynamic-update-slice_fusion.4.cot_ref.refs_2_, bf16[1024,2176]{1,0:T(8,128)(2,1)} %collective-permute-done.27.cot_ref.refs_3_), custom_call_target="tpu_custom_call" | custom-call | flops 536870912 | bytes 1835008 | tf_op jit(solution)/shard_map/pallas_call | solution.py:146
  388.4 4.3 convolution_convert_fusion.1
  392.7 4.4 convolution_convert_fusion
  398.2 8.1 collective-permute-done.46
  407.3 3.4 add_convert_fusion
  414.3 16.7 %shard_map.203 = f32[2048,1024]{1,0:T(8,128)} custom-call(bf16[1024,2048]{1,0:T(8,128)(2,1)} %constant_dynamic-update-slice_fusion.14.moe_ref.refs_0_, bf16[1024,2048]{1,0:T(8,128)(2,1)} %collective-permute-done.37.moe_ref.refs_1_, bf16[1024,1024]{1,0:T(8,128)(2,1)} %get-tuple-element.309.refs_2_, bf16[1024,1024]{1,0:T(8,128)(2,1)} %get-tuple-element.310.refs_3_, ...), custom_call_target="tpu_custom_call" | custom-call | flops 1073741824 | bytes 2621440 | tf_op jit(solution)/shard_map/pallas_call | solution.py:146
  430.9 8.2 collective-permute-done.49
  442.3 6.1 add_convert_fusion.2
  451.5 21.6 %shard_map.204 = f32[512,2048]{1,0:T(8,128)} custom-call(bf16[1024,512]{1,0:T(8,128)(2,1)} %get-tuple-element.303.refs_0_, bf16[1024,512]{1,0:T(8,128)(2,1)} %get-tuple-element.304.refs_1_, bf16[1024,2176]{1,0:T(8,128)(2,1)} %copy-done.5, bf16[1024,2176]{1,0:T(8,128)(2,1)} %collective-permute-done.38.cot_ref.refs_3_, f32[512,2048]{1,0:T(8,128)} %shard_map.202.refs_4_), custom_call_target="tpu_custom_call" | custom-call | flops 536870912 | bytes 1835008 | tf_op jit(solution)/shard_map/pallas_call | solution.py:146
  475.4 12.1 %collective-permute-done.52 = bf16[128,2176]{1,0:T(8,128)(2,1)S(1)} collective-permute-done((bf16[128,2176]{1,0:T(8,128)(2,1)}, bf16[128,2176]{1,0:T(8,128)(2,1)S(1)}, u32[]{:S(2)}, u32[]{:S(2)}) %collective-permute-start.52) | collective-permute-done | bytes 557088 | tf_op jit(solution)/shard_map/ppermute | solution.py:32
  489.2 6.0 collective-permute-start.53
  500.6 11.7 %reshape.433 = f32[2048,2,2,256]{3,2,1,0:T(2,128)} reshape(f32[2048,1024]{1,0:T(8,128)} %shard_map.203) | data formatting | bytes 16777216 | tf_op jit(solution)/shard_map/reshape | solution.py:690
  512.3 5.4 slice_bitcast_fusion.1
  517.7 4.8 pad_maximum_fusion
  535.2 12.3 %collective-permute-done.60 = bf16[2,64,2048]{2,1,0:T(8,128)(2,1)S(1)} collective-permute-done((bf16[2,64,2048]{2,1,0:T(8,128)(2,1)S(1)}, bf16[2,64,2048]{2,1,0:T(8,128)(2,1)S(1)}, u32[]{:S(2)}, u32[]{:S(2)}) %collective-permute-start.60) | collective-permute-done | bytes 524320 | tf_op jit(solution)/shard_map/ppermute | solution.py:32
  547.5 7.7 collective-permute-done.59
  556.6 7.0 shard_map.206
  563.6 7.2 shard_map.205
  577.8 4.9 collective-permute-done.63
  594.9 6.9 shard_map.208
  601.8 6.9 shard_map.207
  611.0 9.5 %shard_map.209 = bf16[3,2048,512]{2,1,0:T(8,128)(2,1)} custom-call(bf16[512,2048]{1,0:T(8,128)(2,1)} %bitcast.175, bf16[512,1536]{1,0:T(8,128)(2,1)} %pad_maximum_fusion.4.right_ref), custom_call_target="tpu_custom_call" | custom-call | flops 402653184 | bytes 786432 | tf_op jit(solution)/shard_map/pallas_call | solution.py:146
  651.2 5.8 collective-permute-done.70
  658.7 7.7 collective-permute-done.71
  672.1 4.4 collective-permute-done.73
  676.5 3.6 collective-permute-done.75
  680.1 4.1 collective-permute-done.74
  694.7 32.3 %reduce-scatter.2.cloned.1.call-done = bf16[1024,512]{1,0:T(8,128)(2,1)} async-done(((bf16[8192,512]{1,0:T(8,128)(2,1)}), bf16[1024,512]{1,0:T(8,128)(2,1)}) %reduce-scatter.2.cloned.1.call-update) | async-done | bytes 1048592 | tf_op jit(solution)/shard_map/reduce_scatter | solution.py:759
  727.9 3.6 collective-permute-start.80
  737.6 20.8 %collective-permute-done.81 = f32[20,2048]{1,0:T(8,128)S(1)} collective-permute-done((f32[20,2048]{1,0:T(8,128)S(1)}, f32[20,2048]{1,0:T(8,128)S(1)}, u32[]{:S(2)}, u32[]{:S(2)}) %collective-permute-start.81) | collective-permute-done | bytes 163872 | tf_op jit(solution)/shard_map/ppermute | solution.py:37
  758.5 4.1 collective-permute-done.83
  762.5 24.4 %collective-permute-done.84 = bf16[64,2048]{1,0:T(8,128)(2,1)S(1)} collective-permute-done((bf16[64,2048]{1,0:T(8,128)(2,1)S(1)}, bf16[64,2048]{1,0:T(8,128)(2,1)S(1)}, u32[]{:S(2)}, u32[]{:S(2)}) %collective-permute-start.84) | collective-permute-done | bytes 262176 | tf_op jit(solution)/shard_map/ppermute | solution.py:37
  787.7 27.3 %collective-permute-start.86 = (bf16[64,2048]{1,0:T(8,128)(2,1)S(1)}, bf16[64,2048]{1,0:T(8,128)(2,1)S(1)}, u32[]{:S(2)}, u32[]{:S(2)}) collective-permute-start(bf16[64,2048]{1,0:T(8,128)(2,1)S(1)} %slice.599), channel_id=1, source_target_pairs={{0,2},{1,3},{2,0},{3,1},{4,6},{5,7},{6,4},{7,5},{8,10},{9,11},{10,... | collective-permute-start | bytes 786440 | tf_op jit(solution)/shard_map/ppermute | solution.py:37
  819.8 9.6 %collective-permute-done.86 = bf16[64,2048]{1,0:T(8,128)(2,1)S(1)} collective-permute-done((bf16[64,2048]{1,0:T(8,128)(2,1)S(1)}, bf16[64,2048]{1,0:T(8,128)(2,1)S(1)}, u32[]{:S(2)}, u32[]{:S(2)}) %collective-permute-start.86) | collective-permute-done | bytes 262176 | tf_op jit(solution)/shard_map/ppermute | solution.py:37
  829.4 15.4 %collective-permute-done.87 = bf16[64,2048]{1,0:T(8,128)(2,1)S(1)} collective-permute-done((bf16[64,2048]{1,0:T(8,128)(2,1)S(1)}, bf16[64,2048]{1,0:T(8,128)(2,1)S(1)}, u32[]{:S(2)}, u32[]{:S(2)}) %collective-permute-start.87) | collective-permute-done | bytes 262176 | tf_op jit(solution)/shard_map/ppermute | solution.py:37
  845.8 13.8 %all-gather.2.cloned.1.call-done = bf16[8192,512]{1,0:T(8,128)(2,1)} async-done(((bf16[1024,512]{1,0:T(8,128)(2,1)}), bf16[8192,512]{1,0:T(8,128)(2,1)}) %all-gather.2.cloned.1.call-update) | async-done | bytes 8388624 | tf_op jit(solution)/shard_map/all_gather | solution.py:784
  864.1 6.6 convert_bitcast_fusion
  (420 shorter events, 234.5 us)
Async XLA Ops:
  7.2 719.8 %reduce-scatter.2.cloned.1.call-start = ((), (), s32[]{:S(2)}) async-start(), calls=%async_computation.1 | async-start | bytes 9437184 | tf_op jit(solution)/shard_map/reduce_scatter | solution.py:759
  10.9 69.6 %collective-permute-start.7 = (bf16[2,64,2176]{2,1,0:T(8,128)(2,1)S(1)}, bf16[2,64,2176]{2,1,0:T(8,128)(2,1)S(1)}, u32[]{:S(2)}, u32[]{:S(2)}) collective-permute-start(bf16[2,64,2176]{2,1,0:T(8,128)(2,1)S(1)} %pad_maximum_fusion.7), channel_id=1, source_target_pairs={{0,4},{1,5},{2,6},{3,7},{4,0},{5,1},{6,2},{7,3},{8,12},{9,13},{10,... | collective-permute-start | bytes 1671176 | tf_op jit(solution)/shard_map/ppermute | solution.py:37
  15.0 65.5 %collective-permute-start.6 = (bf16[2,64,2176]{2,1,0:T(8,128)(2,1)S(1)}, bf16[2,64,2176]{2,1,0:T(8,128)(2,1)S(1)}, u32[]{:S(2)}, u32[]{:S(2)}) collective-permute-start(bf16[2,64,2176]{2,1,0:T(8,128)(2,1)S(1)} %pad_maximum_fusion.7), channel_id=1, source_target_pairs={{0,2},{1,3},{2,0},{3,1},{4,6},{5,7},{6,4},{7,5},{8,10},{9,11},{10,... | collective-permute-start | bytes 1671176 | tf_op jit(solution)/shard_map/ppermute | solution.py:37
  22.1 22.9 %collective-permute-start.1 = (bf16[2,64,2048]{2,1,0:T(8,128)(2,1)S(1)}, bf16[2,64,2048]{2,1,0:T(8,128)(2,1)}, u32[]{:S(2)}, u32[]{:S(2)}) collective-permute-start(bf16[2,64,2048]{2,1,0:T(8,128)(2,1)S(1)} %get-tuple-element.513), channel_id=1, source_target_pairs={{0,16},{8,24},{16,0},{24,8},{1,17},{9,25},{17,1},{25,9},{2,18},{10... | collective-permute-start | bytes 1572872 | tf_op jit(solution)/shard_map/ppermute | solution.py:32
  22.6 22.5 %collective-permute-start = (bf16[2,64,2048]{2,1,0:T(8,128)(2,1)S(1)}, bf16[2,64,2048]{2,1,0:T(8,128)(2,1)}, u32[]{:S(2)}, u32[]{:S(2)}) collective-permute-start(bf16[2,64,2048]{2,1,0:T(8,128)(2,1)S(1)} %get-tuple-element.513), channel_id=1, source_target_pairs={{0,8},{8,0},{16,24},{24,16},{1,9},{9,1},{17,25},{25,17},{2,10},{10... | collective-permute-start | bytes 1572872 | tf_op jit(solution)/shard_map/ppermute | solution.py:32
  84.2 26.1 %collective-permute-start.10 = (bf16[2,64,2048]{2,1,0:T(8,128)(2,1)S(1)}, bf16[2,64,2048]{2,1,0:T(8,128)(2,1)S(1)}, u32[]{:S(2)}, u32[]{:S(2)}) collective-permute-start(bf16[2,64,2048]{2,1,0:T(8,128)(2,1)S(1)} %get-tuple-element.219), channel_id=1, source_target_pairs={{0,16},{8,24},{16,0},{24,8},{1,17},{9,25},{17,1},{25,9},{2,18},{10... | collective-permute-start | bytes 1572872 | tf_op jit(solution)/shard_map/ppermute | solution.py:32
  84.4 25.9 %collective-permute-start.11 = (bf16[2,64,2048]{2,1,0:T(8,128)(2,1)S(1)}, bf16[2,64,2048]{2,1,0:T(8,128)(2,1)S(1)}, u32[]{:S(2)}, u32[]{:S(2)}) collective-permute-start(bf16[2,64,2048]{2,1,0:T(8,128)(2,1)S(1)} %get-tuple-element.220), channel_id=1, source_target_pairs={{0,24},{8,16},{16,8},{24,0},{1,25},{9,17},{17,9},{25,1},{2,26},{10... | collective-permute-start | bytes 1572872 | tf_op jit(solution)/shard_map/ppermute | solution.py:32
  86.3 51.8 %collective-permute-start.16 = (bf16[256,2176]{1,0:T(8,128)(2,1)S(1)}, bf16[256,2176]{1,0:T(8,128)(2,1)S(1)}, u32[]{:S(2)}, u32[]{:S(2)}) collective-permute-start(bf16[256,2176]{1,0:T(8,128)(2,1)S(1)} %get-tuple-element.233), channel_id=1, source_target_pairs={{0,16},{8,24},{16,0},{24,8},{1,17},{9,25},{17,1},{25,9},{2,18},{10... | collective-permute-start | bytes 3342344 | tf_op jit(solution)/shard_map/ppermute | solution.py:32
  88.0 50.1 %collective-permute-start.15 = (bf16[256,2176]{1,0:T(8,128)(2,1)S(1)}, bf16[256,2176]{1,0:T(8,128)(2,1)S(1)}, u32[]{:S(2)}, u32[]{:S(2)}) collective-permute-start(bf16[256,2176]{1,0:T(8,128)(2,1)S(1)} %get-tuple-element.233), channel_id=1, source_target_pairs={{0,8},{8,0},{16,24},{24,16},{1,9},{9,1},{17,25},{25,17},{2,10},{10... | collective-permute-start | bytes 3342344 | tf_op jit(solution)/shard_map/ppermute | solution.py:32
  113.3 24.7 %collective-permute-start.13 = (bf16[64,2048]{1,0:T(8,128)(2,1)S(1)}, bf16[64,2048]{1,0:T(8,128)(2,1)S(1)}, u32[]{:S(2)}, u32[]{:S(2)}) collective-permute-start(bf16[64,2048]{1,0:T(8,128)(2,1)S(1)} %get-tuple-element.521), channel_id=1, source_target_pairs={{0,4},{1,5},{2,6},{3,7},{4,0},{5,1},{6,2},{7,3},{8,12},{9,13},{10,... | collective-permute-start | bytes 786440 | tf_op jit(solution)/shard_map/ppermute | solution.py:37
  138.2 27.1 %collective-permute-start.21 = (bf16[256,2048]{1,0:T(8,128)(2,1)S(1)}, bf16[256,2048]{1,0:T(8,128)(2,1)S(1)}, u32[]{:S(2)}, u32[]{:S(2)}) collective-permute-start(bf16[256,2048]{1,0:T(8,128)(2,1)S(1)} %pad_maximum_fusion.5), channel_id=1, source_target_pairs={{0,16},{8,24},{16,0},{24,8},{1,17},{9,25},{17,1},{25,9},{2,18},{10... | collective-permute-start | bytes 3145736 | tf_op jit(solution)/shard_map/ppermute | solution.py:32
  138.5 26.8 %collective-permute-start.20 = (bf16[256,2048]{1,0:T(8,128)(2,1)S(1)}, bf16[256,2048]{1,0:T(8,128)(2,1)S(1)}, u32[]{:S(2)}, u32[]{:S(2)}) collective-permute-start(bf16[256,2048]{1,0:T(8,128)(2,1)S(1)} %pad_maximum_fusion.5), channel_id=1, source_target_pairs={{0,8},{8,0},{16,24},{24,16},{1,9},{9,1},{17,25},{25,17},{2,10},{10... | collective-permute-start | bytes 3145736 | tf_op jit(solution)/shard_map/ppermute | solution.py:32
  141.8 22.5 %collective-permute-start.18 = (bf16[64,2048]{1,0:T(8,128)(2,1)S(1)}, bf16[64,2048]{1,0:T(8,128)(2,1)S(1)}, u32[]{:S(2)}, u32[]{:S(2)}) collective-permute-start(bf16[64,2048]{1,0:T(8,128)(2,1)S(1)} %get-tuple-element.223), channel_id=1, source_target_pairs={{0,4},{1,5},{2,6},{3,7},{4,0},{5,1},{6,2},{7,3},{8,12},{9,13},{10,... | collective-permute-start | bytes 786440 | tf_op jit(solution)/shard_map/ppermute | solution.py:37
  145.5 18.8 %collective-permute-start.17 = (bf16[64,2048]{1,0:T(8,128)(2,1)S(1)}, bf16[64,2048]{1,0:T(8,128)(2,1)S(1)}, u32[]{:S(2)}, u32[]{:S(2)}) collective-permute-start(bf16[64,2048]{1,0:T(8,128)(2,1)S(1)} %get-tuple-element.223), channel_id=1, source_target_pairs={{0,2},{1,3},{2,0},{3,1},{4,6},{5,7},{6,4},{7,5},{8,10},{9,11},{10,... | collective-permute-start | bytes 786440 | tf_op jit(solution)/shard_map/ppermute | solution.py:37
  169.3 17.8 %collective-permute-start.23 = (bf16[128,2048]{1,0:T(8,128)(2,1)S(1)}, bf16[128,2048]{1,0:T(8,128)(2,1)S(1)}, u32[]{:S(2)}, u32[]{:S(2)}) collective-permute-start(bf16[128,2048]{1,0:T(8,128)(2,1)S(1)} %get-tuple-element.232), channel_id=1, source_target_pairs={{0,8},{8,0},{16,24},{24,16},{1,9},{9,1},{17,25},{25,17},{2,10},{10... | collective-permute-start | bytes 1572872 | tf_op jit(solution)/shard_map/ppermute | solution.py:32
  172.7 21.5 %collective-permute-start.24 = (bf16[128,2176]{1,0:T(8,128)(2,1)S(1)}, bf16[128,2176]{1,0:T(8,128)(2,1)S(1)}, u32[]{:S(2)}, u32[]{:S(2)}) collective-permute-start(bf16[128,2176]{1,0:T(8,128)(2,1)S(1)} %get-tuple-element.236), channel_id=1, source_target_pairs={{0,16},{8,24},{16,0},{24,8},{1,17},{9,25},{17,1},{25,9},{2,18},{10... | collective-permute-start | bytes 1671176 | tf_op jit(solution)/shard_map/ppermute | solution.py:32
  173.1 24.6 %collective-permute-start.25 = (bf16[128,2176]{1,0:T(8,128)(2,1)S(1)}, bf16[128,2176]{1,0:T(8,128)(2,1)S(1)}, u32[]{:S(2)}, u32[]{:S(2)}) collective-permute-start(bf16[128,2176]{1,0:T(8,128)(2,1)S(1)} %get-tuple-element.237), channel_id=1, source_target_pairs={{0,8},{8,0},{16,24},{24,16},{1,9},{9,1},{17,25},{25,17},{2,10},{10... | collective-permute-start | bytes 1671176 | tf_op jit(solution)/shard_map/ppermute | solution.py:32
  198.5 33.0 %collective-permute-start.27 = (bf16[1024,2176]{1,0:T(8,128)(2,1)}, bf16[1024,2176]{1,0:T(8,128)(2,1)}, u32[]{:S(2)}, u32[]{:S(2)}) collective-permute-start(bf16[1024,2176]{1,0:T(8,128)(2,1)} %constant_dynamic-update-slice_fusion.4.cot_ref.refs_2_), channel_id=1, source_target_pairs={{0,1},{1,0},{2,3},{3,2},{4,5},{5,4},{6,7},{7,6},{8,9},{9,8},{10,11... | collective-permute-start | bytes 13369352 | tf_op jit(solution)/shard_map/ppermute | solution.py:37
  198.5 33.0 %collective-permute-start.26 = (bf16[1024,2048]{1,0:T(8,128)(2,1)}, bf16[1024,2048]{1,0:T(8,128)(2,1)}, u32[]{:S(2)}, u32[]{:S(2)}) collective-permute-start(bf16[1024,2048]{1,0:T(8,128)(2,1)} %constant_dynamic-update-slice_fusion.moe_ref.refs_0_), channel_id=1, source_target_pairs={{0,1},{1,0},{2,3},{3,2},{4,5},{5,4},{6,7},{7,6},{8,9},{9,8},{10,11... | collective-permute-start | bytes 12582920 | tf_op jit(solution)/shard_map/ppermute | solution.py:37
  200.0 31.5 %collective-permute-start.29 = (bf16[256,2176]{1,0:T(8,128)(2,1)S(1)}, bf16[256,2176]{1,0:T(8,128)(2,1)S(1)}, u32[]{:S(2)}, u32[]{:S(2)}) collective-permute-start(bf16[256,2176]{1,0:T(8,128)(2,1)S(1)} %get-tuple-element.261), channel_id=1, source_target_pairs={{0,16},{8,24},{16,0},{24,8},{1,17},{9,25},{17,1},{25,9},{2,18},{10... | collective-permute-start | bytes 3342344 | tf_op jit(solution)/shard_map/ppermute | solution.py:32
  200.3 31.2 %collective-permute-start.28 = (bf16[256,2176]{1,0:T(8,128)(2,1)S(1)}, bf16[256,2176]{1,0:T(8,128)(2,1)}, u32[]{:S(2)}, u32[]{:S(2)}) collective-permute-start(bf16[256,2176]{1,0:T(8,128)(2,1)S(1)} %get-tuple-element.261), channel_id=1, source_target_pairs={{0,8},{8,0},{16,24},{24,16},{1,9},{9,1},{17,25},{25,17},{2,10},{10... | collective-permute-start | bytes 3342344 | tf_op jit(solution)/shard_map/ppermute | solution.py:32
  231.6 24.6 %collective-permute-start.31 = (bf16[256,2048]{1,0:T(8,128)(2,1)S(1)}, bf16[256,2048]{1,0:T(8,128)(2,1)S(1)}, u32[]{:S(2)}, u32[]{:S(2)}) collective-permute-start(bf16[256,2048]{1,0:T(8,128)(2,1)S(1)} %copy-done.18), channel_id=1, source_target_pairs={{0,16},{8,24},{16,0},{24,8},{1,17},{9,25},{17,1},{25,9},{2,18},{10... | collective-permute-start | bytes 3145736 | tf_op jit(solution)/shard_map/ppermute | solution.py:32
  231.9 24.4 %collective-permute-start.30 = (bf16[256,2048]{1,0:T(8,128)(2,1)S(1)}, bf16[256,2048]{1,0:T(8,128)(2,1)S(1)}, u32[]{:S(2)}, u32[]{:S(2)}) collective-permute-start(bf16[256,2048]{1,0:T(8,128)(2,1)S(1)} %copy-done.18), channel_id=1, source_target_pairs={{0,8},{8,0},{16,24},{24,16},{1,9},{9,1},{17,25},{25,17},{2,10},{10... | collective-permute-start | bytes 3145736 | tf_op jit(solution)/shard_map/ppermute | solution.py:32
  263.2 41.9 %collective-permute-start.32 = (bf16[1024,2176]{1,0:T(8,128)(2,1)}, bf16[1024,2176]{1,0:T(8,128)(2,1)}, u32[]{:S(2)}, u32[]{:S(2)}) collective-permute-start(bf16[1024,2176]{1,0:T(8,128)(2,1)} %get-tuple-element.260), channel_id=1, source_target_pairs={{0,1},{1,0},{2,3},{3,2},{4,5},{5,4},{6,7},{7,6},{8,9},{9,8},{10,11... | collective-permute-start | bytes 13369352 | tf_op jit(solution)/shard_map/ppermute | solution.py:37
  267.8 27.5 %collective-permute-start.35 = (bf16[128,2048]{1,0:T(8,128)(2,1)}, bf16[128,2048]{1,0:T(8,128)(2,1)}, u32[]{:S(2)}, u32[]{:S(2)}) collective-permute-start(bf16[128,2048]{1,0:T(8,128)(2,1)} %get-tuple-element.269), channel_id=1, source_target_pairs={{0,16},{8,24},{16,0},{24,8},{1,17},{9,25},{17,1},{25,9},{2,18},{10... | collective-permute-start | bytes 1572872 | tf_op jit(solution)/shard_map/ppermute | solution.py:32
  269.2 30.6 %collective-permute-start.36 = (bf16[128,2048]{1,0:T(8,128)(2,1)}, bf16[128,2048]{1,0:T(8,128)(2,1)}, u32[]{:S(2)}, u32[]{:S(2)}) collective-permute-start(bf16[128,2048]{1,0:T(8,128)(2,1)} %get-tuple-element.270), channel_id=1, source_target_pairs={{0,8},{8,0},{16,24},{24,16},{1,9},{9,1},{17,25},{25,17},{2,10},{10... | collective-permute-start | bytes 1572872 | tf_op jit(solution)/shard_map/ppermute | solution.py:32
  272.8 28.9 %collective-permute-start.33 = (bf16[128,2176]{1,0:T(8,128)(2,1)}, bf16[128,2176]{1,0:T(8,128)(2,1)}, u32[]{:S(2)}, u32[]{:S(2)}) collective-permute-start(bf16[128,2176]{1,0:T(8,128)(2,1)} %get-tuple-element.264), channel_id=1, source_target_pairs={{0,16},{8,24},{16,0},{24,8},{1,17},{9,25},{17,1},{25,9},{2,18},{10... | collective-permute-start | bytes 1671176 | tf_op jit(solution)/shard_map/ppermute | solution.py:32
  274.2 29.8 %collective-permute-start.34 = (bf16[128,2176]{1,0:T(8,128)(2,1)}, bf16[128,2176]{1,0:T(8,128)(2,1)}, u32[]{:S(2)}, u32[]{:S(2)}) collective-permute-start(bf16[128,2176]{1,0:T(8,128)(2,1)} %get-tuple-element.265), channel_id=1, source_target_pairs={{0,8},{8,0},{16,24},{24,16},{1,9},{9,1},{17,25},{25,17},{2,10},{10... | collective-permute-start | bytes 1671176 | tf_op jit(solution)/shard_map/ppermute | solution.py:32
  311.5 33.2 %collective-permute-start.39 = (bf16[1024,2048]{1,0:T(8,128)(2,1)}, bf16[1024,2048]{1,0:T(8,128)(2,1)}, u32[]{:S(2)}, u32[]{:S(2)}) collective-permute-start(bf16[1024,2048]{1,0:T(8,128)(2,1)} %convolution_convert_fusion.2), channel_id=1, source_target_pairs={{0,1},{1,0},{2,3},{3,2},{4,5},{5,4},{6,7},{7,6},{8,9},{9,8},{10,11... | collective-permute-start | bytes 12582920 | tf_op jit(solution)/shard_map/ppermute | solution.py:37
  311.6 39.2 %collective-permute-start.38 = (bf16[1024,2176]{1,0:T(8,128)(2,1)S(1)}, bf16[1024,2176]{1,0:T(8,128)(2,1)}, u32[]{:S(2)}, u32[]{:S(2)}) collective-permute-start(bf16[1024,2176]{1,0:T(8,128)(2,1)S(1)} %constant_dynamic-update-slice_fusion.10.cot_ref.refs_2_), channel_id=1, source_target_pairs={{0,1},{1,0},{2,3},{3,2},{4,5},{5,4},{6,7},{7,6},{8,9},{9,8},{10,11... | collective-permute-start | bytes 13369352 | tf_op jit(solution)/shard_map/ppermute | solution.py:37
  312.1 38.7 %collective-permute-start.37 = (bf16[1024,2048]{1,0:T(8,128)(2,1)}, bf16[1024,2048]{1,0:T(8,128)(2,1)}, u32[]{:S(2)}, u32[]{:S(2)}) collective-permute-start(bf16[1024,2048]{1,0:T(8,128)(2,1)} %constant_dynamic-update-slice_fusion.14.moe_ref.refs_0_), channel_id=1, source_target_pairs={{0,1},{1,0},{2,3},{3,2},{4,5},{5,4},{6,7},{7,6},{8,9},{9,8},{10,11... | collective-permute-start | bytes 12582920 | tf_op jit(solution)/shard_map/ppermute | solution.py:37
  314.8 26.0 %collective-permute-start.40 = (bf16[256,2176]{1,0:T(8,128)(2,1)}, bf16[256,2176]{1,0:T(8,128)(2,1)S(1)}, u32[]{:S(2)}, u32[]{:S(2)}) collective-permute-start(bf16[256,2176]{1,0:T(8,128)(2,1)} %get-tuple-element.280), channel_id=1, source_target_pairs={{0,8},{8,0},{16,24},{24,16},{1,9},{9,1},{17,25},{25,17},{2,10},{10... | collective-permute-start | bytes 3342344 | tf_op jit(solution)/shard_map/ppermute | solution.py:32
  316.3 25.6 %collective-permute-start.41 = (bf16[256,2176]{1,0:T(8,128)(2,1)S(1)}, bf16[256,2176]{1,0:T(8,128)(2,1)}, u32[]{:S(2)}, u32[]{:S(2)}) collective-permute-start(bf16[256,2176]{1,0:T(8,128)(2,1)S(1)} %get-tuple-element.281), channel_id=1, source_target_pairs={{0,16},{8,24},{16,0},{24,8},{1,17},{9,25},{17,1},{25,9},{2,18},{10... | collective-permute-start | bytes 3342344 | tf_op jit(solution)/shard_map/ppermute | solution.py:32
  350.8 22.2 %collective-permute-start.42 = (bf16[128,2176]{1,0:T(8,128)(2,1)S(1)}, bf16[128,2176]{1,0:T(8,128)(2,1)S(1)}, u32[]{:S(2)}, u32[]{:S(2)}) collective-permute-start(bf16[128,2176]{1,0:T(8,128)(2,1)S(1)} %slice.518), channel_id=1, source_target_pairs={{0,16},{8,24},{16,0},{24,8},{1,17},{9,25},{17,1},{25,9},{2,18},{10... | collective-permute-start | bytes 1671176 | tf_op jit(solution)/shard_map/ppermute | solution.py:32
  352.2 21.0 %collective-permute-start.43 = (bf16[128,2176]{1,0:T(8,128)(2,1)S(1)}, bf16[128,2176]{1,0:T(8,128)(2,1)S(1)}, u32[]{:S(2)}, u32[]{:S(2)}) collective-permute-start(bf16[128,2176]{1,0:T(8,128)(2,1)S(1)} %slice.519), channel_id=1, source_target_pairs={{0,8},{8,0},{16,24},{24,16},{1,9},{9,1},{17,25},{25,17},{2,10},{10... | collective-permute-start | bytes 1671176 | tf_op jit(solution)/shard_map/ppermute | solution.py:32
  373.4 33.9 %collective-permute-start.44 = (bf16[1024,2176]{1,0:T(8,128)(2,1)}, bf16[1024,2176]{1,0:T(8,128)(2,1)}, u32[]{:S(2)}, u32[]{:S(2)}) collective-permute-start(bf16[1024,2176]{1,0:T(8,128)(2,1)} %get-tuple-element.299), channel_id=1, source_target_pairs={{0,1},{1,0},{2,3},{3,2},{4,5},{5,4},{6,7},{7,6},{8,9},{9,8},{10,11... | collective-permute-start | bytes 13369352 | tf_op jit(solution)/shard_map/ppermute | solution.py:37
  383.9 22.4 %collective-permute-start.46 = (bf16[64,2176]{1,0:T(8,128)(2,1)S(1)}, bf16[64,2176]{1,0:T(8,128)(2,1)S(1)}, u32[]{:S(2)}, u32[]{:S(2)}) collective-permute-start(bf16[64,2176]{1,0:T(8,128)(2,1)S(1)} %get-tuple-element.510), channel_id=1, source_target_pairs={{0,4},{1,5},{2,6},{3,7},{4,0},{5,1},{6,2},{7,3},{8,12},{9,13},{10,... | collective-permute-start | bytes 835592 | tf_op jit(solution)/shard_map/ppermute | solution.py:37
  386.8 19.5 %collective-permute-start.47 = (bf16[64,2176]{1,0:T(8,128)(2,1)S(1)}, bf16[64,2176]{1,0:T(8,128)(2,1)S(1)}, u32[]{:S(2)}, u32[]{:S(2)}) collective-permute-start(bf16[64,2176]{1,0:T(8,128)(2,1)S(1)} %get-tuple-element.511), channel_id=1, source_target_pairs={{0,6},{1,7},{2,4},{3,5},{4,2},{5,3},{6,0},{7,1},{8,14},{9,15},{10,... | collective-permute-start | bytes 835592 | tf_op jit(solution)/shard_map/ppermute | solution.py:37
  410.7 31.5 %collective-permute-start.48 = (bf16[1024,2048]{1,0:T(8,128)(2,1)}, bf16[1024,2048]{1,0:T(8,128)(2,1)}, u32[]{:S(2)}, u32[]{:S(2)}) collective-permute-start(bf16[1024,2048]{1,0:T(8,128)(2,1)} %convolution_convert_fusion), channel_id=1, source_target_pairs={{0,1},{1,0},{2,3},{3,2},{4,5},{5,4},{6,7},{7,6},{8,9},{9,8},{10,11... | collective-permute-start | bytes 12582920 | tf_op jit(solution)/shard_map/ppermute | solution.py:37
  412.0 27.2 %collective-permute-start.49 = (bf16[256,2176]{1,0:T(8,128)(2,1)}, bf16[256,2176]{1,0:T(8,128)(2,1)S(1)}, u32[]{:S(2)}, u32[]{:S(2)}) collective-permute-start(bf16[256,2176]{1,0:T(8,128)(2,1)} %get-tuple-element.313), channel_id=1, source_target_pairs={{0,8},{8,0},{16,24},{24,16},{1,9},{9,1},{17,25},{25,17},{2,10},{10... | collective-permute-start | bytes 3342344 | tf_op jit(solution)/shard_map/ppermute | solution.py:32
  413.3 26.9 %collective-permute-start.50 = (bf16[256,2176]{1,0:T(8,128)(2,1)S(1)}, bf16[256,2176]{1,0:T(8,128)(2,1)}, u32[]{:S(2)}, u32[]{:S(2)}) collective-permute-start(bf16[256,2176]{1,0:T(8,128)(2,1)S(1)} %get-tuple-element.314), channel_id=1, source_target_pairs={{0,16},{8,24},{16,0},{24,8},{1,17},{9,25},{17,1},{25,9},{2,18},{10... | collective-permute-start | bytes 3342344 | tf_op jit(solution)/shard_map/ppermute | solution.py:32
  449.3 24.6 %collective-permute-start.51 = (bf16[128,2176]{1,0:T(8,128)(2,1)S(1)}, bf16[128,2176]{1,0:T(8,128)(2,1)}, u32[]{:S(2)}, u32[]{:S(2)}) collective-permute-start(bf16[128,2176]{1,0:T(8,128)(2,1)S(1)} %slice.530), channel_id=1, source_target_pairs={{0,16},{8,24},{16,0},{24,8},{1,17},{9,25},{17,1},{25,9},{2,18},{10... | collective-permute-start | bytes 1671176 | tf_op jit(solution)/shard_map/ppermute | solution.py:32
  489.2 33.3 %collective-permute-start.53 = (bf16[64,2176]{1,0:T(8,128)(2,1)}, bf16[64,2176]{1,0:T(8,128)(2,1)}, u32[]{:S(2)}, u32[]{:S(2)}) collective-permute-start(bf16[64,2176]{1,0:T(8,128)(2,1)} %slice.534), channel_id=1, source_target_pairs={{0,2},{1,3},{2,0},{3,1},{4,6},{5,7},{6,4},{7,5},{8,10},{9,11},{10,... | collective-permute-start | bytes 835592 | tf_op jit(solution)/shard_map/ppermute | solution.py:37
  495.2 27.4 %collective-permute-start.54 = (bf16[64,2176]{1,0:T(8,128)(2,1)}, bf16[64,2176]{1,0:T(8,128)(2,1)}, u32[]{:S(2)}, u32[]{:S(2)}) collective-permute-start(bf16[64,2176]{1,0:T(8,128)(2,1)} %get-tuple-element.508), channel_id=1, source_target_pairs={{0,4},{1,5},{2,6},{3,7},{4,0},{5,1},{6,2},{7,3},{8,12},{9,13},{10,... | collective-permute-start | bytes 835592 | tf_op jit(solution)/shard_map/ppermute | solution.py:37
  495.2 27.3 %collective-permute-start.55 = (bf16[64,2176]{1,0:T(8,128)(2,1)}, bf16[64,2176]{1,0:T(8,128)(2,1)}, u32[]{:S(2)}, u32[]{:S(2)}) collective-permute-start(bf16[64,2176]{1,0:T(8,128)(2,1)} %get-tuple-element.509), channel_id=1, source_target_pairs={{0,6},{1,7},{2,4},{3,5},{4,2},{5,3},{6,0},{7,1},{8,14},{9,15},{10,... | collective-permute-start | bytes 835592 | tf_op jit(solution)/shard_map/ppermute | solution.py:37
  498.7 25.2 %collective-permute-start.56 = (bf16[256,2048]{1,0:T(8,128)(2,1)}, bf16[256,2048]{1,0:T(8,128)(2,1)S(1)}, u32[]{:S(2)}, u32[]{:S(2)}) collective-permute-start(bf16[256,2048]{1,0:T(8,128)(2,1)} %get-tuple-element.330), channel_id=1, source_target_pairs={{0,8},{8,0},{16,24},{24,16},{1,9},{9,1},{17,25},{25,17},{2,10},{10... | collective-permute-start | bytes 3145736 | tf_op jit(solution)/shard_map/ppermute | solution.py:32
  499.3 25.6 %collective-permute-start.57 = (bf16[256,2048]{1,0:T(8,128)(2,1)S(1)}, bf16[256,2048]{1,0:T(8,128)(2,1)}, u32[]{:S(2)}, u32[]{:S(2)}) collective-permute-start(bf16[256,2048]{1,0:T(8,128)(2,1)S(1)} %get-tuple-element.331), channel_id=1, source_target_pairs={{0,16},{8,24},{16,0},{24,8},{1,17},{9,25},{17,1},{25,9},{2,18},{10... | collective-permute-start | bytes 3145736 | tf_op jit(solution)/shard_map/ppermute | solution.py:32
  533.3 21.9 %collective-permute-start.59 = (bf16[2,64,2048]{2,1,0:T(8,128)(2,1)S(1)}, bf16[2,64,2048]{2,1,0:T(8,128)(2,1)S(1)}, u32[]{:S(2)}, u32[]{:S(2)}) collective-permute-start(bf16[2,64,2048]{2,1,0:T(8,128)(2,1)S(1)} %pad_maximum_fusion.8), channel_id=1, source_target_pairs={{0,16},{8,24},{16,0},{24,8},{1,17},{9,25},{17,1},{25,9},{2,18},{10... | collective-permute-start | bytes 1572872 | tf_op jit(solution)/shard_map/ppermute | solution.py:32
  533.9 21.3 %collective-permute-start.58 = (bf16[2,64,2048]{2,1,0:T(8,128)(2,1)S(1)}, bf16[2,64,2048]{2,1,0:T(8,128)(2,1)S(1)}, u32[]{:S(2)}, u32[]{:S(2)}) collective-permute-start(bf16[2,64,2048]{2,1,0:T(8,128)(2,1)S(1)} %pad_maximum_fusion.8), channel_id=1, source_target_pairs={{0,8},{8,0},{16,24},{24,16},{1,9},{9,1},{17,25},{25,17},{2,10},{10... | collective-permute-start | bytes 1572872 | tf_op jit(solution)/shard_map/ppermute | solution.py:32
  589.4 43.6 %collective-permute-start.64 = (bf16[128,2048]{1,0:T(8,128)(2,1)}, bf16[128,2048]{1,0:T(8,128)(2,1)}, u32[]{:S(2)}, u32[]{:S(2)}) collective-permute-start(bf16[128,2048]{1,0:T(8,128)(2,1)} %slice.569), channel_id=1, source_target_pairs={{0,16},{8,24},{16,0},{24,8},{1,17},{9,25},{17,1},{25,9},{2,18},{10... | collective-permute-start | bytes 1572872 | tf_op jit(solution)/shard_map/ppermute | solution.py:32
  590.1 44.9 %collective-permute-start.65 = (bf16[128,2048]{1,0:T(8,128)(2,1)}, bf16[128,2048]{1,0:T(8,128)(2,1)S(1)}, u32[]{:S(2)}, u32[]{:S(2)}) collective-permute-start(bf16[128,2048]{1,0:T(8,128)(2,1)} %slice.570), channel_id=1, source_target_pairs={{0,8},{8,0},{16,24},{24,16},{1,9},{9,1},{17,25},{25,17},{2,10},{10... | collective-permute-start | bytes 1572872 | tf_op jit(solution)/shard_map/ppermute | solution.py:32
  593.0 42.9 %collective-permute-start.66 = (bf16[256,2048]{1,0:T(8,128)(2,1)}, bf16[256,2048]{1,0:T(8,128)(2,1)}, u32[]{:S(2)}, u32[]{:S(2)}) collective-permute-start(bf16[256,2048]{1,0:T(8,128)(2,1)} %get-tuple-element.359), channel_id=1, source_target_pairs={{0,8},{8,0},{16,24},{24,16},{1,9},{9,1},{17,25},{25,17},{2,10},{10... | collective-permute-start | bytes 3145736 | tf_op jit(solution)/shard_map/ppermute | solution.py:32
  593.6 42.3 %collective-permute-start.67 = (bf16[256,2048]{1,0:T(8,128)(2,1)}, bf16[256,2048]{1,0:T(8,128)(2,1)}, u32[]{:S(2)}, u32[]{:S(2)}) collective-permute-start(bf16[256,2048]{1,0:T(8,128)(2,1)} %get-tuple-element.360), channel_id=1, source_target_pairs={{0,16},{8,24},{16,0},{24,8},{1,17},{9,25},{17,1},{25,9},{2,18},{10... | collective-permute-start | bytes 3145736 | tf_op jit(solution)/shard_map/ppermute | solution.py:32
  639.0 220.7 %all-gather.2.cloned.1.call-start = ((), (), s32[]{:S(2)}) async-start(), calls=%async_computation.2 | async-start | bytes 9437184 | tf_op jit(solution)/shard_map/all_gather | solution.py:784
  646.6 19.8 %collective-permute-start.71 = (bf16[128,2048]{1,0:T(8,128)(2,1)S(1)}, bf16[128,2048]{1,0:T(8,128)(2,1)S(1)}, u32[]{:S(2)}, u32[]{:S(2)}) collective-permute-start(bf16[128,2048]{1,0:T(8,128)(2,1)S(1)} %slice.581), channel_id=1, source_target_pairs={{0,16},{8,24},{16,0},{24,8},{1,17},{9,25},{17,1},{25,9},{2,18},{10... | collective-permute-start | bytes 1572872 | tf_op jit(solution)/shard_map/ppermute | solution.py:32
  648.2 19.2 %collective-permute-start.72 = (bf16[128,2048]{1,0:T(8,128)(2,1)S(1)}, bf16[128,2048]{1,0:T(8,128)(2,1)S(1)}, u32[]{:S(2)}, u32[]{:S(2)}) collective-permute-start(bf16[128,2048]{1,0:T(8,128)(2,1)S(1)} %slice.582), channel_id=1, source_target_pairs={{0,8},{8,0},{16,24},{24,16},{1,9},{9,1},{17,25},{25,17},{2,10},{10... | collective-permute-start | bytes 1572872 | tf_op jit(solution)/shard_map/ppermute | solution.py:32
  727.9 30.5 %collective-permute-start.81 = (f32[20,2048]{1,0:T(8,128)S(1)}, f32[20,2048]{1,0:T(8,128)S(1)}, u32[]{:S(2)}, u32[]{:S(2)}) collective-permute-start(f32[20,2048]{1,0:T(8,128)S(1)} %add.363), channel_id=1, source_target_pairs={{0,4},{1,5},{2,6},{3,7},{4,0},{5,1},{6,2},{7,3},{8,12},{9,13},{10,... | collective-permute-start | bytes 491528 | tf_op jit(solution)/shard_map/ppermute | solution.py:37
  727.9 30.5 %collective-permute-start.80 = (f32[20,2048]{1,0:T(8,128)S(1)}, f32[20,2048]{1,0:T(8,128)S(1)}, u32[]{:S(2)}, u32[]{:S(2)}) collective-permute-start(f32[20,2048]{1,0:T(8,128)S(1)} %add.363), channel_id=1, source_target_pairs={{0,2},{1,3},{2,0},{3,1},{4,6},{5,7},{6,4},{7,5},{8,10},{9,11},{10,... | collective-permute-start | bytes 491528 | tf_op jit(solution)/shard_map/ppermute | solution.py:37
  732.5 30.1 %collective-permute-start.83 = (bf16[64,2048]{1,0:T(8,128)(2,1)S(1)}, bf16[64,2048]{1,0:T(8,128)(2,1)S(1)}, u32[]{:S(2)}, u32[]{:S(2)}) collective-permute-start(bf16[64,2048]{1,0:T(8,128)(2,1)S(1)} %slice.595), channel_id=1, source_target_pairs={{0,2},{1,3},{2,0},{3,1},{4,6},{5,7},{6,4},{7,5},{8,10},{9,11},{10,... | collective-permute-start | bytes 786440 | tf_op jit(solution)/shard_map/ppermute | solution.py:37
  732.6 54.3 %collective-permute-start.84 = (bf16[64,2048]{1,0:T(8,128)(2,1)S(1)}, bf16[64,2048]{1,0:T(8,128)(2,1)S(1)}, u32[]{:S(2)}, u32[]{:S(2)}) collective-permute-start(bf16[64,2048]{1,0:T(8,128)(2,1)S(1)} %get-tuple-element.518), channel_id=1, source_target_pairs={{0,4},{1,5},{2,6},{3,7},{4,0},{5,1},{6,2},{7,3},{8,12},{9,13},{10,... | collective-permute-start | bytes 786440 | tf_op jit(solution)/shard_map/ppermute | solution.py:37
  736.8 50.2 %collective-permute-start.85 = (bf16[64,2048]{1,0:T(8,128)(2,1)S(1)}, bf16[64,2048]{1,0:T(8,128)(2,1)S(1)}, u32[]{:S(2)}, u32[]{:S(2)}) collective-permute-start(bf16[64,2048]{1,0:T(8,128)(2,1)S(1)} %get-tuple-element.519), channel_id=1, source_target_pairs={{0,6},{1,7},{2,4},{3,5},{4,2},{5,3},{6,0},{7,1},{8,14},{9,15},{10,... | collective-permute-start | bytes 786440 | tf_op jit(solution)/shard_map/ppermute | solution.py:37
  787.7 41.7 %collective-permute-start.86 = (bf16[64,2048]{1,0:T(8,128)(2,1)S(1)}, bf16[64,2048]{1,0:T(8,128)(2,1)S(1)}, u32[]{:S(2)}, u32[]{:S(2)}) collective-permute-start(bf16[64,2048]{1,0:T(8,128)(2,1)S(1)} %slice.599), channel_id=1, source_target_pairs={{0,2},{1,3},{2,0},{3,1},{4,6},{5,7},{6,4},{7,5},{8,10},{9,11},{10,... | collective-permute-start | bytes 786440 | tf_op jit(solution)/shard_map/ppermute | solution.py:37
  815.0 29.8 %collective-permute-start.87 = (bf16[64,2048]{1,0:T(8,128)(2,1)S(1)}, bf16[64,2048]{1,0:T(8,128)(2,1)S(1)}, u32[]{:S(2)}, u32[]{:S(2)}) collective-permute-start(bf16[64,2048]{1,0:T(8,128)(2,1)S(1)} %get-tuple-element.516), channel_id=1, source_target_pairs={{0,4},{1,5},{2,6},{3,7},{4,0},{5,1},{6,2},{7,3},{8,12},{9,13},{10,... | collective-permute-start | bytes 786440 | tf_op jit(solution)/shard_map/ppermute | solution.py:37
  817.0 27.8 %collective-permute-start.88 = (bf16[64,2048]{1,0:T(8,128)(2,1)S(1)}, bf16[64,2048]{1,0:T(8,128)(2,1)S(1)}, u32[]{:S(2)}, u32[]{:S(2)}) collective-permute-start(bf16[64,2048]{1,0:T(8,128)(2,1)S(1)} %get-tuple-element.517), channel_id=1, source_target_pairs={{0,6},{1,7},{2,4},{3,5},{4,2},{5,3},{6,0},{7,1},{8,14},{9,15},{10,... | collective-permute-start | bytes 786440 | tf_op jit(solution)/shard_map/ppermute | solution.py:37
  (79 other events, 1247.4 us)
Sparse Core Ops, SparseCore 0:
  639.1 87.8 reduce-scatter.1
  728.6 131.0 all-gather.1

commit v3 on v2

--- a/solution.py
+++ b/solution.py
@@ -108,37 +108,34 @@
     )
 
 
-def scatter_core(own, other):
-    return add_low(own, swap_dp(other, 1)).astype(BF)
-
-
 def cut(rows, count):
     n = rows.shape[-2] // count
     return [rows[..., i * n : (i + 1) * n, :] for i in range(count)]
 
 
-def scatter_plane_near(rows):
-    keep_a, send_a, keep_b, send_b = cut(rows, 4)
-    send_a, send_b = lax.optimization_barrier((send_a, send_b))
+def add_pieces(left, right):
+    return [add_low(one, two).astype(BF) for one, two in zip(left, right)]
+
+
+def scatter_core(own, other):
+    return add_pieces(cut(own, 4), cut(swap_dp(other, 1), 4))
+
+
+def scatter_plane_near(quarters):
+    keep_a, send_a, keep_b, send_b = quarters
     got_a, got_b = swap_tp(send_a, 1), swap_tp(send_b, 2)
-    return add_low(keep_a, got_a).astype(BF), add_low(keep_b, got_b).astype(BF)
-
-
-def scatter_plane_far(part_a, part_b):
-    (keep_a, send_a), (keep_b, send_b) = cut(part_a, 2), cut(part_b, 2)
-    send_a, send_b = lax.optimization_barrier((send_a, send_b))
+    return add_pieces(cut(keep_a, 2), cut(got_a, 2)) + add_pieces(cut(keep_b, 2), cut(got_b, 2))
+
+
+def scatter_plane_far(eighths, partners):
+    keep_a, send_a, keep_b, send_b = eighths
     got_a, got_b = swap_tp(send_a, 2), swap_tp(send_b, 1)
-    return add_low(keep_a, got_a).astype(BF), add_low(keep_b, got_b).astype(BF)
-
-
-def scatter_outer(part_a, part_b, partners):
     half = len(partners) // 2
-    pieces = cut(part_a, half) + cut(part_b, half)
+    return add_pieces(cut(keep_a, half), cut(got_a, half)) + add_pieces(cut(keep_b, half), cut(got_b, half))
+
+
+def scatter_outer(pieces, partners):
     return add_low(*[swap_dp(p, 2 * k) if k else p for p, k in zip(pieces, partners)])
-
-
-def sum_dp(value):
-    return lax.psum(value.astype(BF), "dp").astype(F32)
 
 
 def call_kernel(body, ins, outs, grid=(), in_specs=None, out_specs=None, flops=0, moved=0, **extra):
@@ -157,15 +154,18 @@
     )(*ins)
 
 
-def project_kernel(rows_ref, weight_ref, packed_ref, squares_ref):
+def project_kernel(rows_ref, gain_ref, weight_ref, normed_ref, packed_ref, squares_ref):
     part = pl.program_id(0)
-    packed = jnp.dot(rows_ref[...], weight_ref[...], preferred_element_type=F32)
+
+    @pl.when(part == 0)
+    def _():
+        rows = rows_ref[...].astype(F32)
+        normed_ref[...] = (rows * rms_scale(rows) * gain_ref[...]).astype(BF)
+        squares_ref[...] = jnp.zeros_like(squares_ref)
+
+    packed = jnp.dot(normed_ref[...], weight_ref[...], preferred_element_type=F32)
     packed_ref[...] = packed
     lane = lax.broadcasted_iota(jnp.int32, squares_ref.shape, 1)
-
-    @pl.when(part == 0)
-    def _():
-        squares_ref[...] = jnp.zeros_like(squares_ref)
 
     @pl.when(part < 2)
     def _():
@@ -173,30 +173,33 @@
         squares_ref[...] += jnp.where(lane == part, total, 0.0)
 
 
-def project(normed, qkv_parts):
-    micro, group, width = normed.shape
+def project(gathered, gain, qkv_parts):
+    micro, group, width = gathered.shape
     columns = qkv_parts.shape[2]
     rows = micro * group
-    packed, squares = call_kernel(
+    normed, packed, squares = call_kernel(
         project_kernel,
-        (normed.reshape(rows, width), qkv_parts),
+        (gathered.reshape(rows, width), gain[None], qkv_parts),
         [
+            jax.ShapeDtypeStruct((rows, width), BF),
             jax.ShapeDtypeStruct((rows, 3 * columns), F32),
             jax.ShapeDtypeStruct((rows, LANES), F32),
         ],
         grid=(3,),
         in_specs=[
             pl.BlockSpec((rows, width), lambda i: (0, 0)),
+            pl.BlockSpec((1, width), lambda i: (0, 0)),
             pl.BlockSpec((None, width, columns), lambda i: (i, 0, 0)),
         ],
         out_specs=[
+            pl.BlockSpec((rows, width), lambda i: (0, 0)),
             pl.BlockSpec((rows, columns), lambda i: (0, i)),
             pl.BlockSpec((rows, LANES), lambda i: (0, 0)),
         ],
         flops=2 * rows * width * 3 * columns,
         moved=2 * width * 3 * columns,
     )
-    return packed.reshape(micro, group, 3 * columns), squares.reshape(micro, group, LANES)
+    return (value.reshape(micro, group, -1) for value in (normed, packed, squares))
 
 
 def attend_kernel(
@@ -332,7 +335,7 @@
         ],
         grid=(1,),
         in_specs=[
-            pick(group, width),
+            full(group, width),
             full(columns, width),
             pick(group, 3 * columns),
             pick(heads, group, group),
@@ -397,7 +400,7 @@
         in_specs=[
             full(group, 2 * columns),
             full(group, columns),
-            pick(group, LANES),
+            full(group, LANES),
             pick(group, 3 * columns),
             pick(group, LANES),
             full(3, width, columns),
@@ -439,26 +442,44 @@
     )[0]
 
 
-def qkv_product_kernel(left_ref, right_ref, out_ref):
-    out_ref[...] = contract(left_ref[...], right_ref[...], 0, 0).astype(BF)
-
-
-def qkv_product(normed, d_packed):
-    rows, width = normed.shape
-    columns = d_packed.shape[1] // 3
-    tile = min(width, 1024)
+def shared_grads_kernel(normed_ref, d_packed0_ref, d_packed1_ref, attended_ref, d_branch0_ref, d_branch1_ref, out_ref):
+    columns = attended_ref.shape[2]
+
+    @pl.when(pl.program_id(0) < 3)
+    def _():
+        total = contract(normed_ref[0], d_packed0_ref[...], 0, 0)
+        out_ref[...] = (total + contract(normed_ref[1], d_packed1_ref[...], 0, 0)).astype(BF)
+
+    @pl.when(pl.program_id(0) == 3)
+    def _():
+        for start in range(0, out_ref.shape[0], columns):
+            at = slice(start, start + columns)
+            total = contract(attended_ref[0], d_branch0_ref[:, at], 0, 0)
+            out_ref[at, :] = (total + contract(attended_ref[1], d_branch1_ref[:, at], 0, 0)).astype(BF)
+
+
+def shared_grads(normed, d_packed, attended, d_branch):
+    micro, group, width = normed.shape
+    columns = attended.shape[2]
+    tile = width // 2
+    packed_spec = pl.BlockSpec((group, columns), lambda p, i: (0, jnp.minimum(p, 2)))
+    branch_spec = pl.BlockSpec((group, tile), lambda p, i: (0, jnp.where(p == 3, i, 0)))
     return call_kernel(
-        qkv_product_kernel,
-        (normed, d_packed),
-        [jax.ShapeDtypeStruct((3, width, columns), BF)],
-        grid=(3, width // tile),
+        shared_grads_kernel,
+        (normed, *d_packed, attended, *d_branch),
+        [jax.ShapeDtypeStruct((4 * width, columns), BF)],
+        grid=(4, 2),
         in_specs=[
-            pl.BlockSpec((rows, tile), lambda p, i: (0, i)),
-            pl.BlockSpec((rows, columns), lambda p, i: (0, p)),
-        ],
-        out_specs=[pl.BlockSpec((None, tile, columns), lambda p, i: (p, i, 0))],
-        flops=2 * rows * width * 3 * columns,
-        moved=2 * width * 3 * columns,
+            pl.BlockSpec((micro, group, tile), lambda p, i: (0, 0, i)),
+            packed_spec,
+            packed_spec,
+            pl.BlockSpec((micro, group, columns), lambda p, i: (0, 0, 0)),
+            branch_spec,
+            branch_spec,
+        ],
+        out_specs=[pl.BlockSpec((tile, columns), lambda p, i: (2 * p + i, 0))],
+        flops=2 * micro * group * width * 4 * columns,
+        moved=2 * width * 4 * columns,
     )[0]
 
 
@@ -572,8 +593,6 @@
     mask = jnp.pad(chosen.astype(BF), ((0, 0), (0, 0), (0, -experts % LANES)))
     cot_sent = jnp.concatenate([d_mixed.astype(BF), mask], axis=2)
 
-    grad_router = 0.0
-    grad_moe_gain = 0.0
 
     outer = dp_size // 2
     span = min(outer, 4)
@@ -597,9 +616,9 @@
     def mix(ran):
         return jnp.dot(ran[1], down, preferred_element_type=F32).astype(BF)
 
-    normed = gather_tp((x_hat * attn_gain).astype(BF))
+    gathered = gather_tp(tokens[:, 0])
     cot_z = [swap_dp(cot_sent, 2 * k) for k in zone[1:-1]]
-    normed, cot_late = sync(normed, cot_sent)
+    gathered, cot_late = sync(gathered, cot_sent)
     cot_z.append(swap_dp(cot_late, 2 * zone[-1]))
 
     segment = (places >= first_len).astype(jnp.int32) + (places >= live_end).astype(jnp.int32)
@@ -610,12 +629,12 @@
     sine = jnp.concatenate([-sine, sine], axis=2)
     allowed = (segment[:, :, None] == segment[:, None, :]) & (places[None, :] <= places[:, None])
 
-    packed, squares = project(normed, qkv_parts)
+    normed, packed, squares = project(gathered, attn_gain, qkv_parts)
     squares = sum_tp(squares)
     used, weights, attended, branch = attend(
         packed, squares, qk_gain, cosine, sine, allowed.astype(F32), out_weight
     )
-    branch, *cot_z = sync(branch, cot_sent, *cot_z)
+    branch, gate_up, down, router_wide, *cot_z = sync(branch, gate_up, down, router_wide, cot_sent, *cot_z)
     branch_own, cot_z = scatter_tp_first(branch, jnp.concatenate(cot_z, axis=1))
     cot_z0, cot_z1 = cot_z[0], cot_z[1]
     cot_near0 = gather_plane_near(cot_z0)
@@ -651,51 +670,79 @@
     cot_half1 = gather_plane_far(cot_z1, *rest[:2])
     moe_half1 = gather_plane_far(moe_z1, *rest[2:4])
     mix0 = [mix(own0), mix(other0)]
-    ran0, moe0, cot0 = (own0, other0), (moe_half0, moe_other0), (cot_half0, cot_other0)
-    d_gate_up = gate_up_grads(None, moe0, ran0)
-
-    core0, cot_half1, moe_half1, d_gate_up, *mix0 = sync(core0, cot_half1, moe_half1, d_gate_up, *mix0)
+
+    cot_half1, moe_half1, *rest = sync(cot_half1, moe_half1, *core0, *mix0, *own0, *other0)
+    core0, mix0, own0, other0 = rest[:4], rest[4:6], rest[6:9], rest[9:]
     near0 = scatter_plane_near(core0)
     moe_other1, cot_other1 = swap_dp(moe_half1, 1), swap_dp(cot_half1, 1)
+    own1 = experts_of(moe_half1, cot_half1)
+
+    moe_other1, cot_other1, *rest = sync(moe_other1, cot_other1, *near0, *own1)
+    near0, own1 = rest[:4], rest[4:]
+    far0 = scatter_plane_far(near0, zone)
+    other1 = experts_of(moe_other1, cot_other1)
+
+    rest = sync(*far0, *mix0, *own1, *other1)
+    far0, rest = rest[:span], rest[span:]
+    mix0, own1, other1 = rest[:2], rest[2:5], rest[5:]
+    core1 = scatter_core(own1[0], other1[0])
+    back0 = scatter_outer(far0, zone)
     mix_core0 = scatter_core(*mix0)
-    own1 = experts_of(moe_half1, cot_half1)
-
-    moe_other1, cot_other1, mix_core0, *rest = sync(moe_other1, cot_other1, mix_core0, *near0, *own1)
-    near0, own1 = rest[:2], rest[2:]
-    far0 = scatter_plane_far(*near0)
-    other1 = experts_of(moe_other1, cot_other1)
-
-    mix_core0, *rest = sync(mix_core0, *far0, *own1, *other1)
-    far0, own1, other1 = rest[:2], rest[2:5], rest[5:]
-    core1 = scatter_core(own1[0], other1[0])
-    back0 = scatter_outer(*far0, zone)
     mix1 = [mix(own1), mix(other1)]
-    ran1, moe1, cot1 = (own1, other1), (moe_half1, moe_other1), (cot_half1, cot_other1)
-    d_down = down_grads(None, cot0, ran0)
-
-    core1, back0, mix_core0, d_down, *mix1 = sync(core1, back0, mix_core0, d_down, *mix1)
+
+    back0, *rest = sync(back0, *core1, *mix_core0, *mix1, *own1, *other1)
+    core1, mix_core0, mix1, own1, other1 = rest[:4], rest[4:8], rest[8:10], rest[10:13], rest[13:]
     near1 = scatter_plane_near(core1)
     mix_core1 = scatter_core(*mix1)
-    d_gate_up = gate_up_grads(d_gate_up, moe1, ran1)
-
-    back0, mix_core0, mix_core1, d_gate_up, *near1 = sync(back0, mix_core0, mix_core1, d_gate_up, *near1)
-    far1 = scatter_plane_far(*near1)
-    d_down = down_grads(d_down, cot1, ran1)
-
-    back0, mix_core0, mix_core1, d_gate_up, d_down, *far1 = sync(
-        back0, mix_core0, mix_core1, d_gate_up, d_down, *far1
-    )
-    back1 = scatter_outer(*far1, zone)
+
+    def into_hidden(m, back):
+        expert_grad = back[:, :width]
+        probs = jax.nn.softmax(jnp.dot(moe_own[m], router, preferred_element_type=F32), axis=-1)
+        d_choice = back[:, width : width + experts]
+        d_logits = (probs * (d_choice - jnp.sum(probs * d_choice, axis=1, keepdims=True))).astype(BF)
+        d_moe_in = expert_grad + contract(d_logits, router, 1, 1)
+        d_h_hat = d_moe_in * moe_gain
+        d_hidden = d_mixed[m] + h_scale[m] * (
+            d_h_hat - h_hat[m] * jnp.mean(d_h_hat * h_hat[m], axis=1, keepdims=True)
+        )
+        small = (contract(moe_own[m], d_logits, 0, 0), jnp.sum(d_moe_in * h_hat[m], axis=0))
+        return d_hidden, small
+
+    def into_attention(m, d_branch):
+        return attend_back(
+            m, d_branch, out_weight, used, weights, packed, squares, qk_gain, cosine, sine
+        )
+
+    def into_packed(m, back, dots):
+        return unproject(m, *back[:2], dots, packed, squares, qkv_parts, normed)
+
+    ran0, moe0, cot0 = (own0, other0), (moe_half0, moe_other0), (cot_half0, cot_other0)
+    ran1, moe1, cot1 = (own1, other1), (moe_half1, moe_other1), (cot_half1, cot_other1)
+    whole = len(parts) == 1
+    if whole:
+        d_hidden0, small0 = into_hidden(0, back0)
+        back0 = d_hidden0
+    back0, *rest = sync(back0, *near1, *mix_core0, *mix_core1)
+    near1, mix_core0, mix_core1 = rest[:4], rest[4:8], rest[8:]
+    far1 = scatter_plane_far(near1, zone)
+    if whole:
+        d_branch0 = gather_tp(back0.astype(BF))
+        d_branch0, *rest = sync(d_branch0, *far1, *mix_core0, *mix_core1)
+    else:
+        back0, *rest = sync(back0, *far1, *mix_core0, *mix_core1)
+    far1, mix_core0, mix_core1 = rest[:span], rest[span : span + 4], rest[span + 4 :]
+    back1 = scatter_outer(far1, zone)
     mix_near0 = scatter_plane_near(mix_core0)
-    d_gate_up_out = d_gate_up.reshape(width, local, 2, quarter)
-    d_gate_up_out = jnp.stack([d_gate_up_out[:, e] for e in range(local)])
-    if len(parts) == 1:
-        back1, back0, d_gate_up_out, mix_core1, *mix_near0 = sync(
-            back1, back0, d_gate_up_out, mix_core1, *mix_near0
-        )
-    back = [back0, back1]
+    d_gate_up = d_down = None
     more = [0.0, 0.0]
-    if len(parts) > 1:
+    if whole:
+        to_packed0 = into_attention(0, d_branch0)
+        back1, *rest = sync(back1, *to_packed0, *mix_near0, *mix_core1)
+        to_packed0, mix_near0, mix_core1 = rest[:4], rest[4:8], rest[8:]
+    else:
+        back = [back0, back1]
+        d_gate_up = gate_up_grads(None, moe0 + moe1, ran0 + ran1)
+        d_down = down_grads(None, cot0 + cot1, ran0 + ran1)
         for later in parts[1:]:
             for m in range(micro_count):
                 sent, moe_sent, d_gate_up, d_down, back[m], more[m] = sync(
@@ -713,82 +760,68 @@
                 terms = []
                 for pair in ([r[0] for r in ran], [mix(r) for r in ran]):
                     near = scatter_plane_near(scatter_core(*pair))
-                    terms.append(scatter_outer(*scatter_plane_far(*near), later))
+                    terms.append(scatter_outer(scatter_plane_far(near, later), later))
                 back[m], more[m] = back[m] + terms[0], more[m] + terms[1]
-        d_gate_up_out = d_gate_up.reshape(width, local, 2, quarter)
-        d_gate_up_out = jnp.stack([d_gate_up_out[:, e] for e in range(local)])
-
-    d_branches, d_hiddens = [], []
-    for m in range(micro_count):
-        expert_grad = back[m][:, :width]
-        probs = jax.nn.softmax(jnp.dot(moe_own[m], router, preferred_element_type=F32), axis=-1)
-        d_choice = back[m][:, width : width + experts]
-        d_logits = (probs * (d_choice - jnp.sum(probs * d_choice, axis=1, keepdims=True))).astype(BF)
-        grad_router = grad_router + contract(moe_own[m], d_logits, 0, 0)
-        d_moe_in = expert_grad + contract(d_logits, router, 1, 1)
-        grad_moe_gain = grad_moe_gain + jnp.sum(d_moe_in * h_hat[m], axis=0)
-        d_h_hat = d_moe_in * moe_gain
-        d_hiddens.append(
-            d_mixed[m]
-            + h_scale[m] * (d_h_hat - h_hat[m] * jnp.mean(d_h_hat * h_hat[m], axis=1, keepdims=True))
-        )
-    d_branch = gather_tp(jnp.stack(d_hiddens).astype(BF))
-    d_branch, mix_core1, *mix_near0 = sync(d_branch, mix_core1, *mix_near0)
-    backs = [
-        attend_back(
-            m, d_branch, out_weight, used, weights, packed, squares, qk_gain, cosine, sine
-        )
-        for m in range(micro_count)
-    ]
-    grad_qk = sum(gain_grad for _, _, _, gain_grad in backs)[:2]
-    dots = sum_tp(jnp.stack([b[2] for b in backs]))
-    grad_out = contract(attended.reshape(-1, columns), d_branch.reshape(-1, width), 0, 0).astype(BF)
-    dots, grad_out, mix_core1, *mix_near0 = sync(dots, grad_out, mix_core1, *mix_near0)
-    mix_far0 = scatter_plane_far(*mix_near0)
+        d_hidden0, small0 = into_hidden(0, back[0])
+        back1 = back[1]
+        d_branch0 = gather_tp(d_hidden0.astype(BF))
+        to_packed0 = into_attention(0, d_branch0)
+
+    d_hidden1, small1 = into_hidden(1, back1)
+    d_branch1 = gather_tp(d_hidden1.astype(BF))
+    dots0 = sum_tp(to_packed0[2])
+    d_branch1, dots0, *rest = sync(d_branch1, dots0, *mix_near0, *mix_core1)
+    mix_near0, mix_core1 = rest[:4], rest[4:]
+    to_packed1 = into_attention(1, d_branch1)
+    mix_far0 = scatter_plane_far(mix_near0, zone)
+    dots1 = sum_tp(to_packed1[2])
+    end0 = into_packed(0, to_packed0, dots0)
+    dots1, *rest = sync(dots1, *end0, *mix_far0)
+    end0, mix_far0 = rest[:3], rest[3:]
+    mixed0 = scatter_outer(mix_far0, zone)
+    end1 = into_packed(1, to_packed1, dots1)
+    shared = shared_grads(normed, (end0[0], end1[0]), attended, (d_branch0, d_branch1))
+    shared, mixed0, *rest = sync(shared, mixed0, *mix_core1, *end0[1:], *end1[1:])
+    mix_core1, d_normed, attn_terms = rest[:4], (rest[4], rest[6]), (rest[5], rest[7])
+
+    shared = lax.psum_scatter(shared, "dp", scatter_dimension=0, tiled=True)
     mix_near1 = scatter_plane_near(mix_core1)
-    ends = [
-        unproject(m, *backs[m][:2], dots, packed, squares, qkv_parts, normed) for m in range(micro_count)
-    ]
-    d_packed = jnp.concatenate([end[0] for end in ends])
-    grad_qkv = qkv_product(normed.reshape(-1, width), d_packed)
-    shared = [grad_qkv[p] for p in range(3)]
-    shared += [grad_out[:, i : i + columns] for i in range(0, width, columns)]
-    shared, *rest = sync(jnp.concatenate(shared), *mix_far0, *mix_near1, ends[0][1], ends[1][1])
-    mix_far0, mix_near1, d_normed = rest[:2], rest[2:4], rest[4:]
-
-    shared = lax.psum_scatter(shared, "dp", scatter_dimension=0, tiled=True)
-    mix_far1 = scatter_plane_far(*mix_near1)
     d_normed0 = scatter_tp(d_normed[0])
-    d_normed0, d_normed1, *rest = sync(d_normed0, d_normed[1], *mix_far0, *mix_far1)
-    mix_far0, mix_far1 = rest[:2], rest[2:]
-    d_normed1 = scatter_tp(d_normed1)
-    grad_attn_gain = sum(end[2] for end in ends)[0] / attn_gain
+    grad_attn_gain = (attn_terms[0] + attn_terms[1])[0] / attn_gain
+    grad_qk = (to_packed0[3] + to_packed1[3])[:2]
     wide_qk = jnp.pad(grad_qk, ((0, 0), (0, width - columns)))
+    grad_router, grad_moe_gain = (one + two for one, two in zip(small0, small1))
     small = jnp.concatenate([grad_attn_gain[None], grad_moe_gain[None], grad_router.T], axis=0)
-    d_normed0, d_normed1, small, *rest = sync(d_normed0, d_normed1, small, *mix_far0, *mix_far1)
-    mix_far0, mix_far1 = rest[:2], rest[2:]
+    small, d_normed0, d_normed1, *mix_near1 = sync(small, d_normed0, d_normed[1], *mix_near1)
+    mix_far1 = scatter_plane_far(mix_near1, zone)
     total = small
     for k in range(1, tp_size):
         total = total + swap_tp(small, k)
     small = jnp.concatenate([total, wide_qk], axis=0)
-    small = small + swap_dp(small, 1)
+    small, d_normed0, d_normed1, *mix_far1 = sync(small, d_normed0, d_normed1, *mix_far1)
+    mixed1 = scatter_outer(mix_far1, zone)
+    small = (small + swap_dp(small, 1)).astype(BF)
+    shared, mixed1, small, d_normed0, d_normed1 = sync(shared, mixed1, small, d_normed0, d_normed1)
+    shared = lax.all_gather(shared, "dp", axis=0, tiled=True)
+    small = add_low(small, *[swap_dp(small, 2 * k) for k in range(1, outer)])
+    d_normed1 = scatter_tp(d_normed1)
+    if whole:
+        d_gate_up = gate_up_grads(None, moe0 + moe1, ran0 + ran1)
+        d_down = down_grads(None, cot0 + cot1, ran0 + ran1)
     input_grads = []
-    for m, d_normed in enumerate((d_normed0, d_normed1)):
-        d_x_hat = d_normed * attn_gain
-        d_tokens = d_hiddens[m] + x_scale[m] * (
+    for m, (d_hidden, d_rows) in enumerate(((d_hidden0, d_normed0), (d_hidden1, d_normed1))):
+        d_x_hat = d_rows * attn_gain
+        d_tokens = d_hidden + x_scale[m] * (
             d_x_hat - x_hat[m] * jnp.mean(d_x_hat * x_hat[m], axis=1, keepdims=True)
         )
         input_grads.append(d_tokens.astype(BF))
-    shared, small, d_tokens, *rest = sync(shared, small, jnp.stack(input_grads), *mix_far0, *mix_far1)
-    mix_far0, mix_far1 = rest[:2], rest[2:]
-    shared = lax.all_gather(shared, "dp", axis=0, tiled=True)
-    terms = [swap_dp(small, 2 * k) for k in range(1, outer)]
-    small = sum(terms, small)
-    mixed0 = scatter_outer(*mix_far0, zone)
-    small, mixed0, *mix_far1 = sync(small, mixed0, *mix_far1)
-    mixed = jnp.stack([mixed0 + more[0], scatter_outer(*mix_far1, zone) + more[1]])
+    mixed = jnp.stack([mixed0 + more[0], mixed1 + more[1]])
     out = (hidden + mixed).astype(BF)
-    shared, out = sync(shared, out)
+    d_gate_up = d_gate_up.reshape(width, local, 2, quarter)
+    d_gate_up_out = jnp.stack([d_gate_up[:, e] for e in range(local)])
+    shared, small, d_tokens, out, d_gate_up_out, d_down = sync(
+        shared, small, jnp.stack(input_grads), out, d_gate_up_out, d_down
+    )
     total_qkv = shared[: 3 * width].reshape(3, width, columns)
     total_out = shared[3 * width :].reshape(width // columns, columns, columns)
     total_out = jnp.concatenate([piece for piece in total_out], axis=1).astype(F32)

time: 880 us -> 772 us (0.88); the launches traced: 880 us -> 761 us
  waiting for transfers between devices: 320 us -> 281 us
  local copies, waits for them, and re-layouts: 99.8 us -> 70.9 us
  Pallas kernels: 198 us -> 180 us
  starting transfers between devices: 136 us -> 119 us
  other arithmetic: 85 us -> 71.7 us
    reduce_scatter x1, waiting for transfers between devices: 32.3 us -> 3.58 us  [shards(): shared = lax.psum_scatter(shared, 'dp', scatter_dimension=0, tiled=True)]
    ppermute x33, starting transfers between devices: 74.8 us -> 48.9 us  [swap_dp(): return lax.ppermute(value, 'dp', [(i, i ^ bits) for i in range(size)])]
    pallas_call x15 -> x13, Pallas kernels: 198 us -> 180 us  [call_kernel(): pl.pallas_call(body, out_shape=outs, grid=grid, in_specs=in_specs or [who...]
    unnamed x132 -> x129, local copies, waits for them, and re-layouts: 38.9 us -> 26.2 us
    convert_element_type x16 -> x23, other arithmetic: 37.9 us -> 25.9 us  [the longest x20 24.9 us: add_pieces(): return [add_low(one, two).astype(BF) for one, two in zip(left, right)]]
    ppermute x56 -> x62, waiting for transfers between devices: 154 us -> 165 us  [swap_tp(): return lax.ppermute(value, 'tp', [(i, i ^ bits) for i in range(size)])]
    slice x20 -> x0, local copies, waits for them, and re-layouts: 10.3 us -> none  [cut(): return [rows[..., i * n:(i + 1) * n, :] for i in range(count)]]
    ppermute x33, waiting for transfers between devices: 119 us -> 109 us  [swap_dp(): return lax.ppermute(value, 'dp', [(i, i ^ bits) for i in range(size)])]
  transfers between devices with their start and end apart: 91 -> 97, of which waited for: 44 -> 44; matrix products, arithmetic and copies ran while one was open for 16% -> 16% of each run, Pallas kernels for 21% -> 23%
where the time goes in v3:
time: 772 us; the launch traced here: 761 us
  waiting for transfers between devices  281 us (36%)
  Pallas kernels  180 us (23%)
  starting transfers between devices  119 us (15%)
  other arithmetic  71.7 us (9%)
  local copies, waits for them, and re-layouts  70.9 us (9%)
  matrix products  22.5 us (3%)
  between operations  15.4 us (2%)
    pallas_call x13, Pallas kernels, call_kernel(): pl.pallas_call(body, out_shape=outs, grid=grid, in_specs=in_specs or [who...  180 us
    ppermute x62, waiting for transfers between devices, swap_tp(): return lax.ppermute(value, 'tp', [(i, i ^ bits) for i in range(size)])  165 us
    ppermute x33, waiting for transfers between devices, swap_dp(): return lax.ppermute(value, 'dp', [(i, i ^ bits) for i in range(size)])  109 us
    ppermute x62, starting transfers between devices, swap_tp(): return lax.ppermute(value, 'tp', [(i, i ^ bits) for i in range(size)])  70.2 us
    ppermute x33, starting transfers between devices, swap_dp(): return lax.ppermute(value, 'dp', [(i, i ^ bits) for i in range(size)])  48.9 us
    unnamed x129, local copies, waits for them, and re-layouts  26.2 us
    convert_element_type x20, other arithmetic, add_pieces(): return [add_low(one, two).astype(BF) for one, two in zip(left, right)]  24.9 us
    dot_general x4, matrix products, mix(): return jnp.dot(ran[1], down, preferred_element_type=F32).astype(BF)  17.4 us
  transfers between devices with their start and end apart: 97, of which 44 were waited for; matrix products, arithmetic and copies ran while one was open for 16% of the time, Pallas kernels for 23%

profile of v3, /device:TPU:0, one launch (start us, length us, event | category | flops | bytes accessed | tf_op | source)
XLA Modules:
  0.0 760.8 jit_solution(16909837403866283910)
XLA Ops:
  7.2 4.0 collective-permute-start.2
  20.5 4.7 fusion.28
  28.2 2.7 pad_maximum_fusion.1.gate_up_ref
  30.9 3.8 collective-permute-done.1
  35.0 2.9 pad_maximum_fusion.3
  37.9 9.4 %shard_map.195 = (bf16[512,2048]{1,0:T(8,128)(2,1)}, f32[512,1536]{1,0:T(8,128)}, f32[512,128]{1,0:T(8,128)}) custom-call(bf16[512,2048]{1,0:T(8,128)(2,1)} %bitcast.158, f32[1,2048]{1,0:T(1,128)} %bitcast.180, bf16[3,2048,512]{2,1,0:T(8,128)(2,1)} %bitcast.143), custom_call_target="tpu_custom_call" | custom-call | flops 402653184 | bytes 786432 | tf_op jit(solution)/shard_map/pallas_call | solution.py:143
  53.7 3.2 collective-permute-done.3
  56.9 3.6 collective-permute-start.8
  63.5 2.9 collective-permute-done.4
  67.2 7.7 %shard_map.196 = (bf16[2,256,1536]{2,1,0:T(8,128)(2,1)}, f32[2,4,256,256]{3,2,1,0:T(8,128)}, bf16[2,256,512]{2,1,0:T(8,128)(2,1)}, bf16[2,256,2048]{2,1,0:T(8,128)(2,1)}) custom-call(f32[2,256,1536]{2,1,0:T(8,128)} %bitcast.138, f32[2,256,128]{2,1,0:T(8,128)} %fusion.7.squares_ref, f32[2,512]{1,0:T(2,128)} %gain_ref.5, ...), custom_call_target="tpu_custom_call" | custom-call | flops 167772160 | bytes 2097152 | tf_op jit(solution)/shard_map/pallas_call | solution.py:143
  83.5 9.2 %collective-permute-done.11 = bf16[2,64,2048]{2,1,0:T(8,128)(2,1)S(1)} collective-permute-done((bf16[2,64,2048]{2,1,0:T(8,128)(2,1)S(1)}, bf16[2,64,2048]{2,1,0:T(8,128)(2,1)S(1)}, u32[]{:S(2)}, u32[]{:S(2)}) %collective-permute-start.11) | collective-permute-done | bytes 524320 | tf_op jit(solution)/shard_map/ppermute | solution.py:32
  92.7 9.3 %collective-permute-done.10 = bf16[2,64,2048]{2,1,0:T(8,128)(2,1)S(1)} collective-permute-done((bf16[2,64,2048]{2,1,0:T(8,128)(2,1)S(1)}, bf16[2,64,2048]{2,1,0:T(8,128)(2,1)S(1)}, u32[]{:S(2)}, u32[]{:S(2)}) %collective-permute-start.10) | collective-permute-done | bytes 524320 | tf_op jit(solution)/shard_map/ppermute | solution.py:32
  104.5 3.8 collective-permute-start.14
  108.4 7.0 collective-permute-start.13
  115.4 15.2 %collective-permute-done.13 = bf16[64,2048]{1,0:T(8,128)(2,1)S(1)} collective-permute-done((bf16[64,2048]{1,0:T(8,128)(2,1)S(1)}, bf16[64,2048]{1,0:T(8,128)(2,1)S(1)}, u32[]{:S(2)}, u32[]{:S(2)}) %collective-permute-start.13) | collective-permute-done | bytes 262176 | tf_op jit(solution)/shard_map/ppermute | solution.py:37
  132.9 3.5 collective-permute-start.19
  137.3 6.7 collective-permute-done.19
  144.0 15.1 %collective-permute-done.18 = bf16[64,2048]{1,0:T(8,128)(2,1)S(1)} collective-permute-done((bf16[64,2048]{1,0:T(8,128)(2,1)S(1)}, bf16[64,2048]{1,0:T(8,128)(2,1)S(1)}, u32[]{:S(2)}, u32[]{:S(2)}) %collective-permute-start.18) | collective-permute-done | bytes 262176 | tf_op jit(solution)/shard_map/ppermute | solution.py:37
  169.7 8.0 %collective-permute-done.22 = bf16[128,2048]{1,0:T(8,128)(2,1)S(1)} collective-permute-done((bf16[128,2048]{1,0:T(8,128)(2,1)S(1)}, bf16[128,2048]{1,0:T(8,128)(2,1)S(1)}, u32[]{:S(2)}, u32[]{:S(2)}) %collective-permute-start.22) | collective-permute-done | bytes 524320 | tf_op jit(solution)/shard_map/ppermute | solution.py:32
  181.8 6.8 collective-permute-done.24
  195.5 20.2 %shard_map.197 = (bf16[1024,2176]{1,0:T(8,128)(2,1)}, bf16[1024,512]{1,0:T(8,128)(2,1)}, bf16[1024,1024]{1,0:T(8,128)(2,1)}) custom-call(s32[1]{0:T(128)} %bitcast.19.ids_ref, bf16[1024,2048]{1,0:T(8,128)(2,1)} %constant_dynamic-update-slice_fusion.moe_ref.refs_0_, bf16[1024,2176]{1,0:T(8,128)(2,1)} %constant_dynamic-update-slice_fusion.4.cot_ref.refs_4_, ...), custom_call_target="tpu_custom_call" | custom-call | flops 1342177280 | bytes 1572864 | tf_op jit(solution)/shard_map/pallas_call | solution.py:143
  215.7 4.5 collective-permute-done.28
  222.4 20.4 %shard_map.198 = (bf16[1024,2176]{1,0:T(8,128)(2,1)}, bf16[1024,512]{1,0:T(8,128)(2,1)}, bf16[1024,1024]{1,0:T(8,128)(2,1)}) custom-call(s32[1]{0:T(128)} %bitcast.19.ids_ref, bf16[1024,2048]{1,0:T(8,128)(2,1)} %collective-permute-done.26.moe_ref.refs_1_, bf16[1024,2176]{1,0:T(8,128)(2,1)} %collective-permute-done.27.cot_ref.refs_5_, ...), custom_call_target="tpu_custom_call" | custom-call | flops 1342177280 | bytes 1572864 | tf_op jit(solution)/shard_map/pallas_call | solution.py:143
  257.3 4.4 convolution_convert_fusion.3
  261.7 4.4 convolution_convert_fusion.2
  266.1 7.9 %collective-permute-done.34 = bf16[128,2048]{1,0:T(8,128)(2,1)S(1)} collective-permute-done((bf16[128,2048]{1,0:T(8,128)(2,1)S(1)}, bf16[128,2048]{1,0:T(8,128)(2,1)S(1)}, u32[]{:S(2)}, u32[]{:S(2)}) %collective-permute-start.34) | collective-permute-done | bytes 524320 | tf_op jit(solution)/shard_map/ppermute | solution.py:32
  281.6 2.8 add_convert_fusion.4
  287.5 20.1 %shard_map.199 = (bf16[1024,2176]{1,0:T(8,128)(2,1)}, bf16[1024,512]{1,0:T(8,128)(2,1)}, bf16[1024,1024]{1,0:T(8,128)(2,1)}) custom-call(s32[1]{0:T(128)} %bitcast.19.ids_ref, bf16[1024,2048]{1,0:T(8,128)(2,1)} %constant_dynamic-update-slice_fusion.12.moe_ref.refs_2_, bf16[1024,2176]{1,0:T(8,128)(2,1)} %copy-done.5, bf16[2048,128]{1,0:T(8,128)(2,1)} %pad.17.router_ref, ...), custom_call_target="tpu_custom_call" | custom-call | flops 1342177280 | bytes 1572864 | tf_op jit(solution)/shard_map/pallas_call | solution.py:143
  307.7 4.6 collective-permute-done.39
  312.3 2.6 add_convert_fusion.22
  319.6 20.0 %shard_map.200 = (bf16[1024,2176]{1,0:T(8,128)(2,1)}, bf16[1024,512]{1,0:T(8,128)(2,1)}, bf16[1024,1024]{1,0:T(8,128)(2,1)}) custom-call(s32[1]{0:T(128)} %bitcast.19.ids_ref, bf16[1024,2048]{1,0:T(8,128)(2,1)} %collective-permute-done.37.moe_ref.refs_3_, bf16[1024,2176]{1,0:T(8,128)(2,1)} %collective-permute-done.38.cot_ref.refs_7_, ...), custom_call_target="tpu_custom_call" | custom-call | flops 1342177280 | bytes 1572864 | tf_op jit(solution)/shard_map/pallas_call | solution.py:143
  344.8 4.3 convolution_convert_fusion.1
  349.1 4.4 convolution_convert_fusion
  353.5 12.0 %collective-permute-done.44 = bf16[64,2176]{1,0:T(8,128)(2,1)S(1)} collective-permute-done((bf16[64,2176]{1,0:T(8,128)(2,1)S(1)}, bf16[64,2176]{1,0:T(8,128)(2,1)S(1)}, u32[]{:S(2)}, u32[]{:S(2)}) %collective-permute-start.44) | collective-permute-done | bytes 278560 | tf_op jit(solution)/shard_map/ppermute | solution.py:37
  378.5 21.4 %collective-permute-done.48 = bf16[256,2176]{1,0:T(8,128)(2,1)S(1)} collective-permute-done((bf16[256,2176]{1,0:T(8,128)(2,1)}, bf16[256,2176]{1,0:T(8,128)(2,1)S(1)}, u32[]{:S(2)}, u32[]{:S(2)}) %collective-permute-start.48) | collective-permute-done | bytes 1114144 | tf_op jit(solution)/shard_map/ppermute | solution.py:32
  402.1 4.5 add_convert_fusion.8
  412.6 5.7 collective-permute-done.53
  418.3 13.8 %collective-permute-done.52 = bf16[64,2048]{1,0:T(8,128)(2,1)S(1)} collective-permute-done((bf16[64,2048]{1,0:T(8,128)(2,1)S(1)}, bf16[64,2048]{1,0:T(8,128)(2,1)S(1)}, u32[]{:S(2)}, u32[]{:S(2)}) %collective-permute-start.52) | collective-permute-done | bytes 262176 | tf_op jit(solution)/shard_map/ppermute | solution.py:32
  443.4 7.1 shard_map.201
  450.5 8.7 %collective-permute-done.57 = bf16[64,2176]{1,0:T(8,128)(2,1)} collective-permute-done((bf16[64,2176]{1,0:T(8,128)(2,1)}, bf16[64,2176]{1,0:T(8,128)(2,1)}, u32[]{:S(2)}, u32[]{:S(2)}) %collective-permute-start.57) | collective-permute-done | bytes 278560 | tf_op jit(solution)/shard_map/ppermute | solution.py:37
  473.1 2.8 collective-permute-done.65
  477.1 6.4 collective-permute-done.64
  487.5 7.0 shard_map.202
  499.7 6.8 shard_map.203
  507.3 3.1 collective-permute-done.70
  516.5 7.0 shard_map.204
  523.5 12.3 %shard_map.205 = bf16[8192,512]{1,0:T(8,128)(2,1)} custom-call(bf16[2,256,2048]{2,1,0:T(8,128)(2,1)} %bitcast.157, bf16[256,1536]{1,0:T(8,128)(2,1)} %get-tuple-element.417.d_packed0_ref, bf16[256,1536]{1,0:T(8,128)(2,1)} %get-tuple-element.421.d_packed1_ref, bf16[2,256,512]{2,1,0:T(8,128)(2,1)} %get-tuple-element.422.attended_ref, ...), custom_call_target="tpu_custom_call" | custom-call | flops 536870912 | bytes 1048576 | tf_op jit(solution)/shard_map/pallas_call | solution.py:143
  548.6 3.5 collective-permute-done.77
  552.1 3.2 collective-permute-done.76
  558.3 17.2 %collective-permute-done.78 = bf16[256,2048]{1,0:T(8,128)(2,1)S(1)} collective-permute-done((bf16[256,2048]{1,0:T(8,128)(2,1)}, bf16[256,2048]{1,0:T(8,128)(2,1)S(1)}, u32[]{:S(2)}, u32[]{:S(2)}) %collective-permute-start.78) | collective-permute-done | bytes 1048608 | tf_op jit(solution)/shard_map/ppermute | solution.py:32
  588.9 8.7 %collective-permute-done.83 = bf16[128,2048]{1,0:T(8,128)(2,1)S(1)} collective-permute-done((bf16[128,2048]{1,0:T(8,128)(2,1)S(1)}, bf16[128,2048]{1,0:T(8,128)(2,1)S(1)}, u32[]{:S(2)}, u32[]{:S(2)}) %collective-permute-start.83) | collective-permute-done | bytes 524320 | tf_op jit(solution)/shard_map/ppermute | solution.py:32
  602.4 12.2 %collective-permute-done.87 = bf16[64,2048]{1,0:T(8,128)(2,1)S(1)} collective-permute-done((bf16[64,2048]{1,0:T(8,128)(2,1)S(1)}, bf16[64,2048]{1,0:T(8,128)(2,1)S(1)}, u32[]{:S(2)}, u32[]{:S(2)}) %collective-permute-start.87) | collective-permute-done | bytes 262176 | tf_op jit(solution)/shard_map/ppermute | solution.py:37
  614.6 23.7 %collective-permute-done.86 = bf16[64,2048]{1,0:T(8,128)(2,1)S(1)} collective-permute-done((bf16[64,2048]{1,0:T(8,128)(2,1)S(1)}, bf16[64,2048]{1,0:T(8,128)(2,1)S(1)}, u32[]{:S(2)}, u32[]{:S(2)}) %collective-permute-start.86) | collective-permute-done | bytes 262176 | tf_op jit(solution)/shard_map/ppermute | solution.py:37
  639.2 3.6 reduce-scatter.2.cloned.1.call-done
  642.9 24.4 %shard_map.206 = f32[2048,1024]{1,0:T(8,128)} custom-call(bf16[1024,2048]{1,0:T(8,128)(2,1)} %constant_dynamic-update-slice_fusion.moe_ref.refs_0_, bf16[1024,2048]{1,0:T(8,128)(2,1)} %collective-permute-done.26.moe_ref.refs_1_, bf16[1024,2048]{1,0:T(8,128)(2,1)} %constant_dynamic-update-slice_fusion.12.moe_ref.refs_2_, ...), custom_call_target="tpu_custom_call" | custom-call | flops 2147483648 | bytes 4194304 | tf_op jit(solution)/shard_map/pallas_call | solution.py:143
  667.2 11.7 %reshape.431 = f32[2048,2,2,256]{3,2,1,0:T(2,128)} reshape(f32[2048,1024]{1,0:T(8,128)} %shard_map.206) | data formatting | bytes 16777216 | tf_op jit(solution)/shard_map/reshape | solution.py:820
  679.0 17.2 %shard_map.207 = f32[512,2048]{1,0:T(8,128)} custom-call(bf16[1024,512]{1,0:T(8,128)(2,1)} %get-tuple-element.470.refs_0_, bf16[1024,512]{1,0:T(8,128)(2,1)} %get-tuple-element.471.refs_1_, bf16[1024,512]{1,0:T(8,128)(2,1)} %get-tuple-element.472.refs_2_, bf16[1024,512]{1,0:T(8,128)(2,1)} %get-tuple-element.473.refs_3_, ...), custom_call_target="tpu_custom_call" | custom-call | flops 1073741824 | bytes 3145728 | tf_op jit(solution)/shard_map/pallas_call | solution.py:143
  696.1 5.5 slice_bitcast_fusion.1
  701.7 4.8 pad_maximum_fusion
  707.2 4.7 collective-permute-start.90
  717.1 15.2 %collective-permute-done.90 = bf16[20,2048]{1,0:T(8,128)(2,1)S(1)} collective-permute-done((bf16[20,2048]{1,0:T(8,128)(2,1)S(1)}, bf16[20,2048]{1,0:T(8,128)(2,1)S(1)}, u32[]{:S(2)}, u32[]{:S(2)}) %collective-permute-start.90) | collective-permute-done | bytes 81952 | tf_op jit(solution)/shard_map/ppermute | solution.py:37
  734.0 3.8 all-gather.2.cloned.1.call-done
  739.1 3.4 copy-done.4
  744.6 6.6 convert_bitcast_fusion
  (412 shorter events, 207.4 us)
Async XLA Ops:
  7.2 635.6 %reduce-scatter.2.cloned.1.call-start = ((), (), s32[]{:S(2)}) async-start(), calls=%async_computation.1 | async-start | bytes 9437184 | tf_op jit(solution)/shard_map/reduce_scatter | solution.py:787
  7.2 23.7 %collective-permute-start.2 = (bf16[2,64,2048]{2,1,0:T(8,128)(2,1)}, bf16[2,64,2048]{2,1,0:T(8,128)(2,1)}, u32[]{:S(2)}, u32[]{:S(2)}) collective-permute-start(bf16[2,64,2048]{2,1,0:T(8,128)(2,1)} %bitcast.163), channel_id=1, source_target_pairs={{0,24},{8,16},{16,8},{24,0},{1,25},{9,17},{17,9},{25,1},{2,26},{10... | collective-permute-start | bytes 1572872 | tf_op jit(solution)/shard_map/ppermute | solution.py:32
  11.2 23.5 %collective-permute-start.1 = (bf16[2,64,2048]{2,1,0:T(8,128)(2,1)}, bf16[2,64,2048]{2,1,0:T(8,128)(2,1)}, u32[]{:S(2)}, u32[]{:S(2)}) collective-permute-start(bf16[2,64,2048]{2,1,0:T(8,128)(2,1)} %bitcast.164), channel_id=1, source_target_pairs={{0,16},{8,24},{16,0},{24,8},{1,17},{9,25},{17,1},{25,9},{2,18},{10... | collective-permute-start | bytes 1572872 | tf_op jit(solution)/shard_map/ppermute | solution.py:32
  11.7 23.3 %collective-permute-start = (bf16[2,64,2048]{2,1,0:T(8,128)(2,1)}, bf16[2,64,2048]{2,1,0:T(8,128)(2,1)}, u32[]{:S(2)}, u32[]{:S(2)}) collective-permute-start(bf16[2,64,2048]{2,1,0:T(8,128)(2,1)} %bitcast.165), channel_id=1, source_target_pairs={{0,8},{8,0},{16,24},{24,16},{1,9},{9,1},{17,25},{25,17},{2,10},{10... | collective-permute-start | bytes 1572872 | tf_op jit(solution)/shard_map/ppermute | solution.py:32
  15.4 59.5 %collective-permute-start.6 = (bf16[2,64,2176]{2,1,0:T(8,128)(2,1)S(1)}, bf16[2,64,2176]{2,1,0:T(8,128)(2,1)S(1)}, u32[]{:S(2)}, u32[]{:S(2)}) collective-permute-start(bf16[2,64,2176]{2,1,0:T(8,128)(2,1)S(1)} %pad_maximum_fusion.8), channel_id=1, source_target_pairs={{0,2},{1,3},{2,0},{3,1},{4,6},{5,7},{6,4},{7,5},{8,10},{9,11},{10,... | collective-permute-start | bytes 1671176 | tf_op jit(solution)/shard_map/ppermute | solution.py:37
  17.5 57.5 %collective-permute-start.7 = (bf16[2,64,2176]{2,1,0:T(8,128)(2,1)S(1)}, bf16[2,64,2176]{2,1,0:T(8,128)(2,1)S(1)}, u32[]{:S(2)}, u32[]{:S(2)}) collective-permute-start(bf16[2,64,2176]{2,1,0:T(8,128)(2,1)S(1)} %pad_maximum_fusion.8), channel_id=1, source_target_pairs={{0,4},{1,5},{2,6},{3,7},{4,0},{5,1},{6,2},{7,3},{8,12},{9,13},{10,... | collective-permute-start | bytes 1671176 | tf_op jit(solution)/shard_map/ppermute | solution.py:37
  56.9 18.0 %collective-permute-start.8 = (bf16[2,64,2176]{2,1,0:T(8,128)(2,1)S(1)}, bf16[2,64,2176]{2,1,0:T(8,128)(2,1)S(1)}, u32[]{:S(2)}, u32[]{:S(2)}) collective-permute-start(bf16[2,64,2176]{2,1,0:T(8,128)(2,1)S(1)} %pad_maximum_fusion.8), channel_id=1, source_target_pairs={{0,6},{1,7},{2,4},{3,5},{4,2},{5,3},{6,0},{7,1},{8,14},{9,15},{10,... | collective-permute-start | bytes 1671176 | tf_op jit(solution)/shard_map/ppermute | solution.py:37
  78.3 23.6 %collective-permute-start.10 = (bf16[2,64,2048]{2,1,0:T(8,128)(2,1)S(1)}, bf16[2,64,2048]{2,1,0:T(8,128)(2,1)S(1)}, u32[]{:S(2)}, u32[]{:S(2)}) collective-permute-start(bf16[2,64,2048]{2,1,0:T(8,128)(2,1)S(1)} %get-tuple-element.258), channel_id=1, source_target_pairs={{0,16},{8,24},{16,0},{24,8},{1,17},{9,25},{17,1},{25,9},{2,18},{10... | collective-permute-start | bytes 1572872 | tf_op jit(solution)/shard_map/ppermute | solution.py:32
  78.6 24.1 %collective-permute-start.9 = (bf16[2,64,2048]{2,1,0:T(8,128)(2,1)S(1)}, bf16[2,64,2048]{2,1,0:T(8,128)(2,1)S(1)}, u32[]{:S(2)}, u32[]{:S(2)}) collective-permute-start(bf16[2,64,2048]{2,1,0:T(8,128)(2,1)S(1)} %get-tuple-element.257), channel_id=1, source_target_pairs={{0,8},{8,0},{16,24},{24,16},{1,9},{9,1},{17,25},{25,17},{2,10},{10... | collective-permute-start | bytes 1572872 | tf_op jit(solution)/shard_map/ppermute | solution.py:32
  81.5 49.3 %collective-permute-start.15 = (bf16[256,2176]{1,0:T(8,128)(2,1)S(1)}, bf16[256,2176]{1,0:T(8,128)(2,1)S(1)}, u32[]{:S(2)}, u32[]{:S(2)}) collective-permute-start(bf16[256,2176]{1,0:T(8,128)(2,1)S(1)} %get-tuple-element.272), channel_id=1, source_target_pairs={{0,8},{8,0},{16,24},{24,16},{1,9},{9,1},{17,25},{25,17},{2,10},{10... | collective-permute-start | bytes 3342344 | tf_op jit(solution)/shard_map/ppermute | solution.py:32
  81.8 49.0 %collective-permute-start.16 = (bf16[256,2176]{1,0:T(8,128)(2,1)S(1)}, bf16[256,2176]{1,0:T(8,128)(2,1)S(1)}, u32[]{:S(2)}, u32[]{:S(2)}) collective-permute-start(bf16[256,2176]{1,0:T(8,128)(2,1)S(1)} %get-tuple-element.272), channel_id=1, source_target_pairs={{0,16},{8,24},{16,0},{24,8},{1,17},{9,25},{17,1},{25,9},{2,18},{10... | collective-permute-start | bytes 3342344 | tf_op jit(solution)/shard_map/ppermute | solution.py:32
  108.4 22.3 %collective-permute-start.13 = (bf16[64,2048]{1,0:T(8,128)(2,1)S(1)}, bf16[64,2048]{1,0:T(8,128)(2,1)S(1)}, u32[]{:S(2)}, u32[]{:S(2)}) collective-permute-start(bf16[64,2048]{1,0:T(8,128)(2,1)S(1)} %get-tuple-element.614), channel_id=1, source_target_pairs={{0,4},{1,5},{2,6},{3,7},{4,0},{5,1},{6,2},{7,3},{8,12},{9,13},{10,... | collective-permute-start | bytes 786440 | tf_op jit(solution)/shard_map/ppermute | solution.py:37
  130.8 29.4 %collective-permute-start.20 = (bf16[256,2048]{1,0:T(8,128)(2,1)S(1)}, bf16[256,2048]{1,0:T(8,128)(2,1)S(1)}, u32[]{:S(2)}, u32[]{:S(2)}) collective-permute-start(bf16[256,2048]{1,0:T(8,128)(2,1)S(1)} %pad_maximum_fusion.4), channel_id=1, source_target_pairs={{0,8},{8,0},{16,24},{24,16},{1,9},{9,1},{17,25},{25,17},{2,10},{10... | collective-permute-start | bytes 3145736 | tf_op jit(solution)/shard_map/ppermute | solution.py:32
  132.4 27.9 %collective-permute-start.21 = (bf16[256,2048]{1,0:T(8,128)(2,1)S(1)}, bf16[256,2048]{1,0:T(8,128)(2,1)S(1)}, u32[]{:S(2)}, u32[]{:S(2)}) collective-permute-start(bf16[256,2048]{1,0:T(8,128)(2,1)S(1)} %pad_maximum_fusion.4), channel_id=1, source_target_pairs={{0,16},{8,24},{16,0},{24,8},{1,17},{9,25},{17,1},{25,9},{2,18},{10... | collective-permute-start | bytes 3145736 | tf_op jit(solution)/shard_map/ppermute | solution.py:32
  136.4 22.8 %collective-permute-start.18 = (bf16[64,2048]{1,0:T(8,128)(2,1)S(1)}, bf16[64,2048]{1,0:T(8,128)(2,1)S(1)}, u32[]{:S(2)}, u32[]{:S(2)}) collective-permute-start(bf16[64,2048]{1,0:T(8,128)(2,1)S(1)} %get-tuple-element.262), channel_id=1, source_target_pairs={{0,4},{1,5},{2,6},{3,7},{4,0},{5,1},{6,2},{7,3},{8,12},{9,13},{10,... | collective-permute-start | bytes 786440 | tf_op jit(solution)/shard_map/ppermute | solution.py:37
  137.3 21.8 %collective-permute-start.17 = (bf16[64,2048]{1,0:T(8,128)(2,1)S(1)}, bf16[64,2048]{1,0:T(8,128)(2,1)S(1)}, u32[]{:S(2)}, u32[]{:S(2)}) collective-permute-start(bf16[64,2048]{1,0:T(8,128)(2,1)S(1)} %get-tuple-element.262), channel_id=1, source_target_pairs={{0,2},{1,3},{2,0},{3,1},{4,6},{5,7},{6,4},{7,5},{8,10},{9,11},{10,... | collective-permute-start | bytes 786440 | tf_op jit(solution)/shard_map/ppermute | solution.py:37
  163.2 17.8 %collective-permute-start.23 = (bf16[128,2048]{1,0:T(8,128)(2,1)S(1)}, bf16[128,2048]{1,0:T(8,128)(2,1)S(1)}, u32[]{:S(2)}, u32[]{:S(2)}) collective-permute-start(bf16[128,2048]{1,0:T(8,128)(2,1)S(1)} %get-tuple-element.271), channel_id=1, source_target_pairs={{0,8},{8,0},{16,24},{24,16},{1,9},{9,1},{17,25},{25,17},{2,10},{10... | collective-permute-start | bytes 1572872 | tf_op jit(solution)/shard_map/ppermute | solution.py:32
  167.7 21.0 %collective-permute-start.24 = (bf16[128,2176]{1,0:T(8,128)(2,1)S(1)}, bf16[128,2176]{1,0:T(8,128)(2,1)S(1)}, u32[]{:S(2)}, u32[]{:S(2)}) collective-permute-start(bf16[128,2176]{1,0:T(8,128)(2,1)S(1)} %get-tuple-element.275), channel_id=1, source_target_pairs={{0,16},{8,24},{16,0},{24,8},{1,17},{9,25},{17,1},{25,9},{2,18},{10... | collective-permute-start | bytes 1671176 | tf_op jit(solution)/shard_map/ppermute | solution.py:32
  168.1 23.9 %collective-permute-start.25 = (bf16[128,2176]{1,0:T(8,128)(2,1)S(1)}, bf16[128,2176]{1,0:T(8,128)(2,1)S(1)}, u32[]{:S(2)}, u32[]{:S(2)}) collective-permute-start(bf16[128,2176]{1,0:T(8,128)(2,1)S(1)} %get-tuple-element.276), channel_id=1, source_target_pairs={{0,8},{8,0},{16,24},{24,16},{1,9},{9,1},{17,25},{25,17},{2,10},{10... | collective-permute-start | bytes 1671176 | tf_op jit(solution)/shard_map/ppermute | solution.py:32
  192.9 27.5 %collective-permute-start.27 = (bf16[1024,2176]{1,0:T(8,128)(2,1)}, bf16[1024,2176]{1,0:T(8,128)(2,1)}, u32[]{:S(2)}, u32[]{:S(2)}) collective-permute-start(bf16[1024,2176]{1,0:T(8,128)(2,1)} %constant_dynamic-update-slice_fusion.4.cot_ref.refs_4_), channel_id=1, source_target_pairs={{0,1},{1,0},{2,3},{3,2},{4,5},{5,4},{6,7},{7,6},{8,9},{9,8},{10,11... | collective-permute-start | bytes 13369352 | tf_op jit(solution)/shard_map/ppermute | solution.py:37
  192.9 27.5 %collective-permute-start.26 = (bf16[1024,2048]{1,0:T(8,128)(2,1)}, bf16[1024,2048]{1,0:T(8,128)(2,1)}, u32[]{:S(2)}, u32[]{:S(2)}) collective-permute-start(bf16[1024,2048]{1,0:T(8,128)(2,1)} %constant_dynamic-update-slice_fusion.moe_ref.refs_0_), channel_id=1, source_target_pairs={{0,1},{1,0},{2,3},{3,2},{4,5},{5,4},{6,7},{7,6},{8,9},{9,8},{10,11... | collective-permute-start | bytes 12582920 | tf_op jit(solution)/shard_map/ppermute | solution.py:37
  193.4 26.8 %collective-permute-start.28 = (bf16[256,2176]{1,0:T(8,128)(2,1)}, bf16[256,2176]{1,0:T(8,128)(2,1)}, u32[]{:S(2)}, u32[]{:S(2)}) collective-permute-start(bf16[256,2176]{1,0:T(8,128)(2,1)} %get-tuple-element.301), channel_id=1, source_target_pairs={{0,8},{8,0},{16,24},{24,16},{1,9},{9,1},{17,25},{25,17},{2,10},{10... | collective-permute-start | bytes 3342344 | tf_op jit(solution)/shard_map/ppermute | solution.py:32
  193.9 26.5 %collective-permute-start.29 = (bf16[256,2176]{1,0:T(8,128)(2,1)}, bf16[256,2176]{1,0:T(8,128)(2,1)}, u32[]{:S(2)}, u32[]{:S(2)}) collective-permute-start(bf16[256,2176]{1,0:T(8,128)(2,1)} %get-tuple-element.301), channel_id=1, source_target_pairs={{0,16},{8,24},{16,0},{24,8},{1,17},{9,25},{17,1},{25,9},{2,18},{10... | collective-permute-start | bytes 3342344 | tf_op jit(solution)/shard_map/ppermute | solution.py:32
  220.4 24.1 %collective-permute-start.30 = (bf16[256,2048]{1,0:T(8,128)(2,1)S(1)}, bf16[256,2048]{1,0:T(8,128)(2,1)S(1)}, u32[]{:S(2)}, u32[]{:S(2)}) collective-permute-start(bf16[256,2048]{1,0:T(8,128)(2,1)S(1)} %copy-done.17), channel_id=1, source_target_pairs={{0,8},{8,0},{16,24},{24,16},{1,9},{9,1},{17,25},{25,17},{2,10},{10... | collective-permute-start | bytes 3145736 | tf_op jit(solution)/shard_map/ppermute | solution.py:32
  222.0 23.6 %collective-permute-start.31 = (bf16[256,2048]{1,0:T(8,128)(2,1)S(1)}, bf16[256,2048]{1,0:T(8,128)(2,1)S(1)}, u32[]{:S(2)}, u32[]{:S(2)}) collective-permute-start(bf16[256,2048]{1,0:T(8,128)(2,1)S(1)} %copy-done.17), channel_id=1, source_target_pairs={{0,16},{8,24},{16,0},{24,8},{1,17},{9,25},{17,1},{25,9},{2,18},{10... | collective-permute-start | bytes 3145736 | tf_op jit(solution)/shard_map/ppermute | solution.py:32
  250.5 27.6 %collective-permute-start.32 = (bf16[128,2176]{1,0:T(8,128)(2,1)S(1)}, bf16[128,2176]{1,0:T(8,128)(2,1)S(1)}, u32[]{:S(2)}, u32[]{:S(2)}) collective-permute-start(bf16[128,2176]{1,0:T(8,128)(2,1)S(1)} %get-tuple-element.304), channel_id=1, source_target_pairs={{0,16},{8,24},{16,0},{24,8},{1,17},{9,25},{17,1},{25,9},{2,18},{10... | collective-permute-start | bytes 1671176 | tf_op jit(solution)/shard_map/ppermute | solution.py:32
  251.2 30.3 %collective-permute-start.33 = (bf16[128,2176]{1,0:T(8,128)(2,1)S(1)}, bf16[128,2176]{1,0:T(8,128)(2,1)S(1)}, u32[]{:S(2)}, u32[]{:S(2)}) collective-permute-start(bf16[128,2176]{1,0:T(8,128)(2,1)S(1)} %get-tuple-element.305), channel_id=1, source_target_pairs={{0,8},{8,0},{16,24},{24,16},{1,9},{9,1},{17,25},{25,17},{2,10},{10... | collective-permute-start | bytes 1671176 | tf_op jit(solution)/shard_map/ppermute | solution.py:32
  255.3 18.7 %collective-permute-start.34 = (bf16[128,2048]{1,0:T(8,128)(2,1)S(1)}, bf16[128,2048]{1,0:T(8,128)(2,1)S(1)}, u32[]{:S(2)}, u32[]{:S(2)}) collective-permute-start(bf16[128,2048]{1,0:T(8,128)(2,1)S(1)} %get-tuple-element.309), channel_id=1, source_target_pairs={{0,16},{8,24},{16,0},{24,8},{1,17},{9,25},{17,1},{25,9},{2,18},{10... | collective-permute-start | bytes 1572872 | tf_op jit(solution)/shard_map/ppermute | solution.py:32
  255.9 21.4 %collective-permute-start.35 = (bf16[128,2048]{1,0:T(8,128)(2,1)S(1)}, bf16[128,2048]{1,0:T(8,128)(2,1)S(1)}, u32[]{:S(2)}, u32[]{:S(2)}) collective-permute-start(bf16[128,2048]{1,0:T(8,128)(2,1)S(1)} %get-tuple-element.310), channel_id=1, source_target_pairs={{0,8},{8,0},{16,24},{24,16},{1,9},{9,1},{17,25},{25,17},{2,10},{10... | collective-permute-start | bytes 1572872 | tf_op jit(solution)/shard_map/ppermute | solution.py:32
  257.3 24.3 %collective-permute-start.36 = (bf16[1024,2176]{1,0:T(8,128)(2,1)}, bf16[1024,2176]{1,0:T(8,128)(2,1)S(1)}, u32[]{:S(2)}, u32[]{:S(2)}) collective-permute-start(bf16[1024,2176]{1,0:T(8,128)(2,1)} %get-tuple-element.312), channel_id=1, source_target_pairs={{0,1},{1,0},{2,3},{3,2},{4,5},{5,4},{6,7},{7,6},{8,9},{9,8},{10,11... | collective-permute-start | bytes 13369352 | tf_op jit(solution)/shard_map/ppermute | solution.py:37
  285.0 32.5 %collective-permute-start.38 = (bf16[1024,2176]{1,0:T(8,128)(2,1)S(1)}, bf16[1024,2176]{1,0:T(8,128)(2,1)}, u32[]{:S(2)}, u32[]{:S(2)}) collective-permute-start(bf16[1024,2176]{1,0:T(8,128)(2,1)S(1)} %constant_dynamic-update-slice_fusion.8.cot_ref.refs_6_), channel_id=1, source_target_pairs={{0,1},{1,0},{2,3},{3,2},{4,5},{5,4},{6,7},{7,6},{8,9},{9,8},{10,11... | collective-permute-start | bytes 13369352 | tf_op jit(solution)/shard_map/ppermute | solution.py:37
  285.0 32.5 %collective-permute-start.37 = (bf16[1024,2048]{1,0:T(8,128)(2,1)}, bf16[1024,2048]{1,0:T(8,128)(2,1)}, u32[]{:S(2)}, u32[]{:S(2)}) collective-permute-start(bf16[1024,2048]{1,0:T(8,128)(2,1)} %constant_dynamic-update-slice_fusion.12.moe_ref.refs_2_), channel_id=1, source_target_pairs={{0,1},{1,0},{2,3},{3,2},{4,5},{5,4},{6,7},{7,6},{8,9},{9,8},{10,11... | collective-permute-start | bytes 12582920 | tf_op jit(solution)/shard_map/ppermute | solution.py:37
  285.5 26.8 %collective-permute-start.39 = (bf16[256,2176]{1,0:T(8,128)(2,1)}, bf16[256,2176]{1,0:T(8,128)(2,1)}, u32[]{:S(2)}, u32[]{:S(2)}) collective-permute-start(bf16[256,2176]{1,0:T(8,128)(2,1)} %get-tuple-element.320), channel_id=1, source_target_pairs={{0,8},{8,0},{16,24},{24,16},{1,9},{9,1},{17,25},{25,17},{2,10},{10... | collective-permute-start | bytes 3342344 | tf_op jit(solution)/shard_map/ppermute | solution.py:32
  286.4 28.5 %collective-permute-start.40 = (bf16[256,2176]{1,0:T(8,128)(2,1)}, bf16[256,2176]{1,0:T(8,128)(2,1)}, u32[]{:S(2)}, u32[]{:S(2)}) collective-permute-start(bf16[256,2176]{1,0:T(8,128)(2,1)} %get-tuple-element.322), channel_id=1, source_target_pairs={{0,16},{8,24},{16,0},{24,8},{1,17},{9,25},{17,1},{25,9},{2,18},{10... | collective-permute-start | bytes 3342344 | tf_op jit(solution)/shard_map/ppermute | solution.py:32
  317.5 22.1 %collective-permute-start.41 = (bf16[128,2176]{1,0:T(8,128)(2,1)}, bf16[128,2176]{1,0:T(8,128)(2,1)S(1)}, u32[]{:S(2)}, u32[]{:S(2)}) collective-permute-start(bf16[128,2176]{1,0:T(8,128)(2,1)} %get-tuple-element.327), channel_id=1, source_target_pairs={{0,16},{8,24},{16,0},{24,8},{1,17},{9,25},{17,1},{25,9},{2,18},{10... | collective-permute-start | bytes 1671176 | tf_op jit(solution)/shard_map/ppermute | solution.py:32
  318.5 21.2 %collective-permute-start.42 = (bf16[128,2176]{1,0:T(8,128)(2,1)}, bf16[128,2176]{1,0:T(8,128)(2,1)S(1)}, u32[]{:S(2)}, u32[]{:S(2)}) collective-permute-start(bf16[128,2176]{1,0:T(8,128)(2,1)} %get-tuple-element.329), channel_id=1, source_target_pairs={{0,8},{8,0},{16,24},{24,16},{1,9},{9,1},{17,25},{25,17},{2,10},{10... | collective-permute-start | bytes 1671176 | tf_op jit(solution)/shard_map/ppermute | solution.py:32
  339.9 25.7 %collective-permute-start.47 = (bf16[1024,2048]{1,0:T(8,128)(2,1)}, bf16[1024,2048]{1,0:T(8,128)(2,1)S(1)}, u32[]{:S(2)}, u32[]{:S(2)}) collective-permute-start(bf16[1024,2048]{1,0:T(8,128)(2,1)} %convolution_convert_fusion.2), channel_id=1, source_target_pairs={{0,1},{1,0},{2,3},{3,2},{4,5},{5,4},{6,7},{7,6},{8,9},{9,8},{10,11... | collective-permute-start | bytes 12582920 | tf_op jit(solution)/shard_map/ppermute | solution.py:37
  339.9 28.3 %collective-permute-start.46 = (bf16[1024,2176]{1,0:T(8,128)(2,1)}, bf16[1024,2176]{1,0:T(8,128)(2,1)S(1)}, u32[]{:S(2)}, u32[]{:S(2)}) collective-permute-start(bf16[1024,2176]{1,0:T(8,128)(2,1)} %get-tuple-element.345), channel_id=1, source_target_pairs={{0,1},{1,0},{2,3},{3,2},{4,5},{5,4},{6,7},{7,6},{8,9},{9,8},{10,11... | collective-permute-start | bytes 13369352 | tf_op jit(solution)/shard_map/ppermute | solution.py:37
  342.3 23.2 %collective-permute-start.44 = (bf16[64,2176]{1,0:T(8,128)(2,1)S(1)}, bf16[64,2176]{1,0:T(8,128)(2,1)S(1)}, u32[]{:S(2)}, u32[]{:S(2)}) collective-permute-start(bf16[64,2176]{1,0:T(8,128)(2,1)S(1)} %get-tuple-element.342), channel_id=1, source_target_pairs={{0,4},{1,5},{2,6},{3,7},{4,0},{5,1},{6,2},{7,3},{8,12},{9,13},{10,... | collective-permute-start | bytes 835592 | tf_op jit(solution)/shard_map/ppermute | solution.py:37
  342.3 23.2 %collective-permute-start.43 = (bf16[64,2176]{1,0:T(8,128)(2,1)S(1)}, bf16[64,2176]{1,0:T(8,128)(2,1)S(1)}, u32[]{:S(2)}, u32[]{:S(2)}) collective-permute-start(bf16[64,2176]{1,0:T(8,128)(2,1)S(1)} %get-tuple-element.341), channel_id=1, source_target_pairs={{0,2},{1,3},{2,0},{3,1},{4,6},{5,7},{6,4},{7,5},{8,10},{9,11},{10,... | collective-permute-start | bytes 835592 | tf_op jit(solution)/shard_map/ppermute | solution.py:37
  371.9 29.4 %collective-permute-start.50 = (bf16[1024,2048]{1,0:T(8,128)(2,1)}, bf16[1024,2048]{1,0:T(8,128)(2,1)}, u32[]{:S(2)}, u32[]{:S(2)}) collective-permute-start(bf16[1024,2048]{1,0:T(8,128)(2,1)} %convolution_convert_fusion), channel_id=1, source_target_pairs={{0,1},{1,0},{2,3},{3,2},{4,5},{5,4},{6,7},{7,6},{8,9},{9,8},{10,11... | collective-permute-start | bytes 12582920 | tf_op jit(solution)/shard_map/ppermute | solution.py:37
  372.7 27.2 %collective-permute-start.48 = (bf16[256,2176]{1,0:T(8,128)(2,1)}, bf16[256,2176]{1,0:T(8,128)(2,1)S(1)}, u32[]{:S(2)}, u32[]{:S(2)}) collective-permute-start(bf16[256,2176]{1,0:T(8,128)(2,1)} %get-tuple-element.354), channel_id=1, source_target_pairs={{0,8},{8,0},{16,24},{24,16},{1,9},{9,1},{17,25},{25,17},{2,10},{10... | collective-permute-start | bytes 3342344 | tf_op jit(solution)/shard_map/ppermute | solution.py:32
  374.0 27.0 %collective-permute-start.49 = (bf16[256,2176]{1,0:T(8,128)(2,1)}, bf16[256,2176]{1,0:T(8,128)(2,1)S(1)}, u32[]{:S(2)}, u32[]{:S(2)}) collective-permute-start(bf16[256,2176]{1,0:T(8,128)(2,1)} %get-tuple-element.356), channel_id=1, source_target_pairs={{0,16},{8,24},{16,0},{24,8},{1,17},{9,25},{17,1},{25,9},{2,18},{10... | collective-permute-start | bytes 3342344 | tf_op jit(solution)/shard_map/ppermute | solution.py:32
  406.6 26.6 %collective-permute-start.54 = (bf16[128,2176]{1,0:T(8,128)(2,1)S(1)}, bf16[128,2176]{1,0:T(8,128)(2,1)S(1)}, u32[]{:S(2)}, u32[]{:S(2)}) collective-permute-start(bf16[128,2176]{1,0:T(8,128)(2,1)S(1)} %get-tuple-element.365), channel_id=1, source_target_pairs={{0,16},{8,24},{16,0},{24,8},{1,17},{9,25},{17,1},{25,9},{2,18},{10... | collective-permute-start | bytes 1671176 | tf_op jit(solution)/shard_map/ppermute | solution.py:32
  409.3 22.8 %collective-permute-start.52 = (bf16[64,2048]{1,0:T(8,128)(2,1)S(1)}, bf16[64,2048]{1,0:T(8,128)(2,1)S(1)}, u32[]{:S(2)}, u32[]{:S(2)}) collective-permute-start(bf16[64,2048]{1,0:T(8,128)(2,1)S(1)} %convert_element_type.745), channel_id=1, source_target_pairs={{0,16},{8,24},{16,0},{24,8},{1,17},{9,25},{17,1},{25,9},{2,18},{10... | collective-permute-start | bytes 786440 | tf_op jit(solution)/shard_map/ppermute | solution.py:32
  410.6 21.6 %collective-permute-start.51 = (bf16[64,2048]{1,0:T(8,128)(2,1)S(1)}, bf16[64,2048]{1,0:T(8,128)(2,1)S(1)}, u32[]{:S(2)}, u32[]{:S(2)}) collective-permute-start(bf16[64,2048]{1,0:T(8,128)(2,1)S(1)} %convert_element_type.745), channel_id=1, source_target_pairs={{0,8},{8,0},{16,24},{24,16},{1,9},{9,1},{17,25},{25,17},{2,10},{10... | collective-permute-start | bytes 786440 | tf_op jit(solution)/shard_map/ppermute | solution.py:32
  411.7 22.4 %collective-permute-start.55 = (bf16[128,2176]{1,0:T(8,128)(2,1)S(1)}, bf16[128,2176]{1,0:T(8,128)(2,1)S(1)}, u32[]{:S(2)}, u32[]{:S(2)}) collective-permute-start(bf16[128,2176]{1,0:T(8,128)(2,1)S(1)} %get-tuple-element.367), channel_id=1, source_target_pairs={{0,8},{8,0},{16,24},{24,16},{1,9},{9,1},{17,25},{25,17},{2,10},{10... | collective-permute-start | bytes 1671176 | tf_op jit(solution)/shard_map/ppermute | solution.py:32
  436.9 22.2 %collective-permute-start.57 = (bf16[64,2176]{1,0:T(8,128)(2,1)}, bf16[64,2176]{1,0:T(8,128)(2,1)}, u32[]{:S(2)}, u32[]{:S(2)}) collective-permute-start(bf16[64,2176]{1,0:T(8,128)(2,1)} %get-tuple-element.378), channel_id=1, source_target_pairs={{0,4},{1,5},{2,6},{3,7},{4,0},{5,1},{6,2},{7,3},{8,12},{9,13},{10,... | collective-permute-start | bytes 835592 | tf_op jit(solution)/shard_map/ppermute | solution.py:37
  436.9 22.2 %collective-permute-start.56 = (bf16[64,2176]{1,0:T(8,128)(2,1)}, bf16[64,2176]{1,0:T(8,128)(2,1)}, u32[]{:S(2)}, u32[]{:S(2)}) collective-permute-start(bf16[64,2176]{1,0:T(8,128)(2,1)} %get-tuple-element.377), channel_id=1, source_target_pairs={{0,2},{1,3},{2,0},{3,1},{4,6},{5,7},{6,4},{7,5},{8,10},{9,11},{10,... | collective-permute-start | bytes 835592 | tf_op jit(solution)/shard_map/ppermute | solution.py:37
  439.3 23.4 %collective-permute-start.59 = (bf16[256,2048]{1,0:T(8,128)(2,1)}, bf16[256,2048]{1,0:T(8,128)(2,1)}, u32[]{:S(2)}, u32[]{:S(2)}) collective-permute-start(bf16[256,2048]{1,0:T(8,128)(2,1)} %get-tuple-element.388), channel_id=1, source_target_pairs={{0,8},{8,0},{16,24},{24,16},{1,9},{9,1},{17,25},{25,17},{2,10},{10... | collective-permute-start | bytes 3145736 | tf_op jit(solution)/shard_map/ppermute | solution.py:32
  442.1 23.1 %collective-permute-start.60 = (bf16[256,2048]{1,0:T(8,128)(2,1)}, bf16[256,2048]{1,0:T(8,128)(2,1)S(1)}, u32[]{:S(2)}, u32[]{:S(2)}) collective-permute-start(bf16[256,2048]{1,0:T(8,128)(2,1)} %get-tuple-element.390), channel_id=1, source_target_pairs={{0,16},{8,24},{16,0},{24,8},{1,17},{9,25},{17,1},{25,9},{2,18},{10... | collective-permute-start | bytes 3145736 | tf_op jit(solution)/shard_map/ppermute | solution.py:32
  468.6 17.8 %collective-permute-start.63 = (bf16[64,2048]{1,0:T(8,128)(2,1)S(1)}, bf16[64,2048]{1,0:T(8,128)(2,1)S(1)}, u32[]{:S(2)}, u32[]{:S(2)}) collective-permute-start(bf16[64,2048]{1,0:T(8,128)(2,1)S(1)} %get-tuple-element.518), channel_id=1, source_target_pairs={{0,24},{8,16},{16,8},{24,0},{1,25},{9,17},{17,9},{25,1},{2,26},{10... | collective-permute-start | bytes 786440 | tf_op jit(solution)/shard_map/ppermute | solution.py:32
  512.1 23.7 %collective-permute-start.74 = (bf16[64,2048]{1,0:T(8,128)(2,1)}, bf16[64,2048]{1,0:T(8,128)(2,1)}, u32[]{:S(2)}, u32[]{:S(2)}) collective-permute-start(bf16[64,2048]{1,0:T(8,128)(2,1)} %get-tuple-element.426), channel_id=1, source_target_pairs={{0,6},{1,7},{2,4},{3,5},{4,2},{5,3},{6,0},{7,1},{8,14},{9,15},{10,... | collective-permute-start | bytes 786440 | tf_op jit(solution)/shard_map/ppermute | solution.py:37
  513.8 22.0 %collective-permute-start.73 = (bf16[64,2048]{1,0:T(8,128)(2,1)}, bf16[64,2048]{1,0:T(8,128)(2,1)}, u32[]{:S(2)}, u32[]{:S(2)}) collective-permute-start(bf16[64,2048]{1,0:T(8,128)(2,1)} %get-tuple-element.425), channel_id=1, source_target_pairs={{0,4},{1,5},{2,6},{3,7},{4,0},{5,1},{6,2},{7,3},{8,12},{9,13},{10,... | collective-permute-start | bytes 786440 | tf_op jit(solution)/shard_map/ppermute | solution.py:37
  514.4 21.4 %collective-permute-start.72 = (bf16[64,2048]{1,0:T(8,128)(2,1)}, bf16[64,2048]{1,0:T(8,128)(2,1)}, u32[]{:S(2)}, u32[]{:S(2)}) collective-permute-start(bf16[64,2048]{1,0:T(8,128)(2,1)} %get-tuple-element.424), channel_id=1, source_target_pairs={{0,2},{1,3},{2,0},{3,1},{4,6},{5,7},{6,4},{7,5},{8,10},{9,11},{10,... | collective-permute-start | bytes 786440 | tf_op jit(solution)/shard_map/ppermute | solution.py:37
  537.9 200.0 %all-gather.2.cloned.1.call-start = ((), (), s32[]{:S(2)}) async-start(), calls=%async_computation.2 | async-start | bytes 9437184 | tf_op jit(solution)/shard_map/all_gather | solution.py:805
  545.5 30.0 %collective-permute-start.78 = (bf16[256,2048]{1,0:T(8,128)(2,1)}, bf16[256,2048]{1,0:T(8,128)(2,1)S(1)}, u32[]{:S(2)}, u32[]{:S(2)}) collective-permute-start(bf16[256,2048]{1,0:T(8,128)(2,1)} %get-tuple-element.441), channel_id=1, source_target_pairs={{0,8},{8,0},{16,24},{24,16},{1,9},{9,1},{17,25},{25,17},{2,10},{10... | collective-permute-start | bytes 3145736 | tf_op jit(solution)/shard_map/ppermute | solution.py:32
  547.5 28.4 %collective-permute-start.79 = (bf16[256,2048]{1,0:T(8,128)(2,1)S(1)}, bf16[256,2048]{1,0:T(8,128)(2,1)S(1)}, u32[]{:S(2)}, u32[]{:S(2)}) collective-permute-start(bf16[256,2048]{1,0:T(8,128)(2,1)S(1)} %copy-done.31), channel_id=1, source_target_pairs={{0,16},{8,24},{16,0},{24,8},{1,17},{9,25},{17,1},{25,9},{2,18},{10... | collective-permute-start | bytes 3145736 | tf_op jit(solution)/shard_map/ppermute | solution.py:32
  600.2 38.2 %collective-permute-start.86 = (bf16[64,2048]{1,0:T(8,128)(2,1)S(1)}, bf16[64,2048]{1,0:T(8,128)(2,1)S(1)}, u32[]{:S(2)}, u32[]{:S(2)}) collective-permute-start(bf16[64,2048]{1,0:T(8,128)(2,1)S(1)} %get-tuple-element.455), channel_id=1, source_target_pairs={{0,4},{1,5},{2,6},{3,7},{4,0},{5,1},{6,2},{7,3},{8,12},{9,13},{10,... | collective-permute-start | bytes 786440 | tf_op jit(solution)/shard_map/ppermute | solution.py:37
  600.2 38.2 %collective-permute-start.85 = (bf16[64,2048]{1,0:T(8,128)(2,1)S(1)}, bf16[64,2048]{1,0:T(8,128)(2,1)S(1)}, u32[]{:S(2)}, u32[]{:S(2)}) collective-permute-start(bf16[64,2048]{1,0:T(8,128)(2,1)S(1)} %get-tuple-element.454), channel_id=1, source_target_pairs={{0,2},{1,3},{2,0},{3,1},{4,6},{5,7},{6,4},{7,5},{8,10},{9,11},{10,... | collective-permute-start | bytes 786440 | tf_op jit(solution)/shard_map/ppermute | solution.py:37
  707.2 25.1 %collective-permute-start.90 = (bf16[20,2048]{1,0:T(8,128)(2,1)S(1)}, bf16[20,2048]{1,0:T(8,128)(2,1)S(1)}, u32[]{:S(2)}, u32[]{:S(2)}) collective-permute-start(bf16[20,2048]{1,0:T(8,128)(2,1)S(1)} %add_convert_fusion.50), channel_id=1, source_target_pairs={{0,4},{1,5},{2,6},{3,7},{4,0},{5,1},{6,2},{7,3},{8,12},{9,13},{10,... | collective-permute-start | bytes 245768 | tf_op jit(solution)/shard_map/ppermute | solution.py:37
  711.9 20.4 %collective-permute-start.89 = (bf16[20,2048]{1,0:T(8,128)(2,1)S(1)}, bf16[20,2048]{1,0:T(8,128)(2,1)S(1)}, u32[]{:S(2)}, u32[]{:S(2)}) collective-permute-start(bf16[20,2048]{1,0:T(8,128)(2,1)S(1)} %add_convert_fusion.50), channel_id=1, source_target_pairs={{0,2},{1,3},{2,0},{3,1},{4,6},{5,7},{6,4},{7,5},{8,10},{9,11},{10,... | collective-permute-start | bytes 245768 | tf_op jit(solution)/shard_map/ppermute | solution.py:37
  712.6 19.8 %collective-permute-start.94 = (bf16[64,2048]{1,0:T(8,128)(2,1)S(1)}, bf16[64,2048]{1,0:T(8,128)(2,1)S(1)}, u32[]{:S(2)}, u32[]{:S(2)}) collective-permute-start(bf16[64,2048]{1,0:T(8,128)(2,1)S(1)} %get-tuple-element.589), channel_id=1, source_target_pairs={{0,24},{8,16},{16,8},{24,0},{1,25},{9,17},{17,9},{25,1},{2,26},{10... | collective-permute-start | bytes 786440 | tf_op jit(solution)/shard_map/ppermute | solution.py:32
  715.0 17.4 %collective-permute-start.93 = (bf16[64,2048]{1,0:T(8,128)(2,1)S(1)}, bf16[64,2048]{1,0:T(8,128)(2,1)S(1)}, u32[]{:S(2)}, u32[]{:S(2)}) collective-permute-start(bf16[64,2048]{1,0:T(8,128)(2,1)S(1)} %get-tuple-element.590), channel_id=1, source_target_pairs={{0,16},{8,24},{16,0},{24,8},{1,17},{9,25},{17,1},{25,9},{2,18},{10... | collective-permute-start | bytes 786440 | tf_op jit(solution)/shard_map/ppermute | solution.py:32
  (87 other events, 974.3 us)
Sparse Core Ops, SparseCore 0:
  538.0 104.7 reduce-scatter.1
  644.4 93.3 all-gather.1

commit v4 on v3

--- a/solution.py
+++ b/solution.py
@@ -13,7 +13,7 @@
 BF = jnp.bfloat16
 F32 = jnp.float32
 VMEM_BYTES = 56 * 1024 * 1024
-EXPERT_TILE = 512
+EXPERT_TILE = 256
 COST_SCALE = 8
 
 
@@ -136,6 +136,16 @@
 
 def scatter_outer(pieces, partners):
     return add_low(*[swap_dp(p, 2 * k) if k else p for p, k in zip(pieces, partners)])
+
+
+def scatter_pairs_near(pieces):
+    own, one, two, three = pieces
+    got_own, got_three = cut(swap_dp(jnp.concatenate([one, two], axis=0), 2), 2)
+    return [add_low(own, got_own), add_low(three, got_three).astype(BF)]
+
+
+def scatter_pairs_far(own, three):
+    return own + swap_dp(three, 6).astype(F32)
 
 
 def call_kernel(body, ins, outs, grid=(), in_specs=None, out_specs=None, flops=0, moved=0, **extra):
@@ -442,44 +452,67 @@
     )[0]
 
 
-def shared_grads_kernel(normed_ref, d_packed0_ref, d_packed1_ref, attended_ref, d_branch0_ref, d_branch1_ref, out_ref):
-    columns = attended_ref.shape[2]
-
-    @pl.when(pl.program_id(0) < 3)
+def rows_pair(left0_ref, left1_ref, right0, right1):
+    return (contract(left0_ref[...], right0, 0, 0) + contract(left1_ref[...], right1, 0, 0)).astype(BF)
+
+
+def early_grads_kernel(
+    normed0_ref, normed1_ref, d_value0_ref, d_value1_ref, attended0_ref, attended1_ref, d_branch0_ref,
+    d_branch1_ref, out_ref,
+):
+    columns = attended0_ref.shape[1]
+
+    @pl.when(pl.program_id(0) == 0)
     def _():
-        total = contract(normed_ref[0], d_packed0_ref[...], 0, 0)
-        out_ref[...] = (total + contract(normed_ref[1], d_packed1_ref[...], 0, 0)).astype(BF)
-
-    @pl.when(pl.program_id(0) == 3)
+        out_ref[...] = rows_pair(normed0_ref, normed1_ref, d_value0_ref[...], d_value1_ref[...])
+
+    @pl.when(pl.program_id(0) == 1)
     def _():
         for start in range(0, out_ref.shape[0], columns):
             at = slice(start, start + columns)
-            total = contract(attended_ref[0], d_branch0_ref[:, at], 0, 0)
-            out_ref[at, :] = (total + contract(attended_ref[1], d_branch1_ref[:, at], 0, 0)).astype(BF)
-
-
-def shared_grads(normed, d_packed, attended, d_branch):
+            out_ref[at, :] = rows_pair(
+                attended0_ref, attended1_ref, d_branch0_ref[:, at], d_branch1_ref[:, at]
+            )
+
+
+def early_grads(normed, d_value, attended, d_branch):
     micro, group, width = normed.shape
     columns = attended.shape[2]
     tile = width // 2
-    packed_spec = pl.BlockSpec((group, columns), lambda p, i: (0, jnp.minimum(p, 2)))
-    branch_spec = pl.BlockSpec((group, tile), lambda p, i: (0, jnp.where(p == 3, i, 0)))
+    normed_specs = [pl.BlockSpec((None, group, tile), lambda p, i, m=m: (m, 0, i)) for m in range(micro)]
+    value_spec = pl.BlockSpec((group, columns), lambda p, i: (0, 0))
+    attended_specs = [pl.BlockSpec((None, group, columns), lambda p, i, m=m: (m, 0, 0)) for m in range(micro)]
+    branch_spec = pl.BlockSpec((group, tile), lambda p, i: (0, jnp.where(p == 1, i, 0)))
     return call_kernel(
-        shared_grads_kernel,
-        (normed, *d_packed, attended, *d_branch),
-        [jax.ShapeDtypeStruct((4 * width, columns), BF)],
-        grid=(4, 2),
-        in_specs=[
-            pl.BlockSpec((micro, group, tile), lambda p, i: (0, 0, i)),
-            packed_spec,
-            packed_spec,
-            pl.BlockSpec((micro, group, columns), lambda p, i: (0, 0, 0)),
-            branch_spec,
-            branch_spec,
-        ],
+        early_grads_kernel,
+        (normed, normed, *d_value, attended, attended, *d_branch),
+        [jax.ShapeDtypeStruct((2 * width, columns), BF)],
+        grid=(2, 2),
+        in_specs=normed_specs + [value_spec] * 2 + attended_specs + [branch_spec] * 2,
         out_specs=[pl.BlockSpec((tile, columns), lambda p, i: (2 * p + i, 0))],
-        flops=2 * micro * group * width * 4 * columns,
-        moved=2 * width * 4 * columns,
+        flops=2 * micro * group * width * 2 * columns,
+        moved=2 * width * 2 * columns,
+    )[0]
+
+
+def late_grads_kernel(normed0_ref, normed1_ref, d_packed0_ref, d_packed1_ref, out_ref):
+    out_ref[...] = rows_pair(normed0_ref, normed1_ref, d_packed0_ref[...], d_packed1_ref[...])
+
+
+def late_grads(normed, d_packed):
+    micro, group, width = normed.shape
+    columns = d_packed[0].shape[1] // 3
+    tile = width // 2
+    normed_specs = [pl.BlockSpec((None, group, tile), lambda i, p, m=m: (m, 0, i)) for m in range(micro)]
+    return call_kernel(
+        late_grads_kernel,
+        (normed, normed, *d_packed),
+        [jax.ShapeDtypeStruct((2 * width, columns), BF)],
+        grid=(2, 2),
+        in_specs=normed_specs + [pl.BlockSpec((group, columns), lambda i, p: (0, p))] * 2,
+        out_specs=[pl.BlockSpec((tile, columns), lambda i, p: (2 * p + i, 0))],
+        flops=2 * micro * group * width * 2 * columns,
+        moved=2 * width * 2 * columns,
     )[0]
 
 
@@ -775,16 +808,19 @@
     to_packed1 = into_attention(1, d_branch1)
     mix_far0 = scatter_plane_far(mix_near0, zone)
     dots1 = sum_tp(to_packed1[2])
+    d_value = (to_packed0[1], to_packed1[1])
+    early = early_grads(normed, d_value, attended, (d_branch0, d_branch1))
+    early = lax.psum_scatter(early, "dp", scatter_dimension=0, tiled=True)
     end0 = into_packed(0, to_packed0, dots0)
     dots1, *rest = sync(dots1, *end0, *mix_far0)
     end0, mix_far0 = rest[:3], rest[3:]
-    mixed0 = scatter_outer(mix_far0, zone)
+    mixed0 = scatter_pairs_far(*scatter_pairs_near(mix_far0))
     end1 = into_packed(1, to_packed1, dots1)
-    shared = shared_grads(normed, (end0[0], end1[0]), attended, (d_branch0, d_branch1))
-    shared, mixed0, *rest = sync(shared, mixed0, *mix_core1, *end0[1:], *end1[1:])
+    late = late_grads(normed, (end0[0], end1[0]))
+    late, *rest = sync(late, *mix_core1, *end0[1:], *end1[1:])
     mix_core1, d_normed, attn_terms = rest[:4], (rest[4], rest[6]), (rest[5], rest[7])
 
-    shared = lax.psum_scatter(shared, "dp", scatter_dimension=0, tiled=True)
+    late = lax.psum_scatter(late, "dp", scatter_dimension=0, tiled=True)
     mix_near1 = scatter_plane_near(mix_core1)
     d_normed0 = scatter_tp(d_normed[0])
     grad_attn_gain = (attn_terms[0] + attn_terms[1])[0] / attn_gain
@@ -792,17 +828,18 @@
     wide_qk = jnp.pad(grad_qk, ((0, 0), (0, width - columns)))
     grad_router, grad_moe_gain = (one + two for one, two in zip(small0, small1))
     small = jnp.concatenate([grad_attn_gain[None], grad_moe_gain[None], grad_router.T], axis=0)
-    small, d_normed0, d_normed1, *mix_near1 = sync(small, d_normed0, d_normed[1], *mix_near1)
+    small, mixed0, d_normed0, d_normed1, *mix_near1 = sync(small, mixed0, d_normed0, d_normed[1], *mix_near1)
     mix_far1 = scatter_plane_far(mix_near1, zone)
     total = small
     for k in range(1, tp_size):
         total = total + swap_tp(small, k)
     small = jnp.concatenate([total, wide_qk], axis=0)
     small, d_normed0, d_normed1, *mix_far1 = sync(small, d_normed0, d_normed1, *mix_far1)
-    mixed1 = scatter_outer(mix_far1, zone)
+    mixed1 = scatter_pairs_near(mix_far1)
     small = (small + swap_dp(small, 1)).astype(BF)
-    shared, mixed1, small, d_normed0, d_normed1 = sync(shared, mixed1, small, d_normed0, d_normed1)
-    shared = lax.all_gather(shared, "dp", axis=0, tiled=True)
+    early, late, small, d_normed0, d_normed1, *mixed1 = sync(early, late, small, d_normed0, d_normed1, *mixed1)
+    shared = lax.all_gather(jnp.stack([late, early]), "dp", axis=1, tiled=True)
+    mixed1 = scatter_pairs_far(*mixed1)
     small = add_low(small, *[swap_dp(small, 2 * k) for k in range(1, outer)])
     d_normed1 = scatter_tp(d_normed1)
     if whole:
@@ -822,8 +859,8 @@
     shared, small, d_tokens, out, d_gate_up_out, d_down = sync(
         shared, small, jnp.stack(input_grads), out, d_gate_up_out, d_down
     )
-    total_qkv = shared[: 3 * width].reshape(3, width, columns)
-    total_out = shared[3 * width :].reshape(width // columns, columns, columns)
+    total_qkv = shared.reshape(4, width, columns)[:3]
+    total_out = shared[1, width:].reshape(width // columns, columns, columns)
     total_out = jnp.concatenate([piece for piece in total_out], axis=1).astype(F32)
     return (
         out[:, None],

time: 772 us -> 754 us (0.977)
  waiting for transfers between devices: 281 us -> 271 us
    ppermute x62, waiting for transfers between devices: 165 us -> 157 us  [swap_tp(): return lax.ppermute(value, 'tp', [(i, i ^ bits) for i in range(size)])]
    pallas_call x13 -> x14, Pallas kernels: 180 us -> 173 us  [call_kernel(): pl.pallas_call(body, out_shape=outs, grid=grid, in_specs=in_specs or [who...]
    ppermute x33 -> x31, starting transfers between devices: 48.9 us -> 44.3 us  [swap_dp(): return lax.ppermute(value, 'dp', [(i, i ^ bits) for i in range(size)])]
    ppermute x33 -> x31, waiting for transfers between devices: 109 us -> 113 us  [swap_dp(): return lax.ppermute(value, 'dp', [(i, i ^ bits) for i in range(size)])]
  transfers between devices with their start and end apart: 97 -> 96, of which waited for: 44 -> 45; matrix products, arithmetic and copies ran while one was open for 16% -> 16% of each run, Pallas kernels for 23% -> 21%
where the time goes in v4:
time: 754 us; the launch traced here: 742 us
  waiting for transfers between devices  271 us (36%)
  Pallas kernels  173 us (23%)
  starting transfers between devices  117 us (16%)
  other arithmetic  78.1 us (10%)
  local copies, waits for them, and re-layouts  65.5 us (9%)
  matrix products  22 us (3%)
  between operations  15.1 us (2%)
    pallas_call x14, Pallas kernels, call_kernel(): pl.pallas_call(body, out_shape=outs, grid=grid, in_specs=in_specs or [who...  173 us
    ppermute x62, waiting for transfers between devices, swap_tp(): return lax.ppermute(value, 'tp', [(i, i ^ bits) for i in range(size)])  157 us
    ppermute x31, waiting for transfers between devices, swap_dp(): return lax.ppermute(value, 'dp', [(i, i ^ bits) for i in range(size)])  113 us
    ppermute x62, starting transfers between devices, swap_tp(): return lax.ppermute(value, 'tp', [(i, i ^ bits) for i in range(size)])  72.1 us
    ppermute x31, starting transfers between devices, swap_dp(): return lax.ppermute(value, 'dp', [(i, i ^ bits) for i in range(size)])  44.3 us
    convert_element_type x20, other arithmetic, add_pieces(): return [add_low(one, two).astype(BF) for one, two in zip(left, right)]  25.4 us
    unnamed x129, local copies, waits for them, and re-layouts  22.6 us
    dot_general x4, matrix products, mix(): return jnp.dot(ran[1], down, preferred_element_type=F32).astype(BF)  17.4 us
  transfers between devices with their start and end apart: 96, of which 45 were waited for; matrix products, arithmetic and copies ran while one was open for 16% of the time, Pallas kernels for 21%

profile of v4, /device:TPU:0, one launch (start us, length us, event | category | flops | bytes accessed | tf_op | source)
XLA Modules:
  0.0 742.1 jit_solution(8206941367888132822)
XLA Ops:
  7.2 4.0 collective-permute-start.2
  20.5 4.7 fusion.27
  28.2 2.7 pad_maximum_fusion.1.gate_up_ref
  30.9 3.8 collective-permute-done.1
  35.0 2.9 pad_maximum_fusion.3
  37.9 9.4 %shard_map.195 = (bf16[512,2048]{1,0:T(8,128)(2,1)}, f32[512,1536]{1,0:T(8,128)}, f32[512,128]{1,0:T(8,128)}) custom-call(bf16[512,2048]{1,0:T(8,128)(2,1)} %bitcast.170, f32[1,2048]{1,0:T(1,128)} %bitcast.194, bf16[3,2048,512]{2,1,0:T(8,128)(2,1)} %bitcast.159), custom_call_target="tpu_custom_call" | custom-call | flops 402653184 | bytes 786432 | tf_op jit(solution)/shard_map/pallas_call | solution.py:153
  53.8 3.0 collective-permute-done.3
  56.8 3.6 collective-permute-start.8
  62.5 4.0 collective-permute-done.4
  67.3 7.7 %shard_map.196 = (bf16[2,256,1536]{2,1,0:T(8,128)(2,1)}, f32[2,4,256,256]{3,2,1,0:T(8,128)}, bf16[2,256,512]{2,1,0:T(8,128)(2,1)}, bf16[2,256,2048]{2,1,0:T(8,128)(2,1)}) custom-call(f32[2,256,1536]{2,1,0:T(8,128)} %bitcast.148, f32[2,256,128]{2,1,0:T(8,128)} %fusion.7.squares_ref, f32[2,512]{1,0:T(2,128)} %gain_ref.5, ...), custom_call_target="tpu_custom_call" | custom-call | flops 167772160 | bytes 2097152 | tf_op jit(solution)/shard_map/pallas_call | solution.py:153
  84.9 9.1 %collective-permute-done.11 = bf16[2,64,2048]{2,1,0:T(8,128)(2,1)S(1)} collective-permute-done((bf16[2,64,2048]{2,1,0:T(8,128)(2,1)S(1)}, bf16[2,64,2048]{2,1,0:T(8,128)(2,1)S(1)}, u32[]{:S(2)}, u32[]{:S(2)}) %collective-permute-start.11) | collective-permute-done | bytes 524320 | tf_op jit(solution)/shard_map/ppermute | solution.py:32
  94.0 9.3 %collective-permute-done.10 = bf16[2,64,2048]{2,1,0:T(8,128)(2,1)S(1)} collective-permute-done((bf16[2,64,2048]{2,1,0:T(8,128)(2,1)S(1)}, bf16[2,64,2048]{2,1,0:T(8,128)(2,1)S(1)}, u32[]{:S(2)}, u32[]{:S(2)}) %collective-permute-start.10) | collective-permute-done | bytes 524320 | tf_op jit(solution)/shard_map/ppermute | solution.py:32
  105.9 3.8 collective-permute-start.14
  109.7 6.8 collective-permute-start.13
  116.6 15.4 %collective-permute-done.13 = bf16[64,2048]{1,0:T(8,128)(2,1)S(1)} collective-permute-done((bf16[64,2048]{1,0:T(8,128)(2,1)S(1)}, bf16[64,2048]{1,0:T(8,128)(2,1)S(1)}, u32[]{:S(2)}, u32[]{:S(2)}) %collective-permute-start.13) | collective-permute-done | bytes 262176 | tf_op jit(solution)/shard_map/ppermute | solution.py:37
  134.2 3.5 collective-permute-start.19
  138.6 6.8 collective-permute-done.19
  145.4 15.1 %collective-permute-done.18 = bf16[64,2048]{1,0:T(8,128)(2,1)S(1)} collective-permute-done((bf16[64,2048]{1,0:T(8,128)(2,1)S(1)}, bf16[64,2048]{1,0:T(8,128)(2,1)S(1)}, u32[]{:S(2)}, u32[]{:S(2)}) %collective-permute-start.18) | collective-permute-done | bytes 262176 | tf_op jit(solution)/shard_map/ppermute | solution.py:37
  171.0 8.0 %collective-permute-done.22 = bf16[128,2048]{1,0:T(8,128)(2,1)S(1)} collective-permute-done((bf16[128,2048]{1,0:T(8,128)(2,1)S(1)}, bf16[128,2048]{1,0:T(8,128)(2,1)S(1)}, u32[]{:S(2)}, u32[]{:S(2)}) %collective-permute-start.22) | collective-permute-done | bytes 524320 | tf_op jit(solution)/shard_map/ppermute | solution.py:32
  183.3 6.8 collective-permute-done.24
  196.8 18.4 %shard_map.197 = (bf16[1024,2176]{1,0:T(8,128)(2,1)}, bf16[1024,512]{1,0:T(8,128)(2,1)}, bf16[1024,1024]{1,0:T(8,128)(2,1)}) custom-call(s32[1]{0:T(128)} %bitcast.17.ids_ref, bf16[1024,2048]{1,0:T(8,128)(2,1)} %constant_dynamic-update-slice_fusion.moe_ref.refs_0_, bf16[1024,2176]{1,0:T(8,128)(2,1)} %constant_dynamic-update-slice_fusion.4.cot_ref.refs_4_, ...), custom_call_target="tpu_custom_call" | custom-call | flops 1342177280 | bytes 1572864 | tf_op jit(solution)/shard_map/pallas_call | solution.py:153
  215.2 6.3 collective-permute-done.28
  223.8 18.0 %shard_map.198 = (bf16[1024,2176]{1,0:T(8,128)(2,1)}, bf16[1024,512]{1,0:T(8,128)(2,1)}, bf16[1024,1024]{1,0:T(8,128)(2,1)}) custom-call(s32[1]{0:T(128)} %bitcast.17.ids_ref, bf16[1024,2048]{1,0:T(8,128)(2,1)} %collective-permute-done.26.moe_ref.refs_1_, bf16[1024,2176]{1,0:T(8,128)(2,1)} %collective-permute-done.27.cot_ref.refs_5_, ...), custom_call_target="tpu_custom_call" | custom-call | flops 1342177280 | bytes 1572864 | tf_op jit(solution)/shard_map/pallas_call | solution.py:153
  241.7 4.1 collective-permute-done.30
  258.9 4.4 convolution_convert_fusion.3
  263.3 4.4 convolution_convert_fusion.2
  267.7 7.9 %collective-permute-done.34 = bf16[128,2048]{1,0:T(8,128)(2,1)S(1)} collective-permute-done((bf16[128,2048]{1,0:T(8,128)(2,1)S(1)}, bf16[128,2048]{1,0:T(8,128)(2,1)S(1)}, u32[]{:S(2)}, u32[]{:S(2)}) %collective-permute-start.34) | collective-permute-done | bytes 524320 | tf_op jit(solution)/shard_map/ppermute | solution.py:32
  288.9 18.1 %shard_map.199 = (bf16[1024,2176]{1,0:T(8,128)(2,1)}, bf16[1024,512]{1,0:T(8,128)(2,1)}, bf16[1024,1024]{1,0:T(8,128)(2,1)}) custom-call(s32[1]{0:T(128)} %bitcast.17.ids_ref, bf16[1024,2048]{1,0:T(8,128)(2,1)} %constant_dynamic-update-slice_fusion.12.moe_ref.refs_2_, bf16[1024,2176]{1,0:T(8,128)(2,1)} %copy-done.4, bf16[2048,128]{1,0:T(8,128)(2,1)} %pad.17.router_ref, ...), custom_call_target="tpu_custom_call" | custom-call | flops 1342177280 | bytes 1572864 | tf_op jit(solution)/shard_map/pallas_call | solution.py:153
  307.0 6.6 collective-permute-done.39
  319.8 17.9 %shard_map.200 = (bf16[1024,2176]{1,0:T(8,128)(2,1)}, bf16[1024,512]{1,0:T(8,128)(2,1)}, bf16[1024,1024]{1,0:T(8,128)(2,1)}) custom-call(s32[1]{0:T(128)} %bitcast.17.ids_ref, bf16[1024,2048]{1,0:T(8,128)(2,1)} %collective-permute-done.37.moe_ref.refs_3_, bf16[1024,2176]{1,0:T(8,128)(2,1)} %collective-permute-done.38.cot_ref.refs_7_, ...), custom_call_target="tpu_custom_call" | custom-call | flops 1342177280 | bytes 1572864 | tf_op jit(solution)/shard_map/pallas_call | solution.py:153
  340.1 2.9 collective-permute-start.43
  343.0 4.3 convolution_convert_fusion.1
  347.3 4.4 convolution_convert_fusion
  351.7 11.5 %collective-permute-done.44 = bf16[64,2176]{1,0:T(8,128)(2,1)S(1)} collective-permute-done((bf16[64,2176]{1,0:T(8,128)(2,1)S(1)}, bf16[64,2176]{1,0:T(8,128)(2,1)S(1)}, u32[]{:S(2)}, u32[]{:S(2)}) %collective-permute-start.44) | collective-permute-done | bytes 278560 | tf_op jit(solution)/shard_map/ppermute | solution.py:37
  367.1 2.7 add_convert_fusion
  376.0 21.4 %collective-permute-done.48 = bf16[256,2176]{1,0:T(8,128)(2,1)S(1)} collective-permute-done((bf16[256,2176]{1,0:T(8,128)(2,1)}, bf16[256,2176]{1,0:T(8,128)(2,1)S(1)}, u32[]{:S(2)}, u32[]{:S(2)}) %collective-permute-start.48) | collective-permute-done | bytes 1114144 | tf_op jit(solution)/shard_map/ppermute | solution.py:32
  399.6 4.1 add_convert_fusion.8
  409.7 5.8 collective-permute-done.53
  415.4 13.8 %collective-permute-done.52 = bf16[64,2048]{1,0:T(8,128)(2,1)S(1)} collective-permute-done((bf16[64,2048]{1,0:T(8,128)(2,1)S(1)}, bf16[64,2048]{1,0:T(8,128)(2,1)S(1)}, u32[]{:S(2)}, u32[]{:S(2)}) %collective-permute-start.52) | collective-permute-done | bytes 262176 | tf_op jit(solution)/shard_map/ppermute | solution.py:32
  439.3 7.1 shard_map.201
  446.4 10.3 %collective-permute-done.57 = bf16[64,2176]{1,0:T(8,128)(2,1)} collective-permute-done((bf16[64,2176]{1,0:T(8,128)(2,1)}, bf16[64,2176]{1,0:T(8,128)(2,1)}, u32[]{:S(2)}, u32[]{:S(2)}) %collective-permute-start.57) | collective-permute-done | bytes 278560 | tf_op jit(solution)/shard_map/ppermute | solution.py:37
  471.4 3.1 collective-permute-done.65
  475.6 6.3 collective-permute-done.64
  486.0 7.0 shard_map.202
  493.0 7.3 shard_map.203
  506.4 6.9 shard_map.204
  514.1 2.9 collective-permute-done.70
  518.7 7.0 shard_map.205
  525.7 6.5 shard_map.206
  543.4 14.5 %collective-permute-done.72 = bf16[128,2048]{1,0:T(8,128)(2,1)S(1)} collective-permute-done((bf16[128,2048]{1,0:T(8,128)(2,1)S(1)}, bf16[128,2048]{1,0:T(8,128)(2,1)S(1)}, u32[]{:S(2)}, u32[]{:S(2)}) %collective-permute-start.72) | collective-permute-done | bytes 524320 | tf_op jit(solution)/shard_map/ppermute | solution.py:37
  562.7 5.2 collective-permute-done.73
  568.7 3.3 collective-permute-done.77
  572.4 8.9 %collective-permute-done.78 = bf16[256,2048]{1,0:T(8,128)(2,1)S(1)} collective-permute-done((bf16[256,2048]{1,0:T(8,128)(2,1)S(1)}, bf16[256,2048]{1,0:T(8,128)(2,1)S(1)}, u32[]{:S(2)}, u32[]{:S(2)}) %collective-permute-start.78) | collective-permute-done | bytes 1048608 | tf_op jit(solution)/shard_map/ppermute | solution.py:32
  590.5 2.8 collective-permute-done.80
  594.9 7.5 %collective-permute-done.82 = bf16[128,2048]{1,0:T(8,128)(2,1)S(1)} collective-permute-done((bf16[128,2048]{1,0:T(8,128)(2,1)S(1)}, bf16[128,2048]{1,0:T(8,128)(2,1)S(1)}, u32[]{:S(2)}, u32[]{:S(2)}) %collective-permute-start.82) | collective-permute-done | bytes 524320 | tf_op jit(solution)/shard_map/ppermute | solution.py:32
  604.3 15.0 %collective-permute-done.85 = bf16[128,2048]{1,0:T(8,128)(2,1)S(1)} collective-permute-done((bf16[128,2048]{1,0:T(8,128)(2,1)S(1)}, bf16[128,2048]{1,0:T(8,128)(2,1)S(1)}, u32[]{:S(2)}, u32[]{:S(2)}) %collective-permute-start.85) | collective-permute-done | bytes 524320 | tf_op jit(solution)/shard_map/ppermute | solution.py:37
  622.6 24.5 %shard_map.207 = f32[2048,1024]{1,0:T(8,128)} custom-call(bf16[1024,2048]{1,0:T(8,128)(2,1)} %constant_dynamic-update-slice_fusion.moe_ref.refs_0_, bf16[1024,2048]{1,0:T(8,128)(2,1)} %collective-permute-done.26.moe_ref.refs_1_, bf16[1024,2048]{1,0:T(8,128)(2,1)} %constant_dynamic-update-slice_fusion.12.moe_ref.refs_2_, ...), custom_call_target="tpu_custom_call" | custom-call | flops 2147483648 | bytes 4194304 | tf_op jit(solution)/shard_map/pallas_call | solution.py:153
  647.1 11.7 %reshape.430 = f32[2048,2,2,256]{3,2,1,0:T(2,128)} reshape(f32[2048,1024]{1,0:T(8,128)} %shard_map.207) | data formatting | bytes 16777216 | tf_op jit(solution)/shard_map/reshape | solution.py:857
  658.9 17.2 %shard_map.208 = f32[512,2048]{1,0:T(8,128)} custom-call(bf16[1024,512]{1,0:T(8,128)(2,1)} %get-tuple-element.474.refs_0_, bf16[1024,512]{1,0:T(8,128)(2,1)} %get-tuple-element.475.refs_1_, bf16[1024,512]{1,0:T(8,128)(2,1)} %get-tuple-element.476.refs_2_, bf16[1024,512]{1,0:T(8,128)(2,1)} %get-tuple-element.477.refs_3_, ...), custom_call_target="tpu_custom_call" | custom-call | flops 1073741824 | bytes 3145728 | tf_op jit(solution)/shard_map/pallas_call | solution.py:153
  676.0 5.5 slice_bitcast_fusion.1
  681.6 4.8 pad_maximum_fusion
  697.4 10.5 %collective-permute-done.87 = bf16[20,2048]{1,0:T(8,128)(2,1)S(1)} collective-permute-done((bf16[20,2048]{1,0:T(8,128)(2,1)S(1)}, bf16[20,2048]{1,0:T(8,128)(2,1)S(1)}, u32[]{:S(2)}, u32[]{:S(2)}) %collective-permute-start.87) | collective-permute-done | bytes 81952 | tf_op jit(solution)/shard_map/ppermute | solution.py:37
  712.0 5.6 collective-permute-done.92
  723.4 9.4 %convert_bitcast_fusion = f32[2048,3,512]{2,0,1:T(8,128)} fusion(bf16[4,2048,512]{2,1,0:T(8,128)(2,1)} %bitcast.171), kind=kLoop, calls=%fused_computation | loop fusion | flops 3145728 | bytes 18874368 | tf_op jit(solution)/shard_map/transpose | solution.py:869
  (415 shorter events, 208.6 us)
Async XLA Ops:
  7.2 613.1 %reduce-scatter.3.cloned.1.call-start = ((), (), s32[]{:S(2)}) async-start(), calls=%async_computation.2 | async-start | bytes 4718592 | tf_op jit(solution)/shard_map/reduce_scatter | solution.py:813
  7.2 23.7 %collective-permute-start.2 = (bf16[2,64,2048]{2,1,0:T(8,128)(2,1)}, bf16[2,64,2048]{2,1,0:T(8,128)(2,1)}, u32[]{:S(2)}, u32[]{:S(2)}) collective-permute-start(bf16[2,64,2048]{2,1,0:T(8,128)(2,1)} %bitcast.176), channel_id=1, source_target_pairs={{0,24},{8,16},{16,8},{24,0},{1,25},{9,17},{17,9},{25,1},{2,26},{10... | collective-permute-start | bytes 1572872 | tf_op jit(solution)/shard_map/ppermute | solution.py:32
  11.2 23.5 %collective-permute-start.1 = (bf16[2,64,2048]{2,1,0:T(8,128)(2,1)}, bf16[2,64,2048]{2,1,0:T(8,128)(2,1)}, u32[]{:S(2)}, u32[]{:S(2)}) collective-permute-start(bf16[2,64,2048]{2,1,0:T(8,128)(2,1)} %bitcast.177), channel_id=1, source_target_pairs={{0,16},{8,24},{16,0},{24,8},{1,17},{9,25},{17,1},{25,9},{2,18},{10... | collective-permute-start | bytes 1572872 | tf_op jit(solution)/shard_map/ppermute | solution.py:32
  11.7 23.3 %collective-permute-start = (bf16[2,64,2048]{2,1,0:T(8,128)(2,1)}, bf16[2,64,2048]{2,1,0:T(8,128)(2,1)}, u32[]{:S(2)}, u32[]{:S(2)}) collective-permute-start(bf16[2,64,2048]{2,1,0:T(8,128)(2,1)} %bitcast.178), channel_id=1, source_target_pairs={{0,8},{8,0},{16,24},{24,16},{1,9},{9,1},{17,25},{25,17},{2,10},{10... | collective-permute-start | bytes 1572872 | tf_op jit(solution)/shard_map/ppermute | solution.py:32
  15.4 59.6 %collective-permute-start.6 = (bf16[2,64,2176]{2,1,0:T(8,128)(2,1)S(1)}, bf16[2,64,2176]{2,1,0:T(8,128)(2,1)}, u32[]{:S(2)}, u32[]{:S(2)}) collective-permute-start(bf16[2,64,2176]{2,1,0:T(8,128)(2,1)S(1)} %pad_maximum_fusion.9), channel_id=1, source_target_pairs={{0,2},{1,3},{2,0},{3,1},{4,6},{5,7},{6,4},{7,5},{8,10},{9,11},{10,... | collective-permute-start | bytes 1671176 | tf_op jit(solution)/shard_map/ppermute | solution.py:37
  17.5 57.6 %collective-permute-start.7 = (bf16[2,64,2176]{2,1,0:T(8,128)(2,1)S(1)}, bf16[2,64,2176]{2,1,0:T(8,128)(2,1)}, u32[]{:S(2)}, u32[]{:S(2)}) collective-permute-start(bf16[2,64,2176]{2,1,0:T(8,128)(2,1)S(1)} %pad_maximum_fusion.9), channel_id=1, source_target_pairs={{0,4},{1,5},{2,6},{3,7},{4,0},{5,1},{6,2},{7,3},{8,12},{9,13},{10,... | collective-permute-start | bytes 1671176 | tf_op jit(solution)/shard_map/ppermute | solution.py:37
  56.8 18.2 %collective-permute-start.8 = (bf16[2,64,2176]{2,1,0:T(8,128)(2,1)S(1)}, bf16[2,64,2176]{2,1,0:T(8,128)(2,1)S(1)}, u32[]{:S(2)}, u32[]{:S(2)}) collective-permute-start(bf16[2,64,2176]{2,1,0:T(8,128)(2,1)S(1)} %pad_maximum_fusion.9), channel_id=1, source_target_pairs={{0,6},{1,7},{2,4},{3,5},{4,2},{5,3},{6,0},{7,1},{8,14},{9,15},{10,... | collective-permute-start | bytes 1671176 | tf_op jit(solution)/shard_map/ppermute | solution.py:37
  79.7 23.7 %collective-permute-start.10 = (bf16[2,64,2048]{2,1,0:T(8,128)(2,1)S(1)}, bf16[2,64,2048]{2,1,0:T(8,128)(2,1)S(1)}, u32[]{:S(2)}, u32[]{:S(2)}) collective-permute-start(bf16[2,64,2048]{2,1,0:T(8,128)(2,1)S(1)} %get-tuple-element.260), channel_id=1, source_target_pairs={{0,16},{8,24},{16,0},{24,8},{1,17},{9,25},{17,1},{25,9},{2,18},{10... | collective-permute-start | bytes 1572872 | tf_op jit(solution)/shard_map/ppermute | solution.py:32
  80.0 24.1 %collective-permute-start.9 = (bf16[2,64,2048]{2,1,0:T(8,128)(2,1)S(1)}, bf16[2,64,2048]{2,1,0:T(8,128)(2,1)S(1)}, u32[]{:S(2)}, u32[]{:S(2)}) collective-permute-start(bf16[2,64,2048]{2,1,0:T(8,128)(2,1)S(1)} %get-tuple-element.259), channel_id=1, source_target_pairs={{0,8},{8,0},{16,24},{24,16},{1,9},{9,1},{17,25},{25,17},{2,10},{10... | collective-permute-start | bytes 1572872 | tf_op jit(solution)/shard_map/ppermute | solution.py:32
  82.9 49.3 %collective-permute-start.15 = (bf16[256,2176]{1,0:T(8,128)(2,1)S(1)}, bf16[256,2176]{1,0:T(8,128)(2,1)S(1)}, u32[]{:S(2)}, u32[]{:S(2)}) collective-permute-start(bf16[256,2176]{1,0:T(8,128)(2,1)S(1)} %get-tuple-element.274), channel_id=1, source_target_pairs={{0,8},{8,0},{16,24},{24,16},{1,9},{9,1},{17,25},{25,17},{2,10},{10... | collective-permute-start | bytes 3342344 | tf_op jit(solution)/shard_map/ppermute | solution.py:32
  83.2 49.0 %collective-permute-start.16 = (bf16[256,2176]{1,0:T(8,128)(2,1)S(1)}, bf16[256,2176]{1,0:T(8,128)(2,1)S(1)}, u32[]{:S(2)}, u32[]{:S(2)}) collective-permute-start(bf16[256,2176]{1,0:T(8,128)(2,1)S(1)} %get-tuple-element.274), channel_id=1, source_target_pairs={{0,16},{8,24},{16,0},{24,8},{1,17},{9,25},{17,1},{25,9},{2,18},{10... | collective-permute-start | bytes 3342344 | tf_op jit(solution)/shard_map/ppermute | solution.py:32
  109.7 22.3 %collective-permute-start.13 = (bf16[64,2048]{1,0:T(8,128)(2,1)S(1)}, bf16[64,2048]{1,0:T(8,128)(2,1)S(1)}, u32[]{:S(2)}, u32[]{:S(2)}) collective-permute-start(bf16[64,2048]{1,0:T(8,128)(2,1)S(1)} %get-tuple-element.620), channel_id=1, source_target_pairs={{0,4},{1,5},{2,6},{3,7},{4,0},{5,1},{6,2},{7,3},{8,12},{9,13},{10,... | collective-permute-start | bytes 786440 | tf_op jit(solution)/shard_map/ppermute | solution.py:37
  132.2 29.4 %collective-permute-start.20 = (bf16[256,2048]{1,0:T(8,128)(2,1)S(1)}, bf16[256,2048]{1,0:T(8,128)(2,1)S(1)}, u32[]{:S(2)}, u32[]{:S(2)}) collective-permute-start(bf16[256,2048]{1,0:T(8,128)(2,1)S(1)} %pad_maximum_fusion.4), channel_id=1, source_target_pairs={{0,8},{8,0},{16,24},{24,16},{1,9},{9,1},{17,25},{25,17},{2,10},{10... | collective-permute-start | bytes 3145736 | tf_op jit(solution)/shard_map/ppermute | solution.py:32
  133.6 28.1 %collective-permute-start.21 = (bf16[256,2048]{1,0:T(8,128)(2,1)S(1)}, bf16[256,2048]{1,0:T(8,128)(2,1)S(1)}, u32[]{:S(2)}, u32[]{:S(2)}) collective-permute-start(bf16[256,2048]{1,0:T(8,128)(2,1)S(1)} %pad_maximum_fusion.4), channel_id=1, source_target_pairs={{0,16},{8,24},{16,0},{24,8},{1,17},{9,25},{17,1},{25,9},{2,18},{10... | collective-permute-start | bytes 3145736 | tf_op jit(solution)/shard_map/ppermute | solution.py:32
  137.8 22.8 %collective-permute-start.18 = (bf16[64,2048]{1,0:T(8,128)(2,1)S(1)}, bf16[64,2048]{1,0:T(8,128)(2,1)S(1)}, u32[]{:S(2)}, u32[]{:S(2)}) collective-permute-start(bf16[64,2048]{1,0:T(8,128)(2,1)S(1)} %get-tuple-element.264), channel_id=1, source_target_pairs={{0,4},{1,5},{2,6},{3,7},{4,0},{5,1},{6,2},{7,3},{8,12},{9,13},{10,... | collective-permute-start | bytes 786440 | tf_op jit(solution)/shard_map/ppermute | solution.py:37
  138.5 22.0 %collective-permute-start.17 = (bf16[64,2048]{1,0:T(8,128)(2,1)S(1)}, bf16[64,2048]{1,0:T(8,128)(2,1)S(1)}, u32[]{:S(2)}, u32[]{:S(2)}) collective-permute-start(bf16[64,2048]{1,0:T(8,128)(2,1)S(1)} %get-tuple-element.264), channel_id=1, source_target_pairs={{0,2},{1,3},{2,0},{3,1},{4,6},{5,7},{6,4},{7,5},{8,10},{9,11},{10,... | collective-permute-start | bytes 786440 | tf_op jit(solution)/shard_map/ppermute | solution.py:37
  164.6 17.8 %collective-permute-start.23 = (bf16[128,2048]{1,0:T(8,128)(2,1)S(1)}, bf16[128,2048]{1,0:T(8,128)(2,1)S(1)}, u32[]{:S(2)}, u32[]{:S(2)}) collective-permute-start(bf16[128,2048]{1,0:T(8,128)(2,1)S(1)} %get-tuple-element.273), channel_id=1, source_target_pairs={{0,8},{8,0},{16,24},{24,16},{1,9},{9,1},{17,25},{25,17},{2,10},{10... | collective-permute-start | bytes 1572872 | tf_op jit(solution)/shard_map/ppermute | solution.py:32
  169.0 21.0 %collective-permute-start.24 = (bf16[128,2176]{1,0:T(8,128)(2,1)S(1)}, bf16[128,2176]{1,0:T(8,128)(2,1)S(1)}, u32[]{:S(2)}, u32[]{:S(2)}) collective-permute-start(bf16[128,2176]{1,0:T(8,128)(2,1)S(1)} %get-tuple-element.277), channel_id=1, source_target_pairs={{0,16},{8,24},{16,0},{24,8},{1,17},{9,25},{17,1},{25,9},{2,18},{10... | collective-permute-start | bytes 1671176 | tf_op jit(solution)/shard_map/ppermute | solution.py:32
  169.4 24.0 %collective-permute-start.25 = (bf16[128,2176]{1,0:T(8,128)(2,1)S(1)}, bf16[128,2176]{1,0:T(8,128)(2,1)S(1)}, u32[]{:S(2)}, u32[]{:S(2)}) collective-permute-start(bf16[128,2176]{1,0:T(8,128)(2,1)S(1)} %get-tuple-element.278), channel_id=1, source_target_pairs={{0,8},{8,0},{16,24},{24,16},{1,9},{9,1},{17,25},{25,17},{2,10},{10... | collective-permute-start | bytes 1671176 | tf_op jit(solution)/shard_map/ppermute | solution.py:32
  194.3 27.4 %collective-permute-start.27 = (bf16[1024,2176]{1,0:T(8,128)(2,1)}, bf16[1024,2176]{1,0:T(8,128)(2,1)}, u32[]{:S(2)}, u32[]{:S(2)}) collective-permute-start(bf16[1024,2176]{1,0:T(8,128)(2,1)} %constant_dynamic-update-slice_fusion.4.cot_ref.refs_4_), channel_id=1, source_target_pairs={{0,1},{1,0},{2,3},{3,2},{4,5},{5,4},{6,7},{7,6},{8,9},{9,8},{10,11... | collective-permute-start | bytes 13369352 | tf_op jit(solution)/shard_map/ppermute | solution.py:37
  194.3 27.4 %collective-permute-start.26 = (bf16[1024,2048]{1,0:T(8,128)(2,1)}, bf16[1024,2048]{1,0:T(8,128)(2,1)}, u32[]{:S(2)}, u32[]{:S(2)}) collective-permute-start(bf16[1024,2048]{1,0:T(8,128)(2,1)} %constant_dynamic-update-slice_fusion.moe_ref.refs_0_), channel_id=1, source_target_pairs={{0,1},{1,0},{2,3},{3,2},{4,5},{5,4},{6,7},{7,6},{8,9},{9,8},{10,11... | collective-permute-start | bytes 12582920 | tf_op jit(solution)/shard_map/ppermute | solution.py:37
  194.8 26.8 %collective-permute-start.28 = (bf16[256,2176]{1,0:T(8,128)(2,1)}, bf16[256,2176]{1,0:T(8,128)(2,1)}, u32[]{:S(2)}, u32[]{:S(2)}) collective-permute-start(bf16[256,2176]{1,0:T(8,128)(2,1)} %get-tuple-element.303), channel_id=1, source_target_pairs={{0,8},{8,0},{16,24},{24,16},{1,9},{9,1},{17,25},{25,17},{2,10},{10... | collective-permute-start | bytes 3342344 | tf_op jit(solution)/shard_map/ppermute | solution.py:32
  195.2 26.5 %collective-permute-start.29 = (bf16[256,2176]{1,0:T(8,128)(2,1)}, bf16[256,2176]{1,0:T(8,128)(2,1)}, u32[]{:S(2)}, u32[]{:S(2)}) collective-permute-start(bf16[256,2176]{1,0:T(8,128)(2,1)} %get-tuple-element.303), channel_id=1, source_target_pairs={{0,16},{8,24},{16,0},{24,8},{1,17},{9,25},{17,1},{25,9},{2,18},{10... | collective-permute-start | bytes 3342344 | tf_op jit(solution)/shard_map/ppermute | solution.py:32
  221.7 24.2 %collective-permute-start.30 = (bf16[256,2048]{1,0:T(8,128)(2,1)S(1)}, bf16[256,2048]{1,0:T(8,128)(2,1)S(1)}, u32[]{:S(2)}, u32[]{:S(2)}) collective-permute-start(bf16[256,2048]{1,0:T(8,128)(2,1)S(1)} %copy-done.16), channel_id=1, source_target_pairs={{0,8},{8,0},{16,24},{24,16},{1,9},{9,1},{17,25},{25,17},{2,10},{10... | collective-permute-start | bytes 3145736 | tf_op jit(solution)/shard_map/ppermute | solution.py:32
  223.4 23.6 %collective-permute-start.31 = (bf16[256,2048]{1,0:T(8,128)(2,1)S(1)}, bf16[256,2048]{1,0:T(8,128)(2,1)S(1)}, u32[]{:S(2)}, u32[]{:S(2)}) collective-permute-start(bf16[256,2048]{1,0:T(8,128)(2,1)S(1)} %copy-done.16), channel_id=1, source_target_pairs={{0,16},{8,24},{16,0},{24,8},{1,17},{9,25},{17,1},{25,9},{2,18},{10... | collective-permute-start | bytes 3145736 | tf_op jit(solution)/shard_map/ppermute | solution.py:32
  252.1 27.6 %collective-permute-start.32 = (bf16[128,2176]{1,0:T(8,128)(2,1)S(1)}, bf16[128,2176]{1,0:T(8,128)(2,1)S(1)}, u32[]{:S(2)}, u32[]{:S(2)}) collective-permute-start(bf16[128,2176]{1,0:T(8,128)(2,1)S(1)} %get-tuple-element.306), channel_id=1, source_target_pairs={{0,16},{8,24},{16,0},{24,8},{1,17},{9,25},{17,1},{25,9},{2,18},{10... | collective-permute-start | bytes 1671176 | tf_op jit(solution)/shard_map/ppermute | solution.py:32
  252.8 30.3 %collective-permute-start.33 = (bf16[128,2176]{1,0:T(8,128)(2,1)S(1)}, bf16[128,2176]{1,0:T(8,128)(2,1)S(1)}, u32[]{:S(2)}, u32[]{:S(2)}) collective-permute-start(bf16[128,2176]{1,0:T(8,128)(2,1)S(1)} %get-tuple-element.307), channel_id=1, source_target_pairs={{0,8},{8,0},{16,24},{24,16},{1,9},{9,1},{17,25},{25,17},{2,10},{10... | collective-permute-start | bytes 1671176 | tf_op jit(solution)/shard_map/ppermute | solution.py:32
  256.9 18.7 %collective-permute-start.34 = (bf16[128,2048]{1,0:T(8,128)(2,1)S(1)}, bf16[128,2048]{1,0:T(8,128)(2,1)S(1)}, u32[]{:S(2)}, u32[]{:S(2)}) collective-permute-start(bf16[128,2048]{1,0:T(8,128)(2,1)S(1)} %get-tuple-element.311), channel_id=1, source_target_pairs={{0,16},{8,24},{16,0},{24,8},{1,17},{9,25},{17,1},{25,9},{2,18},{10... | collective-permute-start | bytes 1572872 | tf_op jit(solution)/shard_map/ppermute | solution.py:32
  257.5 21.4 %collective-permute-start.35 = (bf16[128,2048]{1,0:T(8,128)(2,1)S(1)}, bf16[128,2048]{1,0:T(8,128)(2,1)S(1)}, u32[]{:S(2)}, u32[]{:S(2)}) collective-permute-start(bf16[128,2048]{1,0:T(8,128)(2,1)S(1)} %get-tuple-element.312), channel_id=1, source_target_pairs={{0,8},{8,0},{16,24},{24,16},{1,9},{9,1},{17,25},{25,17},{2,10},{10... | collective-permute-start | bytes 1572872 | tf_op jit(solution)/shard_map/ppermute | solution.py:32
  258.9 24.3 %collective-permute-start.36 = (bf16[1024,2176]{1,0:T(8,128)(2,1)S(1)}, bf16[1024,2176]{1,0:T(8,128)(2,1)S(1)}, u32[]{:S(2)}, u32[]{:S(2)}) collective-permute-start(bf16[1024,2176]{1,0:T(8,128)(2,1)S(1)} %copy-done.48), channel_id=1, source_target_pairs={{0,1},{1,0},{2,3},{3,2},{4,5},{5,4},{6,7},{7,6},{8,9},{9,8},{10,11... | collective-permute-start | bytes 13369352 | tf_op jit(solution)/shard_map/ppermute | solution.py:37
  286.3 31.3 %collective-permute-start.38 = (bf16[1024,2176]{1,0:T(8,128)(2,1)S(1)}, bf16[1024,2176]{1,0:T(8,128)(2,1)}, u32[]{:S(2)}, u32[]{:S(2)}) collective-permute-start(bf16[1024,2176]{1,0:T(8,128)(2,1)S(1)} %constant_dynamic-update-slice_fusion.8.cot_ref.refs_6_), channel_id=1, source_target_pairs={{0,1},{1,0},{2,3},{3,2},{4,5},{5,4},{6,7},{7,6},{8,9},{9,8},{10,11... | collective-permute-start | bytes 13369352 | tf_op jit(solution)/shard_map/ppermute | solution.py:37
  286.3 31.3 %collective-permute-start.37 = (bf16[1024,2048]{1,0:T(8,128)(2,1)}, bf16[1024,2048]{1,0:T(8,128)(2,1)}, u32[]{:S(2)}, u32[]{:S(2)}) collective-permute-start(bf16[1024,2048]{1,0:T(8,128)(2,1)} %constant_dynamic-update-slice_fusion.12.moe_ref.refs_2_), channel_id=1, source_target_pairs={{0,1},{1,0},{2,3},{3,2},{4,5},{5,4},{6,7},{7,6},{8,9},{9,8},{10,11... | collective-permute-start | bytes 12582920 | tf_op jit(solution)/shard_map/ppermute | solution.py:37
  286.8 26.8 %collective-permute-start.39 = (bf16[256,2176]{1,0:T(8,128)(2,1)}, bf16[256,2176]{1,0:T(8,128)(2,1)}, u32[]{:S(2)}, u32[]{:S(2)}) collective-permute-start(bf16[256,2176]{1,0:T(8,128)(2,1)} %get-tuple-element.322), channel_id=1, source_target_pairs={{0,8},{8,0},{16,24},{24,16},{1,9},{9,1},{17,25},{25,17},{2,10},{10... | collective-permute-start | bytes 3342344 | tf_op jit(solution)/shard_map/ppermute | solution.py:32
  287.7 28.4 %collective-permute-start.40 = (bf16[256,2176]{1,0:T(8,128)(2,1)}, bf16[256,2176]{1,0:T(8,128)(2,1)}, u32[]{:S(2)}, u32[]{:S(2)}) collective-permute-start(bf16[256,2176]{1,0:T(8,128)(2,1)} %get-tuple-element.324), channel_id=1, source_target_pairs={{0,16},{8,24},{16,0},{24,8},{1,17},{9,25},{17,1},{25,9},{2,18},{10... | collective-permute-start | bytes 3342344 | tf_op jit(solution)/shard_map/ppermute | solution.py:32
  317.7 20.1 %collective-permute-start.41 = (bf16[128,2176]{1,0:T(8,128)(2,1)}, bf16[128,2176]{1,0:T(8,128)(2,1)S(1)}, u32[]{:S(2)}, u32[]{:S(2)}) collective-permute-start(bf16[128,2176]{1,0:T(8,128)(2,1)} %get-tuple-element.329), channel_id=1, source_target_pairs={{0,16},{8,24},{16,0},{24,8},{1,17},{9,25},{17,1},{25,9},{2,18},{10... | collective-permute-start | bytes 1671176 | tf_op jit(solution)/shard_map/ppermute | solution.py:32
  318.6 19.2 %collective-permute-start.42 = (bf16[128,2176]{1,0:T(8,128)(2,1)S(1)}, bf16[128,2176]{1,0:T(8,128)(2,1)S(1)}, u32[]{:S(2)}, u32[]{:S(2)}) collective-permute-start(bf16[128,2176]{1,0:T(8,128)(2,1)S(1)} %get-tuple-element.331), channel_id=1, source_target_pairs={{0,8},{8,0},{16,24},{24,16},{1,9},{9,1},{17,25},{25,17},{2,10},{10... | collective-permute-start | bytes 1671176 | tf_op jit(solution)/shard_map/ppermute | solution.py:32
  338.0 25.4 %collective-permute-start.47 = (bf16[1024,2048]{1,0:T(8,128)(2,1)}, bf16[1024,2048]{1,0:T(8,128)(2,1)S(1)}, u32[]{:S(2)}, u32[]{:S(2)}) collective-permute-start(bf16[1024,2048]{1,0:T(8,128)(2,1)} %convolution_convert_fusion.2), channel_id=1, source_target_pairs={{0,1},{1,0},{2,3},{3,2},{4,5},{5,4},{6,7},{7,6},{8,9},{9,8},{10,11... | collective-permute-start | bytes 12582920 | tf_op jit(solution)/shard_map/ppermute | solution.py:37
  338.1 27.9 %collective-permute-start.46 = (bf16[1024,2176]{1,0:T(8,128)(2,1)}, bf16[1024,2176]{1,0:T(8,128)(2,1)S(1)}, u32[]{:S(2)}, u32[]{:S(2)}) collective-permute-start(bf16[1024,2176]{1,0:T(8,128)(2,1)} %get-tuple-element.347), channel_id=1, source_target_pairs={{0,1},{1,0},{2,3},{3,2},{4,5},{5,4},{6,7},{7,6},{8,9},{9,8},{10,11... | collective-permute-start | bytes 13369352 | tf_op jit(solution)/shard_map/ppermute | solution.py:37
  340.1 23.2 %collective-permute-start.44 = (bf16[64,2176]{1,0:T(8,128)(2,1)S(1)}, bf16[64,2176]{1,0:T(8,128)(2,1)S(1)}, u32[]{:S(2)}, u32[]{:S(2)}) collective-permute-start(bf16[64,2176]{1,0:T(8,128)(2,1)S(1)} %get-tuple-element.344), channel_id=1, source_target_pairs={{0,4},{1,5},{2,6},{3,7},{4,0},{5,1},{6,2},{7,3},{8,12},{9,13},{10,... | collective-permute-start | bytes 835592 | tf_op jit(solution)/shard_map/ppermute | solution.py:37
  340.1 23.2 %collective-permute-start.43 = (bf16[64,2176]{1,0:T(8,128)(2,1)S(1)}, bf16[64,2176]{1,0:T(8,128)(2,1)S(1)}, u32[]{:S(2)}, u32[]{:S(2)}) collective-permute-start(bf16[64,2176]{1,0:T(8,128)(2,1)S(1)} %get-tuple-element.343), channel_id=1, source_target_pairs={{0,2},{1,3},{2,0},{3,1},{4,6},{5,7},{6,4},{7,5},{8,10},{9,11},{10,... | collective-permute-start | bytes 835592 | tf_op jit(solution)/shard_map/ppermute | solution.py:37
  369.8 29.0 %collective-permute-start.50 = (bf16[1024,2048]{1,0:T(8,128)(2,1)}, bf16[1024,2048]{1,0:T(8,128)(2,1)}, u32[]{:S(2)}, u32[]{:S(2)}) collective-permute-start(bf16[1024,2048]{1,0:T(8,128)(2,1)} %convolution_convert_fusion), channel_id=1, source_target_pairs={{0,1},{1,0},{2,3},{3,2},{4,5},{5,4},{6,7},{7,6},{8,9},{9,8},{10,11... | collective-permute-start | bytes 12582920 | tf_op jit(solution)/shard_map/ppermute | solution.py:37
  370.2 27.2 %collective-permute-start.48 = (bf16[256,2176]{1,0:T(8,128)(2,1)}, bf16[256,2176]{1,0:T(8,128)(2,1)S(1)}, u32[]{:S(2)}, u32[]{:S(2)}) collective-permute-start(bf16[256,2176]{1,0:T(8,128)(2,1)} %get-tuple-element.356), channel_id=1, source_target_pairs={{0,8},{8,0},{16,24},{24,16},{1,9},{9,1},{17,25},{25,17},{2,10},{10... | collective-permute-start | bytes 3342344 | tf_op jit(solution)/shard_map/ppermute | solution.py:32
  371.6 27.0 %collective-permute-start.49 = (bf16[256,2176]{1,0:T(8,128)(2,1)}, bf16[256,2176]{1,0:T(8,128)(2,1)S(1)}, u32[]{:S(2)}, u32[]{:S(2)}) collective-permute-start(bf16[256,2176]{1,0:T(8,128)(2,1)} %get-tuple-element.358), channel_id=1, source_target_pairs={{0,16},{8,24},{16,0},{24,8},{1,17},{9,25},{17,1},{25,9},{2,18},{10... | collective-permute-start | bytes 3342344 | tf_op jit(solution)/shard_map/ppermute | solution.py:32
  403.8 26.5 %collective-permute-start.54 = (bf16[128,2176]{1,0:T(8,128)(2,1)S(1)}, bf16[128,2176]{1,0:T(8,128)(2,1)S(1)}, u32[]{:S(2)}, u32[]{:S(2)}) collective-permute-start(bf16[128,2176]{1,0:T(8,128)(2,1)S(1)} %get-tuple-element.367), channel_id=1, source_target_pairs={{0,16},{8,24},{16,0},{24,8},{1,17},{9,25},{17,1},{25,9},{2,18},{10... | collective-permute-start | bytes 1671176 | tf_op jit(solution)/shard_map/ppermute | solution.py:32
  406.5 22.8 %collective-permute-start.52 = (bf16[64,2048]{1,0:T(8,128)(2,1)S(1)}, bf16[64,2048]{1,0:T(8,128)(2,1)S(1)}, u32[]{:S(2)}, u32[]{:S(2)}) collective-permute-start(bf16[64,2048]{1,0:T(8,128)(2,1)S(1)} %convert_element_type.754), channel_id=1, source_target_pairs={{0,16},{8,24},{16,0},{24,8},{1,17},{9,25},{17,1},{25,9},{2,18},{10... | collective-permute-start | bytes 786440 | tf_op jit(solution)/shard_map/ppermute | solution.py:32
  407.7 21.6 %collective-permute-start.51 = (bf16[64,2048]{1,0:T(8,128)(2,1)S(1)}, bf16[64,2048]{1,0:T(8,128)(2,1)S(1)}, u32[]{:S(2)}, u32[]{:S(2)}) collective-permute-start(bf16[64,2048]{1,0:T(8,128)(2,1)S(1)} %convert_element_type.754), channel_id=1, source_target_pairs={{0,8},{8,0},{16,24},{24,16},{1,9},{9,1},{17,25},{25,17},{2,10},{10... | collective-permute-start | bytes 786440 | tf_op jit(solution)/shard_map/ppermute | solution.py:32
  408.8 22.4 %collective-permute-start.55 = (bf16[128,2176]{1,0:T(8,128)(2,1)S(1)}, bf16[128,2176]{1,0:T(8,128)(2,1)S(1)}, u32[]{:S(2)}, u32[]{:S(2)}) collective-permute-start(bf16[128,2176]{1,0:T(8,128)(2,1)S(1)} %get-tuple-element.369), channel_id=1, source_target_pairs={{0,8},{8,0},{16,24},{24,16},{1,9},{9,1},{17,25},{25,17},{2,10},{10... | collective-permute-start | bytes 1671176 | tf_op jit(solution)/shard_map/ppermute | solution.py:32
  434.5 22.2 %collective-permute-start.57 = (bf16[64,2176]{1,0:T(8,128)(2,1)}, bf16[64,2176]{1,0:T(8,128)(2,1)}, u32[]{:S(2)}, u32[]{:S(2)}) collective-permute-start(bf16[64,2176]{1,0:T(8,128)(2,1)} %get-tuple-element.380), channel_id=1, source_target_pairs={{0,4},{1,5},{2,6},{3,7},{4,0},{5,1},{6,2},{7,3},{8,12},{9,13},{10,... | collective-permute-start | bytes 835592 | tf_op jit(solution)/shard_map/ppermute | solution.py:37
  434.5 22.2 %collective-permute-start.56 = (bf16[64,2176]{1,0:T(8,128)(2,1)}, bf16[64,2176]{1,0:T(8,128)(2,1)}, u32[]{:S(2)}, u32[]{:S(2)}) collective-permute-start(bf16[64,2176]{1,0:T(8,128)(2,1)} %get-tuple-element.379), channel_id=1, source_target_pairs={{0,2},{1,3},{2,0},{3,1},{4,6},{5,7},{6,4},{7,5},{8,10},{9,11},{10,... | collective-permute-start | bytes 835592 | tf_op jit(solution)/shard_map/ppermute | solution.py:37
  436.5 23.4 %collective-permute-start.59 = (bf16[256,2048]{1,0:T(8,128)(2,1)}, bf16[256,2048]{1,0:T(8,128)(2,1)}, u32[]{:S(2)}, u32[]{:S(2)}) collective-permute-start(bf16[256,2048]{1,0:T(8,128)(2,1)} %get-tuple-element.390), channel_id=1, source_target_pairs={{0,8},{8,0},{16,24},{24,16},{1,9},{9,1},{17,25},{25,17},{2,10},{10... | collective-permute-start | bytes 3145736 | tf_op jit(solution)/shard_map/ppermute | solution.py:32
  438.1 24.4 %collective-permute-start.60 = (bf16[256,2048]{1,0:T(8,128)(2,1)}, bf16[256,2048]{1,0:T(8,128)(2,1)S(1)}, u32[]{:S(2)}, u32[]{:S(2)}) collective-permute-start(bf16[256,2048]{1,0:T(8,128)(2,1)} %get-tuple-element.392), channel_id=1, source_target_pairs={{0,16},{8,24},{16,0},{24,8},{1,17},{9,25},{17,1},{25,9},{2,18},{10... | collective-permute-start | bytes 3145736 | tf_op jit(solution)/shard_map/ppermute | solution.py:32
  467.0 17.9 %collective-permute-start.63 = (bf16[64,2048]{1,0:T(8,128)(2,1)S(1)}, bf16[64,2048]{1,0:T(8,128)(2,1)S(1)}, u32[]{:S(2)}, u32[]{:S(2)}) collective-permute-start(bf16[64,2048]{1,0:T(8,128)(2,1)S(1)} %get-tuple-element.522), channel_id=1, source_target_pairs={{0,24},{8,16},{16,8},{24,0},{1,25},{9,17},{17,9},{25,1},{2,26},{10... | collective-permute-start | bytes 786440 | tf_op jit(solution)/shard_map/ppermute | solution.py:32
  500.3 119.9 %reduce-scatter.5.cloned.1.call-start = ((), (), s32[]{:S(2)}) async-start(), calls=%async_computation.3 | async-start | bytes 4718592 | tf_op jit(solution)/shard_map/reduce_scatter | solution.py:823
  532.3 187.6 %all-gather.2.cloned.1.call-start = ((), (), s32[]{:S(2)}) async-start(), calls=%async_computation.4 | async-start | bytes 9437184 | tf_op jit(solution)/shard_map/all_gather | solution.py:841
  536.6 21.4 %collective-permute-start.72 = (bf16[128,2048]{1,0:T(8,128)(2,1)S(1)}, bf16[128,2048]{1,0:T(8,128)(2,1)S(1)}, u32[]{:S(2)}, u32[]{:S(2)}) collective-permute-start(bf16[128,2048]{1,0:T(8,128)(2,1)S(1)} %pad_maximum_fusion.10), channel_id=1, source_target_pairs={{0,2},{1,3},{2,0},{3,1},{4,6},{5,7},{6,4},{7,5},{8,10},{9,11},{10,... | collective-permute-start | bytes 1572872 | tf_op jit(solution)/shard_map/ppermute | solution.py:37
  538.7 20.8 %collective-permute-start.76 = (bf16[64,2048]{1,0:T(8,128)(2,1)S(1)}, bf16[64,2048]{1,0:T(8,128)(2,1)S(1)}, u32[]{:S(2)}, u32[]{:S(2)}) collective-permute-start(bf16[64,2048]{1,0:T(8,128)(2,1)S(1)} %get-tuple-element.600), channel_id=1, source_target_pairs={{0,24},{8,16},{16,8},{24,0},{1,25},{9,17},{17,9},{25,1},{2,26},{10... | collective-permute-start | bytes 786440 | tf_op jit(solution)/shard_map/ppermute | solution.py:32
  540.6 21.0 %collective-permute-start.75 = (bf16[64,2048]{1,0:T(8,128)(2,1)S(1)}, bf16[64,2048]{1,0:T(8,128)(2,1)S(1)}, u32[]{:S(2)}, u32[]{:S(2)}) collective-permute-start(bf16[64,2048]{1,0:T(8,128)(2,1)S(1)} %get-tuple-element.601), channel_id=1, source_target_pairs={{0,16},{8,24},{16,0},{24,8},{1,17},{9,25},{17,1},{25,9},{2,18},{10... | collective-permute-start | bytes 786440 | tf_op jit(solution)/shard_map/ppermute | solution.py:32
  541.3 20.2 %collective-permute-start.74 = (bf16[64,2048]{1,0:T(8,128)(2,1)S(1)}, bf16[64,2048]{1,0:T(8,128)(2,1)S(1)}, u32[]{:S(2)}, u32[]{:S(2)}) collective-permute-start(bf16[64,2048]{1,0:T(8,128)(2,1)S(1)} %get-tuple-element.599), channel_id=1, source_target_pairs={{0,8},{8,0},{16,24},{24,16},{1,9},{9,1},{17,25},{25,17},{2,10},{10... | collective-permute-start | bytes 786440 | tf_op jit(solution)/shard_map/ppermute | solution.py:32
  542.2 29.8 %collective-permute-start.77 = (bf16[256,2048]{1,0:T(8,128)(2,1)S(1)}, bf16[256,2048]{1,0:T(8,128)(2,1)S(1)}, u32[]{:S(2)}, u32[]{:S(2)}) collective-permute-start(bf16[256,2048]{1,0:T(8,128)(2,1)S(1)} %copy-done.32), channel_id=1, source_target_pairs={{0,8},{8,0},{16,24},{24,16},{1,9},{9,1},{17,25},{25,17},{2,10},{10... | collective-permute-start | bytes 3145736 | tf_op jit(solution)/shard_map/ppermute | solution.py:32
  558.0 23.3 %collective-permute-start.78 = (bf16[256,2048]{1,0:T(8,128)(2,1)S(1)}, bf16[256,2048]{1,0:T(8,128)(2,1)S(1)}, u32[]{:S(2)}, u32[]{:S(2)}) collective-permute-start(bf16[256,2048]{1,0:T(8,128)(2,1)S(1)} %copy-done.31), channel_id=1, source_target_pairs={{0,16},{8,24},{16,0},{24,8},{1,17},{9,25},{17,1},{25,9},{2,18},{10... | collective-permute-start | bytes 3145736 | tf_op jit(solution)/shard_map/ppermute | solution.py:32
  688.7 19.2 %collective-permute-start.87 = (bf16[20,2048]{1,0:T(8,128)(2,1)S(1)}, bf16[20,2048]{1,0:T(8,128)(2,1)S(1)}, u32[]{:S(2)}, u32[]{:S(2)}) collective-permute-start(bf16[20,2048]{1,0:T(8,128)(2,1)S(1)} %add_convert_fusion.52), channel_id=1, source_target_pairs={{0,4},{1,5},{2,6},{3,7},{4,0},{5,1},{6,2},{7,3},{8,12},{9,13},{10,... | collective-permute-start | bytes 245768 | tf_op jit(solution)/shard_map/ppermute | solution.py:37
  688.7 21.6 %collective-permute-start.86 = (bf16[20,2048]{1,0:T(8,128)(2,1)S(1)}, bf16[20,2048]{1,0:T(8,128)(2,1)S(1)}, u32[]{:S(2)}, u32[]{:S(2)}) collective-permute-start(bf16[20,2048]{1,0:T(8,128)(2,1)S(1)} %add_convert_fusion.52), channel_id=1, source_target_pairs={{0,2},{1,3},{2,0},{3,1},{4,6},{5,7},{6,4},{7,5},{8,10},{9,11},{10,... | collective-permute-start | bytes 245768 | tf_op jit(solution)/shard_map/ppermute | solution.py:37
  690.8 19.5 %collective-permute-start.91 = (bf16[64,2048]{1,0:T(8,128)(2,1)S(1)}, bf16[64,2048]{1,0:T(8,128)(2,1)S(1)}, u32[]{:S(2)}, u32[]{:S(2)}) collective-permute-start(bf16[64,2048]{1,0:T(8,128)(2,1)S(1)} %get-tuple-element.593), channel_id=1, source_target_pairs={{0,24},{8,16},{16,8},{24,0},{1,25},{9,17},{17,9},{25,1},{2,26},{10... | collective-permute-start | bytes 786440 | tf_op jit(solution)/shard_map/ppermute | solution.py:32
  693.2 17.1 %collective-permute-start.90 = (bf16[64,2048]{1,0:T(8,128)(2,1)S(1)}, bf16[64,2048]{1,0:T(8,128)(2,1)S(1)}, u32[]{:S(2)}, u32[]{:S(2)}) collective-permute-start(bf16[64,2048]{1,0:T(8,128)(2,1)S(1)} %get-tuple-element.594), channel_id=1, source_target_pairs={{0,16},{8,24},{16,0},{24,8},{1,17},{9,25},{17,1},{25,9},{2,18},{10... | collective-permute-start | bytes 786440 | tf_op jit(solution)/shard_map/ppermute | solution.py:32
  (85 other events, 1000.1 us)
Sparse Core Ops, SparseCore 0:
  500.4 58.1 reduce-scatter.2
  561.5 50.2 reduce-scatter.4
  622.7 97.1 all-gather.1

commit v5 on v4

--- a/solution.py
+++ b/solution.py
@@ -92,7 +92,12 @@
     return swap_tp(rows, 1), swap_tp(rows, 2)
 
 
-def gather_plane_far(rows, near, far):
+def far_sends(near, far):
+    n = near.shape[-2] // 2
+    return sync(near[..., :n, :], far[..., n:, :])
+
+
+def gather_plane_far(rows, near, far, sends=None):
     n = rows.shape[-2] // 2
 
     def top(value):
@@ -101,11 +106,14 @@
     def low(value):
         return value[..., n:, :]
 
-    sent_a, sent_b = lax.optimization_barrier((top(near), low(far)))
+    sent_a, sent_b = sends or far_sends(near, far)
     far_a, far_b = swap_tp(sent_a, 2), swap_tp(sent_b, 1)
-    return jnp.concatenate(
-        [top(rows), top(far), top(near), far_a, low(rows), low(near), low(far), far_b], axis=-2
-    )
+    base = jnp.concatenate(
+        [top(rows), top(far), top(near), top(rows), low(rows), low(near), low(far), top(rows)], axis=-2
+    )
+    base = lax.optimization_barrier(base)
+    base = lax.dynamic_update_slice_in_dim(base, far_a, 3 * n, axis=-2)
+    return lax.dynamic_update_slice_in_dim(base, far_b, 7 * n, axis=-2)
 
 
 def cut(rows, count):
@@ -681,9 +689,12 @@
     moe_near0 = gather_plane_near(moe_z0)
     moe_z1 = gather_outer(moe_own1, zone)
 
-    moe_z0, moe_z1, cot_z0, cot_z1, *near = sync(moe_z0, moe_z1, cot_z0, cot_z1, *cot_near0, *moe_near0)
-    cot_half0 = gather_plane_far(cot_z0, *near[:2])
-    moe_half0 = gather_plane_far(moe_z0, *near[2:])
+    cot_sends0 = far_sends(*cot_near0)
+    moe_z0, moe_z1, cot_z0, cot_z1, *near = sync(
+        moe_z0, moe_z1, cot_z0, cot_z1, *cot_near0, *moe_near0, *cot_sends0
+    )
+    cot_half0 = gather_plane_far(cot_z0, *near[:2], near[4:])
+    moe_half0 = gather_plane_far(moe_z0, *near[2:4])
 
     moe_half0, cot_half0, moe_z1, cot_z1 = sync(moe_half0, cot_half0, moe_z1, cot_z1)
     moe_other0, cot_other0 = swap_dp(moe_half0, 1), swap_dp(cot_half0, 1)
@@ -697,10 +708,13 @@
     moe_near1 = gather_plane_near(moe_z1)
     other0 = experts_of(moe_other0, cot_other0)
 
-    moe_z1, cot_z1, *rest = sync(moe_z1, cot_z1, *cot_near1, *moe_near1, *own0, *other0)
-    own0, other0 = rest[4:7], rest[7:]
+    cot_sends1 = far_sends(*cot_near1)
+    moe_z1, cot_z1, *rest = sync(
+        moe_z1, cot_z1, *cot_near1, *moe_near1, *own0, *other0, *cot_sends1
+    )
+    own0, other0, cot_sends1 = rest[4:7], rest[7:10], rest[10:]
     core0 = scatter_core(own0[0], other0[0])
-    cot_half1 = gather_plane_far(cot_z1, *rest[:2])
+    cot_half1 = gather_plane_far(cot_z1, *rest[:2], cot_sends1)
     moe_half1 = gather_plane_far(moe_z1, *rest[2:4])
     mix0 = [mix(own0), mix(other0)]
 

time: 754 us -> 740 us (0.981)
  waiting for transfers between devices: 271 us -> 256 us
    ppermute x62, waiting for transfers between devices: 157 us -> 144 us  [swap_tp(): return lax.ppermute(value, 'tp', [(i, i ^ bits) for i in range(size)])]
  transfers between devices with their start and end apart: 96 -> 96, of which waited for: 45 -> 45; matrix products, arithmetic and copies ran while one was open for 16% -> 18% of each run, Pallas kernels for 21% -> 22%
where the time goes in v5:
time: 740 us; the launch traced here: 730 us
  waiting for transfers between devices  256 us (35%)
  Pallas kernels  173 us (23%)
  starting transfers between devices  114 us (15%)
  other arithmetic  77.9 us (11%)
  local copies, waits for them, and re-layouts  70.7 us (10%)
  matrix products  22.9 us (3%)
  between operations  15.3 us (2%)
    pallas_call x14, Pallas kernels, call_kernel(): pl.pallas_call(body, out_shape=outs, grid=grid, in_specs=in_specs or [who...  173 us
    ppermute x62, waiting for transfers between devices, swap_tp(): return lax.ppermute(value, 'tp', [(i, i ^ bits) for i in range(size)])  144 us
    ppermute x31, waiting for transfers between devices, swap_dp(): return lax.ppermute(value, 'dp', [(i, i ^ bits) for i in range(size)])  110 us
    ppermute x62, starting transfers between devices, swap_tp(): return lax.ppermute(value, 'tp', [(i, i ^ bits) for i in range(size)])  70.2 us
    ppermute x31, starting transfers between devices, swap_dp(): return lax.ppermute(value, 'dp', [(i, i ^ bits) for i in range(size)])  43.7 us
    convert_element_type x20, other arithmetic, add_pieces(): return [add_low(one, two).astype(BF) for one, two in zip(left, right)]  25.4 us
    unnamed x129, local copies, waits for them, and re-layouts  22.2 us
    dot_general x4, matrix products, mix(): return jnp.dot(ran[1], down, preferred_element_type=F32).astype(BF)  17.6 us
  transfers between devices with their start and end apart: 96, of which 45 were waited for; matrix products, arithmetic and copies ran while one was open for 18% of the time, Pallas kernels for 22%

profile of v5, /device:TPU:0, one launch (start us, length us, event | category | flops | bytes accessed | tf_op | source)
XLA Modules:
  0.0 730.4 jit_solution(4494055392755400005)
XLA Ops:
  7.2 4.0 collective-permute-start.2
  20.5 4.7 fusion.27
  28.2 2.7 pad_maximum_fusion.1.gate_up_ref
  30.9 3.8 collective-permute-done.1
  35.0 2.7 pad_maximum_fusion.3
  37.7 9.4 %shard_map.195 = (bf16[512,2048]{1,0:T(8,128)(2,1)}, f32[512,1536]{1,0:T(8,128)}, f32[512,128]{1,0:T(8,128)}) custom-call(bf16[512,2048]{1,0:T(8,128)(2,1)} %bitcast.170, f32[1,2048]{1,0:T(1,128)} %bitcast.194, bf16[3,2048,512]{2,1,0:T(8,128)(2,1)} %bitcast.159), custom_call_target="tpu_custom_call" | custom-call | flops 402653184 | bytes 786432 | tf_op jit(solution)/shard_map/pallas_call | solution.py:161
  53.6 3.1 collective-permute-done.3
  56.7 3.6 collective-permute-start.8
  63.3 3.0 collective-permute-done.4
  67.0 7.9 %shard_map.196 = (bf16[2,256,1536]{2,1,0:T(8,128)(2,1)}, f32[2,4,256,256]{3,2,1,0:T(8,128)}, bf16[2,256,512]{2,1,0:T(8,128)(2,1)}, bf16[2,256,2048]{2,1,0:T(8,128)(2,1)}) custom-call(f32[2,256,1536]{2,1,0:T(8,128)} %bitcast.148, f32[2,256,128]{2,1,0:T(8,128)} %fusion.7.squares_ref, f32[2,512]{1,0:T(2,128)} %gain_ref.5, ...), custom_call_target="tpu_custom_call" | custom-call | flops 167772160 | bytes 2097152 | tf_op jit(solution)/shard_map/pallas_call | solution.py:161
  82.7 10.1 %collective-permute-done.11 = bf16[2,64,2048]{2,1,0:T(8,128)(2,1)S(1)} collective-permute-done((bf16[2,64,2048]{2,1,0:T(8,128)(2,1)S(1)}, bf16[2,64,2048]{2,1,0:T(8,128)(2,1)S(1)}, u32[]{:S(2)}, u32[]{:S(2)}) %collective-permute-start.11) | collective-permute-done | bytes 524320 | tf_op jit(solution)/shard_map/ppermute | solution.py:32
  92.7 9.3 %collective-permute-done.10 = bf16[2,64,2048]{2,1,0:T(8,128)(2,1)S(1)} collective-permute-done((bf16[2,64,2048]{2,1,0:T(8,128)(2,1)S(1)}, bf16[2,64,2048]{2,1,0:T(8,128)(2,1)S(1)}, u32[]{:S(2)}, u32[]{:S(2)}) %collective-permute-start.10) | collective-permute-done | bytes 524320 | tf_op jit(solution)/shard_map/ppermute | solution.py:32
  105.5 3.8 collective-permute-start.14
  109.4 6.8 collective-permute-start.13
  116.2 15.4 %collective-permute-done.13 = bf16[64,2048]{1,0:T(8,128)(2,1)S(1)} collective-permute-done((bf16[64,2048]{1,0:T(8,128)(2,1)S(1)}, bf16[64,2048]{1,0:T(8,128)(2,1)S(1)}, u32[]{:S(2)}, u32[]{:S(2)}) %collective-permute-start.13) | collective-permute-done | bytes 262176 | tf_op jit(solution)/shard_map/ppermute | solution.py:37
  133.9 3.5 collective-permute-start.19
  138.3 6.7 collective-permute-done.19
  145.0 14.5 %collective-permute-done.18 = bf16[64,2048]{1,0:T(8,128)(2,1)S(1)} collective-permute-done((bf16[64,2048]{1,0:T(8,128)(2,1)S(1)}, bf16[64,2048]{1,0:T(8,128)(2,1)S(1)}, u32[]{:S(2)}, u32[]{:S(2)}) %collective-permute-start.18) | collective-permute-done | bytes 262176 | tf_op jit(solution)/shard_map/ppermute | solution.py:37
  176.2 3.7 collective-permute-done.22
  181.6 8.4 %collective-permute-done.24 = bf16[128,2176]{1,0:T(8,128)(2,1)S(1)} collective-permute-done((bf16[128,2176]{1,0:T(8,128)(2,1)S(1)}, bf16[128,2176]{1,0:T(8,128)(2,1)S(1)}, u32[]{:S(2)}, u32[]{:S(2)}) %collective-permute-start.24) | collective-permute-done | bytes 557088 | tf_op jit(solution)/shard_map/ppermute | solution.py:32
  194.9 18.0 %shard_map.197 = (bf16[1024,2176]{1,0:T(8,128)(2,1)}, bf16[1024,512]{1,0:T(8,128)(2,1)}, bf16[1024,1024]{1,0:T(8,128)(2,1)}) custom-call(s32[1]{0:T(128)} %bitcast.17.ids_ref, bf16[1024,2048]{1,0:T(8,128)(2,1)} %constant_dynamic-update-slice_fusion.14.moe_ref.refs_0_, bf16[1024,2176]{1,0:T(8,128)(2,1)} %constant_dynamic-update-slice_fusion.12.cot_ref.refs_4_, ...), custom_call_target="tpu_custom_call" | custom-call | flops 1342177280 | bytes 1572864 | tf_op jit(solution)/shard_map/pallas_call | solution.py:161
  212.8 6.6 collective-permute-done.28
  226.2 18.1 %shard_map.198 = (bf16[1024,2176]{1,0:T(8,128)(2,1)}, bf16[1024,512]{1,0:T(8,128)(2,1)}, bf16[1024,1024]{1,0:T(8,128)(2,1)}) custom-call(s32[1]{0:T(128)} %bitcast.17.ids_ref, bf16[1024,2048]{1,0:T(8,128)(2,1)} %collective-permute-done.26.moe_ref.refs_1_, bf16[1024,2176]{1,0:T(8,128)(2,1)} %collective-permute-done.27.cot_ref.refs_5_, ...), custom_call_target="tpu_custom_call" | custom-call | flops 1342177280 | bytes 1572864 | tf_op jit(solution)/shard_map/pallas_call | solution.py:161
  255.3 4.4 convolution_convert_fusion.3
  264.5 4.4 convolution_convert_fusion.2
  277.1 18.0 %shard_map.199 = (bf16[1024,2176]{1,0:T(8,128)(2,1)}, bf16[1024,512]{1,0:T(8,128)(2,1)}, bf16[1024,1024]{1,0:T(8,128)(2,1)}) custom-call(s32[1]{0:T(128)} %bitcast.17.ids_ref, bf16[1024,2048]{1,0:T(8,128)(2,1)} %constant_dynamic-update-slice_fusion.8.moe_ref.refs_2_, bf16[1024,2176]{1,0:T(8,128)(2,1)} %copy-done.4, bf16[2048,128]{1,0:T(8,128)(2,1)} %pad.17.router_ref, ...), custom_call_target="tpu_custom_call" | custom-call | flops 1342177280 | bytes 1572864 | tf_op jit(solution)/shard_map/pallas_call | solution.py:161
  295.0 7.1 collective-permute-done.39
  308.7 18.5 %shard_map.200 = (bf16[1024,2176]{1,0:T(8,128)(2,1)}, bf16[1024,512]{1,0:T(8,128)(2,1)}, bf16[1024,1024]{1,0:T(8,128)(2,1)}) custom-call(s32[1]{0:T(128)} %bitcast.17.ids_ref, bf16[1024,2048]{1,0:T(8,128)(2,1)} %collective-permute-done.37.moe_ref.refs_3_, bf16[1024,2176]{1,0:T(8,128)(2,1)} %collective-permute-done.38.cot_ref.refs_7_, ...), custom_call_target="tpu_custom_call" | custom-call | flops 1342177280 | bytes 1572864 | tf_op jit(solution)/shard_map/pallas_call | solution.py:161
  329.0 3.5 collective-permute-start.43
  332.6 4.4 convolution_convert_fusion.1
  337.0 4.4 convolution_convert_fusion
  341.4 12.1 %collective-permute-done.44 = bf16[64,2176]{1,0:T(8,128)(2,1)S(1)} collective-permute-done((bf16[64,2176]{1,0:T(8,128)(2,1)S(1)}, bf16[64,2176]{1,0:T(8,128)(2,1)S(1)}, u32[]{:S(2)}, u32[]{:S(2)}) %collective-permute-start.44) | collective-permute-done | bytes 278560 | tf_op jit(solution)/shard_map/ppermute | solution.py:37
  354.5 2.6 add_convert_fusion.12
  366.2 21.1 %collective-permute-done.48 = bf16[256,2176]{1,0:T(8,128)(2,1)S(1)} collective-permute-done((bf16[256,2176]{1,0:T(8,128)(2,1)}, bf16[256,2176]{1,0:T(8,128)(2,1)S(1)}, u32[]{:S(2)}, u32[]{:S(2)}) %collective-permute-start.48) | collective-permute-done | bytes 1114144 | tf_op jit(solution)/shard_map/ppermute | solution.py:32
  389.5 4.1 add_convert_fusion.8
  399.1 5.7 collective-permute-done.53
  404.8 14.3 %collective-permute-done.52 = bf16[64,2048]{1,0:T(8,128)(2,1)S(1)} collective-permute-done((bf16[64,2048]{1,0:T(8,128)(2,1)S(1)}, bf16[64,2048]{1,0:T(8,128)(2,1)S(1)}, u32[]{:S(2)}, u32[]{:S(2)}) %collective-permute-start.52) | collective-permute-done | bytes 262176 | tf_op jit(solution)/shard_map/ppermute | solution.py:32
  423.6 2.8 collective-permute-start.56
  429.9 7.1 shard_map.201
  437.1 8.7 %collective-permute-done.57 = bf16[64,2176]{1,0:T(8,128)(2,1)} collective-permute-done((bf16[64,2176]{1,0:T(8,128)(2,1)}, bf16[64,2176]{1,0:T(8,128)(2,1)}, u32[]{:S(2)}, u32[]{:S(2)}) %collective-permute-start.57) | collective-permute-done | bytes 278560 | tf_op jit(solution)/shard_map/ppermute | solution.py:37
  447.1 2.6 collective-permute-done.59
  460.8 3.0 collective-permute-done.65
  465.2 6.7 collective-permute-done.64
  475.3 7.0 shard_map.202
  482.4 7.3 shard_map.203
  495.9 6.8 shard_map.204
  503.5 2.9 collective-permute-done.70
  508.2 7.0 shard_map.205
  515.2 6.5 shard_map.206
  533.6 13.7 %collective-permute-done.72 = bf16[128,2048]{1,0:T(8,128)(2,1)S(1)} collective-permute-done((bf16[128,2048]{1,0:T(8,128)(2,1)S(1)}, bf16[128,2048]{1,0:T(8,128)(2,1)S(1)}, u32[]{:S(2)}, u32[]{:S(2)}) %collective-permute-start.72) | collective-permute-done | bytes 524320 | tf_op jit(solution)/shard_map/ppermute | solution.py:37
  552.0 5.2 collective-permute-done.73
  558.0 3.9 collective-permute-done.77
  562.4 8.5 %collective-permute-done.78 = bf16[256,2048]{1,0:T(8,128)(2,1)S(1)} collective-permute-done((bf16[256,2048]{1,0:T(8,128)(2,1)S(1)}, bf16[256,2048]{1,0:T(8,128)(2,1)S(1)}, u32[]{:S(2)}, u32[]{:S(2)}) %collective-permute-start.78) | collective-permute-done | bytes 1048608 | tf_op jit(solution)/shard_map/ppermute | solution.py:32
  580.1 2.7 collective-permute-done.80
  584.2 8.0 %collective-permute-done.82 = bf16[128,2048]{1,0:T(8,128)(2,1)S(1)} collective-permute-done((bf16[128,2048]{1,0:T(8,128)(2,1)S(1)}, bf16[128,2048]{1,0:T(8,128)(2,1)S(1)}, u32[]{:S(2)}, u32[]{:S(2)}) %collective-permute-start.82) | collective-permute-done | bytes 524320 | tf_op jit(solution)/shard_map/ppermute | solution.py:32
  594.0 14.7 %collective-permute-done.85 = bf16[128,2048]{1,0:T(8,128)(2,1)S(1)} collective-permute-done((bf16[128,2048]{1,0:T(8,128)(2,1)S(1)}, bf16[128,2048]{1,0:T(8,128)(2,1)S(1)}, u32[]{:S(2)}, u32[]{:S(2)}) %collective-permute-start.85) | collective-permute-done | bytes 524320 | tf_op jit(solution)/shard_map/ppermute | solution.py:37
  611.2 24.6 %shard_map.207 = f32[2048,1024]{1,0:T(8,128)} custom-call(bf16[1024,2048]{1,0:T(8,128)(2,1)} %constant_dynamic-update-slice_fusion.14.moe_ref.refs_0_, bf16[1024,2048]{1,0:T(8,128)(2,1)} %collective-permute-done.26.moe_ref.refs_1_, bf16[1024,2048]{1,0:T(8,128)(2,1)} %constant_dynamic-update-slice_fusion.8.moe_ref.refs_2_, ...), custom_call_target="tpu_custom_call" | custom-call | flops 2147483648 | bytes 4194304 | tf_op jit(solution)/shard_map/pallas_call | solution.py:161
  635.8 11.7 %reshape.430 = f32[2048,2,2,256]{3,2,1,0:T(2,128)} reshape(f32[2048,1024]{1,0:T(8,128)} %shard_map.207) | data formatting | bytes 16777216 | tf_op jit(solution)/shard_map/reshape | solution.py:871
  647.5 17.2 %shard_map.208 = f32[512,2048]{1,0:T(8,128)} custom-call(bf16[1024,512]{1,0:T(8,128)(2,1)} %get-tuple-element.482.refs_0_, bf16[1024,512]{1,0:T(8,128)(2,1)} %get-tuple-element.483.refs_1_, bf16[1024,512]{1,0:T(8,128)(2,1)} %get-tuple-element.484.refs_2_, bf16[1024,512]{1,0:T(8,128)(2,1)} %get-tuple-element.485.refs_3_, ...), custom_call_target="tpu_custom_call" | custom-call | flops 1073741824 | bytes 3145728 | tf_op jit(solution)/shard_map/pallas_call | solution.py:161
  664.7 5.5 slice_bitcast_fusion.1
  670.2 4.8 pad_maximum_fusion
  685.9 10.2 %collective-permute-done.87 = bf16[20,2048]{1,0:T(8,128)(2,1)S(1)} collective-permute-done((bf16[20,2048]{1,0:T(8,128)(2,1)S(1)}, bf16[20,2048]{1,0:T(8,128)(2,1)S(1)}, u32[]{:S(2)}, u32[]{:S(2)}) %collective-permute-start.87) | collective-permute-done | bytes 81952 | tf_op jit(solution)/shard_map/ppermute | solution.py:37
  700.1 5.6 collective-permute-done.92
  711.5 9.4 %convert_bitcast_fusion = f32[2048,3,512]{2,0,1:T(8,128)} fusion(bf16[4,2048,512]{2,1,0:T(8,128)(2,1)} %bitcast.171), kind=kLoop, calls=%fused_computation | loop fusion | flops 3145728 | bytes 18874368 | tf_op jit(solution)/shard_map/transpose | solution.py:883
  (423 shorter events, 206.4 us)
Async XLA Ops:
  7.2 601.6 %reduce-scatter.3.cloned.1.call-start = ((), (), s32[]{:S(2)}) async-start(), calls=%async_computation.2 | async-start | bytes 4718592 | tf_op jit(solution)/shard_map/reduce_scatter | solution.py:827
  7.2 23.7 %collective-permute-start.2 = (bf16[2,64,2048]{2,1,0:T(8,128)(2,1)}, bf16[2,64,2048]{2,1,0:T(8,128)(2,1)S(1)}, u32[]{:S(2)}, u32[]{:S(2)}) collective-permute-start(bf16[2,64,2048]{2,1,0:T(8,128)(2,1)} %bitcast.176), channel_id=1, source_target_pairs={{0,24},{8,16},{16,8},{24,0},{1,25},{9,17},{17,9},{25,1},{2,26},{10... | collective-permute-start | bytes 1572872 | tf_op jit(solution)/shard_map/ppermute | solution.py:32
  11.2 23.5 %collective-permute-start.1 = (bf16[2,64,2048]{2,1,0:T(8,128)(2,1)}, bf16[2,64,2048]{2,1,0:T(8,128)(2,1)}, u32[]{:S(2)}, u32[]{:S(2)}) collective-permute-start(bf16[2,64,2048]{2,1,0:T(8,128)(2,1)} %bitcast.177), channel_id=1, source_target_pairs={{0,16},{8,24},{16,0},{24,8},{1,17},{9,25},{17,1},{25,9},{2,18},{10... | collective-permute-start | bytes 1572872 | tf_op jit(solution)/shard_map/ppermute | solution.py:32
  11.7 23.3 %collective-permute-start = (bf16[2,64,2048]{2,1,0:T(8,128)(2,1)}, bf16[2,64,2048]{2,1,0:T(8,128)(2,1)}, u32[]{:S(2)}, u32[]{:S(2)}) collective-permute-start(bf16[2,64,2048]{2,1,0:T(8,128)(2,1)} %bitcast.178), channel_id=1, source_target_pairs={{0,8},{8,0},{16,24},{24,16},{1,9},{9,1},{17,25},{25,17},{2,10},{10... | collective-permute-start | bytes 1572872 | tf_op jit(solution)/shard_map/ppermute | solution.py:32
  15.4 59.5 %collective-permute-start.6 = (bf16[2,64,2176]{2,1,0:T(8,128)(2,1)S(1)}, bf16[2,64,2176]{2,1,0:T(8,128)(2,1)S(1)}, u32[]{:S(2)}, u32[]{:S(2)}) collective-permute-start(bf16[2,64,2176]{2,1,0:T(8,128)(2,1)S(1)} %pad_maximum_fusion.9), channel_id=1, source_target_pairs={{0,2},{1,3},{2,0},{3,1},{4,6},{5,7},{6,4},{7,5},{8,10},{9,11},{10,... | collective-permute-start | bytes 1671176 | tf_op jit(solution)/shard_map/ppermute | solution.py:37
  17.5 57.5 %collective-permute-start.7 = (bf16[2,64,2176]{2,1,0:T(8,128)(2,1)S(1)}, bf16[2,64,2176]{2,1,0:T(8,128)(2,1)S(1)}, u32[]{:S(2)}, u32[]{:S(2)}) collective-permute-start(bf16[2,64,2176]{2,1,0:T(8,128)(2,1)S(1)} %pad_maximum_fusion.9), channel_id=1, source_target_pairs={{0,4},{1,5},{2,6},{3,7},{4,0},{5,1},{6,2},{7,3},{8,12},{9,13},{10,... | collective-permute-start | bytes 1671176 | tf_op jit(solution)/shard_map/ppermute | solution.py:37
  56.7 18.2 %collective-permute-start.8 = (bf16[2,64,2176]{2,1,0:T(8,128)(2,1)S(1)}, bf16[2,64,2176]{2,1,0:T(8,128)(2,1)S(1)}, u32[]{:S(2)}, u32[]{:S(2)}) collective-permute-start(bf16[2,64,2176]{2,1,0:T(8,128)(2,1)S(1)} %pad_maximum_fusion.9), channel_id=1, source_target_pairs={{0,6},{1,7},{2,4},{3,5},{4,2},{5,3},{6,0},{7,1},{8,14},{9,15},{10,... | collective-permute-start | bytes 1671176 | tf_op jit(solution)/shard_map/ppermute | solution.py:37
  78.4 23.6 %collective-permute-start.10 = (bf16[2,64,2048]{2,1,0:T(8,128)(2,1)S(1)}, bf16[2,64,2048]{2,1,0:T(8,128)(2,1)S(1)}, u32[]{:S(2)}, u32[]{:S(2)}) collective-permute-start(bf16[2,64,2048]{2,1,0:T(8,128)(2,1)S(1)} %get-tuple-element.264), channel_id=1, source_target_pairs={{0,16},{8,24},{16,0},{24,8},{1,17},{9,25},{17,1},{25,9},{2,18},{10... | collective-permute-start | bytes 1572872 | tf_op jit(solution)/shard_map/ppermute | solution.py:32
  78.7 24.1 %collective-permute-start.9 = (bf16[2,64,2048]{2,1,0:T(8,128)(2,1)S(1)}, bf16[2,64,2048]{2,1,0:T(8,128)(2,1)S(1)}, u32[]{:S(2)}, u32[]{:S(2)}) collective-permute-start(bf16[2,64,2048]{2,1,0:T(8,128)(2,1)S(1)} %get-tuple-element.263), channel_id=1, source_target_pairs={{0,8},{8,0},{16,24},{24,16},{1,9},{9,1},{17,25},{25,17},{2,10},{10... | collective-permute-start | bytes 1572872 | tf_op jit(solution)/shard_map/ppermute | solution.py:32
  80.6 51.2 %collective-permute-start.15 = (bf16[256,2176]{1,0:T(8,128)(2,1)S(1)}, bf16[256,2176]{1,0:T(8,128)(2,1)S(1)}, u32[]{:S(2)}, u32[]{:S(2)}) collective-permute-start(bf16[256,2176]{1,0:T(8,128)(2,1)S(1)} %get-tuple-element.280), channel_id=1, source_target_pairs={{0,8},{8,0},{16,24},{24,16},{1,9},{9,1},{17,25},{25,17},{2,10},{10... | collective-permute-start | bytes 3342344 | tf_op jit(solution)/shard_map/ppermute | solution.py:32
  81.0 50.8 %collective-permute-start.16 = (bf16[256,2176]{1,0:T(8,128)(2,1)S(1)}, bf16[256,2176]{1,0:T(8,128)(2,1)S(1)}, u32[]{:S(2)}, u32[]{:S(2)}) collective-permute-start(bf16[256,2176]{1,0:T(8,128)(2,1)S(1)} %get-tuple-element.280), channel_id=1, source_target_pairs={{0,16},{8,24},{16,0},{24,8},{1,17},{9,25},{17,1},{25,9},{2,18},{10... | collective-permute-start | bytes 3342344 | tf_op jit(solution)/shard_map/ppermute | solution.py:32
  109.4 22.3 %collective-permute-start.13 = (bf16[64,2048]{1,0:T(8,128)(2,1)S(1)}, bf16[64,2048]{1,0:T(8,128)(2,1)S(1)}, u32[]{:S(2)}, u32[]{:S(2)}) collective-permute-start(bf16[64,2048]{1,0:T(8,128)(2,1)S(1)} %get-tuple-element.620), channel_id=1, source_target_pairs={{0,4},{1,5},{2,6},{3,7},{4,0},{5,1},{6,2},{7,3},{8,12},{9,13},{10,... | collective-permute-start | bytes 786440 | tf_op jit(solution)/shard_map/ppermute | solution.py:37
  131.8 27.9 %collective-permute-start.20 = (bf16[256,2048]{1,0:T(8,128)(2,1)S(1)}, bf16[256,2048]{1,0:T(8,128)(2,1)S(1)}, u32[]{:S(2)}, u32[]{:S(2)}) collective-permute-start(bf16[256,2048]{1,0:T(8,128)(2,1)S(1)} %pad_maximum_fusion.4), channel_id=1, source_target_pairs={{0,8},{8,0},{16,24},{24,16},{1,9},{9,1},{17,25},{25,17},{2,10},{10... | collective-permute-start | bytes 3145736 | tf_op jit(solution)/shard_map/ppermute | solution.py:32
  133.1 26.5 %collective-permute-start.21 = (bf16[256,2048]{1,0:T(8,128)(2,1)S(1)}, bf16[256,2048]{1,0:T(8,128)(2,1)S(1)}, u32[]{:S(2)}, u32[]{:S(2)}) collective-permute-start(bf16[256,2048]{1,0:T(8,128)(2,1)S(1)} %pad_maximum_fusion.4), channel_id=1, source_target_pairs={{0,16},{8,24},{16,0},{24,8},{1,17},{9,25},{17,1},{25,9},{2,18},{10... | collective-permute-start | bytes 3145736 | tf_op jit(solution)/shard_map/ppermute | solution.py:32
  137.4 22.1 %collective-permute-start.18 = (bf16[64,2048]{1,0:T(8,128)(2,1)S(1)}, bf16[64,2048]{1,0:T(8,128)(2,1)S(1)}, u32[]{:S(2)}, u32[]{:S(2)}) collective-permute-start(bf16[64,2048]{1,0:T(8,128)(2,1)S(1)} %get-tuple-element.268), channel_id=1, source_target_pairs={{0,4},{1,5},{2,6},{3,7},{4,0},{5,1},{6,2},{7,3},{8,12},{9,13},{10,... | collective-permute-start | bytes 786440 | tf_op jit(solution)/shard_map/ppermute | solution.py:37
  137.4 22.1 %collective-permute-start.17 = (bf16[64,2048]{1,0:T(8,128)(2,1)S(1)}, bf16[64,2048]{1,0:T(8,128)(2,1)S(1)}, u32[]{:S(2)}, u32[]{:S(2)}) collective-permute-start(bf16[64,2048]{1,0:T(8,128)(2,1)S(1)} %get-tuple-element.268), channel_id=1, source_target_pairs={{0,2},{1,3},{2,0},{3,1},{4,6},{5,7},{6,4},{7,5},{8,10},{9,11},{10,... | collective-permute-start | bytes 786440 | tf_op jit(solution)/shard_map/ppermute | solution.py:37
  173.4 16.6 %collective-permute-start.24 = (bf16[128,2176]{1,0:T(8,128)(2,1)S(1)}, bf16[128,2176]{1,0:T(8,128)(2,1)S(1)}, u32[]{:S(2)}, u32[]{:S(2)}) collective-permute-start(bf16[128,2176]{1,0:T(8,128)(2,1)S(1)} %slice.670), channel_id=1, source_target_pairs={{0,16},{8,24},{16,0},{24,8},{1,17},{9,25},{17,1},{25,9},{2,18},{10... | collective-permute-start | bytes 1671176 | tf_op jit(solution)/shard_map/ppermute | solution.py:32
  192.3 27.9 %collective-permute-start.27 = (bf16[1024,2176]{1,0:T(8,128)(2,1)}, bf16[1024,2176]{1,0:T(8,128)(2,1)}, u32[]{:S(2)}, u32[]{:S(2)}) collective-permute-start(bf16[1024,2176]{1,0:T(8,128)(2,1)} %constant_dynamic-update-slice_fusion.12.cot_ref.refs_4_), channel_id=1, source_target_pairs={{0,1},{1,0},{2,3},{3,2},{4,5},{5,4},{6,7},{7,6},{8,9},{9,8},{10,11... | collective-permute-start | bytes 13369352 | tf_op jit(solution)/shard_map/ppermute | solution.py:37
  192.3 27.9 %collective-permute-start.26 = (bf16[1024,2048]{1,0:T(8,128)(2,1)}, bf16[1024,2048]{1,0:T(8,128)(2,1)}, u32[]{:S(2)}, u32[]{:S(2)}) collective-permute-start(bf16[1024,2048]{1,0:T(8,128)(2,1)} %constant_dynamic-update-slice_fusion.14.moe_ref.refs_0_), channel_id=1, source_target_pairs={{0,1},{1,0},{2,3},{3,2},{4,5},{5,4},{6,7},{7,6},{8,9},{9,8},{10,11... | collective-permute-start | bytes 12582920 | tf_op jit(solution)/shard_map/ppermute | solution.py:37
  192.8 26.6 %collective-permute-start.28 = (bf16[256,2176]{1,0:T(8,128)(2,1)S(1)}, bf16[256,2176]{1,0:T(8,128)(2,1)}, u32[]{:S(2)}, u32[]{:S(2)}) collective-permute-start(bf16[256,2176]{1,0:T(8,128)(2,1)S(1)} %get-tuple-element.311), channel_id=1, source_target_pairs={{0,8},{8,0},{16,24},{24,16},{1,9},{9,1},{17,25},{25,17},{2,10},{10... | collective-permute-start | bytes 3342344 | tf_op jit(solution)/shard_map/ppermute | solution.py:32
  193.9 26.3 %collective-permute-start.29 = (bf16[256,2176]{1,0:T(8,128)(2,1)S(1)}, bf16[256,2176]{1,0:T(8,128)(2,1)}, u32[]{:S(2)}, u32[]{:S(2)}) collective-permute-start(bf16[256,2176]{1,0:T(8,128)(2,1)S(1)} %get-tuple-element.311), channel_id=1, source_target_pairs={{0,16},{8,24},{16,0},{24,8},{1,17},{9,25},{17,1},{25,9},{2,18},{10... | collective-permute-start | bytes 3342344 | tf_op jit(solution)/shard_map/ppermute | solution.py:32
  220.2 24.1 %collective-permute-start.30 = (bf16[256,2048]{1,0:T(8,128)(2,1)S(1)}, bf16[256,2048]{1,0:T(8,128)(2,1)S(1)}, u32[]{:S(2)}, u32[]{:S(2)}) collective-permute-start(bf16[256,2048]{1,0:T(8,128)(2,1)S(1)} %pad_maximum_fusion.5), channel_id=1, source_target_pairs={{0,8},{8,0},{16,24},{24,16},{1,9},{9,1},{17,25},{25,17},{2,10},{10... | collective-permute-start | bytes 3145736 | tf_op jit(solution)/shard_map/ppermute | solution.py:32
  221.2 23.6 %collective-permute-start.31 = (bf16[256,2048]{1,0:T(8,128)(2,1)S(1)}, bf16[256,2048]{1,0:T(8,128)(2,1)S(1)}, u32[]{:S(2)}, u32[]{:S(2)}) collective-permute-start(bf16[256,2048]{1,0:T(8,128)(2,1)S(1)} %pad_maximum_fusion.5), channel_id=1, source_target_pairs={{0,16},{8,24},{16,0},{24,8},{1,17},{9,25},{17,1},{25,9},{2,18},{10... | collective-permute-start | bytes 3145736 | tf_op jit(solution)/shard_map/ppermute | solution.py:32
  245.8 25.8 %collective-permute-start.32 = (bf16[128,2176]{1,0:T(8,128)(2,1)}, bf16[128,2176]{1,0:T(8,128)(2,1)S(1)}, u32[]{:S(2)}, u32[]{:S(2)}) collective-permute-start(bf16[128,2176]{1,0:T(8,128)(2,1)} %slice.682), channel_id=1, source_target_pairs={{0,16},{8,24},{16,0},{24,8},{1,17},{9,25},{17,1},{25,9},{2,18},{10... | collective-permute-start | bytes 1671176 | tf_op jit(solution)/shard_map/ppermute | solution.py:32
  247.0 24.7 %collective-permute-start.33 = (bf16[128,2176]{1,0:T(8,128)(2,1)}, bf16[128,2176]{1,0:T(8,128)(2,1)S(1)}, u32[]{:S(2)}, u32[]{:S(2)}) collective-permute-start(bf16[128,2176]{1,0:T(8,128)(2,1)} %slice.683), channel_id=1, source_target_pairs={{0,8},{8,0},{16,24},{24,16},{1,9},{9,1},{17,25},{25,17},{2,10},{10... | collective-permute-start | bytes 1671176 | tf_op jit(solution)/shard_map/ppermute | solution.py:32
  253.3 16.7 %collective-permute-start.34 = (bf16[128,2048]{1,0:T(8,128)(2,1)S(1)}, bf16[128,2048]{1,0:T(8,128)(2,1)S(1)}, u32[]{:S(2)}, u32[]{:S(2)}) collective-permute-start(bf16[128,2048]{1,0:T(8,128)(2,1)S(1)} %get-tuple-element.319), channel_id=1, source_target_pairs={{0,16},{8,24},{16,0},{24,8},{1,17},{9,25},{17,1},{25,9},{2,18},{10... | collective-permute-start | bytes 1572872 | tf_op jit(solution)/shard_map/ppermute | solution.py:32
  254.4 16.4 %collective-permute-start.35 = (bf16[128,2048]{1,0:T(8,128)(2,1)S(1)}, bf16[128,2048]{1,0:T(8,128)(2,1)S(1)}, u32[]{:S(2)}, u32[]{:S(2)}) collective-permute-start(bf16[128,2048]{1,0:T(8,128)(2,1)S(1)} %get-tuple-element.320), channel_id=1, source_target_pairs={{0,8},{8,0},{16,24},{24,16},{1,9},{9,1},{17,25},{25,17},{2,10},{10... | collective-permute-start | bytes 1572872 | tf_op jit(solution)/shard_map/ppermute | solution.py:32
  255.3 16.5 %collective-permute-start.36 = (bf16[1024,2176]{1,0:T(8,128)(2,1)}, bf16[1024,2176]{1,0:T(8,128)(2,1)S(1)}, u32[]{:S(2)}, u32[]{:S(2)}) collective-permute-start(bf16[1024,2176]{1,0:T(8,128)(2,1)} %get-tuple-element.322), channel_id=1, source_target_pairs={{0,1},{1,0},{2,3},{3,2},{4,5},{5,4},{6,7},{7,6},{8,9},{9,8},{10,11... | collective-permute-start | bytes 13369352 | tf_op jit(solution)/shard_map/ppermute | solution.py:37
  274.5 32.2 %collective-permute-start.38 = (bf16[1024,2176]{1,0:T(8,128)(2,1)S(1)}, bf16[1024,2176]{1,0:T(8,128)(2,1)}, u32[]{:S(2)}, u32[]{:S(2)}) collective-permute-start(bf16[1024,2176]{1,0:T(8,128)(2,1)S(1)} %constant_dynamic-update-slice_fusion.10.cot_ref.refs_6_), channel_id=1, source_target_pairs={{0,1},{1,0},{2,3},{3,2},{4,5},{5,4},{6,7},{7,6},{8,9},{9,8},{10,11... | collective-permute-start | bytes 13369352 | tf_op jit(solution)/shard_map/ppermute | solution.py:37
  274.8 31.9 %collective-permute-start.37 = (bf16[1024,2048]{1,0:T(8,128)(2,1)}, bf16[1024,2048]{1,0:T(8,128)(2,1)}, u32[]{:S(2)}, u32[]{:S(2)}) collective-permute-start(bf16[1024,2048]{1,0:T(8,128)(2,1)} %constant_dynamic-update-slice_fusion.8.moe_ref.refs_2_), channel_id=1, source_target_pairs={{0,1},{1,0},{2,3},{3,2},{4,5},{5,4},{6,7},{7,6},{8,9},{9,8},{10,11... | collective-permute-start | bytes 12582920 | tf_op jit(solution)/shard_map/ppermute | solution.py:37
  275.0 27.1 %collective-permute-start.39 = (bf16[256,2176]{1,0:T(8,128)(2,1)}, bf16[256,2176]{1,0:T(8,128)(2,1)}, u32[]{:S(2)}, u32[]{:S(2)}) collective-permute-start(bf16[256,2176]{1,0:T(8,128)(2,1)} %get-tuple-element.330), channel_id=1, source_target_pairs={{0,8},{8,0},{16,24},{24,16},{1,9},{9,1},{17,25},{25,17},{2,10},{10... | collective-permute-start | bytes 3342344 | tf_op jit(solution)/shard_map/ppermute | solution.py:32
  275.9 28.5 %collective-permute-start.40 = (bf16[256,2176]{1,0:T(8,128)(2,1)}, bf16[256,2176]{1,0:T(8,128)(2,1)}, u32[]{:S(2)}, u32[]{:S(2)}) collective-permute-start(bf16[256,2176]{1,0:T(8,128)(2,1)} %get-tuple-element.332), channel_id=1, source_target_pairs={{0,16},{8,24},{16,0},{24,8},{1,17},{9,25},{17,1},{25,9},{2,18},{10... | collective-permute-start | bytes 3342344 | tf_op jit(solution)/shard_map/ppermute | solution.py:32
  306.7 20.6 %collective-permute-start.41 = (bf16[128,2176]{1,0:T(8,128)(2,1)}, bf16[128,2176]{1,0:T(8,128)(2,1)S(1)}, u32[]{:S(2)}, u32[]{:S(2)}) collective-permute-start(bf16[128,2176]{1,0:T(8,128)(2,1)} %get-tuple-element.337), channel_id=1, source_target_pairs={{0,16},{8,24},{16,0},{24,8},{1,17},{9,25},{17,1},{25,9},{2,18},{10... | collective-permute-start | bytes 1671176 | tf_op jit(solution)/shard_map/ppermute | solution.py:32
  307.8 19.6 %collective-permute-start.42 = (bf16[128,2176]{1,0:T(8,128)(2,1)}, bf16[128,2176]{1,0:T(8,128)(2,1)S(1)}, u32[]{:S(2)}, u32[]{:S(2)}) collective-permute-start(bf16[128,2176]{1,0:T(8,128)(2,1)} %get-tuple-element.339), channel_id=1, source_target_pairs={{0,8},{8,0},{16,24},{24,16},{1,9},{9,1},{17,25},{25,17},{2,10},{10... | collective-permute-start | bytes 1671176 | tf_op jit(solution)/shard_map/ppermute | solution.py:32
  327.6 26.9 %collective-permute-start.47 = (bf16[1024,2048]{1,0:T(8,128)(2,1)S(1)}, bf16[1024,2048]{1,0:T(8,128)(2,1)S(1)}, u32[]{:S(2)}, u32[]{:S(2)}) collective-permute-start(bf16[1024,2048]{1,0:T(8,128)(2,1)S(1)} %copy-done.48), channel_id=1, source_target_pairs={{0,1},{1,0},{2,3},{3,2},{4,5},{5,4},{6,7},{7,6},{8,9},{9,8},{10,11... | collective-permute-start | bytes 12582920 | tf_op jit(solution)/shard_map/ppermute | solution.py:37
  327.7 29.5 %collective-permute-start.46 = (bf16[1024,2176]{1,0:T(8,128)(2,1)}, bf16[1024,2176]{1,0:T(8,128)(2,1)S(1)}, u32[]{:S(2)}, u32[]{:S(2)}) collective-permute-start(bf16[1024,2176]{1,0:T(8,128)(2,1)} %get-tuple-element.355), channel_id=1, source_target_pairs={{0,1},{1,0},{2,3},{3,2},{4,5},{5,4},{6,7},{7,6},{8,9},{9,8},{10,11... | collective-permute-start | bytes 13369352 | tf_op jit(solution)/shard_map/ppermute | solution.py:37
  328.9 24.7 %collective-permute-start.44 = (bf16[64,2176]{1,0:T(8,128)(2,1)S(1)}, bf16[64,2176]{1,0:T(8,128)(2,1)S(1)}, u32[]{:S(2)}, u32[]{:S(2)}) collective-permute-start(bf16[64,2176]{1,0:T(8,128)(2,1)S(1)} %get-tuple-element.352), channel_id=1, source_target_pairs={{0,4},{1,5},{2,6},{3,7},{4,0},{5,1},{6,2},{7,3},{8,12},{9,13},{10,... | collective-permute-start | bytes 835592 | tf_op jit(solution)/shard_map/ppermute | solution.py:37
  329.0 24.5 %collective-permute-start.43 = (bf16[64,2176]{1,0:T(8,128)(2,1)S(1)}, bf16[64,2176]{1,0:T(8,128)(2,1)S(1)}, u32[]{:S(2)}, u32[]{:S(2)}) collective-permute-start(bf16[64,2176]{1,0:T(8,128)(2,1)S(1)} %get-tuple-element.351), channel_id=1, source_target_pairs={{0,2},{1,3},{2,0},{3,1},{4,6},{5,7},{6,4},{7,5},{8,10},{9,11},{10,... | collective-permute-start | bytes 835592 | tf_op jit(solution)/shard_map/ppermute | solution.py:37
  359.3 29.0 %collective-permute-start.50 = (bf16[1024,2048]{1,0:T(8,128)(2,1)}, bf16[1024,2048]{1,0:T(8,128)(2,1)}, u32[]{:S(2)}, u32[]{:S(2)}) collective-permute-start(bf16[1024,2048]{1,0:T(8,128)(2,1)} %convolution_convert_fusion), channel_id=1, source_target_pairs={{0,1},{1,0},{2,3},{3,2},{4,5},{5,4},{6,7},{7,6},{8,9},{9,8},{10,11... | collective-permute-start | bytes 12582920 | tf_op jit(solution)/shard_map/ppermute | solution.py:37
  360.1 27.2 %collective-permute-start.48 = (bf16[256,2176]{1,0:T(8,128)(2,1)}, bf16[256,2176]{1,0:T(8,128)(2,1)S(1)}, u32[]{:S(2)}, u32[]{:S(2)}) collective-permute-start(bf16[256,2176]{1,0:T(8,128)(2,1)} %get-tuple-element.364), channel_id=1, source_target_pairs={{0,8},{8,0},{16,24},{24,16},{1,9},{9,1},{17,25},{25,17},{2,10},{10... | collective-permute-start | bytes 3342344 | tf_op jit(solution)/shard_map/ppermute | solution.py:32
  361.1 27.0 %collective-permute-start.49 = (bf16[256,2176]{1,0:T(8,128)(2,1)}, bf16[256,2176]{1,0:T(8,128)(2,1)S(1)}, u32[]{:S(2)}, u32[]{:S(2)}) collective-permute-start(bf16[256,2176]{1,0:T(8,128)(2,1)} %get-tuple-element.366), channel_id=1, source_target_pairs={{0,16},{8,24},{16,0},{24,8},{1,17},{9,25},{17,1},{25,9},{2,18},{10... | collective-permute-start | bytes 3342344 | tf_op jit(solution)/shard_map/ppermute | solution.py:32
  393.6 26.6 %collective-permute-start.54 = (bf16[128,2176]{1,0:T(8,128)(2,1)S(1)}, bf16[128,2176]{1,0:T(8,128)(2,1)S(1)}, u32[]{:S(2)}, u32[]{:S(2)}) collective-permute-start(bf16[128,2176]{1,0:T(8,128)(2,1)S(1)} %get-tuple-element.375), channel_id=1, source_target_pairs={{0,16},{8,24},{16,0},{24,8},{1,17},{9,25},{17,1},{25,9},{2,18},{10... | collective-permute-start | bytes 1671176 | tf_op jit(solution)/shard_map/ppermute | solution.py:32
  396.0 23.2 %collective-permute-start.52 = (bf16[64,2048]{1,0:T(8,128)(2,1)S(1)}, bf16[64,2048]{1,0:T(8,128)(2,1)S(1)}, u32[]{:S(2)}, u32[]{:S(2)}) collective-permute-start(bf16[64,2048]{1,0:T(8,128)(2,1)S(1)} %convert_element_type.754), channel_id=1, source_target_pairs={{0,16},{8,24},{16,0},{24,8},{1,17},{9,25},{17,1},{25,9},{2,18},{10... | collective-permute-start | bytes 786440 | tf_op jit(solution)/shard_map/ppermute | solution.py:32
  397.1 22.1 %collective-permute-start.51 = (bf16[64,2048]{1,0:T(8,128)(2,1)S(1)}, bf16[64,2048]{1,0:T(8,128)(2,1)S(1)}, u32[]{:S(2)}, u32[]{:S(2)}) collective-permute-start(bf16[64,2048]{1,0:T(8,128)(2,1)S(1)} %convert_element_type.754), channel_id=1, source_target_pairs={{0,8},{8,0},{16,24},{24,16},{1,9},{9,1},{17,25},{25,17},{2,10},{10... | collective-permute-start | bytes 786440 | tf_op jit(solution)/shard_map/ppermute | solution.py:32
  398.1 22.9 %collective-permute-start.55 = (bf16[128,2176]{1,0:T(8,128)(2,1)S(1)}, bf16[128,2176]{1,0:T(8,128)(2,1)S(1)}, u32[]{:S(2)}, u32[]{:S(2)}) collective-permute-start(bf16[128,2176]{1,0:T(8,128)(2,1)S(1)} %get-tuple-element.377), channel_id=1, source_target_pairs={{0,8},{8,0},{16,24},{24,16},{1,9},{9,1},{17,25},{25,17},{2,10},{10... | collective-permute-start | bytes 1671176 | tf_op jit(solution)/shard_map/ppermute | solution.py:32
  423.6 22.2 %collective-permute-start.57 = (bf16[64,2176]{1,0:T(8,128)(2,1)}, bf16[64,2176]{1,0:T(8,128)(2,1)}, u32[]{:S(2)}, u32[]{:S(2)}) collective-permute-start(bf16[64,2176]{1,0:T(8,128)(2,1)} %get-tuple-element.388), channel_id=1, source_target_pairs={{0,4},{1,5},{2,6},{3,7},{4,0},{5,1},{6,2},{7,3},{8,12},{9,13},{10,... | collective-permute-start | bytes 835592 | tf_op jit(solution)/shard_map/ppermute | solution.py:37
  423.6 22.2 %collective-permute-start.56 = (bf16[64,2176]{1,0:T(8,128)(2,1)}, bf16[64,2176]{1,0:T(8,128)(2,1)}, u32[]{:S(2)}, u32[]{:S(2)}) collective-permute-start(bf16[64,2176]{1,0:T(8,128)(2,1)} %get-tuple-element.387), channel_id=1, source_target_pairs={{0,2},{1,3},{2,0},{3,1},{4,6},{5,7},{6,4},{7,5},{8,10},{9,11},{10,... | collective-permute-start | bytes 835592 | tf_op jit(solution)/shard_map/ppermute | solution.py:37
  426.3 23.4 %collective-permute-start.59 = (bf16[256,2048]{1,0:T(8,128)(2,1)}, bf16[256,2048]{1,0:T(8,128)(2,1)}, u32[]{:S(2)}, u32[]{:S(2)}) collective-permute-start(bf16[256,2048]{1,0:T(8,128)(2,1)} %get-tuple-element.398), channel_id=1, source_target_pairs={{0,8},{8,0},{16,24},{24,16},{1,9},{9,1},{17,25},{25,17},{2,10},{10... | collective-permute-start | bytes 3145736 | tf_op jit(solution)/shard_map/ppermute | solution.py:32
  428.8 23.6 %collective-permute-start.60 = (bf16[256,2048]{1,0:T(8,128)(2,1)}, bf16[256,2048]{1,0:T(8,128)(2,1)S(1)}, u32[]{:S(2)}, u32[]{:S(2)}) collective-permute-start(bf16[256,2048]{1,0:T(8,128)(2,1)} %get-tuple-element.400), channel_id=1, source_target_pairs={{0,16},{8,24},{16,0},{24,8},{1,17},{9,25},{17,1},{25,9},{2,18},{10... | collective-permute-start | bytes 3145736 | tf_op jit(solution)/shard_map/ppermute | solution.py:32
  456.4 17.9 %collective-permute-start.63 = (bf16[64,2048]{1,0:T(8,128)(2,1)S(1)}, bf16[64,2048]{1,0:T(8,128)(2,1)S(1)}, u32[]{:S(2)}, u32[]{:S(2)}) collective-permute-start(bf16[64,2048]{1,0:T(8,128)(2,1)S(1)} %get-tuple-element.530), channel_id=1, source_target_pairs={{0,24},{8,16},{16,8},{24,0},{1,25},{9,17},{17,9},{25,1},{2,26},{10... | collective-permute-start | bytes 786440 | tf_op jit(solution)/shard_map/ppermute | solution.py:32
  457.7 16.6 %collective-permute-start.62 = (bf16[64,2048]{1,0:T(8,128)(2,1)S(1)}, bf16[64,2048]{1,0:T(8,128)(2,1)S(1)}, u32[]{:S(2)}, u32[]{:S(2)}) collective-permute-start(bf16[64,2048]{1,0:T(8,128)(2,1)S(1)} %get-tuple-element.530), channel_id=1, source_target_pairs={{0,16},{8,24},{16,0},{24,8},{1,17},{9,25},{17,1},{25,9},{2,18},{10... | collective-permute-start | bytes 786440 | tf_op jit(solution)/shard_map/ppermute | solution.py:32
  489.7 119.2 %reduce-scatter.5.cloned.1.call-start = ((), (), s32[]{:S(2)}) async-start(), calls=%async_computation.3 | async-start | bytes 4718592 | tf_op jit(solution)/shard_map/reduce_scatter | solution.py:837
  521.8 186.2 %all-gather.2.cloned.1.call-start = ((), (), s32[]{:S(2)}) async-start(), calls=%async_computation.4 | async-start | bytes 9437184 | tf_op jit(solution)/shard_map/all_gather | solution.py:855
  526.7 20.6 %collective-permute-start.72 = (bf16[128,2048]{1,0:T(8,128)(2,1)S(1)}, bf16[128,2048]{1,0:T(8,128)(2,1)S(1)}, u32[]{:S(2)}, u32[]{:S(2)}) collective-permute-start(bf16[128,2048]{1,0:T(8,128)(2,1)S(1)} %pad_maximum_fusion.10), channel_id=1, source_target_pairs={{0,2},{1,3},{2,0},{3,1},{4,6},{5,7},{6,4},{7,5},{8,10},{9,11},{10,... | collective-permute-start | bytes 1572872 | tf_op jit(solution)/shard_map/ppermute | solution.py:37
  528.8 20.0 %collective-permute-start.76 = (bf16[64,2048]{1,0:T(8,128)(2,1)S(1)}, bf16[64,2048]{1,0:T(8,128)(2,1)S(1)}, u32[]{:S(2)}, u32[]{:S(2)}) collective-permute-start(bf16[64,2048]{1,0:T(8,128)(2,1)S(1)} %get-tuple-element.600), channel_id=1, source_target_pairs={{0,24},{8,16},{16,8},{24,0},{1,25},{9,17},{17,9},{25,1},{2,26},{10... | collective-permute-start | bytes 786440 | tf_op jit(solution)/shard_map/ppermute | solution.py:32
  530.5 20.4 %collective-permute-start.75 = (bf16[64,2048]{1,0:T(8,128)(2,1)S(1)}, bf16[64,2048]{1,0:T(8,128)(2,1)S(1)}, u32[]{:S(2)}, u32[]{:S(2)}) collective-permute-start(bf16[64,2048]{1,0:T(8,128)(2,1)S(1)} %get-tuple-element.601), channel_id=1, source_target_pairs={{0,16},{8,24},{16,0},{24,8},{1,17},{9,25},{17,1},{25,9},{2,18},{10... | collective-permute-start | bytes 786440 | tf_op jit(solution)/shard_map/ppermute | solution.py:32
  531.6 19.3 %collective-permute-start.74 = (bf16[64,2048]{1,0:T(8,128)(2,1)S(1)}, bf16[64,2048]{1,0:T(8,128)(2,1)S(1)}, u32[]{:S(2)}, u32[]{:S(2)}) collective-permute-start(bf16[64,2048]{1,0:T(8,128)(2,1)S(1)} %get-tuple-element.599), channel_id=1, source_target_pairs={{0,8},{8,0},{16,24},{24,16},{1,9},{9,1},{17,25},{25,17},{2,10},{10... | collective-permute-start | bytes 786440 | tf_op jit(solution)/shard_map/ppermute | solution.py:32
  532.4 29.6 %collective-permute-start.77 = (bf16[256,2048]{1,0:T(8,128)(2,1)S(1)}, bf16[256,2048]{1,0:T(8,128)(2,1)S(1)}, u32[]{:S(2)}, u32[]{:S(2)}) collective-permute-start(bf16[256,2048]{1,0:T(8,128)(2,1)S(1)} %copy-done.27), channel_id=1, source_target_pairs={{0,8},{8,0},{16,24},{24,16},{1,9},{9,1},{17,25},{25,17},{2,10},{10... | collective-permute-start | bytes 3145736 | tf_op jit(solution)/shard_map/ppermute | solution.py:32
  547.3 23.6 %collective-permute-start.78 = (bf16[256,2048]{1,0:T(8,128)(2,1)S(1)}, bf16[256,2048]{1,0:T(8,128)(2,1)S(1)}, u32[]{:S(2)}, u32[]{:S(2)}) collective-permute-start(bf16[256,2048]{1,0:T(8,128)(2,1)S(1)} %copy-done.26), channel_id=1, source_target_pairs={{0,16},{8,24},{16,0},{24,8},{1,17},{9,25},{17,1},{25,9},{2,18},{10... | collective-permute-start | bytes 3145736 | tf_op jit(solution)/shard_map/ppermute | solution.py:32
  575.6 16.6 %collective-permute-start.82 = (bf16[128,2048]{1,0:T(8,128)(2,1)S(1)}, bf16[128,2048]{1,0:T(8,128)(2,1)S(1)}, u32[]{:S(2)}, u32[]{:S(2)}) collective-permute-start(bf16[128,2048]{1,0:T(8,128)(2,1)S(1)} %get-tuple-element.460), channel_id=1, source_target_pairs={{0,16},{8,24},{16,0},{24,8},{1,17},{9,25},{17,1},{25,9},{2,18},{10... | collective-permute-start | bytes 1572872 | tf_op jit(solution)/shard_map/ppermute | solution.py:32
  677.3 18.8 %collective-permute-start.87 = (bf16[20,2048]{1,0:T(8,128)(2,1)S(1)}, bf16[20,2048]{1,0:T(8,128)(2,1)S(1)}, u32[]{:S(2)}, u32[]{:S(2)}) collective-permute-start(bf16[20,2048]{1,0:T(8,128)(2,1)S(1)} %add_convert_fusion.52), channel_id=1, source_target_pairs={{0,4},{1,5},{2,6},{3,7},{4,0},{5,1},{6,2},{7,3},{8,12},{9,13},{10,... | collective-permute-start | bytes 245768 | tf_op jit(solution)/shard_map/ppermute | solution.py:37
  677.3 21.1 %collective-permute-start.86 = (bf16[20,2048]{1,0:T(8,128)(2,1)S(1)}, bf16[20,2048]{1,0:T(8,128)(2,1)S(1)}, u32[]{:S(2)}, u32[]{:S(2)}) collective-permute-start(bf16[20,2048]{1,0:T(8,128)(2,1)S(1)} %add_convert_fusion.52), channel_id=1, source_target_pairs={{0,2},{1,3},{2,0},{3,1},{4,6},{5,7},{6,4},{7,5},{8,10},{9,11},{10,... | collective-permute-start | bytes 245768 | tf_op jit(solution)/shard_map/ppermute | solution.py:37
  679.4 19.0 %collective-permute-start.91 = (bf16[64,2048]{1,0:T(8,128)(2,1)S(1)}, bf16[64,2048]{1,0:T(8,128)(2,1)S(1)}, u32[]{:S(2)}, u32[]{:S(2)}) collective-permute-start(bf16[64,2048]{1,0:T(8,128)(2,1)S(1)} %get-tuple-element.593), channel_id=1, source_target_pairs={{0,24},{8,16},{16,8},{24,0},{1,25},{9,17},{17,9},{25,1},{2,26},{10... | collective-permute-start | bytes 786440 | tf_op jit(solution)/shard_map/ppermute | solution.py:32
  681.4 17.0 %collective-permute-start.90 = (bf16[64,2048]{1,0:T(8,128)(2,1)S(1)}, bf16[64,2048]{1,0:T(8,128)(2,1)S(1)}, u32[]{:S(2)}, u32[]{:S(2)}) collective-permute-start(bf16[64,2048]{1,0:T(8,128)(2,1)S(1)} %get-tuple-element.594), channel_id=1, source_target_pairs={{0,16},{8,24},{16,0},{24,8},{1,17},{9,25},{17,1},{25,9},{2,18},{10... | collective-permute-start | bytes 786440 | tf_op jit(solution)/shard_map/ppermute | solution.py:32
  (85 other events, 898.0 us)
Sparse Core Ops, SparseCore 0:
  489.8 57.4 reduce-scatter.2
  550.1 49.6 reduce-scatter.4
  611.3 96.6 all-gather.1

commit v6 on v5

--- a/solution.py
+++ b/solution.py
@@ -97,23 +97,33 @@
     return sync(near[..., :n, :], far[..., n:, :])
 
 
-def gather_plane_far(rows, near, far, sends=None):
+def far_base(rows, near, far):
     n = rows.shape[-2] // 2
-
-    def top(value):
-        return value[..., :n, :]
-
-    def low(value):
-        return value[..., n:, :]
-
-    sent_a, sent_b = sends or far_sends(near, far)
-    far_a, far_b = swap_tp(sent_a, 2), swap_tp(sent_b, 1)
-    base = jnp.concatenate(
-        [top(rows), top(far), top(near), top(rows), low(rows), low(near), low(far), top(rows)], axis=-2
-    )
-    base = lax.optimization_barrier(base)
+    (top, low), (near_top, near_low), (far_top, far_low) = (
+        (value[..., :n, :], value[..., n:, :]) for value in (rows, near, far)
+    )
+    base = jnp.concatenate([top, far_top, near_top, top, low, near_low, far_low, top], axis=-2)
+    return lax.optimization_barrier(base)
+
+
+def far_join(base, far_a, far_b):
+    n = far_a.shape[-2]
     base = lax.dynamic_update_slice_in_dim(base, far_a, 3 * n, axis=-2)
     return lax.dynamic_update_slice_in_dim(base, far_b, 7 * n, axis=-2)
+
+
+def gather_plane_far(rows, near, far, sends=None):
+    sent_a, sent_b = sends or far_sends(near, far)
+    return far_join(far_base(rows, near, far), swap_tp(sent_a, 2), swap_tp(sent_b, 1))
+
+
+def gather_pair_far(early, early_base, late):
+    first_a, first_b = swap_tp(early[0], 2), swap_tp(early[1], 1)
+    rows, near, far = late
+    sent_a, sent_b = far_sends(near, far)
+    late_a, late_b = swap_tp(sent_a, 2), swap_tp(sent_b, 1)
+    first_a, rows, near, far = sync(first_a, rows, near, far)
+    return far_join(early_base, first_a, first_b), far_join(far_base(rows, near, far), late_a, late_b)
 
 
 def cut(rows, count):
@@ -689,12 +699,11 @@
     moe_near0 = gather_plane_near(moe_z0)
     moe_z1 = gather_outer(moe_own1, zone)
 
-    cot_sends0 = far_sends(*cot_near0)
+    cot_sends0 = [*far_sends(*cot_near0), far_base(cot_z0, *cot_near0)]
     moe_z0, moe_z1, cot_z0, cot_z1, *near = sync(
         moe_z0, moe_z1, cot_z0, cot_z1, *cot_near0, *moe_near0, *cot_sends0
     )
-    cot_half0 = gather_plane_far(cot_z0, *near[:2], near[4:])
-    moe_half0 = gather_plane_far(moe_z0, *near[2:4])
+    cot_half0, moe_half0 = gather_pair_far(near[4:6], near[6], (moe_z0, *near[2:4]))
 
     moe_half0, cot_half0, moe_z1, cot_z1 = sync(moe_half0, cot_half0, moe_z1, cot_z1)
     moe_other0, cot_other0 = swap_dp(moe_half0, 1), swap_dp(cot_half0, 1)

time: 740 us -> 739 us (level)
    unnamed x129 -> x131, local copies, waits for them, and re-layouts: 22.2 us -> 23.6 us
  transfers between devices with their start and end apart: 96 -> 96, of which waited for: 45 -> 44; matrix products, arithmetic and copies ran while one was open for 18% -> 18% of each run, Pallas kernels for 22% -> 22%
where the time goes in v6:
time: 739 us; the launch traced here: 729 us
  waiting for transfers between devices  254 us (34%)
  Pallas kernels  173 us (23%)
  starting transfers between devices  115 us (16%)
  other arithmetic  77.9 us (11%)
  local copies, waits for them, and re-layouts  70.4 us (10%)
  matrix products  22.9 us (3%)
  between operations  15.3 us (2%)
    pallas_call x14, Pallas kernels, call_kernel(): pl.pallas_call(body, out_shape=outs, grid=grid, in_specs=in_specs or [who...  173 us
    ppermute x62, waiting for transfers between devices, swap_tp(): return lax.ppermute(value, 'tp', [(i, i ^ bits) for i in range(size)])  148 us
    ppermute x31, waiting for transfers between devices, swap_dp(): return lax.ppermute(value, 'dp', [(i, i ^ bits) for i in range(size)])  105 us
    ppermute x62, starting transfers between devices, swap_tp(): return lax.ppermute(value, 'tp', [(i, i ^ bits) for i in range(size)])  71.3 us
    ppermute x31, starting transfers between devices, swap_dp(): return lax.ppermute(value, 'dp', [(i, i ^ bits) for i in range(size)])  43.5 us
    convert_element_type x20, other arithmetic, add_pieces(): return [add_low(one, two).astype(BF) for one, two in zip(left, right)]  25.4 us
    unnamed x131, local copies, waits for them, and re-layouts  23.6 us
    dot_general x4, matrix products, mix(): return jnp.dot(ran[1], down, preferred_element_type=F32).astype(BF)  17.6 us
  transfers between devices with their start and end apart: 96, of which 44 were waited for; matrix products, arithmetic and copies ran while one was open for 18% of the time, Pallas kernels for 22%

profile of v6, /device:TPU:0, one launch (start us, length us, event | category | flops | bytes accessed | tf_op | source)
XLA Modules:
  0.0 729.3 jit_solution(4659369133685870074)
XLA Ops:
  7.2 4.0 collective-permute-start.2
  17.5 2.6 collective-permute-start.7
  20.5 4.7 fusion.27
  28.2 2.7 pad_maximum_fusion.1.gate_up_ref
  30.9 3.8 collective-permute-done.1
  35.0 2.7 pad_maximum_fusion.3
  37.7 9.4 %shard_map.195 = (bf16[512,2048]{1,0:T(8,128)(2,1)}, f32[512,1536]{1,0:T(8,128)}, f32[512,128]{1,0:T(8,128)}) custom-call(bf16[512,2048]{1,0:T(8,128)(2,1)} %bitcast.170, f32[1,2048]{1,0:T(1,128)} %bitcast.194, bf16[3,2048,512]{2,1,0:T(8,128)(2,1)} %bitcast.159), custom_call_target="tpu_custom_call" | custom-call | flops 402653184 | bytes 786432 | tf_op jit(solution)/shard_map/pallas_call | solution.py:171
  53.6 3.1 collective-permute-done.3
  56.7 3.6 collective-permute-start.8
  63.3 3.0 collective-permute-done.4
  67.0 7.9 %shard_map.196 = (bf16[2,256,1536]{2,1,0:T(8,128)(2,1)}, f32[2,4,256,256]{3,2,1,0:T(8,128)}, bf16[2,256,512]{2,1,0:T(8,128)(2,1)}, bf16[2,256,2048]{2,1,0:T(8,128)(2,1)}) custom-call(f32[2,256,1536]{2,1,0:T(8,128)} %bitcast.148, f32[2,256,128]{2,1,0:T(8,128)} %fusion.7.squares_ref, f32[2,512]{1,0:T(2,128)} %gain_ref.5, ...), custom_call_target="tpu_custom_call" | custom-call | flops 167772160 | bytes 2097152 | tf_op jit(solution)/shard_map/pallas_call | solution.py:171
  82.7 10.1 %collective-permute-done.11 = bf16[2,64,2048]{2,1,0:T(8,128)(2,1)S(1)} collective-permute-done((bf16[2,64,2048]{2,1,0:T(8,128)(2,1)S(1)}, bf16[2,64,2048]{2,1,0:T(8,128)(2,1)S(1)}, u32[]{:S(2)}, u32[]{:S(2)}) %collective-permute-start.11) | collective-permute-done | bytes 524320 | tf_op jit(solution)/shard_map/ppermute | solution.py:32
  92.7 9.3 %collective-permute-done.10 = bf16[2,64,2048]{2,1,0:T(8,128)(2,1)S(1)} collective-permute-done((bf16[2,64,2048]{2,1,0:T(8,128)(2,1)S(1)}, bf16[2,64,2048]{2,1,0:T(8,128)(2,1)S(1)}, u32[]{:S(2)}, u32[]{:S(2)}) %collective-permute-start.10) | collective-permute-done | bytes 524320 | tf_op jit(solution)/shard_map/ppermute | solution.py:32
  105.5 3.8 collective-permute-start.14
  109.4 6.8 collective-permute-start.13
  116.2 15.4 %collective-permute-done.13 = bf16[64,2048]{1,0:T(8,128)(2,1)S(1)} collective-permute-done((bf16[64,2048]{1,0:T(8,128)(2,1)S(1)}, bf16[64,2048]{1,0:T(8,128)(2,1)S(1)}, u32[]{:S(2)}, u32[]{:S(2)}) %collective-permute-start.13) | collective-permute-done | bytes 262176 | tf_op jit(solution)/shard_map/ppermute | solution.py:37
  131.8 3.6 collective-permute-start.19
  144.6 13.6 %collective-permute-done.18 = bf16[64,2048]{1,0:T(8,128)(2,1)S(1)} collective-permute-done((bf16[64,2048]{1,0:T(8,128)(2,1)S(1)}, bf16[64,2048]{1,0:T(8,128)(2,1)S(1)}, u32[]{:S(2)}, u32[]{:S(2)}) %collective-permute-start.18) | collective-permute-done | bytes 262176 | tf_op jit(solution)/shard_map/ppermute | solution.py:37
  165.1 11.3 %collective-permute-done.22 = bf16[128,2176]{1,0:T(8,128)(2,1)S(1)} collective-permute-done((bf16[128,2176]{1,0:T(8,128)(2,1)S(1)}, bf16[128,2176]{1,0:T(8,128)(2,1)S(1)}, u32[]{:S(2)}, u32[]{:S(2)}) %collective-permute-start.22) | collective-permute-done | bytes 557088 | tf_op jit(solution)/shard_map/ppermute | solution.py:32
  190.5 18.0 %shard_map.197 = (bf16[1024,2176]{1,0:T(8,128)(2,1)}, bf16[1024,512]{1,0:T(8,128)(2,1)}, bf16[1024,1024]{1,0:T(8,128)(2,1)}) custom-call(s32[1]{0:T(128)} %bitcast.17.ids_ref, bf16[1024,2048]{1,0:T(8,128)(2,1)} %constant_dynamic-update-slice_fusion.14.moe_ref.refs_0_, bf16[1024,2176]{1,0:T(8,128)(2,1)} %constant_dynamic-update-slice_fusion.12.cot_ref.refs_4_, ...), custom_call_target="tpu_custom_call" | custom-call | flops 1342177280 | bytes 1572864 | tf_op jit(solution)/shard_map/pallas_call | solution.py:171
  208.5 6.6 collective-permute-done.28
  222.1 18.1 %shard_map.198 = (bf16[1024,2176]{1,0:T(8,128)(2,1)}, bf16[1024,512]{1,0:T(8,128)(2,1)}, bf16[1024,1024]{1,0:T(8,128)(2,1)}) custom-call(s32[1]{0:T(128)} %bitcast.17.ids_ref, bf16[1024,2048]{1,0:T(8,128)(2,1)} %collective-permute-done.26.moe_ref.refs_1_, bf16[1024,2176]{1,0:T(8,128)(2,1)} %collective-permute-done.27.cot_ref.refs_5_, ...), custom_call_target="tpu_custom_call" | custom-call | flops 1342177280 | bytes 1572864 | tf_op jit(solution)/shard_map/pallas_call | solution.py:171
  251.2 4.4 convolution_convert_fusion.3
  260.3 4.4 convolution_convert_fusion.2
  267.8 2.6 add_convert_fusion.4
  273.1 17.9 %shard_map.199 = (bf16[1024,2176]{1,0:T(8,128)(2,1)}, bf16[1024,512]{1,0:T(8,128)(2,1)}, bf16[1024,1024]{1,0:T(8,128)(2,1)}) custom-call(s32[1]{0:T(128)} %bitcast.17.ids_ref, bf16[1024,2048]{1,0:T(8,128)(2,1)} %constant_dynamic-update-slice_fusion.8.moe_ref.refs_2_, bf16[1024,2176]{1,0:T(8,128)(2,1)} %copy-done.4, bf16[2048,128]{1,0:T(8,128)(2,1)} %pad.17.router_ref, ...), custom_call_target="tpu_custom_call" | custom-call | flops 1342177280 | bytes 1572864 | tf_op jit(solution)/shard_map/pallas_call | solution.py:171
  291.0 6.9 collective-permute-done.39
  304.6 18.5 %shard_map.200 = (bf16[1024,2176]{1,0:T(8,128)(2,1)}, bf16[1024,512]{1,0:T(8,128)(2,1)}, bf16[1024,1024]{1,0:T(8,128)(2,1)}) custom-call(s32[1]{0:T(128)} %bitcast.17.ids_ref, bf16[1024,2048]{1,0:T(8,128)(2,1)} %collective-permute-done.37.moe_ref.refs_3_, bf16[1024,2176]{1,0:T(8,128)(2,1)} %collective-permute-done.38.cot_ref.refs_7_, ...), custom_call_target="tpu_custom_call" | custom-call | flops 1342177280 | bytes 1572864 | tf_op jit(solution)/shard_map/pallas_call | solution.py:171
  324.0 3.4 collective-permute-start.45
  328.4 4.4 convolution_convert_fusion.1
  332.9 4.4 convolution_convert_fusion
  337.3 14.4 %collective-permute-done.44 = bf16[64,2176]{1,0:T(8,128)(2,1)S(1)} collective-permute-done((bf16[64,2176]{1,0:T(8,128)(2,1)S(1)}, bf16[64,2176]{1,0:T(8,128)(2,1)S(1)}, u32[]{:S(2)}, u32[]{:S(2)}) %collective-permute-start.44) | collective-permute-done | bytes 278560 | tf_op jit(solution)/shard_map/ppermute | solution.py:37
  352.7 2.6 add_convert_fusion.12
  364.4 21.0 %collective-permute-done.48 = bf16[256,2176]{1,0:T(8,128)(2,1)S(1)} collective-permute-done((bf16[256,2176]{1,0:T(8,128)(2,1)}, bf16[256,2176]{1,0:T(8,128)(2,1)S(1)}, u32[]{:S(2)}, u32[]{:S(2)}) %collective-permute-start.48) | collective-permute-done | bytes 1114144 | tf_op jit(solution)/shard_map/ppermute | solution.py:32
  387.6 4.1 add_convert_fusion.8
  397.3 5.9 collective-permute-done.53
  403.2 14.0 %collective-permute-done.52 = bf16[64,2048]{1,0:T(8,128)(2,1)S(1)} collective-permute-done((bf16[64,2048]{1,0:T(8,128)(2,1)S(1)}, bf16[64,2048]{1,0:T(8,128)(2,1)S(1)}, u32[]{:S(2)}, u32[]{:S(2)}) %collective-permute-start.52) | collective-permute-done | bytes 262176 | tf_op jit(solution)/shard_map/ppermute | solution.py:32
  428.1 7.1 shard_map.201
  435.3 9.3 %collective-permute-done.57 = bf16[64,2176]{1,0:T(8,128)(2,1)} collective-permute-done((bf16[64,2176]{1,0:T(8,128)(2,1)}, bf16[64,2176]{1,0:T(8,128)(2,1)}, u32[]{:S(2)}, u32[]{:S(2)}) %collective-permute-start.57) | collective-permute-done | bytes 278560 | tf_op jit(solution)/shard_map/ppermute | solution.py:37
  447.8 2.6 add_convert_fusion.30
  459.0 3.2 collective-permute-done.65
  463.7 6.3 collective-permute-done.64
  473.8 7.0 shard_map.202
  480.8 7.3 shard_map.203
  494.5 6.8 shard_map.204
  502.1 2.9 collective-permute-done.70
  506.8 7.0 shard_map.205
  513.7 6.5 shard_map.206
  531.8 14.4 %collective-permute-done.72 = bf16[128,2048]{1,0:T(8,128)(2,1)S(1)} collective-permute-done((bf16[128,2048]{1,0:T(8,128)(2,1)S(1)}, bf16[128,2048]{1,0:T(8,128)(2,1)S(1)}, u32[]{:S(2)}, u32[]{:S(2)}) %collective-permute-start.72) | collective-permute-done | bytes 524320 | tf_op jit(solution)/shard_map/ppermute | solution.py:37
  550.9 5.2 collective-permute-done.73
  557.0 3.0 collective-permute-done.77
  560.4 9.7 %collective-permute-done.78 = bf16[256,2048]{1,0:T(8,128)(2,1)S(1)} collective-permute-done((bf16[256,2048]{1,0:T(8,128)(2,1)S(1)}, bf16[256,2048]{1,0:T(8,128)(2,1)S(1)}, u32[]{:S(2)}, u32[]{:S(2)}) %collective-permute-start.78) | collective-permute-done | bytes 1048608 | tf_op jit(solution)/shard_map/ppermute | solution.py:32
  579.2 2.7 collective-permute-done.80
  583.0 8.6 %collective-permute-done.82 = bf16[128,2048]{1,0:T(8,128)(2,1)S(1)} collective-permute-done((bf16[128,2048]{1,0:T(8,128)(2,1)S(1)}, bf16[128,2048]{1,0:T(8,128)(2,1)S(1)}, u32[]{:S(2)}, u32[]{:S(2)}) %collective-permute-start.82) | collective-permute-done | bytes 524320 | tf_op jit(solution)/shard_map/ppermute | solution.py:32
  593.4 14.0 %collective-permute-done.85 = bf16[128,2048]{1,0:T(8,128)(2,1)S(1)} collective-permute-done((bf16[128,2048]{1,0:T(8,128)(2,1)S(1)}, bf16[128,2048]{1,0:T(8,128)(2,1)S(1)}, u32[]{:S(2)}, u32[]{:S(2)}) %collective-permute-start.85) | collective-permute-done | bytes 524320 | tf_op jit(solution)/shard_map/ppermute | solution.py:37
  609.9 24.6 %shard_map.207 = f32[2048,1024]{1,0:T(8,128)} custom-call(bf16[1024,2048]{1,0:T(8,128)(2,1)} %constant_dynamic-update-slice_fusion.14.moe_ref.refs_0_, bf16[1024,2048]{1,0:T(8,128)(2,1)} %collective-permute-done.26.moe_ref.refs_1_, bf16[1024,2048]{1,0:T(8,128)(2,1)} %constant_dynamic-update-slice_fusion.8.moe_ref.refs_2_, ...), custom_call_target="tpu_custom_call" | custom-call | flops 2147483648 | bytes 4194304 | tf_op jit(solution)/shard_map/pallas_call | solution.py:171
  634.5 11.7 %reshape.430 = f32[2048,2,2,256]{3,2,1,0:T(2,128)} reshape(f32[2048,1024]{1,0:T(8,128)} %shard_map.207) | data formatting | bytes 16777216 | tf_op jit(solution)/shard_map/reshape | solution.py:880
  646.3 17.2 %shard_map.208 = f32[512,2048]{1,0:T(8,128)} custom-call(bf16[1024,512]{1,0:T(8,128)(2,1)} %get-tuple-element.486.refs_0_, bf16[1024,512]{1,0:T(8,128)(2,1)} %get-tuple-element.487.refs_1_, bf16[1024,512]{1,0:T(8,128)(2,1)} %get-tuple-element.488.refs_2_, bf16[1024,512]{1,0:T(8,128)(2,1)} %get-tuple-element.489.refs_3_, ...), custom_call_target="tpu_custom_call" | custom-call | flops 1073741824 | bytes 3145728 | tf_op jit(solution)/shard_map/pallas_call | solution.py:171
  663.4 5.5 slice_bitcast_fusion.1
  669.0 4.8 pad_maximum_fusion
  685.0 10.0 %collective-permute-done.87 = bf16[20,2048]{1,0:T(8,128)(2,1)S(1)} collective-permute-done((bf16[20,2048]{1,0:T(8,128)(2,1)S(1)}, bf16[20,2048]{1,0:T(8,128)(2,1)S(1)}, u32[]{:S(2)}, u32[]{:S(2)}) %collective-permute-start.87) | collective-permute-done | bytes 81952 | tf_op jit(solution)/shard_map/ppermute | solution.py:37
  699.0 5.6 collective-permute-done.92
  710.4 9.4 %convert_bitcast_fusion = f32[2048,3,512]{2,0,1:T(8,128)} fusion(bf16[4,2048,512]{2,1,0:T(8,128)(2,1)} %bitcast.171), kind=kLoop, calls=%fused_computation | loop fusion | flops 3145728 | bytes 18874368 | tf_op jit(solution)/shard_map/transpose | solution.py:892
  719.8 2.6 maximum_convert_fusion
  (423 shorter events, 205.9 us)
Async XLA Ops:
  7.2 600.4 %reduce-scatter.3.cloned.1.call-start = ((), (), s32[]{:S(2)}) async-start(), calls=%async_computation.2 | async-start | bytes 4718592 | tf_op jit(solution)/shard_map/reduce_scatter | solution.py:836
  7.2 23.7 %collective-permute-start.2 = (bf16[2,64,2048]{2,1,0:T(8,128)(2,1)}, bf16[2,64,2048]{2,1,0:T(8,128)(2,1)S(1)}, u32[]{:S(2)}, u32[]{:S(2)}) collective-permute-start(bf16[2,64,2048]{2,1,0:T(8,128)(2,1)} %bitcast.176), channel_id=1, source_target_pairs={{0,24},{8,16},{16,8},{24,0},{1,25},{9,17},{17,9},{25,1},{2,26},{10... | collective-permute-start | bytes 1572872 | tf_op jit(solution)/shard_map/ppermute | solution.py:32
  11.2 23.5 %collective-permute-start.1 = (bf16[2,64,2048]{2,1,0:T(8,128)(2,1)}, bf16[2,64,2048]{2,1,0:T(8,128)(2,1)}, u32[]{:S(2)}, u32[]{:S(2)}) collective-permute-start(bf16[2,64,2048]{2,1,0:T(8,128)(2,1)} %bitcast.177), channel_id=1, source_target_pairs={{0,16},{8,24},{16,0},{24,8},{1,17},{9,25},{17,1},{25,9},{2,18},{10... | collective-permute-start | bytes 1572872 | tf_op jit(solution)/shard_map/ppermute | solution.py:32
  11.7 23.3 %collective-permute-start = (bf16[2,64,2048]{2,1,0:T(8,128)(2,1)}, bf16[2,64,2048]{2,1,0:T(8,128)(2,1)}, u32[]{:S(2)}, u32[]{:S(2)}) collective-permute-start(bf16[2,64,2048]{2,1,0:T(8,128)(2,1)} %bitcast.178), channel_id=1, source_target_pairs={{0,8},{8,0},{16,24},{24,16},{1,9},{9,1},{17,25},{25,17},{2,10},{10... | collective-permute-start | bytes 1572872 | tf_op jit(solution)/shard_map/ppermute | solution.py:32
  15.4 59.5 %collective-permute-start.6 = (bf16[2,64,2176]{2,1,0:T(8,128)(2,1)S(1)}, bf16[2,64,2176]{2,1,0:T(8,128)(2,1)S(1)}, u32[]{:S(2)}, u32[]{:S(2)}) collective-permute-start(bf16[2,64,2176]{2,1,0:T(8,128)(2,1)S(1)} %pad_maximum_fusion.9), channel_id=1, source_target_pairs={{0,2},{1,3},{2,0},{3,1},{4,6},{5,7},{6,4},{7,5},{8,10},{9,11},{10,... | collective-permute-start | bytes 1671176 | tf_op jit(solution)/shard_map/ppermute | solution.py:37
  17.5 57.5 %collective-permute-start.7 = (bf16[2,64,2176]{2,1,0:T(8,128)(2,1)S(1)}, bf16[2,64,2176]{2,1,0:T(8,128)(2,1)S(1)}, u32[]{:S(2)}, u32[]{:S(2)}) collective-permute-start(bf16[2,64,2176]{2,1,0:T(8,128)(2,1)S(1)} %pad_maximum_fusion.9), channel_id=1, source_target_pairs={{0,4},{1,5},{2,6},{3,7},{4,0},{5,1},{6,2},{7,3},{8,12},{9,13},{10,... | collective-permute-start | bytes 1671176 | tf_op jit(solution)/shard_map/ppermute | solution.py:37
  56.7 18.2 %collective-permute-start.8 = (bf16[2,64,2176]{2,1,0:T(8,128)(2,1)S(1)}, bf16[2,64,2176]{2,1,0:T(8,128)(2,1)S(1)}, u32[]{:S(2)}, u32[]{:S(2)}) collective-permute-start(bf16[2,64,2176]{2,1,0:T(8,128)(2,1)S(1)} %pad_maximum_fusion.9), channel_id=1, source_target_pairs={{0,6},{1,7},{2,4},{3,5},{4,2},{5,3},{6,0},{7,1},{8,14},{9,15},{10,... | collective-permute-start | bytes 1671176 | tf_op jit(solution)/shard_map/ppermute | solution.py:37
  78.4 23.6 %collective-permute-start.10 = (bf16[2,64,2048]{2,1,0:T(8,128)(2,1)S(1)}, bf16[2,64,2048]{2,1,0:T(8,128)(2,1)S(1)}, u32[]{:S(2)}, u32[]{:S(2)}) collective-permute-start(bf16[2,64,2048]{2,1,0:T(8,128)(2,1)S(1)} %get-tuple-element.266), channel_id=1, source_target_pairs={{0,16},{8,24},{16,0},{24,8},{1,17},{9,25},{17,1},{25,9},{2,18},{10... | collective-permute-start | bytes 1572872 | tf_op jit(solution)/shard_map/ppermute | solution.py:32
  78.7 24.1 %collective-permute-start.9 = (bf16[2,64,2048]{2,1,0:T(8,128)(2,1)S(1)}, bf16[2,64,2048]{2,1,0:T(8,128)(2,1)S(1)}, u32[]{:S(2)}, u32[]{:S(2)}) collective-permute-start(bf16[2,64,2048]{2,1,0:T(8,128)(2,1)S(1)} %get-tuple-element.265), channel_id=1, source_target_pairs={{0,8},{8,0},{16,24},{24,16},{1,9},{9,1},{17,25},{25,17},{2,10},{10... | collective-permute-start | bytes 1572872 | tf_op jit(solution)/shard_map/ppermute | solution.py:32
  80.6 51.2 %collective-permute-start.15 = (bf16[256,2176]{1,0:T(8,128)(2,1)S(1)}, bf16[256,2176]{1,0:T(8,128)(2,1)S(1)}, u32[]{:S(2)}, u32[]{:S(2)}) collective-permute-start(bf16[256,2176]{1,0:T(8,128)(2,1)S(1)} %get-tuple-element.271), channel_id=1, source_target_pairs={{0,8},{8,0},{16,24},{24,16},{1,9},{9,1},{17,25},{25,17},{2,10},{10... | collective-permute-start | bytes 3342344 | tf_op jit(solution)/shard_map/ppermute | solution.py:32
  81.0 50.8 %collective-permute-start.16 = (bf16[256,2176]{1,0:T(8,128)(2,1)S(1)}, bf16[256,2176]{1,0:T(8,128)(2,1)S(1)}, u32[]{:S(2)}, u32[]{:S(2)}) collective-permute-start(bf16[256,2176]{1,0:T(8,128)(2,1)S(1)} %get-tuple-element.271), channel_id=1, source_target_pairs={{0,16},{8,24},{16,0},{24,8},{1,17},{9,25},{17,1},{25,9},{2,18},{10... | collective-permute-start | bytes 3342344 | tf_op jit(solution)/shard_map/ppermute | solution.py:32
  109.4 22.3 %collective-permute-start.13 = (bf16[64,2048]{1,0:T(8,128)(2,1)S(1)}, bf16[64,2048]{1,0:T(8,128)(2,1)S(1)}, u32[]{:S(2)}, u32[]{:S(2)}) collective-permute-start(bf16[64,2048]{1,0:T(8,128)(2,1)S(1)} %get-tuple-element.624), channel_id=1, source_target_pairs={{0,4},{1,5},{2,6},{3,7},{4,0},{5,1},{6,2},{7,3},{8,12},{9,13},{10,... | collective-permute-start | bytes 786440 | tf_op jit(solution)/shard_map/ppermute | solution.py:37
  135.4 22.8 %collective-permute-start.18 = (bf16[64,2048]{1,0:T(8,128)(2,1)S(1)}, bf16[64,2048]{1,0:T(8,128)(2,1)S(1)}, u32[]{:S(2)}, u32[]{:S(2)}) collective-permute-start(bf16[64,2048]{1,0:T(8,128)(2,1)S(1)} %get-tuple-element.270), channel_id=1, source_target_pairs={{0,4},{1,5},{2,6},{3,7},{4,0},{5,1},{6,2},{7,3},{8,12},{9,13},{10,... | collective-permute-start | bytes 786440 | tf_op jit(solution)/shard_map/ppermute | solution.py:37
  135.4 22.8 %collective-permute-start.17 = (bf16[64,2048]{1,0:T(8,128)(2,1)S(1)}, bf16[64,2048]{1,0:T(8,128)(2,1)S(1)}, u32[]{:S(2)}, u32[]{:S(2)}) collective-permute-start(bf16[64,2048]{1,0:T(8,128)(2,1)S(1)} %get-tuple-element.270), channel_id=1, source_target_pairs={{0,2},{1,3},{2,0},{3,1},{4,6},{5,7},{6,4},{7,5},{8,10},{9,11},{10,... | collective-permute-start | bytes 786440 | tf_op jit(solution)/shard_map/ppermute | solution.py:37
  136.2 24.3 %collective-permute-start.20 = (bf16[256,2048]{1,0:T(8,128)(2,1)S(1)}, bf16[256,2048]{1,0:T(8,128)(2,1)S(1)}, u32[]{:S(2)}, u32[]{:S(2)}) collective-permute-start(bf16[256,2048]{1,0:T(8,128)(2,1)S(1)} %pad_maximum_fusion.4), channel_id=1, source_target_pairs={{0,8},{8,0},{16,24},{24,16},{1,9},{9,1},{17,25},{25,17},{2,10},{10... | collective-permute-start | bytes 3145736 | tf_op jit(solution)/shard_map/ppermute | solution.py:32
  137.5 23.3 %collective-permute-start.21 = (bf16[256,2048]{1,0:T(8,128)(2,1)S(1)}, bf16[256,2048]{1,0:T(8,128)(2,1)S(1)}, u32[]{:S(2)}, u32[]{:S(2)}) collective-permute-start(bf16[256,2048]{1,0:T(8,128)(2,1)S(1)} %pad_maximum_fusion.4), channel_id=1, source_target_pairs={{0,16},{8,24},{16,0},{24,8},{1,17},{9,25},{17,1},{25,9},{2,18},{10... | collective-permute-start | bytes 3145736 | tf_op jit(solution)/shard_map/ppermute | solution.py:32
  162.4 22.3 %collective-permute-start.23 = (bf16[128,2048]{1,0:T(8,128)(2,1)S(1)}, bf16[128,2048]{1,0:T(8,128)(2,1)S(1)}, u32[]{:S(2)}, u32[]{:S(2)}) collective-permute-start(bf16[128,2048]{1,0:T(8,128)(2,1)S(1)} %slice.672), channel_id=1, source_target_pairs={{0,16},{8,24},{16,0},{24,8},{1,17},{9,25},{17,1},{25,9},{2,18},{10... | collective-permute-start | bytes 1572872 | tf_op jit(solution)/shard_map/ppermute | solution.py:32
  163.0 22.4 %collective-permute-start.24 = (bf16[128,2048]{1,0:T(8,128)(2,1)S(1)}, bf16[128,2048]{1,0:T(8,128)(2,1)S(1)}, u32[]{:S(2)}, u32[]{:S(2)}) collective-permute-start(bf16[128,2048]{1,0:T(8,128)(2,1)S(1)} %slice.673), channel_id=1, source_target_pairs={{0,8},{8,0},{16,24},{24,16},{1,9},{9,1},{17,25},{25,17},{2,10},{10... | collective-permute-start | bytes 1572872 | tf_op jit(solution)/shard_map/ppermute | solution.py:32
  164.5 22.7 %collective-permute-start.25 = (bf16[128,2176]{1,0:T(8,128)(2,1)S(1)}, bf16[128,2176]{1,0:T(8,128)(2,1)S(1)}, u32[]{:S(2)}, u32[]{:S(2)}) collective-permute-start(bf16[128,2176]{1,0:T(8,128)(2,1)S(1)} %get-tuple-element.288), channel_id=1, source_target_pairs={{0,8},{8,0},{16,24},{24,16},{1,9},{9,1},{17,25},{25,17},{2,10},{10... | collective-permute-start | bytes 1671176 | tf_op jit(solution)/shard_map/ppermute | solution.py:32
  188.0 28.3 %collective-permute-start.27 = (bf16[1024,2176]{1,0:T(8,128)(2,1)}, bf16[1024,2176]{1,0:T(8,128)(2,1)}, u32[]{:S(2)}, u32[]{:S(2)}) collective-permute-start(bf16[1024,2176]{1,0:T(8,128)(2,1)} %constant_dynamic-update-slice_fusion.12.cot_ref.refs_4_), channel_id=1, source_target_pairs={{0,1},{1,0},{2,3},{3,2},{4,5},{5,4},{6,7},{7,6},{8,9},{9,8},{10,11... | collective-permute-start | bytes 13369352 | tf_op jit(solution)/shard_map/ppermute | solution.py:37
  188.0 28.3 %collective-permute-start.26 = (bf16[1024,2048]{1,0:T(8,128)(2,1)}, bf16[1024,2048]{1,0:T(8,128)(2,1)}, u32[]{:S(2)}, u32[]{:S(2)}) collective-permute-start(bf16[1024,2048]{1,0:T(8,128)(2,1)} %constant_dynamic-update-slice_fusion.14.moe_ref.refs_0_), channel_id=1, source_target_pairs={{0,1},{1,0},{2,3},{3,2},{4,5},{5,4},{6,7},{7,6},{8,9},{9,8},{10,11... | collective-permute-start | bytes 12582920 | tf_op jit(solution)/shard_map/ppermute | solution.py:37
  188.5 26.6 %collective-permute-start.28 = (bf16[256,2176]{1,0:T(8,128)(2,1)S(1)}, bf16[256,2176]{1,0:T(8,128)(2,1)}, u32[]{:S(2)}, u32[]{:S(2)}) collective-permute-start(bf16[256,2176]{1,0:T(8,128)(2,1)S(1)} %get-tuple-element.315), channel_id=1, source_target_pairs={{0,8},{8,0},{16,24},{24,16},{1,9},{9,1},{17,25},{25,17},{2,10},{10... | collective-permute-start | bytes 3342344 | tf_op jit(solution)/shard_map/ppermute | solution.py:32
  190.0 26.3 %collective-permute-start.29 = (bf16[256,2176]{1,0:T(8,128)(2,1)S(1)}, bf16[256,2176]{1,0:T(8,128)(2,1)}, u32[]{:S(2)}, u32[]{:S(2)}) collective-permute-start(bf16[256,2176]{1,0:T(8,128)(2,1)S(1)} %get-tuple-element.315), channel_id=1, source_target_pairs={{0,16},{8,24},{16,0},{24,8},{1,17},{9,25},{17,1},{25,9},{2,18},{10... | collective-permute-start | bytes 3342344 | tf_op jit(solution)/shard_map/ppermute | solution.py:32
  216.3 24.0 %collective-permute-start.30 = (bf16[256,2048]{1,0:T(8,128)(2,1)S(1)}, bf16[256,2048]{1,0:T(8,128)(2,1)S(1)}, u32[]{:S(2)}, u32[]{:S(2)}) collective-permute-start(bf16[256,2048]{1,0:T(8,128)(2,1)S(1)} %pad_maximum_fusion.5), channel_id=1, source_target_pairs={{0,8},{8,0},{16,24},{24,16},{1,9},{9,1},{17,25},{25,17},{2,10},{10... | collective-permute-start | bytes 3145736 | tf_op jit(solution)/shard_map/ppermute | solution.py:32
  216.8 23.7 %collective-permute-start.31 = (bf16[256,2048]{1,0:T(8,128)(2,1)S(1)}, bf16[256,2048]{1,0:T(8,128)(2,1)S(1)}, u32[]{:S(2)}, u32[]{:S(2)}) collective-permute-start(bf16[256,2048]{1,0:T(8,128)(2,1)S(1)} %pad_maximum_fusion.5), channel_id=1, source_target_pairs={{0,16},{8,24},{16,0},{24,8},{1,17},{9,25},{17,1},{25,9},{2,18},{10... | collective-permute-start | bytes 3145736 | tf_op jit(solution)/shard_map/ppermute | solution.py:32
  241.7 26.0 %collective-permute-start.32 = (bf16[128,2176]{1,0:T(8,128)(2,1)}, bf16[128,2176]{1,0:T(8,128)(2,1)S(1)}, u32[]{:S(2)}, u32[]{:S(2)}) collective-permute-start(bf16[128,2176]{1,0:T(8,128)(2,1)} %slice.674), channel_id=1, source_target_pairs={{0,16},{8,24},{16,0},{24,8},{1,17},{9,25},{17,1},{25,9},{2,18},{10... | collective-permute-start | bytes 1671176 | tf_op jit(solution)/shard_map/ppermute | solution.py:32
  243.0 24.7 %collective-permute-start.33 = (bf16[128,2176]{1,0:T(8,128)(2,1)}, bf16[128,2176]{1,0:T(8,128)(2,1)S(1)}, u32[]{:S(2)}, u32[]{:S(2)}) collective-permute-start(bf16[128,2176]{1,0:T(8,128)(2,1)} %slice.675), channel_id=1, source_target_pairs={{0,8},{8,0},{16,24},{24,16},{1,9},{9,1},{17,25},{25,17},{2,10},{10... | collective-permute-start | bytes 1671176 | tf_op jit(solution)/shard_map/ppermute | solution.py:32
  249.1 16.8 %collective-permute-start.34 = (bf16[128,2048]{1,0:T(8,128)(2,1)S(1)}, bf16[128,2048]{1,0:T(8,128)(2,1)S(1)}, u32[]{:S(2)}, u32[]{:S(2)}) collective-permute-start(bf16[128,2048]{1,0:T(8,128)(2,1)S(1)} %get-tuple-element.323), channel_id=1, source_target_pairs={{0,16},{8,24},{16,0},{24,8},{1,17},{9,25},{17,1},{25,9},{2,18},{10... | collective-permute-start | bytes 1572872 | tf_op jit(solution)/shard_map/ppermute | solution.py:32
  251.1 16.6 %collective-permute-start.36 = (bf16[1024,2176]{1,0:T(8,128)(2,1)}, bf16[1024,2176]{1,0:T(8,128)(2,1)S(1)}, u32[]{:S(2)}, u32[]{:S(2)}) collective-permute-start(bf16[1024,2176]{1,0:T(8,128)(2,1)} %get-tuple-element.326), channel_id=1, source_target_pairs={{0,1},{1,0},{2,3},{3,2},{4,5},{5,4},{6,7},{7,6},{8,9},{9,8},{10,11... | collective-permute-start | bytes 13369352 | tf_op jit(solution)/shard_map/ppermute | solution.py:37
  270.5 32.0 %collective-permute-start.38 = (bf16[1024,2176]{1,0:T(8,128)(2,1)S(1)}, bf16[1024,2176]{1,0:T(8,128)(2,1)}, u32[]{:S(2)}, u32[]{:S(2)}) collective-permute-start(bf16[1024,2176]{1,0:T(8,128)(2,1)S(1)} %constant_dynamic-update-slice_fusion.10.cot_ref.refs_6_), channel_id=1, source_target_pairs={{0,1},{1,0},{2,3},{3,2},{4,5},{5,4},{6,7},{7,6},{8,9},{9,8},{10,11... | collective-permute-start | bytes 13369352 | tf_op jit(solution)/shard_map/ppermute | solution.py:37
  270.6 31.9 %collective-permute-start.37 = (bf16[1024,2048]{1,0:T(8,128)(2,1)}, bf16[1024,2048]{1,0:T(8,128)(2,1)}, u32[]{:S(2)}, u32[]{:S(2)}) collective-permute-start(bf16[1024,2048]{1,0:T(8,128)(2,1)} %constant_dynamic-update-slice_fusion.8.moe_ref.refs_2_), channel_id=1, source_target_pairs={{0,1},{1,0},{2,3},{3,2},{4,5},{5,4},{6,7},{7,6},{8,9},{9,8},{10,11... | collective-permute-start | bytes 12582920 | tf_op jit(solution)/shard_map/ppermute | solution.py:37
  271.0 26.9 %collective-permute-start.39 = (bf16[256,2176]{1,0:T(8,128)(2,1)}, bf16[256,2176]{1,0:T(8,128)(2,1)}, u32[]{:S(2)}, u32[]{:S(2)}) collective-permute-start(bf16[256,2176]{1,0:T(8,128)(2,1)} %get-tuple-element.334), channel_id=1, source_target_pairs={{0,8},{8,0},{16,24},{24,16},{1,9},{9,1},{17,25},{25,17},{2,10},{10... | collective-permute-start | bytes 3342344 | tf_op jit(solution)/shard_map/ppermute | solution.py:32
  271.9 28.3 %collective-permute-start.40 = (bf16[256,2176]{1,0:T(8,128)(2,1)}, bf16[256,2176]{1,0:T(8,128)(2,1)}, u32[]{:S(2)}, u32[]{:S(2)}) collective-permute-start(bf16[256,2176]{1,0:T(8,128)(2,1)} %get-tuple-element.336), channel_id=1, source_target_pairs={{0,16},{8,24},{16,0},{24,8},{1,17},{9,25},{17,1},{25,9},{2,18},{10... | collective-permute-start | bytes 3342344 | tf_op jit(solution)/shard_map/ppermute | solution.py:32
  302.6 20.6 %collective-permute-start.41 = (bf16[128,2176]{1,0:T(8,128)(2,1)}, bf16[128,2176]{1,0:T(8,128)(2,1)S(1)}, u32[]{:S(2)}, u32[]{:S(2)}) collective-permute-start(bf16[128,2176]{1,0:T(8,128)(2,1)} %get-tuple-element.341), channel_id=1, source_target_pairs={{0,16},{8,24},{16,0},{24,8},{1,17},{9,25},{17,1},{25,9},{2,18},{10... | collective-permute-start | bytes 1671176 | tf_op jit(solution)/shard_map/ppermute | solution.py:32
  303.8 19.5 %collective-permute-start.42 = (bf16[128,2176]{1,0:T(8,128)(2,1)}, bf16[128,2176]{1,0:T(8,128)(2,1)S(1)}, u32[]{:S(2)}, u32[]{:S(2)}) collective-permute-start(bf16[128,2176]{1,0:T(8,128)(2,1)} %get-tuple-element.343), channel_id=1, source_target_pairs={{0,8},{8,0},{16,24},{24,16},{1,9},{9,1},{17,25},{25,17},{2,10},{10... | collective-permute-start | bytes 1671176 | tf_op jit(solution)/shard_map/ppermute | solution.py:32
  323.5 29.2 %collective-permute-start.47 = (bf16[1024,2048]{1,0:T(8,128)(2,1)S(1)}, bf16[1024,2048]{1,0:T(8,128)(2,1)S(1)}, u32[]{:S(2)}, u32[]{:S(2)}) collective-permute-start(bf16[1024,2048]{1,0:T(8,128)(2,1)S(1)} %copy-done.48), channel_id=1, source_target_pairs={{0,1},{1,0},{2,3},{3,2},{4,5},{5,4},{6,7},{7,6},{8,9},{9,8},{10,11... | collective-permute-start | bytes 12582920 | tf_op jit(solution)/shard_map/ppermute | solution.py:37
  323.5 31.8 %collective-permute-start.46 = (bf16[1024,2176]{1,0:T(8,128)(2,1)}, bf16[1024,2176]{1,0:T(8,128)(2,1)S(1)}, u32[]{:S(2)}, u32[]{:S(2)}) collective-permute-start(bf16[1024,2176]{1,0:T(8,128)(2,1)} %get-tuple-element.359), channel_id=1, source_target_pairs={{0,1},{1,0},{2,3},{3,2},{4,5},{5,4},{6,7},{7,6},{8,9},{9,8},{10,11... | collective-permute-start | bytes 13369352 | tf_op jit(solution)/shard_map/ppermute | solution.py:37
  327.4 24.2 %collective-permute-start.44 = (bf16[64,2176]{1,0:T(8,128)(2,1)S(1)}, bf16[64,2176]{1,0:T(8,128)(2,1)S(1)}, u32[]{:S(2)}, u32[]{:S(2)}) collective-permute-start(bf16[64,2176]{1,0:T(8,128)(2,1)S(1)} %get-tuple-element.356), channel_id=1, source_target_pairs={{0,4},{1,5},{2,6},{3,7},{4,0},{5,1},{6,2},{7,3},{8,12},{9,13},{10,... | collective-permute-start | bytes 835592 | tf_op jit(solution)/shard_map/ppermute | solution.py:37
  327.4 24.2 %collective-permute-start.43 = (bf16[64,2176]{1,0:T(8,128)(2,1)S(1)}, bf16[64,2176]{1,0:T(8,128)(2,1)S(1)}, u32[]{:S(2)}, u32[]{:S(2)}) collective-permute-start(bf16[64,2176]{1,0:T(8,128)(2,1)S(1)} %get-tuple-element.355), channel_id=1, source_target_pairs={{0,2},{1,3},{2,0},{3,1},{4,6},{5,7},{6,4},{7,5},{8,10},{9,11},{10,... | collective-permute-start | bytes 835592 | tf_op jit(solution)/shard_map/ppermute | solution.py:37
  357.4 29.4 %collective-permute-start.50 = (bf16[1024,2048]{1,0:T(8,128)(2,1)}, bf16[1024,2048]{1,0:T(8,128)(2,1)}, u32[]{:S(2)}, u32[]{:S(2)}) collective-permute-start(bf16[1024,2048]{1,0:T(8,128)(2,1)} %convolution_convert_fusion), channel_id=1, source_target_pairs={{0,1},{1,0},{2,3},{3,2},{4,5},{5,4},{6,7},{7,6},{8,9},{9,8},{10,11... | collective-permute-start | bytes 12582920 | tf_op jit(solution)/shard_map/ppermute | solution.py:37
  358.2 27.2 %collective-permute-start.48 = (bf16[256,2176]{1,0:T(8,128)(2,1)}, bf16[256,2176]{1,0:T(8,128)(2,1)S(1)}, u32[]{:S(2)}, u32[]{:S(2)}) collective-permute-start(bf16[256,2176]{1,0:T(8,128)(2,1)} %get-tuple-element.368), channel_id=1, source_target_pairs={{0,8},{8,0},{16,24},{24,16},{1,9},{9,1},{17,25},{25,17},{2,10},{10... | collective-permute-start | bytes 3342344 | tf_op jit(solution)/shard_map/ppermute | solution.py:32
  359.6 27.0 %collective-permute-start.49 = (bf16[256,2176]{1,0:T(8,128)(2,1)}, bf16[256,2176]{1,0:T(8,128)(2,1)S(1)}, u32[]{:S(2)}, u32[]{:S(2)}) collective-permute-start(bf16[256,2176]{1,0:T(8,128)(2,1)} %get-tuple-element.370), channel_id=1, source_target_pairs={{0,16},{8,24},{16,0},{24,8},{1,17},{9,25},{17,1},{25,9},{2,18},{10... | collective-permute-start | bytes 3342344 | tf_op jit(solution)/shard_map/ppermute | solution.py:32
  391.7 26.6 %collective-permute-start.54 = (bf16[128,2176]{1,0:T(8,128)(2,1)S(1)}, bf16[128,2176]{1,0:T(8,128)(2,1)S(1)}, u32[]{:S(2)}, u32[]{:S(2)}) collective-permute-start(bf16[128,2176]{1,0:T(8,128)(2,1)S(1)} %get-tuple-element.379), channel_id=1, source_target_pairs={{0,16},{8,24},{16,0},{24,8},{1,17},{9,25},{17,1},{25,9},{2,18},{10... | collective-permute-start | bytes 1671176 | tf_op jit(solution)/shard_map/ppermute | solution.py:32
  394.5 22.7 %collective-permute-start.52 = (bf16[64,2048]{1,0:T(8,128)(2,1)S(1)}, bf16[64,2048]{1,0:T(8,128)(2,1)S(1)}, u32[]{:S(2)}, u32[]{:S(2)}) collective-permute-start(bf16[64,2048]{1,0:T(8,128)(2,1)S(1)} %convert_element_type.754), channel_id=1, source_target_pairs={{0,16},{8,24},{16,0},{24,8},{1,17},{9,25},{17,1},{25,9},{2,18},{10... | collective-permute-start | bytes 786440 | tf_op jit(solution)/shard_map/ppermute | solution.py:32
  395.3 22.0 %collective-permute-start.51 = (bf16[64,2048]{1,0:T(8,128)(2,1)S(1)}, bf16[64,2048]{1,0:T(8,128)(2,1)S(1)}, u32[]{:S(2)}, u32[]{:S(2)}) collective-permute-start(bf16[64,2048]{1,0:T(8,128)(2,1)S(1)} %convert_element_type.754), channel_id=1, source_target_pairs={{0,8},{8,0},{16,24},{24,16},{1,9},{9,1},{17,25},{25,17},{2,10},{10... | collective-permute-start | bytes 786440 | tf_op jit(solution)/shard_map/ppermute | solution.py:32
  396.6 22.6 %collective-permute-start.55 = (bf16[128,2176]{1,0:T(8,128)(2,1)S(1)}, bf16[128,2176]{1,0:T(8,128)(2,1)S(1)}, u32[]{:S(2)}, u32[]{:S(2)}) collective-permute-start(bf16[128,2176]{1,0:T(8,128)(2,1)S(1)} %get-tuple-element.381), channel_id=1, source_target_pairs={{0,8},{8,0},{16,24},{24,16},{1,9},{9,1},{17,25},{25,17},{2,10},{10... | collective-permute-start | bytes 1671176 | tf_op jit(solution)/shard_map/ppermute | solution.py:32
  422.4 22.2 %collective-permute-start.57 = (bf16[64,2176]{1,0:T(8,128)(2,1)}, bf16[64,2176]{1,0:T(8,128)(2,1)}, u32[]{:S(2)}, u32[]{:S(2)}) collective-permute-start(bf16[64,2176]{1,0:T(8,128)(2,1)} %get-tuple-element.392), channel_id=1, source_target_pairs={{0,4},{1,5},{2,6},{3,7},{4,0},{5,1},{6,2},{7,3},{8,12},{9,13},{10,... | collective-permute-start | bytes 835592 | tf_op jit(solution)/shard_map/ppermute | solution.py:37
  422.4 22.2 %collective-permute-start.56 = (bf16[64,2176]{1,0:T(8,128)(2,1)}, bf16[64,2176]{1,0:T(8,128)(2,1)}, u32[]{:S(2)}, u32[]{:S(2)}) collective-permute-start(bf16[64,2176]{1,0:T(8,128)(2,1)} %get-tuple-element.391), channel_id=1, source_target_pairs={{0,2},{1,3},{2,0},{3,1},{4,6},{5,7},{6,4},{7,5},{8,10},{9,11},{10,... | collective-permute-start | bytes 835592 | tf_op jit(solution)/shard_map/ppermute | solution.py:37
  424.5 23.4 %collective-permute-start.59 = (bf16[256,2048]{1,0:T(8,128)(2,1)}, bf16[256,2048]{1,0:T(8,128)(2,1)}, u32[]{:S(2)}, u32[]{:S(2)}) collective-permute-start(bf16[256,2048]{1,0:T(8,128)(2,1)} %get-tuple-element.402), channel_id=1, source_target_pairs={{0,8},{8,0},{16,24},{24,16},{1,9},{9,1},{17,25},{25,17},{2,10},{10... | collective-permute-start | bytes 3145736 | tf_op jit(solution)/shard_map/ppermute | solution.py:32
  427.3 23.2 %collective-permute-start.60 = (bf16[256,2048]{1,0:T(8,128)(2,1)}, bf16[256,2048]{1,0:T(8,128)(2,1)S(1)}, u32[]{:S(2)}, u32[]{:S(2)}) collective-permute-start(bf16[256,2048]{1,0:T(8,128)(2,1)} %get-tuple-element.404), channel_id=1, source_target_pairs={{0,16},{8,24},{16,0},{24,8},{1,17},{9,25},{17,1},{25,9},{2,18},{10... | collective-permute-start | bytes 3145736 | tf_op jit(solution)/shard_map/ppermute | solution.py:32
  454.8 17.9 %collective-permute-start.63 = (bf16[64,2048]{1,0:T(8,128)(2,1)S(1)}, bf16[64,2048]{1,0:T(8,128)(2,1)S(1)}, u32[]{:S(2)}, u32[]{:S(2)}) collective-permute-start(bf16[64,2048]{1,0:T(8,128)(2,1)S(1)} %get-tuple-element.534), channel_id=1, source_target_pairs={{0,24},{8,16},{16,8},{24,0},{1,25},{9,17},{17,9},{25,1},{2,26},{10... | collective-permute-start | bytes 786440 | tf_op jit(solution)/shard_map/ppermute | solution.py:32
  488.1 119.5 %reduce-scatter.5.cloned.1.call-start = ((), (), s32[]{:S(2)}) async-start(), calls=%async_computation.3 | async-start | bytes 4718592 | tf_op jit(solution)/shard_map/reduce_scatter | solution.py:846
  520.3 186.6 %all-gather.2.cloned.1.call-start = ((), (), s32[]{:S(2)}) async-start(), calls=%async_computation.4 | async-start | bytes 9437184 | tf_op jit(solution)/shard_map/all_gather | solution.py:864
  525.2 21.0 %collective-permute-start.72 = (bf16[128,2048]{1,0:T(8,128)(2,1)S(1)}, bf16[128,2048]{1,0:T(8,128)(2,1)S(1)}, u32[]{:S(2)}, u32[]{:S(2)}) collective-permute-start(bf16[128,2048]{1,0:T(8,128)(2,1)S(1)} %pad_maximum_fusion.10), channel_id=1, source_target_pairs={{0,2},{1,3},{2,0},{3,1},{4,6},{5,7},{6,4},{7,5},{8,10},{9,11},{10,... | collective-permute-start | bytes 1572872 | tf_op jit(solution)/shard_map/ppermute | solution.py:37
  527.3 20.5 %collective-permute-start.76 = (bf16[64,2048]{1,0:T(8,128)(2,1)S(1)}, bf16[64,2048]{1,0:T(8,128)(2,1)S(1)}, u32[]{:S(2)}, u32[]{:S(2)}) collective-permute-start(bf16[64,2048]{1,0:T(8,128)(2,1)S(1)} %get-tuple-element.608), channel_id=1, source_target_pairs={{0,24},{8,16},{16,8},{24,0},{1,25},{9,17},{17,9},{25,1},{2,26},{10... | collective-permute-start | bytes 786440 | tf_op jit(solution)/shard_map/ppermute | solution.py:32
  529.0 20.9 %collective-permute-start.75 = (bf16[64,2048]{1,0:T(8,128)(2,1)S(1)}, bf16[64,2048]{1,0:T(8,128)(2,1)S(1)}, u32[]{:S(2)}, u32[]{:S(2)}) collective-permute-start(bf16[64,2048]{1,0:T(8,128)(2,1)S(1)} %get-tuple-element.609), channel_id=1, source_target_pairs={{0,16},{8,24},{16,0},{24,8},{1,17},{9,25},{17,1},{25,9},{2,18},{10... | collective-permute-start | bytes 786440 | tf_op jit(solution)/shard_map/ppermute | solution.py:32
  529.8 20.1 %collective-permute-start.74 = (bf16[64,2048]{1,0:T(8,128)(2,1)S(1)}, bf16[64,2048]{1,0:T(8,128)(2,1)S(1)}, u32[]{:S(2)}, u32[]{:S(2)}) collective-permute-start(bf16[64,2048]{1,0:T(8,128)(2,1)S(1)} %get-tuple-element.607), channel_id=1, source_target_pairs={{0,8},{8,0},{16,24},{24,16},{1,9},{9,1},{17,25},{25,17},{2,10},{10... | collective-permute-start | bytes 786440 | tf_op jit(solution)/shard_map/ppermute | solution.py:32
  530.9 29.1 %collective-permute-start.77 = (bf16[256,2048]{1,0:T(8,128)(2,1)S(1)}, bf16[256,2048]{1,0:T(8,128)(2,1)S(1)}, u32[]{:S(2)}, u32[]{:S(2)}) collective-permute-start(bf16[256,2048]{1,0:T(8,128)(2,1)S(1)} %copy-done.27), channel_id=1, source_target_pairs={{0,8},{8,0},{16,24},{24,16},{1,9},{9,1},{17,25},{25,17},{2,10},{10... | collective-permute-start | bytes 3145736 | tf_op jit(solution)/shard_map/ppermute | solution.py:32
  546.2 23.8 %collective-permute-start.78 = (bf16[256,2048]{1,0:T(8,128)(2,1)S(1)}, bf16[256,2048]{1,0:T(8,128)(2,1)S(1)}, u32[]{:S(2)}, u32[]{:S(2)}) collective-permute-start(bf16[256,2048]{1,0:T(8,128)(2,1)S(1)} %copy-done.26), channel_id=1, source_target_pairs={{0,16},{8,24},{16,0},{24,8},{1,17},{9,25},{17,1},{25,9},{2,18},{10... | collective-permute-start | bytes 3145736 | tf_op jit(solution)/shard_map/ppermute | solution.py:32
  574.7 16.9 %collective-permute-start.82 = (bf16[128,2048]{1,0:T(8,128)(2,1)S(1)}, bf16[128,2048]{1,0:T(8,128)(2,1)S(1)}, u32[]{:S(2)}, u32[]{:S(2)}) collective-permute-start(bf16[128,2048]{1,0:T(8,128)(2,1)S(1)} %get-tuple-element.464), channel_id=1, source_target_pairs={{0,16},{8,24},{16,0},{24,8},{1,17},{9,25},{17,1},{25,9},{2,18},{10... | collective-permute-start | bytes 1572872 | tf_op jit(solution)/shard_map/ppermute | solution.py:32
  676.1 18.9 %collective-permute-start.87 = (bf16[20,2048]{1,0:T(8,128)(2,1)S(1)}, bf16[20,2048]{1,0:T(8,128)(2,1)S(1)}, u32[]{:S(2)}, u32[]{:S(2)}) collective-permute-start(bf16[20,2048]{1,0:T(8,128)(2,1)S(1)} %add_convert_fusion.52), channel_id=1, source_target_pairs={{0,4},{1,5},{2,6},{3,7},{4,0},{5,1},{6,2},{7,3},{8,12},{9,13},{10,... | collective-permute-start | bytes 245768 | tf_op jit(solution)/shard_map/ppermute | solution.py:37
  676.1 21.2 %collective-permute-start.86 = (bf16[20,2048]{1,0:T(8,128)(2,1)S(1)}, bf16[20,2048]{1,0:T(8,128)(2,1)S(1)}, u32[]{:S(2)}, u32[]{:S(2)}) collective-permute-start(bf16[20,2048]{1,0:T(8,128)(2,1)S(1)} %add_convert_fusion.52), channel_id=1, source_target_pairs={{0,2},{1,3},{2,0},{3,1},{4,6},{5,7},{6,4},{7,5},{8,10},{9,11},{10,... | collective-permute-start | bytes 245768 | tf_op jit(solution)/shard_map/ppermute | solution.py:37
  678.2 19.1 %collective-permute-start.91 = (bf16[64,2048]{1,0:T(8,128)(2,1)S(1)}, bf16[64,2048]{1,0:T(8,128)(2,1)S(1)}, u32[]{:S(2)}, u32[]{:S(2)}) collective-permute-start(bf16[64,2048]{1,0:T(8,128)(2,1)S(1)} %get-tuple-element.601), channel_id=1, source_target_pairs={{0,24},{8,16},{16,8},{24,0},{1,25},{9,17},{17,9},{25,1},{2,26},{10... | collective-permute-start | bytes 786440 | tf_op jit(solution)/shard_map/ppermute | solution.py:32
  680.3 17.0 %collective-permute-start.90 = (bf16[64,2048]{1,0:T(8,128)(2,1)S(1)}, bf16[64,2048]{1,0:T(8,128)(2,1)S(1)}, u32[]{:S(2)}, u32[]{:S(2)}) collective-permute-start(bf16[64,2048]{1,0:T(8,128)(2,1)S(1)} %get-tuple-element.602), channel_id=1, source_target_pairs={{0,16},{8,24},{16,0},{24,8},{1,17},{9,25},{17,1},{25,9},{2,18},{10... | collective-permute-start | bytes 786440 | tf_op jit(solution)/shard_map/ppermute | solution.py:32
  (85 other events, 906.5 us)
Sparse Core Ops, SparseCore 0:
  488.2 57.8 reduce-scatter.2
  549.0 49.6 reduce-scatter.4
  610.0 96.8 all-gather.1

commit v7 on v6

--- a/solution.py
+++ b/solution.py
@@ -13,7 +13,7 @@
 BF = jnp.bfloat16
 F32 = jnp.float32
 VMEM_BYTES = 56 * 1024 * 1024
-EXPERT_TILE = 256
+EXPERT_TILE = 128
 COST_SCALE = 8
 
 

time: 739 us -> 761 us (1.030)
  Pallas kernels: 173 us -> 210 us
  waiting for transfers between devices: 254 us -> 240 us
    pallas_call x14, Pallas kernels: 173 us -> 210 us  [call_kernel(): pl.pallas_call(body, out_shape=outs, grid=grid, in_specs=in_specs or [who...]
    ppermute x62, waiting for transfers between devices: 148 us -> 133 us  [swap_tp(): return lax.ppermute(value, 'tp', [(i, i ^ bits) for i in range(size)])]
  transfers between devices with their start and end apart: 96 -> 96, of which waited for: 44 -> 41; matrix products, arithmetic and copies ran while one was open for 18% -> 18% of each run, Pallas kernels for 22% -> 26%
where the time goes in v7:
time: 761 us; the launch traced here: 752 us
  waiting for transfers between devices  240 us (32%)
  Pallas kernels  210 us (28%)
  starting transfers between devices  115 us (15%)
  other arithmetic  77.9 us (10%)
  local copies, waits for them, and re-layouts  70.6 us (9%)
  matrix products  22.9 us (3%)
  between operations  15.5 us (2%)
    pallas_call x14, Pallas kernels, call_kernel(): pl.pallas_call(body, out_shape=outs, grid=grid, in_specs=in_specs or [who...  210 us
    ppermute x62, waiting for transfers between devices, swap_tp(): return lax.ppermute(value, 'tp', [(i, i ^ bits) for i in range(size)])  133 us
    ppermute x31, waiting for transfers between devices, swap_dp(): return lax.ppermute(value, 'dp', [(i, i ^ bits) for i in range(size)])  106 us
    ppermute x62, starting transfers between devices, swap_tp(): return lax.ppermute(value, 'tp', [(i, i ^ bits) for i in range(size)])  71.1 us
    ppermute x31, starting transfers between devices, swap_dp(): return lax.ppermute(value, 'dp', [(i, i ^ bits) for i in range(size)])  43.4 us
    convert_element_type x20, other arithmetic, add_pieces(): return [add_low(one, two).astype(BF) for one, two in zip(left, right)]  25.4 us
    unnamed x131, local copies, waits for them, and re-layouts  23.9 us
    dot_general x4, matrix products, mix(): return jnp.dot(ran[1], down, preferred_element_type=F32).astype(BF)  17.7 us
  transfers between devices with their start and end apart: 96, of which 41 were waited for; matrix products, arithmetic and copies ran while one was open for 18% of the time, Pallas kernels for 26%

profile of v7, /device:TPU:0, one launch (start us, length us, event | category | flops | bytes accessed | tf_op | source)
XLA Modules:
  0.0 751.8 jit_solution(14226861989220070322)
XLA Ops:
  7.2 4.0 collective-permute-start.2
  17.5 2.6 collective-permute-start.7
  20.5 4.7 fusion.27
  28.2 2.7 pad_maximum_fusion.1.gate_up_ref
  30.9 3.8 collective-permute-done.1
  35.0 2.7 pad_maximum_fusion.3
  37.7 9.4 %shard_map.195 = (bf16[512,2048]{1,0:T(8,128)(2,1)}, f32[512,1536]{1,0:T(8,128)}, f32[512,128]{1,0:T(8,128)}) custom-call(bf16[512,2048]{1,0:T(8,128)(2,1)} %bitcast.170, f32[1,2048]{1,0:T(1,128)} %bitcast.194, bf16[3,2048,512]{2,1,0:T(8,128)(2,1)} %bitcast.159), custom_call_target="tpu_custom_call" | custom-call | flops 402653184 | bytes 786432 | tf_op jit(solution)/shard_map/pallas_call | solution.py:171
  53.6 3.1 collective-permute-done.3
  56.7 3.6 collective-permute-start.8
  63.3 3.0 collective-permute-done.4
  67.0 7.9 %shard_map.196 = (bf16[2,256,1536]{2,1,0:T(8,128)(2,1)}, f32[2,4,256,256]{3,2,1,0:T(8,128)}, bf16[2,256,512]{2,1,0:T(8,128)(2,1)}, bf16[2,256,2048]{2,1,0:T(8,128)(2,1)}) custom-call(f32[2,256,1536]{2,1,0:T(8,128)} %bitcast.148, f32[2,256,128]{2,1,0:T(8,128)} %fusion.7.squares_ref, f32[2,512]{1,0:T(2,128)} %gain_ref.5, ...), custom_call_target="tpu_custom_call" | custom-call | flops 167772160 | bytes 2097152 | tf_op jit(solution)/shard_map/pallas_call | solution.py:171
  82.7 10.1 %collective-permute-done.11 = bf16[2,64,2048]{2,1,0:T(8,128)(2,1)S(1)} collective-permute-done((bf16[2,64,2048]{2,1,0:T(8,128)(2,1)S(1)}, bf16[2,64,2048]{2,1,0:T(8,128)(2,1)S(1)}, u32[]{:S(2)}, u32[]{:S(2)}) %collective-permute-start.11) | collective-permute-done | bytes 524320 | tf_op jit(solution)/shard_map/ppermute | solution.py:32
  92.8 9.3 %collective-permute-done.10 = bf16[2,64,2048]{2,1,0:T(8,128)(2,1)S(1)} collective-permute-done((bf16[2,64,2048]{2,1,0:T(8,128)(2,1)S(1)}, bf16[2,64,2048]{2,1,0:T(8,128)(2,1)S(1)}, u32[]{:S(2)}, u32[]{:S(2)}) %collective-permute-start.10) | collective-permute-done | bytes 524320 | tf_op jit(solution)/shard_map/ppermute | solution.py:32
  105.6 3.8 collective-permute-start.14
  109.4 6.7 collective-permute-start.13
  116.2 15.4 %collective-permute-done.13 = bf16[64,2048]{1,0:T(8,128)(2,1)S(1)} collective-permute-done((bf16[64,2048]{1,0:T(8,128)(2,1)S(1)}, bf16[64,2048]{1,0:T(8,128)(2,1)S(1)}, u32[]{:S(2)}, u32[]{:S(2)}) %collective-permute-start.13) | collective-permute-done | bytes 262176 | tf_op jit(solution)/shard_map/ppermute | solution.py:37
  131.8 3.6 collective-permute-start.19
  144.7 13.5 %collective-permute-done.18 = bf16[64,2048]{1,0:T(8,128)(2,1)S(1)} collective-permute-done((bf16[64,2048]{1,0:T(8,128)(2,1)S(1)}, bf16[64,2048]{1,0:T(8,128)(2,1)S(1)}, u32[]{:S(2)}, u32[]{:S(2)}) %collective-permute-start.18) | collective-permute-done | bytes 262176 | tf_op jit(solution)/shard_map/ppermute | solution.py:37
  158.3 2.3 collective-permute-done.20
  165.1 11.3 %collective-permute-done.22 = bf16[128,2176]{1,0:T(8,128)(2,1)S(1)} collective-permute-done((bf16[128,2176]{1,0:T(8,128)(2,1)S(1)}, bf16[128,2176]{1,0:T(8,128)(2,1)S(1)}, u32[]{:S(2)}, u32[]{:S(2)}) %collective-permute-start.22) | collective-permute-done | bytes 557088 | tf_op jit(solution)/shard_map/ppermute | solution.py:32
  190.6 27.0 %shard_map.197 = (bf16[1024,2176]{1,0:T(8,128)(2,1)}, bf16[1024,512]{1,0:T(8,128)(2,1)}, bf16[1024,1024]{1,0:T(8,128)(2,1)}) custom-call(s32[1]{0:T(128)} %bitcast.17.ids_ref, bf16[1024,2048]{1,0:T(8,128)(2,1)} %constant_dynamic-update-slice_fusion.14.moe_ref.refs_0_, bf16[1024,2176]{1,0:T(8,128)(2,1)} %constant_dynamic-update-slice_fusion.12.cot_ref.refs_4_, ...), custom_call_target="tpu_custom_call" | custom-call | flops 1342177280 | bytes 1572864 | tf_op jit(solution)/shard_map/pallas_call | solution.py:171
  223.6 27.4 %shard_map.198 = (bf16[1024,2176]{1,0:T(8,128)(2,1)}, bf16[1024,512]{1,0:T(8,128)(2,1)}, bf16[1024,1024]{1,0:T(8,128)(2,1)}) custom-call(s32[1]{0:T(128)} %bitcast.17.ids_ref, bf16[1024,2048]{1,0:T(8,128)(2,1)} %collective-permute-done.26.moe_ref.refs_1_, bf16[1024,2176]{1,0:T(8,128)(2,1)} %collective-permute-done.27.cot_ref.refs_5_, ...), custom_call_target="tpu_custom_call" | custom-call | flops 1342177280 | bytes 1572864 | tf_op jit(solution)/shard_map/pallas_call | solution.py:171
  261.9 4.4 convolution_convert_fusion.3
  271.1 4.4 convolution_convert_fusion.2
  279.5 2.6 add_convert_fusion.4
  284.7 27.0 %shard_map.199 = (bf16[1024,2176]{1,0:T(8,128)(2,1)}, bf16[1024,512]{1,0:T(8,128)(2,1)}, bf16[1024,1024]{1,0:T(8,128)(2,1)}) custom-call(s32[1]{0:T(128)} %bitcast.17.ids_ref, bf16[1024,2048]{1,0:T(8,128)(2,1)} %constant_dynamic-update-slice_fusion.8.moe_ref.refs_2_, bf16[1024,2176]{1,0:T(8,128)(2,1)} %copy-done.4, bf16[2048,128]{1,0:T(8,128)(2,1)} %pad.17.router_ref, ...), custom_call_target="tpu_custom_call" | custom-call | flops 1342177280 | bytes 1572864 | tf_op jit(solution)/shard_map/pallas_call | solution.py:171
  318.4 27.3 %shard_map.200 = (bf16[1024,2176]{1,0:T(8,128)(2,1)}, bf16[1024,512]{1,0:T(8,128)(2,1)}, bf16[1024,1024]{1,0:T(8,128)(2,1)}) custom-call(s32[1]{0:T(128)} %bitcast.17.ids_ref, bf16[1024,2048]{1,0:T(8,128)(2,1)} %collective-permute-done.37.moe_ref.refs_3_, bf16[1024,2176]{1,0:T(8,128)(2,1)} %collective-permute-done.38.cot_ref.refs_7_, ...), custom_call_target="tpu_custom_call" | custom-call | flops 1342177280 | bytes 1572864 | tf_op jit(solution)/shard_map/pallas_call | solution.py:171
  346.6 3.4 collective-permute-start.45
  351.0 4.5 convolution_convert_fusion.1
  355.5 4.4 convolution_convert_fusion
  359.9 14.3 %collective-permute-done.44 = bf16[64,2176]{1,0:T(8,128)(2,1)S(1)} collective-permute-done((bf16[64,2176]{1,0:T(8,128)(2,1)S(1)}, bf16[64,2176]{1,0:T(8,128)(2,1)S(1)}, u32[]{:S(2)}, u32[]{:S(2)}) %collective-permute-start.44) | collective-permute-done | bytes 278560 | tf_op jit(solution)/shard_map/ppermute | solution.py:37
  375.2 2.6 add_convert_fusion.12
  387.0 20.9 %collective-permute-done.48 = bf16[256,2176]{1,0:T(8,128)(2,1)S(1)} collective-permute-done((bf16[256,2176]{1,0:T(8,128)(2,1)}, bf16[256,2176]{1,0:T(8,128)(2,1)S(1)}, u32[]{:S(2)}, u32[]{:S(2)}) %collective-permute-start.48) | collective-permute-done | bytes 1114144 | tf_op jit(solution)/shard_map/ppermute | solution.py:32
  410.1 4.1 add_convert_fusion.8
  419.9 5.7 collective-permute-done.53
  425.7 14.1 %collective-permute-done.52 = bf16[64,2048]{1,0:T(8,128)(2,1)S(1)} collective-permute-done((bf16[64,2048]{1,0:T(8,128)(2,1)S(1)}, bf16[64,2048]{1,0:T(8,128)(2,1)S(1)}, u32[]{:S(2)}, u32[]{:S(2)}) %collective-permute-start.52) | collective-permute-done | bytes 262176 | tf_op jit(solution)/shard_map/ppermute | solution.py:32
  442.6 2.4 collective-permute-start.58
  450.8 7.1 shard_map.201
  457.9 9.3 %collective-permute-done.57 = bf16[64,2176]{1,0:T(8,128)(2,1)} collective-permute-done((bf16[64,2176]{1,0:T(8,128)(2,1)}, bf16[64,2176]{1,0:T(8,128)(2,1)}, u32[]{:S(2)}, u32[]{:S(2)}) %collective-permute-start.57) | collective-permute-done | bytes 278560 | tf_op jit(solution)/shard_map/ppermute | solution.py:37
  470.4 2.6 add_convert_fusion.30
  481.7 3.0 collective-permute-done.65
  486.2 6.3 collective-permute-done.64
  496.2 7.0 shard_map.202
  503.3 7.3 shard_map.203
  517.0 6.8 shard_map.204
  524.6 2.9 collective-permute-done.70
  529.3 7.0 shard_map.205
  536.2 6.5 shard_map.206
  554.4 14.3 %collective-permute-done.72 = bf16[128,2048]{1,0:T(8,128)(2,1)S(1)} collective-permute-done((bf16[128,2048]{1,0:T(8,128)(2,1)S(1)}, bf16[128,2048]{1,0:T(8,128)(2,1)S(1)}, u32[]{:S(2)}, u32[]{:S(2)}) %collective-permute-start.72) | collective-permute-done | bytes 524320 | tf_op jit(solution)/shard_map/ppermute | solution.py:37
  573.4 5.2 collective-permute-done.73
  579.4 3.3 collective-permute-done.77
  583.1 9.3 %collective-permute-done.78 = bf16[256,2048]{1,0:T(8,128)(2,1)S(1)} collective-permute-done((bf16[256,2048]{1,0:T(8,128)(2,1)S(1)}, bf16[256,2048]{1,0:T(8,128)(2,1)S(1)}, u32[]{:S(2)}, u32[]{:S(2)}) %collective-permute-start.78) | collective-permute-done | bytes 1048608 | tf_op jit(solution)/shard_map/ppermute | solution.py:32
  601.6 2.7 collective-permute-done.80
  605.6 8.3 %collective-permute-done.82 = bf16[128,2048]{1,0:T(8,128)(2,1)S(1)} collective-permute-done((bf16[128,2048]{1,0:T(8,128)(2,1)S(1)}, bf16[128,2048]{1,0:T(8,128)(2,1)S(1)}, u32[]{:S(2)}, u32[]{:S(2)}) %collective-permute-start.82) | collective-permute-done | bytes 524320 | tf_op jit(solution)/shard_map/ppermute | solution.py:32
  615.7 14.5 %collective-permute-done.85 = bf16[128,2048]{1,0:T(8,128)(2,1)S(1)} collective-permute-done((bf16[128,2048]{1,0:T(8,128)(2,1)S(1)}, bf16[128,2048]{1,0:T(8,128)(2,1)S(1)}, u32[]{:S(2)}, u32[]{:S(2)}) %collective-permute-start.85) | collective-permute-done | bytes 524320 | tf_op jit(solution)/shard_map/ppermute | solution.py:37
  632.6 24.7 %shard_map.207 = f32[2048,1024]{1,0:T(8,128)} custom-call(bf16[1024,2048]{1,0:T(8,128)(2,1)} %constant_dynamic-update-slice_fusion.14.moe_ref.refs_0_, bf16[1024,2048]{1,0:T(8,128)(2,1)} %collective-permute-done.26.moe_ref.refs_1_, bf16[1024,2048]{1,0:T(8,128)(2,1)} %constant_dynamic-update-slice_fusion.8.moe_ref.refs_2_, ...), custom_call_target="tpu_custom_call" | custom-call | flops 2147483648 | bytes 4194304 | tf_op jit(solution)/shard_map/pallas_call | solution.py:171
  657.3 11.8 %reshape.430 = f32[2048,2,2,256]{3,2,1,0:T(2,128)} reshape(f32[2048,1024]{1,0:T(8,128)} %shard_map.207) | data formatting | bytes 16777216 | tf_op jit(solution)/shard_map/reshape | solution.py:880
  669.0 17.2 %shard_map.208 = f32[512,2048]{1,0:T(8,128)} custom-call(bf16[1024,512]{1,0:T(8,128)(2,1)} %get-tuple-element.486.refs_0_, bf16[1024,512]{1,0:T(8,128)(2,1)} %get-tuple-element.487.refs_1_, bf16[1024,512]{1,0:T(8,128)(2,1)} %get-tuple-element.488.refs_2_, bf16[1024,512]{1,0:T(8,128)(2,1)} %get-tuple-element.489.refs_3_, ...), custom_call_target="tpu_custom_call" | custom-call | flops 1073741824 | bytes 3145728 | tf_op jit(solution)/shard_map/pallas_call | solution.py:171
  686.2 5.5 slice_bitcast_fusion.1
  691.7 4.8 pad_maximum_fusion
  707.4 10.2 %collective-permute-done.87 = bf16[20,2048]{1,0:T(8,128)(2,1)S(1)} collective-permute-done((bf16[20,2048]{1,0:T(8,128)(2,1)S(1)}, bf16[20,2048]{1,0:T(8,128)(2,1)S(1)}, u32[]{:S(2)}, u32[]{:S(2)}) %collective-permute-start.87) | collective-permute-done | bytes 81952 | tf_op jit(solution)/shard_map/ppermute | solution.py:37
  721.5 5.7 collective-permute-done.92
  732.9 9.4 %convert_bitcast_fusion = f32[2048,3,512]{2,0,1:T(8,128)} fusion(bf16[4,2048,512]{2,1,0:T(8,128)(2,1)} %bitcast.171), kind=kLoop, calls=%fused_computation | loop fusion | flops 3145728 | bytes 18874368 | tf_op jit(solution)/shard_map/transpose | solution.py:892
  742.2 2.6 maximum_convert_fusion
  (423 shorter events, 201.2 us)
Async XLA Ops:
  7.2 623.1 %reduce-scatter.3.cloned.1.call-start = ((), (), s32[]{:S(2)}) async-start(), calls=%async_computation.2 | async-start | bytes 4718592 | tf_op jit(solution)/shard_map/reduce_scatter | solution.py:836
  7.2 23.7 %collective-permute-start.2 = (bf16[2,64,2048]{2,1,0:T(8,128)(2,1)}, bf16[2,64,2048]{2,1,0:T(8,128)(2,1)S(1)}, u32[]{:S(2)}, u32[]{:S(2)}) collective-permute-start(bf16[2,64,2048]{2,1,0:T(8,128)(2,1)} %bitcast.176), channel_id=1, source_target_pairs={{0,24},{8,16},{16,8},{24,0},{1,25},{9,17},{17,9},{25,1},{2,26},{10... | collective-permute-start | bytes 1572872 | tf_op jit(solution)/shard_map/ppermute | solution.py:32
  11.2 23.5 %collective-permute-start.1 = (bf16[2,64,2048]{2,1,0:T(8,128)(2,1)}, bf16[2,64,2048]{2,1,0:T(8,128)(2,1)}, u32[]{:S(2)}, u32[]{:S(2)}) collective-permute-start(bf16[2,64,2048]{2,1,0:T(8,128)(2,1)} %bitcast.177), channel_id=1, source_target_pairs={{0,16},{8,24},{16,0},{24,8},{1,17},{9,25},{17,1},{25,9},{2,18},{10... | collective-permute-start | bytes 1572872 | tf_op jit(solution)/shard_map/ppermute | solution.py:32
  11.7 23.3 %collective-permute-start = (bf16[2,64,2048]{2,1,0:T(8,128)(2,1)}, bf16[2,64,2048]{2,1,0:T(8,128)(2,1)}, u32[]{:S(2)}, u32[]{:S(2)}) collective-permute-start(bf16[2,64,2048]{2,1,0:T(8,128)(2,1)} %bitcast.178), channel_id=1, source_target_pairs={{0,8},{8,0},{16,24},{24,16},{1,9},{9,1},{17,25},{25,17},{2,10},{10... | collective-permute-start | bytes 1572872 | tf_op jit(solution)/shard_map/ppermute | solution.py:32
  15.4 59.6 %collective-permute-start.6 = (bf16[2,64,2176]{2,1,0:T(8,128)(2,1)S(1)}, bf16[2,64,2176]{2,1,0:T(8,128)(2,1)S(1)}, u32[]{:S(2)}, u32[]{:S(2)}) collective-permute-start(bf16[2,64,2176]{2,1,0:T(8,128)(2,1)S(1)} %pad_maximum_fusion.9), channel_id=1, source_target_pairs={{0,2},{1,3},{2,0},{3,1},{4,6},{5,7},{6,4},{7,5},{8,10},{9,11},{10,... | collective-permute-start | bytes 1671176 | tf_op jit(solution)/shard_map/ppermute | solution.py:37
  17.5 57.5 %collective-permute-start.7 = (bf16[2,64,2176]{2,1,0:T(8,128)(2,1)S(1)}, bf16[2,64,2176]{2,1,0:T(8,128)(2,1)S(1)}, u32[]{:S(2)}, u32[]{:S(2)}) collective-permute-start(bf16[2,64,2176]{2,1,0:T(8,128)(2,1)S(1)} %pad_maximum_fusion.9), channel_id=1, source_target_pairs={{0,4},{1,5},{2,6},{3,7},{4,0},{5,1},{6,2},{7,3},{8,12},{9,13},{10,... | collective-permute-start | bytes 1671176 | tf_op jit(solution)/shard_map/ppermute | solution.py:37
  56.7 18.3 %collective-permute-start.8 = (bf16[2,64,2176]{2,1,0:T(8,128)(2,1)S(1)}, bf16[2,64,2176]{2,1,0:T(8,128)(2,1)S(1)}, u32[]{:S(2)}, u32[]{:S(2)}) collective-permute-start(bf16[2,64,2176]{2,1,0:T(8,128)(2,1)S(1)} %pad_maximum_fusion.9), channel_id=1, source_target_pairs={{0,6},{1,7},{2,4},{3,5},{4,2},{5,3},{6,0},{7,1},{8,14},{9,15},{10,... | collective-permute-start | bytes 1671176 | tf_op jit(solution)/shard_map/ppermute | solution.py:37
  78.4 23.6 %collective-permute-start.10 = (bf16[2,64,2048]{2,1,0:T(8,128)(2,1)S(1)}, bf16[2,64,2048]{2,1,0:T(8,128)(2,1)S(1)}, u32[]{:S(2)}, u32[]{:S(2)}) collective-permute-start(bf16[2,64,2048]{2,1,0:T(8,128)(2,1)S(1)} %get-tuple-element.266), channel_id=1, source_target_pairs={{0,16},{8,24},{16,0},{24,8},{1,17},{9,25},{17,1},{25,9},{2,18},{10... | collective-permute-start | bytes 1572872 | tf_op jit(solution)/shard_map/ppermute | solution.py:32
  78.7 24.1 %collective-permute-start.9 = (bf16[2,64,2048]{2,1,0:T(8,128)(2,1)S(1)}, bf16[2,64,2048]{2,1,0:T(8,128)(2,1)S(1)}, u32[]{:S(2)}, u32[]{:S(2)}) collective-permute-start(bf16[2,64,2048]{2,1,0:T(8,128)(2,1)S(1)} %get-tuple-element.265), channel_id=1, source_target_pairs={{0,8},{8,0},{16,24},{24,16},{1,9},{9,1},{17,25},{25,17},{2,10},{10... | collective-permute-start | bytes 1572872 | tf_op jit(solution)/shard_map/ppermute | solution.py:32
  80.7 51.2 %collective-permute-start.15 = (bf16[256,2176]{1,0:T(8,128)(2,1)S(1)}, bf16[256,2176]{1,0:T(8,128)(2,1)S(1)}, u32[]{:S(2)}, u32[]{:S(2)}) collective-permute-start(bf16[256,2176]{1,0:T(8,128)(2,1)S(1)} %get-tuple-element.271), channel_id=1, source_target_pairs={{0,8},{8,0},{16,24},{24,16},{1,9},{9,1},{17,25},{25,17},{2,10},{10... | collective-permute-start | bytes 3342344 | tf_op jit(solution)/shard_map/ppermute | solution.py:32
  81.0 50.8 %collective-permute-start.16 = (bf16[256,2176]{1,0:T(8,128)(2,1)S(1)}, bf16[256,2176]{1,0:T(8,128)(2,1)S(1)}, u32[]{:S(2)}, u32[]{:S(2)}) collective-permute-start(bf16[256,2176]{1,0:T(8,128)(2,1)S(1)} %get-tuple-element.271), channel_id=1, source_target_pairs={{0,16},{8,24},{16,0},{24,8},{1,17},{9,25},{17,1},{25,9},{2,18},{10... | collective-permute-start | bytes 3342344 | tf_op jit(solution)/shard_map/ppermute | solution.py:32
  109.4 22.3 %collective-permute-start.13 = (bf16[64,2048]{1,0:T(8,128)(2,1)S(1)}, bf16[64,2048]{1,0:T(8,128)(2,1)S(1)}, u32[]{:S(2)}, u32[]{:S(2)}) collective-permute-start(bf16[64,2048]{1,0:T(8,128)(2,1)S(1)} %get-tuple-element.624), channel_id=1, source_target_pairs={{0,4},{1,5},{2,6},{3,7},{4,0},{5,1},{6,2},{7,3},{8,12},{9,13},{10,... | collective-permute-start | bytes 786440 | tf_op jit(solution)/shard_map/ppermute | solution.py:37
  135.4 22.8 %collective-permute-start.18 = (bf16[64,2048]{1,0:T(8,128)(2,1)S(1)}, bf16[64,2048]{1,0:T(8,128)(2,1)S(1)}, u32[]{:S(2)}, u32[]{:S(2)}) collective-permute-start(bf16[64,2048]{1,0:T(8,128)(2,1)S(1)} %get-tuple-element.270), channel_id=1, source_target_pairs={{0,4},{1,5},{2,6},{3,7},{4,0},{5,1},{6,2},{7,3},{8,12},{9,13},{10,... | collective-permute-start | bytes 786440 | tf_op jit(solution)/shard_map/ppermute | solution.py:37
  135.4 22.8 %collective-permute-start.17 = (bf16[64,2048]{1,0:T(8,128)(2,1)S(1)}, bf16[64,2048]{1,0:T(8,128)(2,1)S(1)}, u32[]{:S(2)}, u32[]{:S(2)}) collective-permute-start(bf16[64,2048]{1,0:T(8,128)(2,1)S(1)} %get-tuple-element.270), channel_id=1, source_target_pairs={{0,2},{1,3},{2,0},{3,1},{4,6},{5,7},{6,4},{7,5},{8,10},{9,11},{10,... | collective-permute-start | bytes 786440 | tf_op jit(solution)/shard_map/ppermute | solution.py:37
  136.3 24.3 %collective-permute-start.20 = (bf16[256,2048]{1,0:T(8,128)(2,1)S(1)}, bf16[256,2048]{1,0:T(8,128)(2,1)S(1)}, u32[]{:S(2)}, u32[]{:S(2)}) collective-permute-start(bf16[256,2048]{1,0:T(8,128)(2,1)S(1)} %pad_maximum_fusion.4), channel_id=1, source_target_pairs={{0,8},{8,0},{16,24},{24,16},{1,9},{9,1},{17,25},{25,17},{2,10},{10... | collective-permute-start | bytes 3145736 | tf_op jit(solution)/shard_map/ppermute | solution.py:32
  137.5 23.3 %collective-permute-start.21 = (bf16[256,2048]{1,0:T(8,128)(2,1)S(1)}, bf16[256,2048]{1,0:T(8,128)(2,1)S(1)}, u32[]{:S(2)}, u32[]{:S(2)}) collective-permute-start(bf16[256,2048]{1,0:T(8,128)(2,1)S(1)} %pad_maximum_fusion.4), channel_id=1, source_target_pairs={{0,16},{8,24},{16,0},{24,8},{1,17},{9,25},{17,1},{25,9},{2,18},{10... | collective-permute-start | bytes 3145736 | tf_op jit(solution)/shard_map/ppermute | solution.py:32
  162.4 22.3 %collective-permute-start.23 = (bf16[128,2048]{1,0:T(8,128)(2,1)S(1)}, bf16[128,2048]{1,0:T(8,128)(2,1)S(1)}, u32[]{:S(2)}, u32[]{:S(2)}) collective-permute-start(bf16[128,2048]{1,0:T(8,128)(2,1)S(1)} %slice.672), channel_id=1, source_target_pairs={{0,16},{8,24},{16,0},{24,8},{1,17},{9,25},{17,1},{25,9},{2,18},{10... | collective-permute-start | bytes 1572872 | tf_op jit(solution)/shard_map/ppermute | solution.py:32
  163.0 22.5 %collective-permute-start.24 = (bf16[128,2048]{1,0:T(8,128)(2,1)S(1)}, bf16[128,2048]{1,0:T(8,128)(2,1)S(1)}, u32[]{:S(2)}, u32[]{:S(2)}) collective-permute-start(bf16[128,2048]{1,0:T(8,128)(2,1)S(1)} %slice.673), channel_id=1, source_target_pairs={{0,8},{8,0},{16,24},{24,16},{1,9},{9,1},{17,25},{25,17},{2,10},{10... | collective-permute-start | bytes 1572872 | tf_op jit(solution)/shard_map/ppermute | solution.py:32
  164.5 22.7 %collective-permute-start.25 = (bf16[128,2176]{1,0:T(8,128)(2,1)S(1)}, bf16[128,2176]{1,0:T(8,128)(2,1)S(1)}, u32[]{:S(2)}, u32[]{:S(2)}) collective-permute-start(bf16[128,2176]{1,0:T(8,128)(2,1)S(1)} %get-tuple-element.288), channel_id=1, source_target_pairs={{0,8},{8,0},{16,24},{24,16},{1,9},{9,1},{17,25},{25,17},{2,10},{10... | collective-permute-start | bytes 1671176 | tf_op jit(solution)/shard_map/ppermute | solution.py:32
  188.0 29.6 %collective-permute-start.27 = (bf16[1024,2176]{1,0:T(8,128)(2,1)}, bf16[1024,2176]{1,0:T(8,128)(2,1)}, u32[]{:S(2)}, u32[]{:S(2)}) collective-permute-start(bf16[1024,2176]{1,0:T(8,128)(2,1)} %constant_dynamic-update-slice_fusion.12.cot_ref.refs_4_), channel_id=1, source_target_pairs={{0,1},{1,0},{2,3},{3,2},{4,5},{5,4},{6,7},{7,6},{8,9},{9,8},{10,11... | collective-permute-start | bytes 13369352 | tf_op jit(solution)/shard_map/ppermute | solution.py:37
  188.0 29.6 %collective-permute-start.26 = (bf16[1024,2048]{1,0:T(8,128)(2,1)}, bf16[1024,2048]{1,0:T(8,128)(2,1)}, u32[]{:S(2)}, u32[]{:S(2)}) collective-permute-start(bf16[1024,2048]{1,0:T(8,128)(2,1)} %constant_dynamic-update-slice_fusion.14.moe_ref.refs_0_), channel_id=1, source_target_pairs={{0,1},{1,0},{2,3},{3,2},{4,5},{5,4},{6,7},{7,6},{8,9},{9,8},{10,11... | collective-permute-start | bytes 12582920 | tf_op jit(solution)/shard_map/ppermute | solution.py:37
  188.5 29.0 %collective-permute-start.28 = (bf16[256,2176]{1,0:T(8,128)(2,1)S(1)}, bf16[256,2176]{1,0:T(8,128)(2,1)}, u32[]{:S(2)}, u32[]{:S(2)}) collective-permute-start(bf16[256,2176]{1,0:T(8,128)(2,1)S(1)} %get-tuple-element.315), channel_id=1, source_target_pairs={{0,8},{8,0},{16,24},{24,16},{1,9},{9,1},{17,25},{25,17},{2,10},{10... | collective-permute-start | bytes 3342344 | tf_op jit(solution)/shard_map/ppermute | solution.py:32
  190.0 27.6 %collective-permute-start.29 = (bf16[256,2176]{1,0:T(8,128)(2,1)S(1)}, bf16[256,2176]{1,0:T(8,128)(2,1)}, u32[]{:S(2)}, u32[]{:S(2)}) collective-permute-start(bf16[256,2176]{1,0:T(8,128)(2,1)S(1)} %get-tuple-element.315), channel_id=1, source_target_pairs={{0,16},{8,24},{16,0},{24,8},{1,17},{9,25},{17,1},{25,9},{2,18},{10... | collective-permute-start | bytes 3342344 | tf_op jit(solution)/shard_map/ppermute | solution.py:32
  217.6 33.4 %collective-permute-start.30 = (bf16[256,2048]{1,0:T(8,128)(2,1)S(1)}, bf16[256,2048]{1,0:T(8,128)(2,1)S(1)}, u32[]{:S(2)}, u32[]{:S(2)}) collective-permute-start(bf16[256,2048]{1,0:T(8,128)(2,1)S(1)} %pad_maximum_fusion.5), channel_id=1, source_target_pairs={{0,8},{8,0},{16,24},{24,16},{1,9},{9,1},{17,25},{25,17},{2,10},{10... | collective-permute-start | bytes 3145736 | tf_op jit(solution)/shard_map/ppermute | solution.py:32
  219.1 31.9 %collective-permute-start.31 = (bf16[256,2048]{1,0:T(8,128)(2,1)S(1)}, bf16[256,2048]{1,0:T(8,128)(2,1)S(1)}, u32[]{:S(2)}, u32[]{:S(2)}) collective-permute-start(bf16[256,2048]{1,0:T(8,128)(2,1)S(1)} %pad_maximum_fusion.5), channel_id=1, source_target_pairs={{0,16},{8,24},{16,0},{24,8},{1,17},{9,25},{17,1},{25,9},{2,18},{10... | collective-permute-start | bytes 3145736 | tf_op jit(solution)/shard_map/ppermute | solution.py:32
  252.4 26.9 %collective-permute-start.32 = (bf16[128,2176]{1,0:T(8,128)(2,1)}, bf16[128,2176]{1,0:T(8,128)(2,1)S(1)}, u32[]{:S(2)}, u32[]{:S(2)}) collective-permute-start(bf16[128,2176]{1,0:T(8,128)(2,1)} %slice.674), channel_id=1, source_target_pairs={{0,16},{8,24},{16,0},{24,8},{1,17},{9,25},{17,1},{25,9},{2,18},{10... | collective-permute-start | bytes 1671176 | tf_op jit(solution)/shard_map/ppermute | solution.py:32
  253.9 25.5 %collective-permute-start.33 = (bf16[128,2176]{1,0:T(8,128)(2,1)}, bf16[128,2176]{1,0:T(8,128)(2,1)S(1)}, u32[]{:S(2)}, u32[]{:S(2)}) collective-permute-start(bf16[128,2176]{1,0:T(8,128)(2,1)} %slice.675), channel_id=1, source_target_pairs={{0,8},{8,0},{16,24},{24,16},{1,9},{9,1},{17,25},{25,17},{2,10},{10... | collective-permute-start | bytes 1671176 | tf_op jit(solution)/shard_map/ppermute | solution.py:32
  259.8 17.5 %collective-permute-start.34 = (bf16[128,2048]{1,0:T(8,128)(2,1)S(1)}, bf16[128,2048]{1,0:T(8,128)(2,1)S(1)}, u32[]{:S(2)}, u32[]{:S(2)}) collective-permute-start(bf16[128,2048]{1,0:T(8,128)(2,1)S(1)} %get-tuple-element.323), channel_id=1, source_target_pairs={{0,16},{8,24},{16,0},{24,8},{1,17},{9,25},{17,1},{25,9},{2,18},{10... | collective-permute-start | bytes 1572872 | tf_op jit(solution)/shard_map/ppermute | solution.py:32
  261.3 17.2 %collective-permute-start.35 = (bf16[128,2048]{1,0:T(8,128)(2,1)S(1)}, bf16[128,2048]{1,0:T(8,128)(2,1)S(1)}, u32[]{:S(2)}, u32[]{:S(2)}) collective-permute-start(bf16[128,2048]{1,0:T(8,128)(2,1)S(1)} %get-tuple-element.324), channel_id=1, source_target_pairs={{0,8},{8,0},{16,24},{24,16},{1,9},{9,1},{17,25},{25,17},{2,10},{10... | collective-permute-start | bytes 1572872 | tf_op jit(solution)/shard_map/ppermute | solution.py:32
  261.9 17.6 %collective-permute-start.36 = (bf16[1024,2176]{1,0:T(8,128)(2,1)}, bf16[1024,2176]{1,0:T(8,128)(2,1)S(1)}, u32[]{:S(2)}, u32[]{:S(2)}) collective-permute-start(bf16[1024,2176]{1,0:T(8,128)(2,1)} %get-tuple-element.326), channel_id=1, source_target_pairs={{0,1},{1,0},{2,3},{3,2},{4,5},{5,4},{6,7},{7,6},{8,9},{9,8},{10,11... | collective-permute-start | bytes 13369352 | tf_op jit(solution)/shard_map/ppermute | solution.py:37
  282.2 34.2 %collective-permute-start.38 = (bf16[1024,2176]{1,0:T(8,128)(2,1)S(1)}, bf16[1024,2176]{1,0:T(8,128)(2,1)}, u32[]{:S(2)}, u32[]{:S(2)}) collective-permute-start(bf16[1024,2176]{1,0:T(8,128)(2,1)S(1)} %constant_dynamic-update-slice_fusion.10.cot_ref.refs_6_), channel_id=1, source_target_pairs={{0,1},{1,0},{2,3},{3,2},{4,5},{5,4},{6,7},{7,6},{8,9},{9,8},{10,11... | collective-permute-start | bytes 13369352 | tf_op jit(solution)/shard_map/ppermute | solution.py:37
  282.2 34.2 %collective-permute-start.37 = (bf16[1024,2048]{1,0:T(8,128)(2,1)}, bf16[1024,2048]{1,0:T(8,128)(2,1)}, u32[]{:S(2)}, u32[]{:S(2)}) collective-permute-start(bf16[1024,2048]{1,0:T(8,128)(2,1)} %constant_dynamic-update-slice_fusion.8.moe_ref.refs_2_), channel_id=1, source_target_pairs={{0,1},{1,0},{2,3},{3,2},{4,5},{5,4},{6,7},{7,6},{8,9},{9,8},{10,11... | collective-permute-start | bytes 12582920 | tf_op jit(solution)/shard_map/ppermute | solution.py:37
  282.7 29.1 %collective-permute-start.39 = (bf16[256,2176]{1,0:T(8,128)(2,1)}, bf16[256,2176]{1,0:T(8,128)(2,1)}, u32[]{:S(2)}, u32[]{:S(2)}) collective-permute-start(bf16[256,2176]{1,0:T(8,128)(2,1)} %get-tuple-element.334), channel_id=1, source_target_pairs={{0,8},{8,0},{16,24},{24,16},{1,9},{9,1},{17,25},{25,17},{2,10},{10... | collective-permute-start | bytes 3342344 | tf_op jit(solution)/shard_map/ppermute | solution.py:32
  283.8 30.2 %collective-permute-start.40 = (bf16[256,2176]{1,0:T(8,128)(2,1)}, bf16[256,2176]{1,0:T(8,128)(2,1)}, u32[]{:S(2)}, u32[]{:S(2)}) collective-permute-start(bf16[256,2176]{1,0:T(8,128)(2,1)} %get-tuple-element.336), channel_id=1, source_target_pairs={{0,16},{8,24},{16,0},{24,8},{1,17},{9,25},{17,1},{25,9},{2,18},{10... | collective-permute-start | bytes 3342344 | tf_op jit(solution)/shard_map/ppermute | solution.py:32
  316.4 29.3 %collective-permute-start.41 = (bf16[128,2176]{1,0:T(8,128)(2,1)}, bf16[128,2176]{1,0:T(8,128)(2,1)S(1)}, u32[]{:S(2)}, u32[]{:S(2)}) collective-permute-start(bf16[128,2176]{1,0:T(8,128)(2,1)} %get-tuple-element.341), channel_id=1, source_target_pairs={{0,16},{8,24},{16,0},{24,8},{1,17},{9,25},{17,1},{25,9},{2,18},{10... | collective-permute-start | bytes 1671176 | tf_op jit(solution)/shard_map/ppermute | solution.py:32
  317.5 28.4 %collective-permute-start.42 = (bf16[128,2176]{1,0:T(8,128)(2,1)}, bf16[128,2176]{1,0:T(8,128)(2,1)S(1)}, u32[]{:S(2)}, u32[]{:S(2)}) collective-permute-start(bf16[128,2176]{1,0:T(8,128)(2,1)} %get-tuple-element.343), channel_id=1, source_target_pairs={{0,8},{8,0},{16,24},{24,16},{1,9},{9,1},{17,25},{25,17},{2,10},{10... | collective-permute-start | bytes 1671176 | tf_op jit(solution)/shard_map/ppermute | solution.py:32
  346.0 29.1 %collective-permute-start.47 = (bf16[1024,2048]{1,0:T(8,128)(2,1)S(1)}, bf16[1024,2048]{1,0:T(8,128)(2,1)S(1)}, u32[]{:S(2)}, u32[]{:S(2)}) collective-permute-start(bf16[1024,2048]{1,0:T(8,128)(2,1)S(1)} %copy-done.48), channel_id=1, source_target_pairs={{0,1},{1,0},{2,3},{3,2},{4,5},{5,4},{6,7},{7,6},{8,9},{9,8},{10,11... | collective-permute-start | bytes 12582920 | tf_op jit(solution)/shard_map/ppermute | solution.py:37
  346.1 31.7 %collective-permute-start.46 = (bf16[1024,2176]{1,0:T(8,128)(2,1)}, bf16[1024,2176]{1,0:T(8,128)(2,1)S(1)}, u32[]{:S(2)}, u32[]{:S(2)}) collective-permute-start(bf16[1024,2176]{1,0:T(8,128)(2,1)} %get-tuple-element.359), channel_id=1, source_target_pairs={{0,1},{1,0},{2,3},{3,2},{4,5},{5,4},{6,7},{7,6},{8,9},{9,8},{10,11... | collective-permute-start | bytes 13369352 | tf_op jit(solution)/shard_map/ppermute | solution.py:37
  350.0 24.2 %collective-permute-start.44 = (bf16[64,2176]{1,0:T(8,128)(2,1)S(1)}, bf16[64,2176]{1,0:T(8,128)(2,1)S(1)}, u32[]{:S(2)}, u32[]{:S(2)}) collective-permute-start(bf16[64,2176]{1,0:T(8,128)(2,1)S(1)} %get-tuple-element.356), channel_id=1, source_target_pairs={{0,4},{1,5},{2,6},{3,7},{4,0},{5,1},{6,2},{7,3},{8,12},{9,13},{10,... | collective-permute-start | bytes 835592 | tf_op jit(solution)/shard_map/ppermute | solution.py:37
  350.0 24.2 %collective-permute-start.43 = (bf16[64,2176]{1,0:T(8,128)(2,1)S(1)}, bf16[64,2176]{1,0:T(8,128)(2,1)S(1)}, u32[]{:S(2)}, u32[]{:S(2)}) collective-permute-start(bf16[64,2176]{1,0:T(8,128)(2,1)S(1)} %get-tuple-element.355), channel_id=1, source_target_pairs={{0,2},{1,3},{2,0},{3,1},{4,6},{5,7},{6,4},{7,5},{8,10},{9,11},{10,... | collective-permute-start | bytes 835592 | tf_op jit(solution)/shard_map/ppermute | solution.py:37
  379.9 29.4 %collective-permute-start.50 = (bf16[1024,2048]{1,0:T(8,128)(2,1)}, bf16[1024,2048]{1,0:T(8,128)(2,1)}, u32[]{:S(2)}, u32[]{:S(2)}) collective-permute-start(bf16[1024,2048]{1,0:T(8,128)(2,1)} %convolution_convert_fusion), channel_id=1, source_target_pairs={{0,1},{1,0},{2,3},{3,2},{4,5},{5,4},{6,7},{7,6},{8,9},{9,8},{10,11... | collective-permute-start | bytes 12582920 | tf_op jit(solution)/shard_map/ppermute | solution.py:37
  380.7 27.2 %collective-permute-start.48 = (bf16[256,2176]{1,0:T(8,128)(2,1)}, bf16[256,2176]{1,0:T(8,128)(2,1)S(1)}, u32[]{:S(2)}, u32[]{:S(2)}) collective-permute-start(bf16[256,2176]{1,0:T(8,128)(2,1)} %get-tuple-element.368), channel_id=1, source_target_pairs={{0,8},{8,0},{16,24},{24,16},{1,9},{9,1},{17,25},{25,17},{2,10},{10... | collective-permute-start | bytes 3342344 | tf_op jit(solution)/shard_map/ppermute | solution.py:32
  382.1 27.0 %collective-permute-start.49 = (bf16[256,2176]{1,0:T(8,128)(2,1)}, bf16[256,2176]{1,0:T(8,128)(2,1)S(1)}, u32[]{:S(2)}, u32[]{:S(2)}) collective-permute-start(bf16[256,2176]{1,0:T(8,128)(2,1)} %get-tuple-element.370), channel_id=1, source_target_pairs={{0,16},{8,24},{16,0},{24,8},{1,17},{9,25},{17,1},{25,9},{2,18},{10... | collective-permute-start | bytes 3342344 | tf_op jit(solution)/shard_map/ppermute | solution.py:32
  414.2 26.6 %collective-permute-start.54 = (bf16[128,2176]{1,0:T(8,128)(2,1)S(1)}, bf16[128,2176]{1,0:T(8,128)(2,1)S(1)}, u32[]{:S(2)}, u32[]{:S(2)}) collective-permute-start(bf16[128,2176]{1,0:T(8,128)(2,1)S(1)} %get-tuple-element.379), channel_id=1, source_target_pairs={{0,16},{8,24},{16,0},{24,8},{1,17},{9,25},{17,1},{25,9},{2,18},{10... | collective-permute-start | bytes 1671176 | tf_op jit(solution)/shard_map/ppermute | solution.py:32
  417.0 22.8 %collective-permute-start.52 = (bf16[64,2048]{1,0:T(8,128)(2,1)S(1)}, bf16[64,2048]{1,0:T(8,128)(2,1)S(1)}, u32[]{:S(2)}, u32[]{:S(2)}) collective-permute-start(bf16[64,2048]{1,0:T(8,128)(2,1)S(1)} %convert_element_type.754), channel_id=1, source_target_pairs={{0,16},{8,24},{16,0},{24,8},{1,17},{9,25},{17,1},{25,9},{2,18},{10... | collective-permute-start | bytes 786440 | tf_op jit(solution)/shard_map/ppermute | solution.py:32
  417.9 21.9 %collective-permute-start.51 = (bf16[64,2048]{1,0:T(8,128)(2,1)S(1)}, bf16[64,2048]{1,0:T(8,128)(2,1)S(1)}, u32[]{:S(2)}, u32[]{:S(2)}) collective-permute-start(bf16[64,2048]{1,0:T(8,128)(2,1)S(1)} %convert_element_type.754), channel_id=1, source_target_pairs={{0,8},{8,0},{16,24},{24,16},{1,9},{9,1},{17,25},{25,17},{2,10},{10... | collective-permute-start | bytes 786440 | tf_op jit(solution)/shard_map/ppermute | solution.py:32
  419.0 22.7 %collective-permute-start.55 = (bf16[128,2176]{1,0:T(8,128)(2,1)S(1)}, bf16[128,2176]{1,0:T(8,128)(2,1)S(1)}, u32[]{:S(2)}, u32[]{:S(2)}) collective-permute-start(bf16[128,2176]{1,0:T(8,128)(2,1)S(1)} %get-tuple-element.381), channel_id=1, source_target_pairs={{0,8},{8,0},{16,24},{24,16},{1,9},{9,1},{17,25},{25,17},{2,10},{10... | collective-permute-start | bytes 1671176 | tf_op jit(solution)/shard_map/ppermute | solution.py:32
  445.0 22.2 %collective-permute-start.57 = (bf16[64,2176]{1,0:T(8,128)(2,1)}, bf16[64,2176]{1,0:T(8,128)(2,1)}, u32[]{:S(2)}, u32[]{:S(2)}) collective-permute-start(bf16[64,2176]{1,0:T(8,128)(2,1)} %get-tuple-element.392), channel_id=1, source_target_pairs={{0,4},{1,5},{2,6},{3,7},{4,0},{5,1},{6,2},{7,3},{8,12},{9,13},{10,... | collective-permute-start | bytes 835592 | tf_op jit(solution)/shard_map/ppermute | solution.py:37
  445.0 22.2 %collective-permute-start.56 = (bf16[64,2176]{1,0:T(8,128)(2,1)}, bf16[64,2176]{1,0:T(8,128)(2,1)}, u32[]{:S(2)}, u32[]{:S(2)}) collective-permute-start(bf16[64,2176]{1,0:T(8,128)(2,1)} %get-tuple-element.391), channel_id=1, source_target_pairs={{0,2},{1,3},{2,0},{3,1},{4,6},{5,7},{6,4},{7,5},{8,10},{9,11},{10,... | collective-permute-start | bytes 835592 | tf_op jit(solution)/shard_map/ppermute | solution.py:37
  447.0 23.4 %collective-permute-start.59 = (bf16[256,2048]{1,0:T(8,128)(2,1)}, bf16[256,2048]{1,0:T(8,128)(2,1)}, u32[]{:S(2)}, u32[]{:S(2)}) collective-permute-start(bf16[256,2048]{1,0:T(8,128)(2,1)} %get-tuple-element.402), channel_id=1, source_target_pairs={{0,8},{8,0},{16,24},{24,16},{1,9},{9,1},{17,25},{25,17},{2,10},{10... | collective-permute-start | bytes 3145736 | tf_op jit(solution)/shard_map/ppermute | solution.py:32
  449.8 23.2 %collective-permute-start.60 = (bf16[256,2048]{1,0:T(8,128)(2,1)}, bf16[256,2048]{1,0:T(8,128)(2,1)S(1)}, u32[]{:S(2)}, u32[]{:S(2)}) collective-permute-start(bf16[256,2048]{1,0:T(8,128)(2,1)} %get-tuple-element.404), channel_id=1, source_target_pairs={{0,16},{8,24},{16,0},{24,8},{1,17},{9,25},{17,1},{25,9},{2,18},{10... | collective-permute-start | bytes 3145736 | tf_op jit(solution)/shard_map/ppermute | solution.py:32
  477.3 17.9 %collective-permute-start.63 = (bf16[64,2048]{1,0:T(8,128)(2,1)S(1)}, bf16[64,2048]{1,0:T(8,128)(2,1)S(1)}, u32[]{:S(2)}, u32[]{:S(2)}) collective-permute-start(bf16[64,2048]{1,0:T(8,128)(2,1)S(1)} %get-tuple-element.534), channel_id=1, source_target_pairs={{0,24},{8,16},{16,8},{24,0},{1,25},{9,17},{17,9},{25,1},{2,26},{10... | collective-permute-start | bytes 786440 | tf_op jit(solution)/shard_map/ppermute | solution.py:32
  510.6 119.8 %reduce-scatter.5.cloned.1.call-start = ((), (), s32[]{:S(2)}) async-start(), calls=%async_computation.3 | async-start | bytes 4718592 | tf_op jit(solution)/shard_map/reduce_scatter | solution.py:846
  542.8 186.5 %all-gather.2.cloned.1.call-start = ((), (), s32[]{:S(2)}) async-start(), calls=%async_computation.4 | async-start | bytes 9437184 | tf_op jit(solution)/shard_map/all_gather | solution.py:864
  547.7 21.0 %collective-permute-start.72 = (bf16[128,2048]{1,0:T(8,128)(2,1)S(1)}, bf16[128,2048]{1,0:T(8,128)(2,1)S(1)}, u32[]{:S(2)}, u32[]{:S(2)}) collective-permute-start(bf16[128,2048]{1,0:T(8,128)(2,1)S(1)} %pad_maximum_fusion.10), channel_id=1, source_target_pairs={{0,2},{1,3},{2,0},{3,1},{4,6},{5,7},{6,4},{7,5},{8,10},{9,11},{10,... | collective-permute-start | bytes 1572872 | tf_op jit(solution)/shard_map/ppermute | solution.py:37
  549.8 20.4 %collective-permute-start.76 = (bf16[64,2048]{1,0:T(8,128)(2,1)S(1)}, bf16[64,2048]{1,0:T(8,128)(2,1)S(1)}, u32[]{:S(2)}, u32[]{:S(2)}) collective-permute-start(bf16[64,2048]{1,0:T(8,128)(2,1)S(1)} %get-tuple-element.608), channel_id=1, source_target_pairs={{0,24},{8,16},{16,8},{24,0},{1,25},{9,17},{17,9},{25,1},{2,26},{10... | collective-permute-start | bytes 786440 | tf_op jit(solution)/shard_map/ppermute | solution.py:32
  551.4 20.9 %collective-permute-start.75 = (bf16[64,2048]{1,0:T(8,128)(2,1)S(1)}, bf16[64,2048]{1,0:T(8,128)(2,1)S(1)}, u32[]{:S(2)}, u32[]{:S(2)}) collective-permute-start(bf16[64,2048]{1,0:T(8,128)(2,1)S(1)} %get-tuple-element.609), channel_id=1, source_target_pairs={{0,16},{8,24},{16,0},{24,8},{1,17},{9,25},{17,1},{25,9},{2,18},{10... | collective-permute-start | bytes 786440 | tf_op jit(solution)/shard_map/ppermute | solution.py:32
  552.3 20.0 %collective-permute-start.74 = (bf16[64,2048]{1,0:T(8,128)(2,1)S(1)}, bf16[64,2048]{1,0:T(8,128)(2,1)S(1)}, u32[]{:S(2)}, u32[]{:S(2)}) collective-permute-start(bf16[64,2048]{1,0:T(8,128)(2,1)S(1)} %get-tuple-element.607), channel_id=1, source_target_pairs={{0,8},{8,0},{16,24},{24,16},{1,9},{9,1},{17,25},{25,17},{2,10},{10... | collective-permute-start | bytes 786440 | tf_op jit(solution)/shard_map/ppermute | solution.py:32
  553.4 29.4 %collective-permute-start.77 = (bf16[256,2048]{1,0:T(8,128)(2,1)S(1)}, bf16[256,2048]{1,0:T(8,128)(2,1)S(1)}, u32[]{:S(2)}, u32[]{:S(2)}) collective-permute-start(bf16[256,2048]{1,0:T(8,128)(2,1)S(1)} %copy-done.27), channel_id=1, source_target_pairs={{0,8},{8,0},{16,24},{24,16},{1,9},{9,1},{17,25},{25,17},{2,10},{10... | collective-permute-start | bytes 3145736 | tf_op jit(solution)/shard_map/ppermute | solution.py:32
  568.7 23.7 %collective-permute-start.78 = (bf16[256,2048]{1,0:T(8,128)(2,1)S(1)}, bf16[256,2048]{1,0:T(8,128)(2,1)S(1)}, u32[]{:S(2)}, u32[]{:S(2)}) collective-permute-start(bf16[256,2048]{1,0:T(8,128)(2,1)S(1)} %copy-done.26), channel_id=1, source_target_pairs={{0,16},{8,24},{16,0},{24,8},{1,17},{9,25},{17,1},{25,9},{2,18},{10... | collective-permute-start | bytes 3145736 | tf_op jit(solution)/shard_map/ppermute | solution.py:32
  698.7 18.8 %collective-permute-start.87 = (bf16[20,2048]{1,0:T(8,128)(2,1)S(1)}, bf16[20,2048]{1,0:T(8,128)(2,1)S(1)}, u32[]{:S(2)}, u32[]{:S(2)}) collective-permute-start(bf16[20,2048]{1,0:T(8,128)(2,1)S(1)} %add_convert_fusion.52), channel_id=1, source_target_pairs={{0,4},{1,5},{2,6},{3,7},{4,0},{5,1},{6,2},{7,3},{8,12},{9,13},{10,... | collective-permute-start | bytes 245768 | tf_op jit(solution)/shard_map/ppermute | solution.py:37
  698.7 21.0 %collective-permute-start.86 = (bf16[20,2048]{1,0:T(8,128)(2,1)S(1)}, bf16[20,2048]{1,0:T(8,128)(2,1)S(1)}, u32[]{:S(2)}, u32[]{:S(2)}) collective-permute-start(bf16[20,2048]{1,0:T(8,128)(2,1)S(1)} %add_convert_fusion.52), channel_id=1, source_target_pairs={{0,2},{1,3},{2,0},{3,1},{4,6},{5,7},{6,4},{7,5},{8,10},{9,11},{10,... | collective-permute-start | bytes 245768 | tf_op jit(solution)/shard_map/ppermute | solution.py:37
  701.0 18.9 %collective-permute-start.91 = (bf16[64,2048]{1,0:T(8,128)(2,1)S(1)}, bf16[64,2048]{1,0:T(8,128)(2,1)S(1)}, u32[]{:S(2)}, u32[]{:S(2)}) collective-permute-start(bf16[64,2048]{1,0:T(8,128)(2,1)S(1)} %get-tuple-element.601), channel_id=1, source_target_pairs={{0,24},{8,16},{16,8},{24,0},{1,25},{9,17},{17,9},{25,1},{2,26},{10... | collective-permute-start | bytes 786440 | tf_op jit(solution)/shard_map/ppermute | solution.py:32
  702.9 17.0 %collective-permute-start.90 = (bf16[64,2048]{1,0:T(8,128)(2,1)S(1)}, bf16[64,2048]{1,0:T(8,128)(2,1)S(1)}, u32[]{:S(2)}, u32[]{:S(2)}) collective-permute-start(bf16[64,2048]{1,0:T(8,128)(2,1)S(1)} %get-tuple-element.602), channel_id=1, source_target_pairs={{0,16},{8,24},{16,0},{24,8},{1,17},{9,25},{17,1},{25,9},{2,18},{10... | collective-permute-start | bytes 786440 | tf_op jit(solution)/shard_map/ppermute | solution.py:32
  (85 other events, 916.5 us)
Sparse Core Ops, SparseCore 0:
  510.7 57.9 reduce-scatter.2
  571.5 49.6 reduce-scatter.4
  632.7 96.5 all-gather.1
